TPU v7x, 32 devices: a whole 2x2x4 slice. The times are simulated.
32 devices in a mesh: group: 4 (over y, x), resp: 8 (over z, core).
Axes of the slice: x: 2, y: 2, z: 4, core: 2. Of those that a mesh axis runs over, the one named last changes fastest.
Arguments:
- prompt_hidden: bfloat16 [4, 512, 5120], P('group', 'resp'), may hold values from -48 to 48
- key_matrix: bfloat16 [5120, 512], P('group'), may hold values from -0.078125 to 0.078125
- key_gain: float32 [128], replicated, may hold values from 0.25 to 1.75
- prompt_token_value: bfloat16 [4, 512, 512], P('group', 'resp'), may hold values from -6 to 6
- resp_query: bfloat16 [4, 8, 256, 4096], P('group', 'resp'), may hold values from -120 to 120
- resp_key: bfloat16 [4, 8, 256, 512], P('group', 'resp'), may hold values from -4 to 4
- response_value: bfloat16 [4, 8, 256, 512], P('group', 'resp'), may hold values from -6 to 6
- grad_out: bfloat16 [4, 8, 256, 4096], P('group', 'resp'), may hold values from -48 to 48
- resp_length: int32 [4, 8], P('group', 'resp'), may hold values from 64 to 256, as said below
Outputs:
- grad_prompt_hidden: bfloat16 [4, 512, 5120], P('group', 'resp')
- grad_key_weight: float32 [5120, 512], P(('group', 'resp'))
- grad_prompt_value: bfloat16 [4, 512, 512], P('group', 'resp')
- grad_resp_query: bfloat16 [4, 8, 256, 4096], P('group', 'resp')
- grad_resp_key: bfloat16 [4, 8, 256, 512], P('group', 'resp')
- grad_resp_value: bfloat16 [4, 8, 256, 512], P('group', 'resp')
Inputs may be any that keep to these rules, and one draw needn't show every extreme that they name: Rows from resp_length to 256 of a response are padding.
All inputs are finite; a program needn't handle non-finite values.
Results may differ from a plain program's by a relative error of at most 0.0067.
Values may be sent and summed in bfloat16 or wider, within the bound.
No kernel may reach another device: no remote copies, remote signals or barrier semaphores. Data moves between devices by JAX's collectives and lax.ppermute only.
A program may use at most 128 MiB of HBM per device.

v0:
```python
from functools import partial

import jax
import jax.numpy as jnp
from jax import lax
from jax.sharding import PartitionSpec as P


def norm_keys(key_pre, key_gain):
    shaped = key_pre.reshape(key_pre.shape[:-1] + (-1, key_gain.shape[0]))
    inverse = lax.rsqrt(jnp.mean(shaped * shaped, axis=-1, keepdims=True) + 1e-06)
    return (shaped * inverse * key_gain).reshape(key_pre.shape)


def contract_rows(left, right):
    return lax.dot_general(
        left, right, (((0,), (0,)), ((), ())), preferred_element_type=jnp.float32
    )


def contract_cols(left, right):
    return lax.dot_general(
        left, right, (((1,), (1,)), ((), ())), preferred_element_type=jnp.float32
    )


def attend_block(
    query_rows,
    incoming_gradient,
    keys_part,
    values_part,
    length,
    first_row,
    prompt_len,
    heads_per_group,
    score_scale,
):
    row_count = query_rows.shape[0]
    scores = contract_cols(query_rows, keys_part) * score_scale
    row_pos = first_row + lax.iota(jnp.int32, row_count) // heads_per_group
    key_index = lax.iota(jnp.int32, keys_part.shape[0])
    visible = (key_index[None, :] < prompt_len) | (
        key_index[None, :] - prompt_len <= row_pos[:, None]
    )
    masked = jnp.where(visible, scores, -jnp.inf)
    row_max = jnp.max(masked, axis=-1, keepdims=True)
    exponent = jnp.where(visible, jnp.exp(masked - row_max), 0.0)
    attn_weights = exponent / jnp.sum(exponent, axis=-1, keepdims=True)
    attn_weights = jnp.where((row_pos < length)[:, None], attn_weights, 0.0)
    dprob = contract_cols(incoming_gradient, values_part)
    row_delta = jnp.sum(attn_weights * dprob, axis=-1, keepdims=True)
    dscore = (attn_weights * (dprob - row_delta) * score_scale).astype(jnp.bfloat16)
    weights_b = attn_weights.astype(jnp.bfloat16)
    query_grad = jnp.dot(dscore, keys_part, preferred_element_type=jnp.float32)
    key_grad = contract_rows(dscore, query_rows)
    value_grad = contract_rows(weights_b, incoming_gradient)
    return (query_grad, key_grad, value_grad)


def head_pass(length, prompt_len, heads_per_group, score_scale, block_rows, carry, items):
    query_head, upstream_head, key_head, value_head = items
    response_rows = query_head.shape[0]
    head_dim = key_head.shape[1]
    key_sum = jnp.zeros(key_head.shape, jnp.float32)
    value_sum = jnp.zeros(value_head.shape, jnp.float32)
    query_blocks = []
    for block_index in range(response_rows // block_rows):
        first_row = block_index * block_rows
        reach = prompt_len + first_row + block_rows
        block_queries = query_head[first_row : first_row + block_rows].reshape(
            block_rows * heads_per_group, head_dim
        )
        block_upstream = upstream_head[first_row : first_row + block_rows].reshape(
            block_rows * heads_per_group, head_dim
        )
        compute = partial(
            attend_block,
            first_row=first_row,
            prompt_len=prompt_len,
            heads_per_group=heads_per_group,
            score_scale=score_scale,
        )
        operands = (block_queries, block_upstream, key_head[:reach], value_head[:reach], length)
        query_grad, key_grad, value_grad = compute(*operands)
        query_blocks.append(query_grad.reshape(block_rows, heads_per_group * head_dim))
        key_sum = key_sum.at[:reach].add(key_grad)
        value_sum = value_sum.at[:reach].add(value_grad)
    return (carry, (jnp.concatenate(query_blocks, axis=0), key_sum, value_sum))


def shards(
    prompt_hidden,
    key_matrix,
    key_gain,
    prompt_token_value,
    resp_query,
    resp_key,
    response_value,
    grad_out,
    resp_length,
):
    block_rows = 128
    hidden = prompt_hidden[0]
    head_dim = key_gain.shape[0]
    key_value_width = key_matrix.shape[1]
    kv_heads = key_value_width // head_dim
    whole_weight = lax.all_gather(key_matrix, "group", axis=0, tiled=True)
    key_pre = jnp.dot(hidden, whole_weight, preferred_element_type=jnp.float32)
    prompt_key = norm_keys(key_pre, key_gain).astype(jnp.bfloat16)
    prompt_keys, prompt_values = (
        lax.all_gather(prompt_key, "resp", axis=0, tiled=True),
        lax.all_gather(prompt_token_value[0], "resp", axis=0, tiled=True),
    )
    prompt_len = prompt_keys.shape[0]
    keys_combined = jnp.concatenate([prompt_keys, resp_key[0, 0]], axis=0)
    values_combined = jnp.concatenate([prompt_values, response_value[0, 0]], axis=0)
    query_rows = resp_query[0, 0]
    incoming_gradient = grad_out[0, 0]
    length = resp_length[0, 0]
    response_rows = query_rows.shape[0]
    key_rows = keys_combined.shape[0]
    heads_per_group = query_rows.shape[1] // key_value_width
    score_scale = head_dim ** (-0.5)
    span_cols = heads_per_group * head_dim
    query_heads = query_rows.reshape(response_rows, kv_heads, span_cols).transpose(1, 0, 2)
    upstream_heads = incoming_gradient.reshape(response_rows, kv_heads, span_cols).transpose(
        1, 0, 2
    )
    key_heads = keys_combined.reshape(key_rows, kv_heads, head_dim).transpose(1, 0, 2)
    value_heads = values_combined.reshape(key_rows, kv_heads, head_dim).transpose(1, 0, 2)
    step = partial(head_pass, length, prompt_len, heads_per_group, score_scale, block_rows)
    _, outputs = lax.scan(
        step, jnp.zeros((), jnp.float32), (query_heads, upstream_heads, key_heads, value_heads)
    )
    query_stack, key_stack, value_stack = outputs
    query_grads = query_stack.transpose(1, 0, 2).reshape(response_rows, -1).astype(jnp.bfloat16)
    key_grads = key_stack.transpose(1, 0, 2).reshape(key_rows, key_value_width)
    value_grads = value_stack.transpose(1, 0, 2).reshape(key_rows, key_value_width)
    prompt_key_grad, prompt_value_grad = (
        lax.psum_scatter(key_grads[:prompt_len], "resp", scatter_dimension=0, tiled=True),
        lax.psum_scatter(value_grads[:prompt_len], "resp", scatter_dimension=0, tiled=True),
    )
    _, pullback = jax.vjp(lambda values: norm_keys(values, key_gain), key_pre)
    key_pre_grad = pullback(prompt_key_grad)[0].astype(jnp.bfloat16)
    grad_hidden = contract_cols(key_pre_grad, whole_weight).astype(jnp.bfloat16)
    grad_weight = lax.psum_scatter(
        contract_rows(hidden, key_pre_grad), ("group", "resp"), scatter_dimension=0, tiled=True
    )
    return (
        grad_hidden[None],
        grad_weight,
        prompt_value_grad.astype(jnp.bfloat16)[None],
        query_grads[None, None],
        key_grads[prompt_len:].astype(jnp.bfloat16)[None, None],
        value_grads[prompt_len:].astype(jnp.bfloat16)[None, None],
    )


def solution(mesh):
    return jax.shard_map(
        shards,
        mesh=mesh,
        in_specs=(
            P("group", "resp", None),
            P("group", None),
            P(),
            P("group", "resp", None),
            P("group", "resp", None, None),
            P("group", "resp", None, None),
            P("group", "resp", None, None),
            P("group", "resp", None, None),
            P("group", "resp"),
        ),
        out_specs=(
            P("group", "resp", None),
            P(("group", "resp"), None),
            P("group", "resp", None),
            P("group", "resp", None, None),
            P("group", "resp", None, None),
            P("group", "resp", None, None),
        ),
        check_vma=False,
    )
```

profile of v0, /device:TPU:0, one launch (start us, length us, event | category | flops | bytes accessed | tf_op | source)
XLA Modules:
  0.0 413.9 jit_solution(14796326800870153422)
XLA Ops:
  8.0 1.8 copy.46
  9.8 1.8 copy.49
  11.6 16.8 %all-gather = bf16[1,512,512]{2,1,0:T(8,128)(2,1)S(1)} all-gather(bf16[1,64,512]{2,1,0:T(8,128)(2,1)} %param.26), channel_id=2, replica_groups=mesh['group'=4,'resp'=8] {'resp'}, dimensions={1}, use_global_device_ids=true | all-gather | bytes 589824 | tf_op jit(solution)/shard_map/all_gather | solution.py:112
  29.4 2.5 copy.42
  31.9 4.2 %copy.47 = bf16[1,1,256,4096]{2,3,1,0:T(8,128)(2,1)} copy(bf16[1,1,256,4096]{3,2,1,0:T(8,128)(2,1)} %param.30) | data formatting | bytes 4194304 | tf_op args[7]
  36.0 38.0 %all-gather.3.cloned.1.call-done = bf16[5120,512]{1,0:T(8,128)(2,1)} async-done(((bf16[1280,512]{1,0:T(8,128)(2,1)}), bf16[5120,512]{1,0:T(8,128)(2,1)}) %all-gather.3.cloned.1.call-update) | async-done | bytes 5242896 | tf_op jit(solution)/shard_map/all_gather | solution.py:107
  74.0 7.8 %copy.43 = bf16[512,5120]{1,0:T(8,128)(2,1)} copy(bf16[512,5120]{0,1:T(8,128)(2,1)} %bitcast.151) | data formatting | bytes 10485760 | tf_op jit(solution)/shard_map/dot_general | solution.py:108
  81.9 4.4 %multiply_reduce_fusion.3 = (f32[64,4]{0,1:T(4,128)S(1)}, f32[64,4,128]{2,0,1:T(8,128)S(1)}) fusion(bf16[4,128,5120]{2,1,0:T(8,128)(2,1)} %bitcast.152, bf16[1,64,5120]{2,1,0:T(8,128)(2,1)S(1)} %copy-done), kind=kOutput, calls=%fused_computation.77 | convolution fusion | flops 335609600 | bytes 6030336 | tf_op jit(solution)/shard_map/dot_general | solution.py:108
  86.4 14.8 %all_gather.10 = bf16[512,512]{1,0:T(8,128)(2,1)S(1)} all-gather(bf16[64,512]{1,0:T(8,128)(2,1)S(1)} %copy_bitcast_fusion.1), channel_id=1, replica_groups=mesh['group'=4,'resp'=8] {'resp'}, dimensions={0}, use_global_device_ids=true | all-gather | bytes 589824 | tf_op jit(solution)/shard_map/all_gather | solution.py:111
  102.7 78.2 %while.23 = (s32[]{:T(128)}, bf16[4,256,1024]{2,1,0:T(8,128)(2,1)}, f32[4,768,128]{1,2,0:T(8,128)}, f32[4,768,128]{2,1,0:T(8,128)}, s32[]{:T(128)}, /*index=5*/b...) while((s32[]{:T(128)}, bf16[4,256,1024]{2,1,0:T(8,128)(2,1)}, ...), condition=%wide.region_8.9_spmd, body=%wide.region_1.8_spmd.sunk | while | flops 1885684480 | bytes 72769192 | solution.py:132
  109.0 1.4 multiply_reduce_fusion.7
  113.8 1.5 fusion.106
  115.2 1.7 multiply_reduce_fusion.6
  128.5 1.4 multiply_reduce_fusion.7
  133.3 1.5 fusion.106
  134.8 1.7 multiply_reduce_fusion.6
  148.1 1.4 multiply_reduce_fusion.7
  152.8 1.5 fusion.106
  154.3 1.7 multiply_reduce_fusion.6
  167.6 1.4 multiply_reduce_fusion.7
  172.4 1.5 fusion.106
  173.9 1.7 multiply_reduce_fusion.6
  183.6 2.4 copy_bitcast_fusion
  186.1 30.1 %reduce-scatter.10.cloned.1.call-done = f32[64,512]{1,0:T(8,128)} async-done(((f32[512,512]{1,0:T(8,128)}), f32[64,512]{1,0:T(8,128)}) %reduce-scatter.10.cloned.1.call-update) | async-done | bytes 131088
  217.6 5.4 %convolution_bitcast_fusion = f32[5120,512]{0,1:T(8,128)} fusion(bf16[1,64,5120]{2,1,0:T(8,128)(2,1)S(1)} %copy-done, bf16[4,8,8,128]{3,2,1,0:T(8,128)(2,1)S(1)} %fusion.40), kind=kOutput, calls=%fused_computation.60 | convolution fusion | flops 335544320 | bytes 11206656 | tf_op jit(solution)/shard_map/dot_general | solution.py:16
  223.0 11.4 %copy.67 = f32[5120,512]{1,0:T(8,128)} copy(f32[5120,512]{0,1:T(8,128)} %convolution_bitcast_fusion) | data formatting | bytes 20971520
  236.6 3.2 copy.59
  239.8 2.8 convert_element_type.93
  244.4 4.6 %reduce-scatter.8.cloned.1.call-done = f32[64,512]{1,0:T(8,128)} async-done(((f32[512,512]{1,0:T(8,128)}), f32[64,512]{1,0:T(8,128)}) %reduce-scatter.8.cloned.1.call-update) | async-done | bytes 131088 | tf_op jit(solution)/shard_map/reduce_scatter | solution.py:141
  249.0 1.5 convert_bitcast_fusion.1
  250.6 5.0 %fusion.34 = bf16[1,64,5120]{2,1,0:T(8,128)(2,1)} fusion(bf16[5120,512]{1,0:T(8,128)(2,1)} %all-gather.3.cloned.1.call-done, bf16[4,8,8,128]{3,2,1,0:T(8,128)(2,1)S(1)} %fusion.40), kind=kOutput, calls=%fused_computation.62 | convolution fusion | flops 335872000 | bytes 5963776 | tf_op jit(solution)/shard_map/dot_general | solution.py:22
  255.6 151.7 %reduce-scatter.12.cloned.1.call-done = f32[160,512]{1,0:T(8,128)} async-done(((f32[5120,512]{1,0:T(8,128)}), f32[160,512]{1,0:T(8,128)}) %reduce-scatter.12.cloned.1.call-update) | async-done | bytes 327696
  (184 shorter events, 70.6 us)
Async XLA Ops:
  7.2 74.7 %copy-start = (bf16[1,64,5120]{2,1,0:T(8,128)(2,1)S(1)}, bf16[1,64,5120]{2,1,0:T(8,128)(2,1)}, u32[]{:S(2)}) copy-start(bf16[1,64,5120]{2,1,0:T(8,128)(2,1)} %param.23) | copy-start | bytes 1966084
  7.2 22.2 %copy-start.1 = (bf16[1,1,256,4096]{3,2,1,0:T(8,128)(2,1)S(1)}, bf16[1,1,256,4096]{3,2,1,0:T(8,128)(2,1)}, u32[]{:S(2)}) copy-start(bf16[1,1,256,4096]{3,2,1,0:T(8,128)(2,1)} %param.27) | copy-start | bytes 6291460
  7.2 66.8 %all-gather.3.cloned.1.call-start = ((), (), s32[]{:S(2)}) async-start(), calls=%async_computation.3 | async-start | bytes 6553600 | tf_op jit(solution)/shard_map/all_gather | solution.py:107
  7.9 208.2 %reduce-scatter.10.cloned.1.call-start = ((), (), s32[]{:S(2)}) async-start(), calls=%async_computation.5 | async-start | bytes 1179648
  81.9 4.4 %copy-start.5 = (f32[128]{0:T(128)S(1)}, f32[128]{0:T(128)}, u32[]{:S(2)}) copy-start(f32[128]{0:T(128)} %param.25) | copy-start | bytes 1540
  81.9 19.5 %copy-start.2 = (bf16[1,512,512]{1,2,0:T(8,128)(2,1)S(1)}, bf16[1,512,512]{1,2,0:T(8,128)(2,1)}, u32[]{:S(2)}) copy-start(bf16[1,512,512]{1,2,0:T(8,128)(2,1)} %copy.48) | copy-start | bytes 1572868
  81.9 19.5 %copy-start.3 = (bf16[1,1,256,512]{2,3,1,0:T(8,128)(2,1)S(1)}, bf16[1,1,256,512]{2,3,1,0:T(8,128)(2,1)}, u32[]{:S(2)}) copy-start(bf16[1,1,256,512]{2,3,1,0:T(8,128)(2,1)} %copy.46) | copy-start | bytes 786436
  81.9 19.5 %copy-start.4 = (bf16[1,1,256,512]{2,3,1,0:T(8,128)(2,1)S(1)}, bf16[1,1,256,512]{2,3,1,0:T(8,128)(2,1)}, u32[]{:S(2)}) copy-start(bf16[1,1,256,512]{2,3,1,0:T(8,128)(2,1)} %copy.49) | copy-start | bytes 786436
  183.5 65.5 %reduce-scatter.8.cloned.1.call-start = ((), (), s32[]{:S(2)}) async-start(), calls=%async_computation.4 | async-start | bytes 1179648 | tf_op jit(solution)/shard_map/reduce_scatter | solution.py:141
  186.0 221.3 %reduce-scatter.12.cloned.1.call-start = ((), (), s32[]{:S(2)}) async-start(), calls=%async_computation.6 | async-start | bytes 10813440
Sparse Core Ops, SparseCore 0:
  9.9 64.1 all-gather.2
  183.7 32.4 reduce-scatter.9
  218.4 30.5 reduce-scatter.7
  251.8 155.5 reduce-scatter.11
where the time goes:
time: 415 us; the launch traced here: 414 us
  waiting for transfers between devices  225 us (54%)
  local copies, waits for them, and re-layouts  66.5 us (16%)
  matrix products  50.6 us (12%)
  blocking collectives  31.5 us (8%)
  other arithmetic  25 us (6%)
  between operations  13.9 us (3%)
    unnamed x6, waiting for transfers between devices  183 us
    all_gather x1, waiting for transfers between devices, shards(): whole_weight = lax.all_gather(key_matrix, 'group', axis=0, tiled=True)  38 us
    unnamed x20, local copies, waits for them, and re-layouts  24.9 us
    dot_general x17, matrix products, contract_cols(): lax.dot_general(left, right, (((1,), (1,)), ((), ())), preferred_element_...  24.5 us
    dot_general x17, matrix products, contract_rows(): lax.dot_general(left, right, (((0,), (0,)), ((), ())), preferred_element_...  17.1 us
    all_gather x1, blocking collectives, shards(): lax.all_gather(prompt_token_value[0], 'resp', axis=0, tiled=True)  16.8 us
    all_gather x1, blocking collectives, shards(): lax.all_gather(prompt_key, 'resp', axis=0, tiled=True)  14.8 us
    reduce_sum x8, other arithmetic, attend_block(): attn_weights = exponent / jnp.sum(exponent, axis=-1, keepdims=True)  9.92 us
  transfers between devices with their start and end apart: 4, of which 4 were waited for; matrix products, arithmetic and copies ran while one was open for 12% of the time, Pallas kernels for 0%

commit v1 on v0

v1 whole, which is shorter than its diff:
```python
from functools import partial

import jax
import jax.numpy as jnp
from jax import lax
from jax.experimental import pallas as pl
from jax.experimental.pallas import tpu as pltpu
from jax.sharding import PartitionSpec as P

F32, BF16 = jnp.float32, jnp.bfloat16
LOG2E = 1.4426950408889634


def norm_keys(key_pre, key_gain):
    shaped = key_pre.reshape(key_pre.shape[:-1] + (-1, key_gain.shape[0]))
    inverse = lax.rsqrt(jnp.mean(shaped * shaped, axis=-1, keepdims=True) + 1e-06)
    return (shaped * inverse * key_gain).reshape(key_pre.shape)


def dot(left, right, left_dim=1, right_dim=0):
    dims = (((left_dim,), (right_dim,)), ((), ()))
    return lax.dot_general(left, right, dims, preferred_element_type=F32)


def attend_kernel(
    length_ref, query_ref, upstream_ref, prompt_key_ref, prompt_value_ref, key_ref, value_ref,
    query_grad_ref, prompt_key_grad_ref, prompt_value_grad_ref, key_grad_ref, value_grad_ref,
):
    rows = query_ref.shape[0]
    prompt_len, head_dim = prompt_key_ref.shape
    heads = query_ref.shape[1] // head_dim
    scale = head_dim ** -0.5
    keys = jnp.concatenate([prompt_key_ref[...], key_ref[...]], axis=0)
    values = jnp.concatenate([prompt_value_ref[...], value_ref[...]], axis=0)
    keys_t, values_t = keys.T, values.T
    stacked = heads * rows
    live = lax.broadcasted_iota(jnp.int32, (stacked, 1), 0) % rows < length_ref[0, 0]
    own = (stacked, key_ref.shape[0])
    visible = lax.broadcasted_iota(jnp.int32, own, 1) <= lax.broadcasted_iota(jnp.int32, own, 0) % rows

    def head(ref, index):
        return ref[:, index * head_dim : (index + 1) * head_dim]

    queries = jnp.concatenate([head(query_ref, i) for i in range(heads)], axis=0)
    upstream = jnp.concatenate([head(upstream_ref, i) for i in range(heads)], axis=0)
    prompt_scores = dot(queries, keys_t[:, :prompt_len])
    own_scores = jnp.where(visible, dot(queries, keys_t[:, prompt_len:]), -jnp.inf)
    row_max = jnp.maximum(
        jnp.max(prompt_scores, axis=1, keepdims=True), jnp.max(own_scores, axis=1, keepdims=True)
    )
    scores = jnp.concatenate([prompt_scores, own_scores], axis=1)
    unit = scale * LOG2E
    exponent = jnp.exp2(scores * unit - row_max * unit)
    dprob = dot(upstream, values_t)
    total = jnp.sum(exponent, axis=1, keepdims=True)
    weighted = jnp.sum(exponent * dprob, axis=1, keepdims=True)
    inverse = jnp.where(live, 1.0 / total, 0.0)
    row_delta = weighted * inverse
    weights = (exponent * inverse).astype(BF16)
    dscore = (exponent * ((dprob - row_delta) * (inverse * scale))).astype(BF16)
    query_grad = dot(dscore, keys).astype(BF16)
    for i in range(heads):
        query_grad_ref[:, i * head_dim : (i + 1) * head_dim] = query_grad[i * rows : (i + 1) * rows]
    value_grad = dot(upstream.T, weights).T
    key_grad = dot(queries.T, dscore).T
    prompt_key_grad_ref[...] = key_grad[:prompt_len]
    prompt_value_grad_ref[...] = value_grad[:prompt_len]
    key_grad_ref[...] = key_grad[prompt_len:].astype(BF16)
    value_grad_ref[...] = value_grad[prompt_len:].astype(BF16)


def attend(length, queries, upstream, prompt_keys, prompt_values, keys, values, head_dim):
    rows, width = queries.shape
    prompt_len, kv_width = prompt_keys.shape
    kv_heads = kv_width // head_dim

    def block(count, columns):
        return pl.BlockSpec((count, columns), lambda i: (0, i))

    query_block = block(rows, width // kv_heads)
    prompt_block, own_block = block(prompt_len, head_dim), block(rows, head_dim)
    macs = 5 * rows * width * (prompt_len + rows)
    return pl.pallas_call(
        attend_kernel,
        grid=(kv_heads,),
        in_specs=[
            pl.BlockSpec(memory_space=pltpu.SMEM),
            query_block, query_block, prompt_block, prompt_block, own_block, own_block,
        ],
        out_specs=[query_block, prompt_block, prompt_block, own_block, own_block],
        out_shape=[
            jax.ShapeDtypeStruct((rows, width), BF16),
            jax.ShapeDtypeStruct((prompt_len, kv_width), F32),
            jax.ShapeDtypeStruct((prompt_len, kv_width), F32),
            jax.ShapeDtypeStruct((rows, kv_width), BF16),
            jax.ShapeDtypeStruct((rows, kv_width), BF16),
        ],
        compiler_params=pltpu.CompilerParams(vmem_limit_bytes=56 * 2**20),
        cost_estimate=pl.CostEstimate(flops=2 * macs, bytes_accessed=10**7, transcendentals=0),
        name="attend",
    )(length, queries, upstream, prompt_keys, prompt_values, keys, values)


def swap(array, axis, size, distance):
    return lax.ppermute(array, axis, [(i, i ^ distance) for i in range(size)])


def spread(block, size):
    near = [block] + [swap(block, "resp", size, k) for k in range(2, size, 2)]
    near = jnp.concatenate(near, axis=0)
    return jnp.concatenate([near, swap(near, "resp", size, 1)], axis=0)


def collect(sums, size):
    half = sums.shape[0] // 2
    rows = sums.shape[0] // size
    near = sums[:half] + swap(sums[half:], "resp", size, 1)
    total = near[:rows]
    for p in range(1, size // 2):
        total = total + swap(near[p * rows : (p + 1) * rows], "resp", size, 2 * p)
    return total


def shards(
    groups, responses, prompt_hidden, key_matrix, key_gain, prompt_token_value,
    resp_query, resp_key, response_value, grad_out, resp_length,
):
    hidden = prompt_hidden[0]
    tokens = hidden.shape[0]
    depth, kv_width = key_matrix.shape
    head_dim = key_gain.shape[0]
    group, resp = lax.axis_index("group"), lax.axis_index("resp")

    prompt_values = spread(prompt_token_value[0], responses)

    columns, partials = [], []
    for k in range(groups):
        piece = lax.dynamic_slice(hidden, (0, (group ^ k) * depth), (tokens, depth))
        columns.append(swap(piece, "group", groups, k) if k else piece)
        partials.append(dot(columns[k], key_matrix))
    key_pre = partials[0]
    for k in range(1, groups):
        key_pre = key_pre + swap(partials[k], "group", groups, k)
    prompt_key = norm_keys(key_pre, key_gain).astype(BF16)
    prompt_keys = spread(prompt_key, responses)

    chips = responses // 2
    chip_rows = depth // chips
    hidden_t = jnp.concatenate(columns, axis=0).T
    taken = []
    for k in range(0, responses, 2):
        piece = lax.dynamic_slice(
            hidden_t, (((resp ^ k) // 2) * chip_rows, 0), (chip_rows, hidden_t.shape[1])
        )
        taken.append(swap(piece, "resp", responses, k) if k else piece)

    weight = lax.all_gather(key_matrix, "group", axis=0, tiled=True)

    query_grad, key_sums, value_sums, key_grad, value_grad = attend(
        resp_length, resp_query[0, 0], grad_out[0, 0], prompt_keys, prompt_values,
        resp_key[0, 0], response_value[0, 0], head_dim,
    )
    prompt_key_grad = collect(key_sums, responses)
    _, pullback = jax.vjp(lambda values: norm_keys(values, key_gain), key_pre)
    key_pre_grad = pullback(prompt_key_grad)[0].astype(BF16)

    near = [key_pre_grad] + [swap(key_pre_grad, "resp", responses, k) for k in range(2, responses, 2)]
    near = jnp.stack(near, axis=0)
    partial_weight = 0.0
    for k in range(groups):
        block = swap(near, "group", groups, k) if k else near
        for p in range(chips):
            partial_weight += dot(taken[p][:, k * tokens : (k + 1) * tokens], block[p])
    half = chip_rows // 2
    core = resp % 2
    mine = lax.dynamic_slice(partial_weight, (core * half, 0), (half, kv_width))
    other = lax.dynamic_slice(partial_weight, ((1 - core) * half, 0), (half, kv_width))
    grad_weight = mine + swap(other, "resp", responses, 1)

    prompt_value_grad = collect(value_sums, responses)
    grad_hidden = dot(key_pre_grad, weight, 1, 1).astype(BF16)
    return (
        grad_hidden[None],
        grad_weight,
        prompt_value_grad.astype(BF16)[None],
        query_grad[None, None],
        key_grad[None, None],
        value_grad[None, None],
    )


def solution(mesh):
    return jax.shard_map(
        partial(shards, mesh.shape["group"], mesh.shape["resp"]),
        mesh=mesh,
        in_specs=(
            P("group", "resp", None),
            P("group", None),
            P(),
            P("group", "resp", None),
            P("group", "resp", None, None),
            P("group", "resp", None, None),
            P("group", "resp", None, None),
            P("group", "resp", None, None),
            P("group", "resp"),
        ),
        out_specs=(
            P("group", "resp", None),
            P(("group", "resp"), None),
            P("group", "resp", None),
            P("group", "resp", None, None),
            P("group", "resp", None, None),
            P("group", "resp", None, None),
        ),
        check_vma=False,
    )
```

time: 415 us -> 150 us (0.36)
  the two profiles are of different devices: /device:TPU:0 before, /device:TPU:17 now
where the time goes in v1:
time: 150 us
  starting transfers between devices  51.1 us (34%)
  waiting for transfers between devices  41.1 us (27%)
  Pallas kernels  21.3 us (14%)
  between operations  15.1 us (10%)
  matrix products  10.9 us (7%)
  local copies, waits for them, and re-layouts  8.53 us (6%)
  other arithmetic  2.17 us (1%)
    ppermute x32, starting transfers between devices, swap(): return lax.ppermute(array, axis, [(i, i ^ distance) for i in range(size)])  51 us
    ppermute x32, waiting for transfers between devices, swap(): return lax.ppermute(array, axis, [(i, i ^ distance) for i in range(size)])  41.1 us
    pallas_call x1, Pallas kernels, attend(): pl.pallas_call(attend_kernel, grid=(kv_heads,), in_specs=[pl.BlockSpec(me...  21.3 us
    dot_general x21, matrix products, dot(): return lax.dot_general(left, right, dims, preferred_element_type=F32)  10.9 us
    unnamed x19, local copies, waits for them, and re-layouts  3.31 us
  transfers between devices with their start and end apart: 33, of which 16 were waited for; matrix products, arithmetic and copies ran while one was open for 10% of the time, Pallas kernels for 14%

profile of v1, /device:TPU:17, one launch (start us, length us, event | category | flops | bytes accessed | tf_op | source)
XLA Modules:
  0.0 150.1 jit_solution(18117664847814634905)
XLA Ops:
  7.2 1.4 collective-permute-start.10
  8.6 1.3 collective-permute-start.12
  9.9 1.3 dynamic-slice_bitcast_fusion.6
  11.2 1.3 collective-permute-start
  12.5 1.2 collective-permute-start.2
  15.7 2.4 %collective-permute-start.13 = (bf16[256,512]{1,0:T(8,128)(2,1)S(1)}, bf16[256,512]{1,0:T(8,128)(2,1)S(1)}, u32[]{:S(2)}, u32[]{:S(2)}) collective-permute-start(bf16[256,512]{1,0:T(8,128)(2,1)S(1)} %pad_maximum_fusion.2), channel_id=1, source_target_pairs={{0,1},{1,0},{2,3},{3,2},{4,5},{5,4},{6,7},{7,6},{8,9},{9,8},{10,11... | collective-permute-start | bytes 786440 | tf_op jit(solution)/shard_map/ppermute | solution.py:105
  19.1 1.3 collective-permute-start.1
  20.7 1.3 collective-permute-start.3
  25.1 2.7 %collective-permute-done.5 = f32[64,512]{1,0:T(8,128)S(1)} collective-permute-done((f32[64,512]{1,0:T(8,128)S(1)}, f32[64,512]{1,0:T(8,128)S(1)}, u32[]{:S(2)}, u32[]{:S(2)}) %collective-permute-start.5) | collective-permute-done | bytes 131104 | tf_op jit(solution)/shard_map/ppermute | solution.py:105
  28.4 4.6 %collective-permute-start.6 = (bf16[64,512]{1,0:T(8,128)(2,1)S(1)}, bf16[64,512]{1,0:T(8,128)(2,1)S(1)}, u32[]{:S(2)}, u32[]{:S(2)}) collective-permute-start(bf16[64,512]{1,0:T(8,128)(2,1)S(1)} %get-tuple-element.17), channel_id=1, source_target_pairs={{0,2},{1,3},{2,0},{3,1},{4,6},{5,7},{6,4},{7,5},{8,10},{9,11},{10,... | collective-permute-start | bytes 196616 | tf_op jit(solution)/shard_map/ppermute | solution.py:105
  33.0 1.3 collective-permute-start.8
  35.1 2.1 %collective-permute-done.7 = bf16[64,512]{1,0:T(8,128)(2,1)S(1)} collective-permute-done((bf16[64,512]{1,0:T(8,128)(2,1)S(1)}, bf16[64,512]{1,0:T(8,128)(2,1)S(1)}, u32[]{:S(2)}, u32[]{:S(2)}) %collective-permute-start.7) | collective-permute-done | bytes 65568 | tf_op jit(solution)/shard_map/ppermute | solution.py:105
  38.2 4.3 %collective-permute-start.9 = (bf16[256,512]{1,0:T(8,128)(2,1)S(1)}, bf16[256,512]{1,0:T(8,128)(2,1)S(1)}, u32[]{:S(2)}, u32[]{:S(2)}) collective-permute-start(bf16[256,512]{1,0:T(8,128)(2,1)S(1)} %pad_maximum_fusion.1), channel_id=1, source_target_pairs={{0,1},{1,0},{2,3},{3,2},{4,5},{5,4},{6,7},{7,6},{8,9},{9,8},{10,11... | collective-permute-start | bytes 786440 | tf_op jit(solution)/shard_map/ppermute | solution.py:105
  44.5 21.3 %attend.1 = (bf16[256,4096]{1,0:T(8,128)(2,1)}, f32[512,512]{1,0:T(8,128)}, f32[512,512]{1,0:T(8,128)}, bf16[256,512]{1,0:T(8,128)(2,1)}, bf16[256,512]{1,0:T(8,128)(2,1)}) custom-call(s32[1,1]{1,0:T(1,128)S(6)} %copy.35.length_ref, bf16[256,4096]{1,0:T(8,128)(2,1)} %bitcast.112, bf16[256,4096]{1,0:T(8,128)(2,1)} %bitcast.113, bf16[512,512]{1,0:T(8,128)(2,1)} %copy-done.4, ...), custom_call_target="tpu_custom_call" | custom-call | flops 8053063680 | bytes 10000000 | tf_op jit(solution)/shard_map/attend/pallas_call | solution.py:83
  65.8 1.2 slice.121
  68.9 1.9 %collective-permute-start.18 = (bf16[320,256]{0,1:T(8,128)(2,1)}, bf16[320,256]{0,1:T(8,128)(2,1)S(1)}, u32[]{:S(2)}, u32[]{:S(2)}) collective-permute-start(bf16[320,256]{0,1:T(8,128)(2,1)} %get-tuple-element.21), channel_id=1, source_target_pairs={{0,2},{1,3},{2,0},{3,1},{4,6},{5,7},{6,4},{7,5},{8,10},{9,11},{10,... | collective-permute-start | bytes 491528 | tf_op jit(solution)/shard_map/ppermute | solution.py:105
  70.8 1.6 %collective-permute-start.20 = (bf16[320,256]{0,1:T(8,128)(2,1)}, bf16[320,256]{0,1:T(8,128)(2,1)S(1)}, u32[]{:S(2)}, u32[]{:S(2)}) collective-permute-start(bf16[320,256]{0,1:T(8,128)(2,1)} %get-tuple-element.20), channel_id=1, source_target_pairs={{0,4},{1,5},{2,6},{3,7},{4,0},{5,1},{6,2},{7,3},{8,12},{9,13},{10,... | collective-permute-start | bytes 491528 | tf_op jit(solution)/shard_map/ppermute | solution.py:105
  72.5 1.5 %collective-permute-start.15 = (f32[64,512]{1,0:T(8,128)S(1)}, f32[64,512]{1,0:T(8,128)S(1)}, u32[]{:S(2)}, u32[]{:S(2)}) collective-permute-start(f32[64,512]{1,0:T(8,128)S(1)} %get-tuple-element.29), channel_id=1, source_target_pairs={{0,2},{1,3},{2,0},{3,1},{4,6},{5,7},{6,4},{7,5},{8,10},{9,11},{10,... | collective-permute-start | bytes 393224 | tf_op jit(solution)/shard_map/ppermute | solution.py:105
  74.1 1.3 collective-permute-start.17
  75.4 7.6 %collective-permute-done.15 = f32[64,512]{1,0:T(8,128)S(1)} collective-permute-done((f32[64,512]{1,0:T(8,128)S(1)}, f32[64,512]{1,0:T(8,128)S(1)}, u32[]{:S(2)}, u32[]{:S(2)}) %collective-permute-start.15) | collective-permute-done | bytes 131104 | tf_op jit(solution)/shard_map/ppermute | solution.py:105
  83.0 1.9 %collective-permute-start.22 = (bf16[320,256]{0,1:T(8,128)(2,1)}, bf16[320,256]{0,1:T(8,128)(2,1)S(1)}, u32[]{:S(2)}, u32[]{:S(2)}) collective-permute-start(bf16[320,256]{0,1:T(8,128)(2,1)} %get-tuple-element.19), channel_id=1, source_target_pairs={{0,6},{1,7},{2,4},{3,5},{4,2},{5,3},{6,0},{7,1},{8,14},{9,15},{10,... | collective-permute-start | bytes 491528 | tf_op jit(solution)/shard_map/ppermute | solution.py:105
  84.9 8.5 %collective-permute-done.16 = f32[64,512]{1,0:T(8,128)S(1)} collective-permute-done((f32[64,512]{1,0:T(8,128)S(1)}, f32[64,512]{1,0:T(8,128)S(1)}, u32[]{:S(2)}, u32[]{:S(2)}) %collective-permute-start.16) | collective-permute-done | bytes 131104 | tf_op jit(solution)/shard_map/ppermute | solution.py:105
  93.5 3.8 %collective-permute-done.17 = f32[64,512]{1,0:T(8,128)S(1)} collective-permute-done((f32[64,512]{1,0:T(8,128)S(1)}, f32[64,512]{1,0:T(8,128)S(1)}, u32[]{:S(2)}, u32[]{:S(2)}) %collective-permute-start.17) | collective-permute-done | bytes 131104 | tf_op jit(solution)/shard_map/ppermute | solution.py:105
  98.0 1.5 %collective-permute-start.29 = (f32[64,512]{1,0:T(8,128)S(1)}, f32[64,512]{1,0:T(8,128)S(1)}, u32[]{:S(2)}, u32[]{:S(2)}) collective-permute-start(f32[64,512]{1,0:T(8,128)S(1)} %get-tuple-element.26), channel_id=1, source_target_pairs={{0,2},{1,3},{2,0},{3,1},{4,6},{5,7},{6,4},{7,5},{8,10},{9,11},{10,... | collective-permute-start | bytes 393224 | tf_op jit(solution)/shard_map/ppermute | solution.py:105
  101.4 1.2 collective-permute-start.23
  102.8 1.5 %collective-permute-done.21 = bf16[64,512]{1,0:T(8,128)(2,1)S(1)} collective-permute-done((bf16[64,512]{1,0:T(8,128)(2,1)S(1)}, bf16[64,512]{1,0:T(8,128)(2,1)S(1)}, u32[]{:S(2)}, u32[]{:S(2)}) %collective-permute-start.21) | collective-permute-done | bytes 65568 | tf_op jit(solution)/shard_map/ppermute | solution.py:105
  105.6 1.7 %collective-permute-start.31 = (f32[64,512]{1,0:T(8,128)S(1)}, f32[64,512]{1,0:T(8,128)S(1)}, u32[]{:S(2)}, u32[]{:S(2)}) collective-permute-start(f32[64,512]{1,0:T(8,128)S(1)} %get-tuple-element.27), channel_id=1, source_target_pairs={{0,6},{1,7},{2,4},{3,5},{4,2},{5,3},{6,0},{7,1},{8,14},{9,15},{10,... | collective-permute-start | bytes 393224 | tf_op jit(solution)/shard_map/ppermute | solution.py:105
  108.3 4.7 %collective-permute-done.25 = bf16[4,64,512]{2,1,0:T(8,128)(2,1)S(1)} collective-permute-done((bf16[4,64,512]{2,1,0:T(8,128)(2,1)S(1)}, bf16[4,64,512]{2,1,0:T(8,128)(2,1)S(1)}, u32[]{:S(2)}, u32[]{:S(2)}) %collective-permute-start.25) | collective-permute-done | bytes 262176 | tf_op jit(solution)/shard_map/ppermute | solution.py:105
  115.0 3.1 %collective-permute-done.24 = bf16[4,64,512]{2,1,0:T(8,128)(2,1)S(1)} collective-permute-done((bf16[4,64,512]{2,1,0:T(8,128)(2,1)S(1)}, bf16[4,64,512]{2,1,0:T(8,128)(2,1)S(1)}, u32[]{:S(2)}, u32[]{:S(2)}) %collective-permute-start.24) | collective-permute-done | bytes 262176 | tf_op jit(solution)/shard_map/ppermute | solution.py:105
  119.8 1.3 collective-permute-done.26
  122.8 13.4 %collective-permute-start.27 = (f32[160,512]{1,0:T(8,128)S(1)}, f32[160,512]{1,0:T(8,128)S(1)}, u32[]{:S(2)}, u32[]{:S(2)}) collective-permute-start(f32[160,512]{1,0:T(8,128)S(1)} %constant_dynamic-slice_fusion), channel_id=1, source_target_pairs={{0,1},{1,0},{2,3},{3,2},{4,5},{5,4},{6,7},{7,6},{8,9},{9,8},{10,11... | collective-permute-start | bytes 983048 | tf_op jit(solution)/shard_map/ppermute | solution.py:105
  138.3 5.0 %fusion = bf16[1,64,5120]{2,1,0:T(8,128)(2,1)} fusion(bf16[64,512]{1,0:T(8,128)(2,1)S(1)} %fusion.14, bf16[5120,512]{1,0:T(8,128)(2,1)} %all-gather.2.cloned.1.call-done), kind=kOutput, calls=%fused_computation.1 | convolution fusion | flops 335872000 | bytes 5963776 | tf_op jit(solution)/shard_map/dot_general | solution.py:22
  (110 shorter events, 24.5 us)
Async XLA Ops:
  7.2 131.1 %all-gather.2.cloned.1.call-start = ((), (), s32[]{:S(2)}) async-start(), calls=%async_computation | async-start | bytes 6553600 | tf_op jit(solution)/shard_map/all_gather | solution.py:157
  7.2 8.2 %collective-permute-start.10 = (bf16[64,512]{1,0:T(8,128)(2,1)}, bf16[64,512]{1,0:T(8,128)(2,1)S(1)}, u32[]{:S(2)}, u32[]{:S(2)}) collective-permute-start(bf16[64,512]{1,0:T(8,128)(2,1)} %bitcast.108), channel_id=1, source_target_pairs={{0,2},{1,3},{2,0},{3,1},{4,6},{5,7},{6,4},{7,5},{8,10},{9,11},{10,... | collective-permute-start | bytes 196616 | tf_op jit(solution)/shard_map/ppermute | solution.py:105
  8.6 7.1 %collective-permute-start.11 = (bf16[64,512]{1,0:T(8,128)(2,1)}, bf16[64,512]{1,0:T(8,128)(2,1)S(1)}, u32[]{:S(2)}, u32[]{:S(2)}) collective-permute-start(bf16[64,512]{1,0:T(8,128)(2,1)} %bitcast.109), channel_id=1, source_target_pairs={{0,4},{1,5},{2,6},{3,7},{4,0},{5,1},{6,2},{7,3},{8,12},{9,13},{10,... | collective-permute-start | bytes 196616 | tf_op jit(solution)/shard_map/ppermute | solution.py:105
  8.6 7.1 %collective-permute-start.12 = (bf16[64,512]{1,0:T(8,128)(2,1)}, bf16[64,512]{1,0:T(8,128)(2,1)S(1)}, u32[]{:S(2)}, u32[]{:S(2)}) collective-permute-start(bf16[64,512]{1,0:T(8,128)(2,1)} %bitcast.110), channel_id=1, source_target_pairs={{0,6},{1,7},{2,4},{3,5},{4,2},{5,3},{6,0},{7,1},{8,14},{9,15},{10,... | collective-permute-start | bytes 196616 | tf_op jit(solution)/shard_map/ppermute | solution.py:105
  11.2 7.5 %collective-permute-start = (bf16[64,1280]{1,0:T(8,128)(2,1)S(1)}, bf16[64,1280]{1,0:T(8,128)(2,1)S(1)}, u32[]{:S(2)}, u32[]{:S(2)}) collective-permute-start(bf16[64,1280]{1,0:T(8,128)(2,1)S(1)} %get-tuple-element.22), channel_id=1, source_target_pairs={{0,8},{8,0},{16,24},{24,16},{1,9},{9,1},{17,25},{25,17},{2,10},{10... | collective-permute-start | bytes 491528 | tf_op jit(solution)/shard_map/ppermute | solution.py:105
  12.5 7.9 %collective-permute-start.2 = (bf16[64,1280]{1,0:T(8,128)(2,1)S(1)}, bf16[64,1280]{1,0:T(8,128)(2,1)S(1)}, u32[]{:S(2)}, u32[]{:S(2)}) collective-permute-start(bf16[64,1280]{1,0:T(8,128)(2,1)S(1)} %get-tuple-element.25), channel_id=1, source_target_pairs={{0,16},{8,24},{16,0},{24,8},{1,17},{9,25},{17,1},{25,9},{2,18},{10... | collective-permute-start | bytes 491528 | tf_op jit(solution)/shard_map/ppermute | solution.py:105
  15.4 6.6 %collective-permute-start.4 = (bf16[64,1280]{1,0:T(8,128)(2,1)S(1)}, bf16[64,1280]{1,0:T(8,128)(2,1)S(1)}, u32[]{:S(2)}, u32[]{:S(2)}) collective-permute-start(bf16[64,1280]{1,0:T(8,128)(2,1)S(1)} %get-tuple-element.24), channel_id=1, source_target_pairs={{0,24},{8,16},{16,8},{24,0},{1,25},{9,17},{17,9},{25,1},{2,26},{10... | collective-permute-start | bytes 491528 | tf_op jit(solution)/shard_map/ppermute | solution.py:105
  15.7 18.6 %collective-permute-start.13 = (bf16[256,512]{1,0:T(8,128)(2,1)S(1)}, bf16[256,512]{1,0:T(8,128)(2,1)S(1)}, u32[]{:S(2)}, u32[]{:S(2)}) collective-permute-start(bf16[256,512]{1,0:T(8,128)(2,1)S(1)} %pad_maximum_fusion.2), channel_id=1, source_target_pairs={{0,1},{1,0},{2,3},{3,2},{4,5},{5,4},{6,7},{7,6},{8,9},{9,8},{10,11... | collective-permute-start | bytes 786440 | tf_op jit(solution)/shard_map/ppermute | solution.py:105
  19.1 5.6 %collective-permute-start.1 = (f32[64,512]{1,0:T(8,128)S(1)}, f32[64,512]{1,0:T(8,128)S(1)}, u32[]{:S(2)}, u32[]{:S(2)}) collective-permute-start(f32[64,512]{1,0:T(8,128)S(1)} %fusion.58), channel_id=1, source_target_pairs={{0,8},{8,0},{16,24},{24,16},{1,9},{9,1},{17,25},{25,17},{2,10},{10... | collective-permute-start | bytes 393224 | tf_op jit(solution)/shard_map/ppermute | solution.py:105
  20.7 4.4 %collective-permute-start.3 = (f32[64,512]{1,0:T(8,128)S(1)}, f32[64,512]{1,0:T(8,128)S(1)}, u32[]{:S(2)}, u32[]{:S(2)}) collective-permute-start(f32[64,512]{1,0:T(8,128)S(1)} %fusion.59), channel_id=1, source_target_pairs={{0,16},{8,24},{16,0},{24,8},{1,17},{9,25},{17,1},{25,9},{2,18},{10... | collective-permute-start | bytes 393224 | tf_op jit(solution)/shard_map/ppermute | solution.py:105
  22.4 5.5 %collective-permute-start.5 = (f32[64,512]{1,0:T(8,128)S(1)}, f32[64,512]{1,0:T(8,128)S(1)}, u32[]{:S(2)}, u32[]{:S(2)}) collective-permute-start(f32[64,512]{1,0:T(8,128)S(1)} %fusion.60), channel_id=1, source_target_pairs={{0,24},{8,16},{16,8},{24,0},{1,25},{9,17},{17,9},{25,1},{2,26},{10... | collective-permute-start | bytes 393224 | tf_op jit(solution)/shard_map/ppermute | solution.py:105
  28.4 6.6 %collective-permute-start.6 = (bf16[64,512]{1,0:T(8,128)(2,1)S(1)}, bf16[64,512]{1,0:T(8,128)(2,1)S(1)}, u32[]{:S(2)}, u32[]{:S(2)}) collective-permute-start(bf16[64,512]{1,0:T(8,128)(2,1)S(1)} %get-tuple-element.17), channel_id=1, source_target_pairs={{0,2},{1,3},{2,0},{3,1},{4,6},{5,7},{6,4},{7,5},{8,10},{9,11},{10,... | collective-permute-start | bytes 196616 | tf_op jit(solution)/shard_map/ppermute | solution.py:105
  33.0 4.1 %collective-permute-start.7 = (bf16[64,512]{1,0:T(8,128)(2,1)S(1)}, bf16[64,512]{1,0:T(8,128)(2,1)S(1)}, u32[]{:S(2)}, u32[]{:S(2)}) collective-permute-start(bf16[64,512]{1,0:T(8,128)(2,1)S(1)} %get-tuple-element.17), channel_id=1, source_target_pairs={{0,4},{1,5},{2,6},{3,7},{4,0},{5,1},{6,2},{7,3},{8,12},{9,13},{10,... | collective-permute-start | bytes 196616 | tf_op jit(solution)/shard_map/ppermute | solution.py:105
  33.0 5.2 %collective-permute-start.8 = (bf16[64,512]{1,0:T(8,128)(2,1)S(1)}, bf16[64,512]{1,0:T(8,128)(2,1)S(1)}, u32[]{:S(2)}, u32[]{:S(2)}) collective-permute-start(bf16[64,512]{1,0:T(8,128)(2,1)S(1)} %get-tuple-element.17), channel_id=1, source_target_pairs={{0,6},{1,7},{2,4},{3,5},{4,2},{5,3},{6,0},{7,1},{8,14},{9,15},{10,... | collective-permute-start | bytes 196616 | tf_op jit(solution)/shard_map/ppermute | solution.py:105
  38.2 5.4 %collective-permute-start.9 = (bf16[256,512]{1,0:T(8,128)(2,1)S(1)}, bf16[256,512]{1,0:T(8,128)(2,1)S(1)}, u32[]{:S(2)}, u32[]{:S(2)}) collective-permute-start(bf16[256,512]{1,0:T(8,128)(2,1)S(1)} %pad_maximum_fusion.1), channel_id=1, source_target_pairs={{0,1},{1,0},{2,3},{3,2},{4,5},{5,4},{6,7},{7,6},{8,9},{9,8},{10,11... | collective-permute-start | bytes 786440 | tf_op jit(solution)/shard_map/ppermute | solution.py:105
  67.0 5.4 %collective-permute-start.14 = (f32[256,512]{1,0:T(8,128)S(1)}, f32[256,512]{1,0:T(8,128)S(1)}, u32[]{:S(2)}, u32[]{:S(2)}) collective-permute-start(f32[256,512]{1,0:T(8,128)S(1)} %slice.121), channel_id=1, source_target_pairs={{0,1},{1,0},{2,3},{3,2},{4,5},{5,4},{6,7},{7,6},{8,9},{9,8},{10,11... | collective-permute-start | bytes 1572872 | tf_op jit(solution)/shard_map/ppermute | solution.py:105
  67.5 6.5 %collective-permute-start.28 = (f32[256,512]{1,0:T(8,128)S(1)}, f32[256,512]{1,0:T(8,128)S(1)}, u32[]{:S(2)}, u32[]{:S(2)}) collective-permute-start(f32[256,512]{1,0:T(8,128)S(1)} %slice.155), channel_id=1, source_target_pairs={{0,1},{1,0},{2,3},{3,2},{4,5},{5,4},{6,7},{7,6},{8,9},{9,8},{10,11... | collective-permute-start | bytes 1572872 | tf_op jit(solution)/shard_map/ppermute | solution.py:105
  68.9 30.7 %collective-permute-start.18 = (bf16[320,256]{0,1:T(8,128)(2,1)}, bf16[320,256]{0,1:T(8,128)(2,1)S(1)}, u32[]{:S(2)}, u32[]{:S(2)}) collective-permute-start(bf16[320,256]{0,1:T(8,128)(2,1)} %get-tuple-element.21), channel_id=1, source_target_pairs={{0,2},{1,3},{2,0},{3,1},{4,6},{5,7},{6,4},{7,5},{8,10},{9,11},{10,... | collective-permute-start | bytes 491528 | tf_op jit(solution)/shard_map/ppermute | solution.py:105
  70.8 43.1 %collective-permute-start.20 = (bf16[320,256]{0,1:T(8,128)(2,1)}, bf16[320,256]{0,1:T(8,128)(2,1)S(1)}, u32[]{:S(2)}, u32[]{:S(2)}) collective-permute-start(bf16[320,256]{0,1:T(8,128)(2,1)} %get-tuple-element.20), channel_id=1, source_target_pairs={{0,4},{1,5},{2,6},{3,7},{4,0},{5,1},{6,2},{7,3},{8,12},{9,13},{10,... | collective-permute-start | bytes 491528 | tf_op jit(solution)/shard_map/ppermute | solution.py:105
  72.5 10.5 %collective-permute-start.15 = (f32[64,512]{1,0:T(8,128)S(1)}, f32[64,512]{1,0:T(8,128)S(1)}, u32[]{:S(2)}, u32[]{:S(2)}) collective-permute-start(f32[64,512]{1,0:T(8,128)S(1)} %get-tuple-element.29), channel_id=1, source_target_pairs={{0,2},{1,3},{2,0},{3,1},{4,6},{5,7},{6,4},{7,5},{8,10},{9,11},{10,... | collective-permute-start | bytes 393224 | tf_op jit(solution)/shard_map/ppermute | solution.py:105
  74.1 19.4 %collective-permute-start.16 = (f32[64,512]{1,0:T(8,128)S(1)}, f32[64,512]{1,0:T(8,128)S(1)}, u32[]{:S(2)}, u32[]{:S(2)}) collective-permute-start(f32[64,512]{1,0:T(8,128)S(1)} %get-tuple-element.31), channel_id=1, source_target_pairs={{0,4},{1,5},{2,6},{3,7},{4,0},{5,1},{6,2},{7,3},{8,12},{9,13},{10,... | collective-permute-start | bytes 393224 | tf_op jit(solution)/shard_map/ppermute | solution.py:105
  74.1 23.2 %collective-permute-start.17 = (f32[64,512]{1,0:T(8,128)S(1)}, f32[64,512]{1,0:T(8,128)S(1)}, u32[]{:S(2)}, u32[]{:S(2)}) collective-permute-start(f32[64,512]{1,0:T(8,128)S(1)} %get-tuple-element.30), channel_id=1, source_target_pairs={{0,6},{1,7},{2,4},{3,5},{4,2},{5,3},{6,0},{7,1},{8,14},{9,15},{10,... | collective-permute-start | bytes 393224 | tf_op jit(solution)/shard_map/ppermute | solution.py:105
  83.0 24.4 %collective-permute-start.22 = (bf16[320,256]{0,1:T(8,128)(2,1)}, bf16[320,256]{0,1:T(8,128)(2,1)S(1)}, u32[]{:S(2)}, u32[]{:S(2)}) collective-permute-start(bf16[320,256]{0,1:T(8,128)(2,1)} %get-tuple-element.19), channel_id=1, source_target_pairs={{0,6},{1,7},{2,4},{3,5},{4,2},{5,3},{6,0},{7,1},{8,14},{9,15},{10,... | collective-permute-start | bytes 491528 | tf_op jit(solution)/shard_map/ppermute | solution.py:105
  98.0 38.2 %collective-permute-start.29 = (f32[64,512]{1,0:T(8,128)S(1)}, f32[64,512]{1,0:T(8,128)S(1)}, u32[]{:S(2)}, u32[]{:S(2)}) collective-permute-start(f32[64,512]{1,0:T(8,128)S(1)} %get-tuple-element.26), channel_id=1, source_target_pairs={{0,2},{1,3},{2,0},{3,1},{4,6},{5,7},{6,4},{7,5},{8,10},{9,11},{10,... | collective-permute-start | bytes 393224 | tf_op jit(solution)/shard_map/ppermute | solution.py:105
  99.6 4.8 %collective-permute-start.21 = (bf16[64,512]{1,0:T(8,128)(2,1)S(1)}, bf16[64,512]{1,0:T(8,128)(2,1)S(1)}, u32[]{:S(2)}, u32[]{:S(2)}) collective-permute-start(bf16[64,512]{1,0:T(8,128)(2,1)S(1)} %fusion.14), channel_id=1, source_target_pairs={{0,4},{1,5},{2,6},{3,7},{4,0},{5,1},{6,2},{7,3},{8,12},{9,13},{10,... | collective-permute-start | bytes 196616 | tf_op jit(solution)/shard_map/ppermute | solution.py:105
  101.4 4.2 %collective-permute-start.23 = (bf16[64,512]{1,0:T(8,128)(2,1)S(1)}, bf16[64,512]{1,0:T(8,128)(2,1)S(1)}, u32[]{:S(2)}, u32[]{:S(2)}) collective-permute-start(bf16[64,512]{1,0:T(8,128)(2,1)S(1)} %fusion.14), channel_id=1, source_target_pairs={{0,6},{1,7},{2,4},{3,5},{4,2},{5,3},{6,0},{7,1},{8,14},{9,15},{10,... | collective-permute-start | bytes 196616 | tf_op jit(solution)/shard_map/ppermute | solution.py:105
  104.4 31.9 %collective-permute-start.30 = (f32[64,512]{1,0:T(8,128)S(1)}, f32[64,512]{1,0:T(8,128)S(1)}, u32[]{:S(2)}, u32[]{:S(2)}) collective-permute-start(f32[64,512]{1,0:T(8,128)S(1)} %get-tuple-element.28), channel_id=1, source_target_pairs={{0,4},{1,5},{2,6},{3,7},{4,0},{5,1},{6,2},{7,3},{8,12},{9,13},{10,... | collective-permute-start | bytes 393224 | tf_op jit(solution)/shard_map/ppermute | solution.py:105
  105.6 30.6 %collective-permute-start.31 = (f32[64,512]{1,0:T(8,128)S(1)}, f32[64,512]{1,0:T(8,128)S(1)}, u32[]{:S(2)}, u32[]{:S(2)}) collective-permute-start(f32[64,512]{1,0:T(8,128)S(1)} %get-tuple-element.27), channel_id=1, source_target_pairs={{0,6},{1,7},{2,4},{3,5},{4,2},{5,3},{6,0},{7,1},{8,14},{9,15},{10,... | collective-permute-start | bytes 393224 | tf_op jit(solution)/shard_map/ppermute | solution.py:105
  107.4 5.6 %collective-permute-start.25 = (bf16[4,64,512]{2,1,0:T(8,128)(2,1)S(1)}, bf16[4,64,512]{2,1,0:T(8,128)(2,1)S(1)}, u32[]{:S(2)}, u32[]{:S(2)}) collective-permute-start(bf16[4,64,512]{2,1,0:T(8,128)(2,1)S(1)} %pad_maximum_fusion.3), channel_id=1, source_target_pairs={{0,16},{8,24},{16,0},{24,8},{1,17},{9,25},{17,1},{25,9},{2,18},{10... | collective-permute-start | bytes 786440 | tf_op jit(solution)/shard_map/ppermute | solution.py:105
  113.0 5.2 %collective-permute-start.24 = (bf16[4,64,512]{2,1,0:T(8,128)(2,1)S(1)}, bf16[4,64,512]{2,1,0:T(8,128)(2,1)S(1)}, u32[]{:S(2)}, u32[]{:S(2)}) collective-permute-start(bf16[4,64,512]{2,1,0:T(8,128)(2,1)S(1)} %pad_maximum_fusion.3), channel_id=1, source_target_pairs={{0,8},{8,0},{16,24},{24,16},{1,9},{9,1},{17,25},{25,17},{2,10},{10... | collective-permute-start | bytes 786440 | tf_op jit(solution)/shard_map/ppermute | solution.py:105
  113.8 7.3 %collective-permute-start.26 = (bf16[4,64,512]{2,1,0:T(8,128)(2,1)S(1)}, bf16[4,64,512]{2,1,0:T(8,128)(2,1)S(1)}, u32[]{:S(2)}, u32[]{:S(2)}) collective-permute-start(bf16[4,64,512]{2,1,0:T(8,128)(2,1)S(1)} %pad_maximum_fusion.3), channel_id=1, source_target_pairs={{0,24},{8,16},{16,8},{24,0},{1,25},{9,17},{17,9},{25,1},{2,26},{10... | collective-permute-start | bytes 786440 | tf_op jit(solution)/shard_map/ppermute | solution.py:105
  122.8 14.7 %collective-permute-start.27 = (f32[160,512]{1,0:T(8,128)S(1)}, f32[160,512]{1,0:T(8,128)S(1)}, u32[]{:S(2)}, u32[]{:S(2)}) collective-permute-start(f32[160,512]{1,0:T(8,128)S(1)} %constant_dynamic-slice_fusion), channel_id=1, source_target_pairs={{0,1},{1,0},{2,3},{3,2},{4,5},{5,4},{6,7},{7,6},{8,9},{9,8},{10,11... | collective-permute-start | bytes 983048 | tf_op jit(solution)/shard_map/ppermute | solution.py:105
  (7 other events, 21.5 us)
Sparse Core Ops, SparseCore 0:
  13.9 66.8 all-gather.1

commit v2 on v1

v2 whole, which is shorter than its diff:
```python
from functools import partial

import jax
import jax.numpy as jnp
from jax import lax
from jax.experimental import pallas as pl
from jax.experimental.pallas import tpu as pltpu
from jax.sharding import PartitionSpec as P

F32, BF16 = jnp.float32, jnp.bfloat16
LOG2E = 1.4426950408889634
PARAMS = pltpu.CompilerParams(vmem_limit_bytes=56 * 2**20)


def norm_keys(key_pre, key_gain):
    shaped = key_pre.reshape(key_pre.shape[:-1] + (-1, key_gain.shape[0]))
    inverse = lax.rsqrt(jnp.mean(shaped * shaped, axis=-1, keepdims=True) + 1e-06)
    return (shaped * inverse * key_gain).reshape(key_pre.shape)


def dot(left, right, left_dim=1, right_dim=0):
    dims = (((left_dim,), (right_dim,)), ((), ()))
    return lax.dot_general(left, right, dims, preferred_element_type=F32)


def cost(macs, nbytes):
    return pl.CostEstimate(flops=2 * macs, bytes_accessed=nbytes, transcendentals=0)


def stack_heads(ref, head_dim):
    heads = ref.shape[1] // head_dim
    return jnp.concatenate([ref[:, i * head_dim : (i + 1) * head_dim] for i in range(heads)], axis=0)


def score_kernel(pieces, length_ref, query_ref, upstream_ref, key_ref, value_ref, *refs):
    key_pieces, value_pieces = refs[:pieces], refs[pieces : 2 * pieces]
    weights_ref, dscore_ref, near_ref, far_ref, key_grad_ref = refs[2 * pieces :]
    rows = query_ref.shape[0]
    own_len, head_dim = key_ref.shape
    scale = head_dim ** -0.5
    keys_t = jnp.concatenate([ref[...] for ref in key_pieces] + [key_ref[...]], axis=0).T
    values_t = jnp.concatenate([ref[...] for ref in value_pieces] + [value_ref[...]], axis=0).T
    prompt_len = keys_t.shape[1] - own_len
    queries, upstream = stack_heads(query_ref, head_dim), stack_heads(upstream_ref, head_dim)
    stacked = queries.shape[0]
    live = lax.broadcasted_iota(jnp.int32, (stacked, 1), 0) % rows < length_ref[0, 0]
    own = (stacked, own_len)
    visible = lax.broadcasted_iota(jnp.int32, own, 1) <= lax.broadcasted_iota(jnp.int32, own, 0) % rows
    prompt_scores = dot(queries, keys_t[:, :prompt_len])
    own_scores = jnp.where(visible, dot(queries, keys_t[:, prompt_len:]), -jnp.inf)
    row_max = jnp.maximum(
        jnp.max(prompt_scores, axis=1, keepdims=True), jnp.max(own_scores, axis=1, keepdims=True)
    )
    scores = jnp.concatenate([prompt_scores, own_scores], axis=1)
    unit = scale * LOG2E
    exponent = jnp.exp2(scores * unit - row_max * unit)
    dprob = dot(upstream, values_t)
    total = jnp.sum(exponent, axis=1, keepdims=True)
    weighted = jnp.sum(exponent * dprob, axis=1, keepdims=True)
    inverse = jnp.where(live, 1.0 / total, 0.0)
    row_delta = weighted * inverse
    weights_ref[0] = (exponent * inverse).astype(BF16)
    dscore = (exponent * ((dprob - row_delta) * (inverse * scale))).astype(BF16)
    dscore_ref[0] = dscore
    key_grad = dot(queries.T, dscore).T
    near_ref[...] = key_grad[: prompt_len // 2]
    far_ref[...] = key_grad[prompt_len // 2 : prompt_len]
    key_grad_ref[...] = key_grad[prompt_len:].astype(BF16)


def column_block(rows, columns):
    return pl.BlockSpec((rows, columns), lambda i: (0, i))


def head_block(*shape):
    return pl.BlockSpec((1,) + shape, lambda i: (i, 0, 0))


def score_pass(length, queries, upstream, key_pieces, value_pieces, keys, values, head_dim):
    rows, width = queries.shape
    kv_width = keys.shape[1]
    kv_heads = kv_width // head_dim
    stacked = rows * width // kv_width
    prompt_len = sum(piece.shape[0] for piece in key_pieces)
    every = prompt_len + rows
    query_block, own_block = column_block(rows, width // kv_heads), column_block(rows, head_dim)
    piece_blocks = [column_block(piece.shape[0], head_dim) for piece in key_pieces]
    half_block = column_block(prompt_len // 2, head_dim)
    pair = jax.ShapeDtypeStruct((kv_heads, stacked, every), BF16)
    half = jax.ShapeDtypeStruct((prompt_len // 2, kv_width), F32)
    return pl.pallas_call(
        partial(score_kernel, len(key_pieces)),
        grid=(kv_heads,),
        in_specs=[
            pl.BlockSpec(memory_space=pltpu.SMEM), query_block, query_block, own_block, own_block,
            *piece_blocks, *piece_blocks,
        ],
        out_specs=[head_block(stacked, every)] * 2 + [half_block] * 2 + [own_block],
        out_shape=[pair, pair, half, half, jax.ShapeDtypeStruct((rows, kv_width), BF16)],
        compiler_params=PARAMS,
        cost_estimate=cost(6 * rows * width * every, 2 * 10**7),
        name="scores",
    )(length, queries, upstream, keys, values, *key_pieces, *value_pieces)


def value_kernel(upstream_ref, weights_ref, near_ref, far_ref, value_grad_ref):
    half, head_dim = near_ref.shape
    upstream = stack_heads(upstream_ref, head_dim)
    value_grad = dot(upstream.T, weights_ref[0]).T
    near_ref[...] = value_grad[:half]
    far_ref[...] = value_grad[half : 2 * half]
    value_grad_ref[...] = value_grad[2 * half :].astype(BF16)


def value_pass(upstream, weights, head_dim):
    rows, width = upstream.shape
    kv_heads, stacked, every = weights.shape
    kv_width = kv_heads * head_dim
    half = (every - rows) // 2
    out = jax.ShapeDtypeStruct((half, kv_width), F32)
    return pl.pallas_call(
        value_kernel,
        grid=(kv_heads,),
        in_specs=[column_block(rows, width // kv_heads), head_block(stacked, every)],
        out_specs=[column_block(half, head_dim)] * 2 + [column_block(rows, head_dim)],
        out_shape=[out, out, jax.ShapeDtypeStruct((rows, kv_width), BF16)],
        compiler_params=PARAMS,
        cost_estimate=cost(rows * width * every, 1 * 10**7),
        name="value_grads",
    )(upstream, weights)


def query_kernel(dscore_ref, key_ref, *refs):
    key_pieces, query_grad_ref = refs[:-1], refs[-1]
    rows, head_dim = query_grad_ref.shape[0], key_ref.shape[1]
    keys = jnp.concatenate([ref[...] for ref in key_pieces] + [key_ref[...]], axis=0)
    query_grad = dot(dscore_ref[0], keys).astype(BF16)
    for i in range(query_grad_ref.shape[1] // head_dim):
        query_grad_ref[:, i * head_dim : (i + 1) * head_dim] = query_grad[i * rows : (i + 1) * rows]


def query_pass(dscore, key_pieces, keys, head_dim):
    kv_heads, stacked, every = dscore.shape
    rows, kv_width = keys.shape
    width = stacked // rows * kv_width
    return pl.pallas_call(
        query_kernel,
        grid=(kv_heads,),
        in_specs=[head_block(stacked, every)]
        + [column_block(piece.shape[0], head_dim) for piece in [keys] + key_pieces],
        out_specs=column_block(rows, width // kv_heads),
        out_shape=jax.ShapeDtypeStruct((rows, width), BF16),
        compiler_params=PARAMS,
        cost_estimate=cost(rows * width * every, 1 * 10**7),
        name="query_grads",
    )(dscore, keys, *key_pieces)


def hidden_kernel(groups, place_ref, grad_ref, own_ref, *refs):
    near, far, out_ref = refs[: groups - 1], refs[groups - 1 : -1], refs[-1]
    group, core = place_ref[0], place_ref[1]
    depth = own_ref.shape[0]
    half = near[0].shape[1]
    near_grad = grad_ref[:, pl.ds(pl.multiple_of(core * half, half), half)]
    far_grad = grad_ref[:, pl.ds(pl.multiple_of((1 - core) * half, half), half)]
    for k in range(groups):
        if k:
            block = dot(near_grad, near[k - 1][...], 1, 1) + dot(far_grad, far[k - 1][...], 1, 1)
        else:
            block = dot(grad_ref[...], own_ref[...], 1, 1)
        start = pl.multiple_of((group ^ k) * depth, depth)
        out_ref[:, pl.ds(start, depth)] = block.astype(BF16)


def hidden_pass(place, key_pre_grad, own, near, far):
    tokens, kv_width = key_pre_grad.shape
    groups = len(near) + 1
    width = groups * own.shape[0]
    return pl.pallas_call(
        partial(hidden_kernel, groups),
        in_specs=[pl.BlockSpec(memory_space=pltpu.SMEM)]
        + [pl.BlockSpec(memory_space=pltpu.VMEM)] * (2 * groups),
        out_specs=pl.BlockSpec(memory_space=pltpu.VMEM),
        out_shape=jax.ShapeDtypeStruct((tokens, width), BF16),
        compiler_params=PARAMS,
        cost_estimate=cost(tokens * width * kv_width, 6 * 10**6),
        name="hidden_grad",
    )(place, key_pre_grad, own, *near, *far)


def weight_kernel(chips, place_ref, *refs):
    taken, blocks = refs[:chips], refs[chips:-3]
    mine_ref, other_ref, product = refs[-3:]
    half = mine_ref.shape[0]
    core = place_ref[1]
    columns = jnp.concatenate([ref[...] for ref in taken], axis=1)
    grads = jnp.concatenate([ref[p] for p in range(chips) for ref in blocks], axis=0)
    product[...] = dot(columns, grads)
    mine_ref[...] = product[pl.ds(pl.multiple_of(core * half, 8), half)]
    other_ref[...] = product[pl.ds(pl.multiple_of((1 - core) * half, 8), half)]


def weight_pass(place, taken, blocks):
    rows = taken[0].shape[0]
    kv_width = blocks[0].shape[-1]
    out = jax.ShapeDtypeStruct((rows // 2, kv_width), F32)
    return pl.pallas_call(
        partial(weight_kernel, len(taken)),
        in_specs=[pl.BlockSpec(memory_space=pltpu.SMEM)]
        + [pl.BlockSpec(memory_space=pltpu.VMEM)] * (len(taken) + len(blocks)),
        out_specs=[pl.BlockSpec(memory_space=pltpu.VMEM)] * 2,
        out_shape=[out, out],
        scratch_shapes=[pltpu.VMEM((rows, kv_width), F32)],
        compiler_params=PARAMS,
        cost_estimate=cost(rows * kv_width * taken[0].shape[1] * len(taken), 3 * 10**6),
        name="weight_grad",
    )(place, *taken, *blocks)


def swap(array, axis, size, distance):
    return lax.ppermute(array, axis, [(i, i ^ distance) for i in range(size)])


def after(array, *others):
    return lax.optimization_barrier((array, *others))[0]


def spread_near(block, size):
    return [block] + [swap(block, "resp", size, k) for k in range(2, size, 2)]


def spread_far(near, size):
    return [swap(piece, "resp", size, 1) for piece in near]


def collect(near, far, size):
    near = near + swap(far, "resp", size, 1)
    rows = near.shape[0] // (size // 2)
    total = near[:rows]
    for p in range(1, size // 2):
        total = total + swap(near[p * rows : (p + 1) * rows], "resp", size, 2 * p)
    return total


def shards(
    groups, responses, prompt_hidden, key_matrix, key_gain, prompt_token_value,
    resp_query, resp_key, response_value, grad_out, resp_length,
):
    hidden = prompt_hidden[0]
    tokens = hidden.shape[0]
    depth, kv_width = key_matrix.shape
    head_dim = key_gain.shape[0]
    group, resp = lax.axis_index("group"), lax.axis_index("resp")
    core = resp % 2
    place = jnp.stack([group, core]).astype(jnp.int32)

    columns = []
    for k in range(groups):
        piece = lax.dynamic_slice(hidden, (0, (group ^ k) * depth), (tokens, depth))
        columns.append(swap(piece, "group", groups, k) if k else piece)
    partials = [dot(piece, key_matrix) for piece in columns]
    key_pre = partials[0]
    for k in range(1, groups):
        key_pre = key_pre + swap(partials[k], "group", groups, k)
    value_near = spread_near(prompt_token_value[0], responses)
    value_pieces = value_near + spread_far(value_near, responses)

    prompt_key = norm_keys(key_pre, key_gain).astype(BF16)
    key_near = spread_near(prompt_key, responses)
    key_pieces = key_near + spread_far(key_near, responses)

    chips = responses // 2
    chip_rows = depth // chips
    hidden_t = jnp.concatenate(columns, axis=0).T
    hidden_t = after(hidden_t, *key_near)
    taken = []
    for k in range(0, responses, 2):
        start = ((resp ^ k) // 2) * chip_rows
        piece = lax.dynamic_slice(hidden_t, (start, 0), (chip_rows, hidden_t.shape[1]))
        taken.append(swap(piece, "resp", responses, k) if k else piece)

    half_width = kv_width // 2
    half_weight = lax.dynamic_slice(key_matrix, (0, core * half_width), (depth, half_width))
    half_weight = after(half_weight, key_pre)
    weight_near = [swap(half_weight, "group", groups, k) for k in range(1, groups)]

    queries, upstream = resp_query[0, 0], grad_out[0, 0]
    weights, dscore, near, far, key_grad = score_pass(
        resp_length, queries, upstream, key_pieces, value_pieces,
        resp_key[0, 0], response_value[0, 0], head_dim,
    )
    prompt_key_grad = collect(near, far, responses)
    _, pullback = jax.vjp(lambda values: norm_keys(values, key_gain), key_pre)
    key_pre_grad = pullback(prompt_key_grad)[0].astype(BF16)

    value_near, value_far, value_grad = value_pass(upstream, weights, head_dim)
    query_grad = query_pass(dscore, key_pieces, resp_key[0, 0], head_dim)

    block = jnp.stack(spread_near(key_pre_grad, responses), axis=0)
    blocks = [block] + [swap(block, "group", groups, k) for k in range(1, groups)]
    mine, other = weight_pass(place, taken, blocks)
    grad_weight = mine + swap(other, "resp", responses, 1)

    weight_far = [swap(piece, "resp", responses, 1) for piece in weight_near]
    grad_hidden = hidden_pass(place, key_pre_grad, key_matrix, weight_near, weight_far)
    prompt_value_grad = collect(value_near, value_far, responses)
    return (
        grad_hidden[None],
        grad_weight,
        prompt_value_grad.astype(BF16)[None],
        query_grad[None, None],
        key_grad[None, None],
        value_grad[None, None],
    )


def solution(mesh):
    return jax.shard_map(
        partial(shards, mesh.shape["group"], mesh.shape["resp"]),
        mesh=mesh,
        in_specs=(
            P("group", "resp", None),
            P("group", None),
            P(),
            P("group", "resp", None),
            P("group", "resp", None, None),
            P("group", "resp", None, None),
            P("group", "resp", None, None),
            P("group", "resp", None, None),
            P("group", "resp"),
        ),
        out_specs=(
            P("group", "resp", None),
            P(("group", "resp"), None),
            P("group", "resp", None),
            P("group", "resp", None, None),
            P("group", "resp", None, None),
            P("group", "resp", None, None),
        ),
        check_vma=False,
    )
```

time: 150 us -> 160 us (1.067)
  the two profiles are of different devices: /device:TPU:17 before, /device:TPU:0 now
where the time goes in v2:
time: 160 us
  waiting for transfers between devices  50.6 us (32%)
  starting transfers between devices  46.4 us (29%)
  Pallas kernels  45 us (28%)
  local copies, waits for them, and re-layouts  9.04 us (6%)
  other arithmetic  5.18 us (3%)
  between operations  1.96 us (1%)
    ppermute x44, waiting for transfers between devices, swap(): return lax.ppermute(array, axis, [(i, i ^ distance) for i in range(size)])  50.6 us
    ppermute x44, starting transfers between devices, swap(): return lax.ppermute(array, axis, [(i, i ^ distance) for i in range(size)])  46.4 us
    pallas_call x1, Pallas kernels, score_pass(): pl.pallas_call(partial(score_kernel, len(key_pieces)), grid=(kv_heads,),...  21.1 us
    pallas_call x1, Pallas kernels, query_pass(): pl.pallas_call(query_kernel, grid=(kv_heads,), in_specs=[head_block(stack...  8.29 us
    pallas_call x1, Pallas kernels, value_pass(): pl.pallas_call(value_kernel, grid=(kv_heads,), in_specs=[column_block(row...  7.71 us
    pallas_call x1, Pallas kernels, hidden_pass(): pl.pallas_call(partial(hidden_kernel, groups), in_specs=[pl.BlockSpec(mem...  5.03 us
    unnamed x68, local copies, waits for them, and re-layouts  3.79 us
  transfers between devices with their start and end apart: 44, of which 16 were waited for; matrix products, arithmetic and copies ran while one was open for 6% of the time, Pallas kernels for 15%

profile of v2, /device:TPU:0, one launch (start us, length us, event | category | flops | bytes accessed | tf_op | source)
XLA Modules:
  0.0 159.6 jit_solution(13328762205942021217)
XLA Ops:
  0.6 3.1 %collective-permute-start.13 = (bf16[64,512]{1,0:T(8,128)(2,1)}, bf16[64,512]{1,0:T(8,128)(2,1)S(1)}, u32[]{:S(2)}, u32[]{:S(2)}) collective-permute-start(bf16[64,512]{1,0:T(8,128)(2,1)} %bitcast.69), channel_id=1, source_target_pairs={{0,2},{1,3},{2,0},{3,1},{4,6},{5,7},{6,4},{7,5},{8,10},{9,11},{10,... | collective-permute-start | bytes 196616 | tf_op jit(solution)/shard_map/ppermute | solution.py:221
  3.7 2.6 %collective-permute-start.14 = (bf16[64,512]{1,0:T(8,128)(2,1)}, bf16[64,512]{1,0:T(8,128)(2,1)S(1)}, u32[]{:S(2)}, u32[]{:S(2)}) collective-permute-start(bf16[64,512]{1,0:T(8,128)(2,1)} %bitcast.70), channel_id=1, source_target_pairs={{0,4},{1,5},{2,6},{3,7},{4,0},{5,1},{6,2},{7,3},{8,12},{9,13},{10,... | collective-permute-start | bytes 196616 | tf_op jit(solution)/shard_map/ppermute | solution.py:221
  8.5 1.5 collective-permute-start
  10.2 1.6 collective-permute-start.2
  12.9 6.5 %collective-permute-done = bf16[64,1280]{0,1:T(8,128)(2,1)S(1)} collective-permute-done((bf16[64,1280]{0,1:T(8,128)(2,1)}, bf16[64,1280]{0,1:T(8,128)(2,1)S(1)}, u32[]{:S(2)}, u32[]{:S(2)}) %collective-permute-start) | collective-permute-done | bytes 163872 | tf_op jit(solution)/shard_map/ppermute | solution.py:221
  19.7 1.6 collective-permute-start.1
  21.3 4.9 %collective-permute-done.2 = bf16[64,1280]{0,1:T(8,128)(2,1)S(1)} collective-permute-done((bf16[64,1280]{0,1:T(8,128)(2,1)S(1)}, bf16[64,1280]{0,1:T(8,128)(2,1)S(1)}, u32[]{:S(2)}, u32[]{:S(2)}) %collective-permute-start.2) | collective-permute-done | bytes 163872 | tf_op jit(solution)/shard_map/ppermute | solution.py:221
  26.6 2.6 %collective-permute-start.3 = (f32[64,512]{1,0:T(8,128)S(1)}, f32[64,512]{1,0:T(8,128)S(1)}, u32[]{:S(2)}, u32[]{:S(2)}) collective-permute-start(f32[64,512]{1,0:T(8,128)S(1)} %fusion.15), channel_id=1, source_target_pairs={{0,16},{8,24},{16,0},{24,8},{1,17},{9,25},{17,1},{25,9},{2,18},{10... | collective-permute-start | bytes 393224 | tf_op jit(solution)/shard_map/ppermute | solution.py:221
  30.4 1.7 %collective-permute-done.3 = f32[64,512]{1,0:T(8,128)S(1)} collective-permute-done((f32[64,512]{1,0:T(8,128)S(1)}, f32[64,512]{1,0:T(8,128)S(1)}, u32[]{:S(2)}, u32[]{:S(2)}) %collective-permute-start.3) | collective-permute-done | bytes 131104 | tf_op jit(solution)/shard_map/ppermute | solution.py:221
  32.2 3.3 %collective-permute-done.5 = f32[64,512]{1,0:T(8,128)S(1)} collective-permute-done((f32[64,512]{1,0:T(8,128)S(1)}, f32[64,512]{1,0:T(8,128)S(1)}, u32[]{:S(2)}, u32[]{:S(2)}) %collective-permute-start.5) | collective-permute-done | bytes 131104 | tf_op jit(solution)/shard_map/ppermute | solution.py:221
  36.9 3.7 %collective-permute-start.8 = (bf16[64,512]{1,0:T(8,128)(2,1)S(1)}, bf16[64,512]{1,0:T(8,128)(2,1)S(1)}, u32[]{:S(2)}, u32[]{:S(2)}) collective-permute-start(bf16[64,512]{1,0:T(8,128)(2,1)S(1)} %fusion.4.refs_0_), channel_id=1, source_target_pairs={{0,6},{1,7},{2,4},{3,5},{4,2},{5,3},{6,0},{7,1},{8,14},{9,15},{10,... | collective-permute-start | bytes 196616 | tf_op jit(solution)/shard_map/ppermute | solution.py:221
  45.5 21.1 %scores.1 = (bf16[4,2048,768]{2,1,0:T(8,128)(2,1)}, bf16[4,2048,768]{2,1,0:T(8,128)(2,1)}, f32[256,512]{1,0:T(8,128)}, f32[256,512]{1,0:T(8,128)}, bf16[256,512]{1,0:T(8,128)(2,1)}) custom-call(s32[1,1]{1,0:T(1,128)S(6)} %copy.38.length_ref, bf16[256,4096]{1,0:T(8,128)(2,1)} %bitcast.66, bf16[256,4096]{1,0:T(8,128)(2,1)} %bitcast.50, ...), custom_call_target="tpu_custom_call" | custom-call | flops 9663676416 | bytes 20000000 | tf_op jit(solution)/shard_map/scores/pallas_call | solution.py:91
  71.0 2.7 %collective-permute-start.22 = (f32[64,512]{1,0:T(8,128)S(1)}, f32[64,512]{1,0:T(8,128)S(1)}, u32[]{:S(2)}, u32[]{:S(2)}) collective-permute-start(f32[64,512]{1,0:T(8,128)S(1)} %get-tuple-element.43), channel_id=1, source_target_pairs={{0,4},{1,5},{2,6},{3,7},{4,0},{5,1},{6,2},{7,3},{8,12},{9,13},{10,... | collective-permute-start | bytes 393224 | tf_op jit(solution)/shard_map/ppermute | solution.py:221
  79.3 4.6 %collective-permute-done.22 = f32[64,512]{1,0:T(8,128)S(1)} collective-permute-done((f32[64,512]{1,0:T(8,128)S(1)}, f32[64,512]{1,0:T(8,128)S(1)}, u32[]{:S(2)}, u32[]{:S(2)}) %collective-permute-start.22) | collective-permute-done | bytes 131104 | tf_op jit(solution)/shard_map/ppermute | solution.py:221
  83.9 3.4 %collective-permute-start.31 = (bf16[320,256]{1,0:T(8,128)(2,1)S(1)}, bf16[320,256]{1,0:T(8,128)(2,1)S(1)}, u32[]{:S(2)}, u32[]{:S(2)}) collective-permute-start(bf16[320,256]{1,0:T(8,128)(2,1)S(1)} %get-tuple-element.31), channel_id=1, source_target_pairs={{0,4},{1,5},{2,6},{3,7},{4,0},{5,1},{6,2},{7,3},{8,12},{9,13},{10,... | collective-permute-start | bytes 491528 | tf_op jit(solution)/shard_map/ppermute | solution.py:221
  87.9 4.0 %collective-permute-done.30.refs_1_ = bf16[320,256]{1,0:T(8,128)(2,1)S(1)} collective-permute-done((bf16[320,256]{1,0:T(8,128)(2,1)S(1)}, bf16[320,256]{1,0:T(8,128)(2,1)S(1)}, u32[]{:S(2)}, u32[]{:S(2)}) %collective-permute-start.30) | collective-permute-done | bytes 163872 | tf_op jit(solution)/shard_map/ppermute | solution.py:221
  91.9 2.6 %collective-permute-done.31.refs_2_ = bf16[320,256]{1,0:T(8,128)(2,1)S(1)} collective-permute-done((bf16[320,256]{1,0:T(8,128)(2,1)S(1)}, bf16[320,256]{1,0:T(8,128)(2,1)S(1)}, u32[]{:S(2)}, u32[]{:S(2)}) %collective-permute-start.31) | collective-permute-done | bytes 163872 | tf_op jit(solution)/shard_map/ppermute | solution.py:221
  94.5 7.7 %value_grads.1 = (f32[256,512]{1,0:T(8,128)}, f32[256,512]{1,0:T(8,128)}, bf16[256,512]{1,0:T(8,128)(2,1)}) custom-call(bf16[256,4096]{1,0:T(8,128)(2,1)} %bitcast.51, bf16[4,2048,768]{2,1,0:T(8,128)(2,1)} %get-tuple-element.24.weights_ref), custom_call_target="tpu_custom_call" | custom-call | flops 1610612736 | bytes 10000000 | tf_op jit(solution)/shard_map/value_grads/pallas_call | solution.py:121
  102.3 1.9 %collective-permute-start.35 = (bf16[64,512]{1,0:T(8,128)(2,1)S(1)}, bf16[64,512]{1,0:T(8,128)(2,1)S(1)}, u32[]{:S(2)}, u32[]{:S(2)}) collective-permute-start(bf16[64,512]{1,0:T(8,128)(2,1)S(1)} %fusion.2.grad_ref), channel_id=1, source_target_pairs={{0,6},{1,7},{2,4},{3,5},{4,2},{5,3},{6,0},{7,1},{8,14},{9,15},{10,... | collective-permute-start | bytes 196616 | tf_op jit(solution)/shard_map/ppermute | solution.py:221
  104.2 4.5 %collective-permute-done.35 = bf16[64,512]{1,0:T(8,128)(2,1)S(1)} collective-permute-done((bf16[64,512]{1,0:T(8,128)(2,1)S(1)}, bf16[64,512]{1,0:T(8,128)(2,1)S(1)}, u32[]{:S(2)}, u32[]{:S(2)}) %collective-permute-start.35) | collective-permute-done | bytes 65568 | tf_op jit(solution)/shard_map/ppermute | solution.py:221
  108.7 1.8 %collective-permute-start.32 = (bf16[320,256]{1,0:T(8,128)(2,1)S(1)}, bf16[320,256]{1,0:T(8,128)(2,1)S(1)}, u32[]{:S(2)}, u32[]{:S(2)}) collective-permute-start(bf16[320,256]{1,0:T(8,128)(2,1)S(1)} %copy-done.17), channel_id=1, source_target_pairs={{0,6},{1,7},{2,4},{3,5},{4,2},{5,3},{6,0},{7,1},{8,14},{9,15},{10,... | collective-permute-start | bytes 491528 | tf_op jit(solution)/shard_map/ppermute | solution.py:221
  110.6 5.7 %collective-permute-done.32.refs_3_ = bf16[320,256]{1,0:T(8,128)(2,1)S(1)} collective-permute-done((bf16[320,256]{1,0:T(8,128)(2,1)S(1)}, bf16[320,256]{1,0:T(8,128)(2,1)S(1)}, u32[]{:S(2)}, u32[]{:S(2)}) %collective-permute-start.32) | collective-permute-done | bytes 163872 | tf_op jit(solution)/shard_map/ppermute | solution.py:221
  116.7 1.7 %collective-permute-start.37 = (bf16[4,64,512]{2,1,0:T(8,128)(2,1)S(1)}, bf16[4,64,512]{2,1,0:T(8,128)(2,1)S(1)}, u32[]{:S(2)}, u32[]{:S(2)}) collective-permute-start(bf16[4,64,512]{2,1,0:T(8,128)(2,1)S(1)} %pad_maximum_fusion.refs_4_), channel_id=1, source_target_pairs={{0,16},{8,24},{16,0},{24,8},{1,17},{9,25},{17,1},{25,9},{2,18},{10... | collective-permute-start | bytes 786440 | tf_op jit(solution)/shard_map/ppermute | solution.py:221
  121.5 4.0 %collective-permute-done.36.refs_5_ = bf16[4,64,512]{2,1,0:T(8,128)(2,1)S(1)} collective-permute-done((bf16[4,64,512]{2,1,0:T(8,128)(2,1)S(1)}, bf16[4,64,512]{2,1,0:T(8,128)(2,1)S(1)}, u32[]{:S(2)}, u32[]{:S(2)}) %collective-permute-start.36) | collective-permute-done | bytes 262176 | tf_op jit(solution)/shard_map/ppermute | solution.py:221
  125.6 2.5 %collective-permute-done.37.refs_6_ = bf16[4,64,512]{2,1,0:T(8,128)(2,1)S(1)} collective-permute-done((bf16[4,64,512]{2,1,0:T(8,128)(2,1)S(1)}, bf16[4,64,512]{2,1,0:T(8,128)(2,1)S(1)}, u32[]{:S(2)}, u32[]{:S(2)}) %collective-permute-start.37) | collective-permute-done | bytes 262176 | tf_op jit(solution)/shard_map/ppermute | solution.py:221
  128.1 4.8 %collective-permute-start.41 = (f32[64,512]{1,0:T(8,128)S(1)}, f32[64,512]{1,0:T(8,128)S(1)}, u32[]{:S(2)}, u32[]{:S(2)}) collective-permute-start(f32[64,512]{1,0:T(8,128)S(1)} %get-tuple-element.38), channel_id=1, source_target_pairs={{0,2},{1,3},{2,0},{3,1},{4,6},{5,7},{6,4},{7,5},{8,10},{9,11},{10,... | collective-permute-start | bytes 393224 | tf_op jit(solution)/shard_map/ppermute | solution.py:221
  132.9 1.7 %collective-permute-start.42 = (f32[64,512]{1,0:T(8,128)S(1)}, f32[64,512]{1,0:T(8,128)S(1)}, u32[]{:S(2)}, u32[]{:S(2)}) collective-permute-start(f32[64,512]{1,0:T(8,128)S(1)} %get-tuple-element.40), channel_id=1, source_target_pairs={{0,4},{1,5},{2,6},{3,7},{4,0},{5,1},{6,2},{7,3},{8,12},{9,13},{10,... | collective-permute-start | bytes 393224 | tf_op jit(solution)/shard_map/ppermute | solution.py:221
  135.2 2.8 %weight_grad.1 = (f32[160,512]{1,0:T(8,128)}, f32[160,512]{1,0:T(8,128)}) custom-call(s32[2]{0:T(128)} %pad_add_fusion.place_ref, bf16[320,256]{1,0:T(8,128)(2,1)} %get-tuple-element.33.refs_0_, bf16[320,256]{1,0:T(8,128)(2,1)} %copy-done.15, bf16[320,256]{1,0:T(8,128)(2,1)} %copy-done.16, bf16[320,256]{1,0:T(8,128)(2,1)} %copy-done.18, ...), custom_call_target="tpu_custom_call" | custom-call | flops 335544320 | bytes 3000000 | tf_op jit(solution)/shard_map/weight_grad/pallas_call | solution.py:207
  138.1 1.5 collective-permute-start.43
  139.6 3.3 %collective-permute-done.42 = f32[64,512]{1,0:T(8,128)S(1)} collective-permute-done((f32[64,512]{1,0:T(8,128)S(1)}, f32[64,512]{1,0:T(8,128)S(1)}, u32[]{:S(2)}, u32[]{:S(2)}) %collective-permute-start.42) | collective-permute-done | bytes 131104 | tf_op jit(solution)/shard_map/ppermute | solution.py:221
  142.9 8.3 %query_grads.1 = bf16[256,4096]{1,0:T(8,128)(2,1)} custom-call(bf16[4,2048,768]{2,1,0:T(8,128)(2,1)} %get-tuple-element.27.dscore_ref, bf16[256,512]{1,0:T(8,128)(2,1)} %bitcast.62, bf16[64,512]{1,0:T(8,128)(2,1)} %copy-done.11, bf16[64,512]{1,0:T(8,128)(2,1)} %copy-done.19, bf16[64,512]{1,0:T(8,128)(2,1)} %copy-done.20, bf16[64,512]{1,0:T(8,128)(2,1)} %copy-done.21, ...), custom_call_target="tpu_custom_call" | custom-call | flops 1610612736 | bytes 10000000 | tf_op jit(solution)/shard_map/query_grads/pallas_call | solution.py:146
  153.8 5.0 %hidden_grad.1 = bf16[64,5120]{1,0:T(8,128)(2,1)} custom-call(s32[2]{0:T(128)} %pad_add_fusion.place_ref, bf16[64,512]{1,0:T(8,128)(2,1)} %copy-done.8, bf16[1280,512]{1,0:T(8,128)(2,1)} %own_ref.1, bf16[1280,256]{1,0:T(8,128)(2,1)} %copy-done.2, bf16[1280,256]{1,0:T(8,128)(2,1)} %copy-done.3, bf16[1280,256]{1,0:T(8,128)(2,1)} %copy-done.4, ...), custom_call_target="tpu_custom_call" | custom-call | flops 335544320 | bytes 6000000 | tf_op jit(solution)/shard_map/hidden_grad/pallas_call | solution.py:179
  (166 shorter events, 28.9 us)
Async XLA Ops:
  0.6 29.0 %collective-permute-start.13 = (bf16[64,512]{1,0:T(8,128)(2,1)}, bf16[64,512]{1,0:T(8,128)(2,1)S(1)}, u32[]{:S(2)}, u32[]{:S(2)}) collective-permute-start(bf16[64,512]{1,0:T(8,128)(2,1)} %bitcast.69), channel_id=1, source_target_pairs={{0,2},{1,3},{2,0},{3,1},{4,6},{5,7},{6,4},{7,5},{8,10},{9,11},{10,... | collective-permute-start | bytes 196616 | tf_op jit(solution)/shard_map/ppermute | solution.py:221
  3.7 26.2 %collective-permute-start.14 = (bf16[64,512]{1,0:T(8,128)(2,1)}, bf16[64,512]{1,0:T(8,128)(2,1)S(1)}, u32[]{:S(2)}, u32[]{:S(2)}) collective-permute-start(bf16[64,512]{1,0:T(8,128)(2,1)} %bitcast.70), channel_id=1, source_target_pairs={{0,4},{1,5},{2,6},{3,7},{4,0},{5,1},{6,2},{7,3},{8,12},{9,13},{10,... | collective-permute-start | bytes 196616 | tf_op jit(solution)/shard_map/ppermute | solution.py:221
  8.5 10.9 %collective-permute-start = (bf16[64,1280]{0,1:T(8,128)(2,1)}, bf16[64,1280]{0,1:T(8,128)(2,1)S(1)}, u32[]{:S(2)}, u32[]{:S(2)}) collective-permute-start(bf16[64,1280]{0,1:T(8,128)(2,1)} %bitcast.7), channel_id=1, source_target_pairs={{0,8},{8,0},{16,24},{24,16},{1,9},{9,1},{17,25},{25,17},{2,10},{10... | collective-permute-start | bytes 491528 | tf_op jit(solution)/shard_map/ppermute | solution.py:221
  10.2 16.0 %collective-permute-start.2 = (bf16[64,1280]{0,1:T(8,128)(2,1)S(1)}, bf16[64,1280]{0,1:T(8,128)(2,1)S(1)}, u32[]{:S(2)}, u32[]{:S(2)}) collective-permute-start(bf16[64,1280]{0,1:T(8,128)(2,1)S(1)} %bitcast.60), channel_id=1, source_target_pairs={{0,16},{8,24},{16,0},{24,8},{1,17},{9,25},{17,1},{25,9},{2,18},{10... | collective-permute-start | bytes 491528 | tf_op jit(solution)/shard_map/ppermute | solution.py:221
  12.0 17.2 %collective-permute-start.4 = (bf16[64,1280]{0,1:T(8,128)(2,1)S(1)}, bf16[64,1280]{0,1:T(8,128)(2,1)S(1)}, u32[]{:S(2)}, u32[]{:S(2)}) collective-permute-start(bf16[64,1280]{0,1:T(8,128)(2,1)S(1)} %bitcast.59), channel_id=1, source_target_pairs={{0,24},{8,16},{16,8},{24,0},{1,25},{9,17},{17,9},{25,1},{2,26},{10... | collective-permute-start | bytes 491528 | tf_op jit(solution)/shard_map/ppermute | solution.py:221
  19.7 10.2 %collective-permute-start.1 = (f32[64,512]{1,0:T(8,128)S(1)}, f32[64,512]{1,0:T(8,128)S(1)}, u32[]{:S(2)}, u32[]{:S(2)}) collective-permute-start(f32[64,512]{1,0:T(8,128)S(1)} %fusion.14), channel_id=1, source_target_pairs={{0,8},{8,0},{16,24},{24,16},{1,9},{9,1},{17,25},{25,17},{2,10},{10... | collective-permute-start | bytes 393224 | tf_op jit(solution)/shard_map/ppermute | solution.py:221
  29.7 6.9 %collective-permute-start.15 = (bf16[64,512]{1,0:T(8,128)(2,1)S(1)}, bf16[64,512]{1,0:T(8,128)(2,1)S(1)}, u32[]{:S(2)}, u32[]{:S(2)}) collective-permute-start(bf16[64,512]{1,0:T(8,128)(2,1)S(1)} %bitcast.72), channel_id=1, source_target_pairs={{0,6},{1,7},{2,4},{3,5},{4,2},{5,3},{6,0},{7,1},{8,14},{9,15},{10,... | collective-permute-start | bytes 196616 | tf_op jit(solution)/shard_map/ppermute | solution.py:221
  29.9 7.0 %collective-permute-start.16 = (bf16[64,512]{1,0:T(8,128)(2,1)S(1)}, bf16[64,512]{1,0:T(8,128)(2,1)}, u32[]{:S(2)}, u32[]{:S(2)}) collective-permute-start(bf16[64,512]{1,0:T(8,128)(2,1)S(1)} %bitcast.73), channel_id=1, source_target_pairs={{0,1},{1,0},{2,3},{3,2},{4,5},{5,4},{6,7},{7,6},{8,9},{9,8},{10,11... | collective-permute-start | bytes 196616 | tf_op jit(solution)/shard_map/ppermute | solution.py:221
  29.9 10.6 %collective-permute-start.17 = (bf16[64,512]{1,0:T(8,128)(2,1)S(1)}, bf16[64,512]{1,0:T(8,128)(2,1)S(1)}, u32[]{:S(2)}, u32[]{:S(2)}) collective-permute-start(bf16[64,512]{1,0:T(8,128)(2,1)S(1)} %collective-permute-done.13.refs_9_), channel_id=1, source_target_pairs={{0,1},{1,0},{2,3},{3,2},{4,5},{5,4},{6,7},{7,6},{8,9},{9,8},{10,11... | collective-permute-start | bytes 196616 | tf_op jit(solution)/shard_map/ppermute | solution.py:221
  32.1 9.0 %collective-permute-start.18 = (bf16[64,512]{1,0:T(8,128)(2,1)S(1)}, bf16[64,512]{1,0:T(8,128)(2,1)S(1)}, u32[]{:S(2)}, u32[]{:S(2)}) collective-permute-start(bf16[64,512]{1,0:T(8,128)(2,1)S(1)} %collective-permute-done.14.refs_10_), channel_id=1, source_target_pairs={{0,1},{1,0},{2,3},{3,2},{4,5},{5,4},{6,7},{7,6},{8,9},{9,8},{10,11... | collective-permute-start | bytes 196616 | tf_op jit(solution)/shard_map/ppermute | solution.py:221
  70.1 7.8 %collective-permute-start.21 = (f32[64,512]{1,0:T(8,128)S(1)}, f32[64,512]{1,0:T(8,128)S(1)}, u32[]{:S(2)}, u32[]{:S(2)}) collective-permute-start(f32[64,512]{1,0:T(8,128)S(1)} %get-tuple-element.41), channel_id=1, source_target_pairs={{0,2},{1,3},{2,0},{3,1},{4,6},{5,7},{6,4},{7,5},{8,10},{9,11},{10,... | collective-permute-start | bytes 393224 | tf_op jit(solution)/shard_map/ppermute | solution.py:221
  71.0 12.9 %collective-permute-start.22 = (f32[64,512]{1,0:T(8,128)S(1)}, f32[64,512]{1,0:T(8,128)S(1)}, u32[]{:S(2)}, u32[]{:S(2)}) collective-permute-start(f32[64,512]{1,0:T(8,128)S(1)} %get-tuple-element.43), channel_id=1, source_target_pairs={{0,4},{1,5},{2,6},{3,7},{4,0},{5,1},{6,2},{7,3},{8,12},{9,13},{10,... | collective-permute-start | bytes 393224 | tf_op jit(solution)/shard_map/ppermute | solution.py:221
  73.8 10.2 %collective-permute-start.23 = (f32[64,512]{1,0:T(8,128)S(1)}, f32[64,512]{1,0:T(8,128)S(1)}, u32[]{:S(2)}, u32[]{:S(2)}) collective-permute-start(f32[64,512]{1,0:T(8,128)S(1)} %get-tuple-element.42), channel_id=1, source_target_pairs={{0,6},{1,7},{2,4},{3,5},{4,2},{5,3},{6,0},{7,1},{8,14},{9,15},{10,... | collective-permute-start | bytes 393224 | tf_op jit(solution)/shard_map/ppermute | solution.py:221
  75.0 43.4 %collective-permute-start.24 = (bf16[1280,256]{1,0:T(8,128)(2,1)}, bf16[1280,256]{1,0:T(8,128)(2,1)S(1)}, u32[]{:S(2)}, u32[]{:S(2)}) collective-permute-start(bf16[1280,256]{1,0:T(8,128)(2,1)} %constant_dynamic-slice_fusion.4), channel_id=1, source_target_pairs={{0,8},{8,0},{16,24},{24,16},{1,9},{9,1},{17,25},{25,17},{2,10},{10... | collective-permute-start | bytes 1966088 | tf_op jit(solution)/shard_map/ppermute | solution.py:221
  75.6 45.3 %collective-permute-start.25 = (bf16[1280,256]{1,0:T(8,128)(2,1)}, bf16[1280,256]{1,0:T(8,128)(2,1)S(1)}, u32[]{:S(2)}, u32[]{:S(2)}) collective-permute-start(bf16[1280,256]{1,0:T(8,128)(2,1)} %constant_dynamic-slice_fusion.4), channel_id=1, source_target_pairs={{0,16},{8,24},{16,0},{24,8},{1,17},{9,25},{17,1},{25,9},{2,18},{10... | collective-permute-start | bytes 1966088 | tf_op jit(solution)/shard_map/ppermute | solution.py:221
  77.9 43.1 %collective-permute-start.26 = (bf16[1280,256]{1,0:T(8,128)(2,1)}, bf16[1280,256]{1,0:T(8,128)(2,1)S(1)}, u32[]{:S(2)}, u32[]{:S(2)}) collective-permute-start(bf16[1280,256]{1,0:T(8,128)(2,1)} %constant_dynamic-slice_fusion.4), channel_id=1, source_target_pairs={{0,24},{8,16},{16,8},{24,0},{1,25},{9,17},{17,9},{25,1},{2,26},{10... | collective-permute-start | bytes 1966088 | tf_op jit(solution)/shard_map/ppermute | solution.py:221
  83.9 8.0 %collective-permute-start.30 = (bf16[320,256]{1,0:T(8,128)(2,1)S(1)}, bf16[320,256]{1,0:T(8,128)(2,1)S(1)}, u32[]{:S(2)}, u32[]{:S(2)}) collective-permute-start(bf16[320,256]{1,0:T(8,128)(2,1)S(1)} %get-tuple-element.32), channel_id=1, source_target_pairs={{0,2},{1,3},{2,0},{3,1},{4,6},{5,7},{6,4},{7,5},{8,10},{9,11},{10,... | collective-permute-start | bytes 491528 | tf_op jit(solution)/shard_map/ppermute | solution.py:221
  83.9 10.6 %collective-permute-start.31 = (bf16[320,256]{1,0:T(8,128)(2,1)S(1)}, bf16[320,256]{1,0:T(8,128)(2,1)S(1)}, u32[]{:S(2)}, u32[]{:S(2)}) collective-permute-start(bf16[320,256]{1,0:T(8,128)(2,1)S(1)} %get-tuple-element.31), channel_id=1, source_target_pairs={{0,4},{1,5},{2,6},{3,7},{4,0},{5,1},{6,2},{7,3},{8,12},{9,13},{10,... | collective-permute-start | bytes 491528 | tf_op jit(solution)/shard_map/ppermute | solution.py:221
  91.9 10.3 %collective-permute-start.33 = (bf16[64,512]{1,0:T(8,128)(2,1)S(1)}, bf16[64,512]{1,0:T(8,128)(2,1)S(1)}, u32[]{:S(2)}, u32[]{:S(2)}) collective-permute-start(bf16[64,512]{1,0:T(8,128)(2,1)S(1)} %fusion.2.grad_ref), channel_id=1, source_target_pairs={{0,2},{1,3},{2,0},{3,1},{4,6},{5,7},{6,4},{7,5},{8,10},{9,11},{10,... | collective-permute-start | bytes 196616 | tf_op jit(solution)/shard_map/ppermute | solution.py:221
  94.5 7.8 %collective-permute-start.34 = (bf16[64,512]{1,0:T(8,128)(2,1)S(1)}, bf16[64,512]{1,0:T(8,128)(2,1)S(1)}, u32[]{:S(2)}, u32[]{:S(2)}) collective-permute-start(bf16[64,512]{1,0:T(8,128)(2,1)S(1)} %fusion.2.grad_ref), channel_id=1, source_target_pairs={{0,4},{1,5},{2,6},{3,7},{4,0},{5,1},{6,2},{7,3},{8,12},{9,13},{10,... | collective-permute-start | bytes 196616 | tf_op jit(solution)/shard_map/ppermute | solution.py:221
  102.2 14.5 %collective-permute-start.40 = (f32[256,512]{1,0:T(8,128)}, f32[256,512]{1,0:T(8,128)S(1)}, u32[]{:S(2)}, u32[]{:S(2)}) collective-permute-start(f32[256,512]{1,0:T(8,128)} %get-tuple-element.26), channel_id=1, source_target_pairs={{0,1},{1,0},{2,3},{3,2},{4,5},{5,4},{6,7},{7,6},{8,9},{9,8},{10,11... | collective-permute-start | bytes 1572872 | tf_op jit(solution)/shard_map/ppermute | solution.py:221
  108.7 7.5 %collective-permute-start.32 = (bf16[320,256]{1,0:T(8,128)(2,1)S(1)}, bf16[320,256]{1,0:T(8,128)(2,1)S(1)}, u32[]{:S(2)}, u32[]{:S(2)}) collective-permute-start(bf16[320,256]{1,0:T(8,128)(2,1)S(1)} %copy-done.17), channel_id=1, source_target_pairs={{0,6},{1,7},{2,4},{3,5},{4,2},{5,3},{6,0},{7,1},{8,14},{9,15},{10,... | collective-permute-start | bytes 491528 | tf_op jit(solution)/shard_map/ppermute | solution.py:221
  116.3 9.2 %collective-permute-start.36 = (bf16[4,64,512]{2,1,0:T(8,128)(2,1)S(1)}, bf16[4,64,512]{2,1,0:T(8,128)(2,1)S(1)}, u32[]{:S(2)}, u32[]{:S(2)}) collective-permute-start(bf16[4,64,512]{2,1,0:T(8,128)(2,1)S(1)} %pad_maximum_fusion.refs_4_), channel_id=1, source_target_pairs={{0,8},{8,0},{16,24},{24,16},{1,9},{9,1},{17,25},{25,17},{2,10},{10... | collective-permute-start | bytes 786440 | tf_op jit(solution)/shard_map/ppermute | solution.py:221
  116.7 11.4 %collective-permute-start.37 = (bf16[4,64,512]{2,1,0:T(8,128)(2,1)S(1)}, bf16[4,64,512]{2,1,0:T(8,128)(2,1)S(1)}, u32[]{:S(2)}, u32[]{:S(2)}) collective-permute-start(bf16[4,64,512]{2,1,0:T(8,128)(2,1)S(1)} %pad_maximum_fusion.refs_4_), channel_id=1, source_target_pairs={{0,16},{8,24},{16,0},{24,8},{1,17},{9,25},{17,1},{25,9},{2,18},{10... | collective-permute-start | bytes 786440 | tf_op jit(solution)/shard_map/ppermute | solution.py:221
  118.4 14.5 %collective-permute-start.38 = (bf16[4,64,512]{2,1,0:T(8,128)(2,1)S(1)}, bf16[4,64,512]{2,1,0:T(8,128)(2,1)S(1)}, u32[]{:S(2)}, u32[]{:S(2)}) collective-permute-start(bf16[4,64,512]{2,1,0:T(8,128)(2,1)S(1)} %pad_maximum_fusion.refs_4_), channel_id=1, source_target_pairs={{0,24},{8,16},{16,8},{24,0},{1,25},{9,17},{17,9},{25,1},{2,26},{10... | collective-permute-start | bytes 786440 | tf_op jit(solution)/shard_map/ppermute | solution.py:221
  120.9 31.0 %collective-permute-start.27 = (bf16[1280,256]{1,0:T(8,128)(2,1)S(1)}, bf16[1280,256]{1,0:T(8,128)(2,1)S(1)}, u32[]{:S(2)}, u32[]{:S(2)}) collective-permute-start(bf16[1280,256]{1,0:T(8,128)(2,1)S(1)} %collective-permute-done.24.refs_0_), channel_id=1, source_target_pairs={{0,1},{1,0},{2,3},{3,2},{4,5},{5,4},{6,7},{7,6},{8,9},{9,8},{10,11... | collective-permute-start | bytes 1966088 | tf_op jit(solution)/shard_map/ppermute | solution.py:221
  121.0 30.9 %collective-permute-start.28 = (bf16[1280,256]{1,0:T(8,128)(2,1)S(1)}, bf16[1280,256]{1,0:T(8,128)(2,1)S(1)}, u32[]{:S(2)}, u32[]{:S(2)}) collective-permute-start(bf16[1280,256]{1,0:T(8,128)(2,1)S(1)} %collective-permute-done.25.refs_1_), channel_id=1, source_target_pairs={{0,1},{1,0},{2,3},{3,2},{4,5},{5,4},{6,7},{7,6},{8,9},{9,8},{10,11... | collective-permute-start | bytes 1966088 | tf_op jit(solution)/shard_map/ppermute | solution.py:221
  125.5 26.4 %collective-permute-start.29 = (bf16[1280,256]{1,0:T(8,128)(2,1)S(1)}, bf16[1280,256]{1,0:T(8,128)(2,1)S(1)}, u32[]{:S(2)}, u32[]{:S(2)}) collective-permute-start(bf16[1280,256]{1,0:T(8,128)(2,1)S(1)} %collective-permute-done.26.refs_2_), channel_id=1, source_target_pairs={{0,1},{1,0},{2,3},{3,2},{4,5},{5,4},{6,7},{7,6},{8,9},{9,8},{10,11... | collective-permute-start | bytes 1966088 | tf_op jit(solution)/shard_map/ppermute | solution.py:221
  128.1 10.0 %collective-permute-start.41 = (f32[64,512]{1,0:T(8,128)S(1)}, f32[64,512]{1,0:T(8,128)S(1)}, u32[]{:S(2)}, u32[]{:S(2)}) collective-permute-start(f32[64,512]{1,0:T(8,128)S(1)} %get-tuple-element.38), channel_id=1, source_target_pairs={{0,2},{1,3},{2,0},{3,1},{4,6},{5,7},{6,4},{7,5},{8,10},{9,11},{10,... | collective-permute-start | bytes 393224 | tf_op jit(solution)/shard_map/ppermute | solution.py:221
  132.9 10.0 %collective-permute-start.42 = (f32[64,512]{1,0:T(8,128)S(1)}, f32[64,512]{1,0:T(8,128)S(1)}, u32[]{:S(2)}, u32[]{:S(2)}) collective-permute-start(f32[64,512]{1,0:T(8,128)S(1)} %get-tuple-element.40), channel_id=1, source_target_pairs={{0,4},{1,5},{2,6},{3,7},{4,0},{5,1},{6,2},{7,3},{8,12},{9,13},{10,... | collective-permute-start | bytes 393224 | tf_op jit(solution)/shard_map/ppermute | solution.py:221
  138.1 13.1 %collective-permute-start.43 = (f32[64,512]{1,0:T(8,128)S(1)}, f32[64,512]{1,0:T(8,128)S(1)}, u32[]{:S(2)}, u32[]{:S(2)}) collective-permute-start(f32[64,512]{1,0:T(8,128)S(1)} %get-tuple-element.39), channel_id=1, source_target_pairs={{0,6},{1,7},{2,4},{3,5},{4,2},{5,3},{6,0},{7,1},{8,14},{9,15},{10,... | collective-permute-start | bytes 393224 | tf_op jit(solution)/shard_map/ppermute | solution.py:221
  142.9 15.9 %collective-permute-start.39 = (f32[160,512]{1,0:T(8,128)}, f32[160,512]{1,0:T(8,128)S(1)}, u32[]{:S(2)}, u32[]{:S(2)}) collective-permute-start(f32[160,512]{1,0:T(8,128)} %get-tuple-element.23), channel_id=1, source_target_pairs={{0,1},{1,0},{2,3},{3,2},{4,5},{5,4},{6,7},{7,6},{8,9},{9,8},{10,11... | collective-permute-start | bytes 983048 | tf_op jit(solution)/shard_map/ppermute | solution.py:221
  (46 other events, 331.6 us)

commit v3 on v2

--- a/solution.py
+++ b/solution.py
@@ -32,17 +32,20 @@
     return jnp.concatenate([ref[:, i * head_dim : (i + 1) * head_dim] for i in range(heads)], axis=0)
 
 
-def score_kernel(pieces, length_ref, query_ref, upstream_ref, key_ref, value_ref, *refs):
+def attend_kernel(pieces, chained, length_ref, query_ref, upstream_ref, key_ref, value_ref, *refs):
     key_pieces, value_pieces = refs[:pieces], refs[pieces : 2 * pieces]
-    weights_ref, dscore_ref, near_ref, far_ref, key_grad_ref = refs[2 * pieces :]
+    query_grad_ref, key_grad_ref, value_grad_ref, *halves = refs[2 * pieces + 3 * chained :]
+    key_near_ref, key_far_ref, value_near_ref, value_far_ref = halves
     rows = query_ref.shape[0]
     own_len, head_dim = key_ref.shape
+    heads = query_ref.shape[1] // head_dim
     scale = head_dim ** -0.5
-    keys_t = jnp.concatenate([ref[...] for ref in key_pieces] + [key_ref[...]], axis=0).T
-    values_t = jnp.concatenate([ref[...] for ref in value_pieces] + [value_ref[...]], axis=0).T
-    prompt_len = keys_t.shape[1] - own_len
+    keys = jnp.concatenate([ref[...] for ref in key_pieces] + [key_ref[...]], axis=0)
+    values = jnp.concatenate([ref[...] for ref in value_pieces] + [value_ref[...]], axis=0)
+    keys_t, values_t = keys.T, values.T
+    prompt_len = keys.shape[0] - own_len
     queries, upstream = stack_heads(query_ref, head_dim), stack_heads(upstream_ref, head_dim)
-    stacked = queries.shape[0]
+    stacked = heads * rows
     live = lax.broadcasted_iota(jnp.int32, (stacked, 1), 0) % rows < length_ref[0, 0]
     own = (stacked, own_len)
     visible = lax.broadcasted_iota(jnp.int32, own, 1) <= lax.broadcasted_iota(jnp.int32, own, 0) % rows
@@ -59,101 +62,49 @@
     weighted = jnp.sum(exponent * dprob, axis=1, keepdims=True)
     inverse = jnp.where(live, 1.0 / total, 0.0)
     row_delta = weighted * inverse
-    weights_ref[0] = (exponent * inverse).astype(BF16)
+    weights = (exponent * inverse).astype(BF16)
     dscore = (exponent * ((dprob - row_delta) * (inverse * scale))).astype(BF16)
-    dscore_ref[0] = dscore
+    query_grad = dot(dscore, keys).astype(BF16)
+    for i in range(heads):
+        query_grad_ref[:, i * head_dim : (i + 1) * head_dim] = query_grad[i * rows : (i + 1) * rows]
     key_grad = dot(queries.T, dscore).T
-    near_ref[...] = key_grad[: prompt_len // 2]
-    far_ref[...] = key_grad[prompt_len // 2 : prompt_len]
+    value_grad = dot(upstream.T, weights).T
+    half = prompt_len // 2
+    key_near_ref[...], key_far_ref[...] = key_grad[:half], key_grad[half:prompt_len]
+    value_near_ref[...], value_far_ref[...] = value_grad[:half], value_grad[half:prompt_len]
     key_grad_ref[...] = key_grad[prompt_len:].astype(BF16)
-
-
-def column_block(rows, columns):
-    return pl.BlockSpec((rows, columns), lambda i: (0, i))
-
-
-def head_block(*shape):
-    return pl.BlockSpec((1,) + shape, lambda i: (i, 0, 0))
-
-
-def score_pass(length, queries, upstream, key_pieces, value_pieces, keys, values, head_dim):
+    value_grad_ref[...] = value_grad[prompt_len:].astype(BF16)
+
+
+def attend(length, queries, upstream, key_pieces, value_pieces, keys, values, head_dim, first, count, earlier):
     rows, width = queries.shape
     kv_width = keys.shape[1]
     kv_heads = kv_width // head_dim
-    stacked = rows * width // kv_width
     prompt_len = sum(piece.shape[0] for piece in key_pieces)
-    every = prompt_len + rows
-    query_block, own_block = column_block(rows, width // kv_heads), column_block(rows, head_dim)
-    piece_blocks = [column_block(piece.shape[0], head_dim) for piece in key_pieces]
-    half_block = column_block(prompt_len // 2, head_dim)
-    pair = jax.ShapeDtypeStruct((kv_heads, stacked, every), BF16)
-    half = jax.ShapeDtypeStruct((prompt_len // 2, kv_width), F32)
+
+    def block(rows, columns, offset=first):
+        return pl.BlockSpec((rows, columns), lambda i: (0, i + offset))
+
+    query_block, own_block = block(rows, width // kv_heads), block(rows, head_dim)
+    piece_blocks = [block(piece.shape[0], head_dim) for piece in key_pieces]
+    half = jax.ShapeDtypeStruct((prompt_len // 2, count * head_dim), F32)
+    own = jax.ShapeDtypeStruct((rows, kv_width), BF16)
+    before = 5 + 2 * len(key_pieces)
+    macs = 5 * rows * width * (prompt_len + rows) * count // kv_heads
     return pl.pallas_call(
-        partial(score_kernel, len(key_pieces)),
-        grid=(kv_heads,),
+        partial(attend_kernel, len(key_pieces), bool(earlier)),
+        grid=(count,),
         in_specs=[
             pl.BlockSpec(memory_space=pltpu.SMEM), query_block, query_block, own_block, own_block,
-            *piece_blocks, *piece_blocks,
+            *piece_blocks, *piece_blocks, *[pl.BlockSpec(memory_space=pl.ANY) for _ in earlier],
         ],
-        out_specs=[head_block(stacked, every)] * 2 + [half_block] * 2 + [own_block],
-        out_shape=[pair, pair, half, half, jax.ShapeDtypeStruct((rows, kv_width), BF16)],
+        out_specs=[query_block, own_block, own_block] + [block(prompt_len // 2, head_dim, 0)] * 4,
+        out_shape=[jax.ShapeDtypeStruct((rows, width), BF16), own, own] + [half] * 4,
+        input_output_aliases={before + i: i for i in range(len(earlier))},
         compiler_params=PARAMS,
-        cost_estimate=cost(6 * rows * width * every, 2 * 10**7),
-        name="scores",
-    )(length, queries, upstream, keys, values, *key_pieces, *value_pieces)
-
-
-def value_kernel(upstream_ref, weights_ref, near_ref, far_ref, value_grad_ref):
-    half, head_dim = near_ref.shape
-    upstream = stack_heads(upstream_ref, head_dim)
-    value_grad = dot(upstream.T, weights_ref[0]).T
-    near_ref[...] = value_grad[:half]
-    far_ref[...] = value_grad[half : 2 * half]
-    value_grad_ref[...] = value_grad[2 * half :].astype(BF16)
-
-
-def value_pass(upstream, weights, head_dim):
-    rows, width = upstream.shape
-    kv_heads, stacked, every = weights.shape
-    kv_width = kv_heads * head_dim
-    half = (every - rows) // 2
-    out = jax.ShapeDtypeStruct((half, kv_width), F32)
-    return pl.pallas_call(
-        value_kernel,
-        grid=(kv_heads,),
-        in_specs=[column_block(rows, width // kv_heads), head_block(stacked, every)],
-        out_specs=[column_block(half, head_dim)] * 2 + [column_block(rows, head_dim)],
-        out_shape=[out, out, jax.ShapeDtypeStruct((rows, kv_width), BF16)],
-        compiler_params=PARAMS,
-        cost_estimate=cost(rows * width * every, 1 * 10**7),
-        name="value_grads",
-    )(upstream, weights)
-
-
-def query_kernel(dscore_ref, key_ref, *refs):
-    key_pieces, query_grad_ref = refs[:-1], refs[-1]
-    rows, head_dim = query_grad_ref.shape[0], key_ref.shape[1]
-    keys = jnp.concatenate([ref[...] for ref in key_pieces] + [key_ref[...]], axis=0)
-    query_grad = dot(dscore_ref[0], keys).astype(BF16)
-    for i in range(query_grad_ref.shape[1] // head_dim):
-        query_grad_ref[:, i * head_dim : (i + 1) * head_dim] = query_grad[i * rows : (i + 1) * rows]
-
-
-def query_pass(dscore, key_pieces, keys, head_dim):
-    kv_heads, stacked, every = dscore.shape
-    rows, kv_width = keys.shape
-    width = stacked // rows * kv_width
-    return pl.pallas_call(
-        query_kernel,
-        grid=(kv_heads,),
-        in_specs=[head_block(stacked, every)]
-        + [column_block(piece.shape[0], head_dim) for piece in [keys] + key_pieces],
-        out_specs=column_block(rows, width // kv_heads),
-        out_shape=jax.ShapeDtypeStruct((rows, width), BF16),
-        compiler_params=PARAMS,
-        cost_estimate=cost(rows * width * every, 1 * 10**7),
-        name="query_grads",
-    )(dscore, keys, *key_pieces)
+        cost_estimate=cost(2 * macs, 5 * 10**6),
+        name="attend",
+    )(length, queries, upstream, keys, values, *key_pieces, *value_pieces, *earlier)
 
 
 def hidden_kernel(groups, place_ref, grad_ref, own_ref, *refs):
@@ -233,8 +184,11 @@
     return [swap(piece, "resp", size, 1) for piece in near]
 
 
-def collect(near, far, size):
-    near = near + swap(far, "resp", size, 1)
+def pair_sum(near, far, size):
+    return near + swap(far, "resp", size, 1)
+
+
+def chip_sum(near, size):
     rows = near.shape[0] // (size // 2)
     total = near[:rows]
     for p in range(1, size // 2):
@@ -262,7 +216,7 @@
     key_pre = partials[0]
     for k in range(1, groups):
         key_pre = key_pre + swap(partials[k], "group", groups, k)
-    value_near = spread_near(prompt_token_value[0], responses)
+    value_near = spread_near(after(prompt_token_value[0], *columns), responses)
     value_pieces = value_near + spread_far(value_near, responses)
 
     prompt_key = norm_keys(key_pre, key_gain).astype(BF16)
@@ -285,16 +239,21 @@
     weight_near = [swap(half_weight, "group", groups, k) for k in range(1, groups)]
 
     queries, upstream = resp_query[0, 0], grad_out[0, 0]
-    weights, dscore, near, far, key_grad = score_pass(
-        resp_length, queries, upstream, key_pieces, value_pieces,
-        resp_key[0, 0], response_value[0, 0], head_dim,
-    )
-    prompt_key_grad = collect(near, far, responses)
+    rest = (queries, upstream, key_pieces, value_pieces, resp_key[0, 0], response_value[0, 0], head_dim)
+    count = kv_width // head_dim // 2
+    earlier, key_parts, value_parts, length = [], [], [], resp_length
+    for first in (0, count):
+        *earlier, key_near, key_far, value_near, value_far = attend(length, *rest, first, count, earlier)
+        key_near = pair_sum(key_near, key_far, responses)
+        value_near = pair_sum(value_near, value_far, responses)
+        length = after(resp_length, key_near, value_near, *taken)
+        key_parts.append(chip_sum(key_near, responses))
+        value_parts.append(chip_sum(value_near, responses))
+    query_grad, key_grad, value_grad = earlier
+    prompt_key_grad = jnp.concatenate(key_parts, axis=1)
+    prompt_value_grad = jnp.concatenate(value_parts, axis=1)
     _, pullback = jax.vjp(lambda values: norm_keys(values, key_gain), key_pre)
     key_pre_grad = pullback(prompt_key_grad)[0].astype(BF16)
-
-    value_near, value_far, value_grad = value_pass(upstream, weights, head_dim)
-    query_grad = query_pass(dscore, key_pieces, resp_key[0, 0], head_dim)
 
     block = jnp.stack(spread_near(key_pre_grad, responses), axis=0)
     blocks = [block] + [swap(block, "group", groups, k) for k in range(1, groups)]
@@ -303,7 +262,6 @@
 
     weight_far = [swap(piece, "resp", responses, 1) for piece in weight_near]
     grad_hidden = hidden_pass(place, key_pre_grad, key_matrix, weight_near, weight_far)
-    prompt_value_grad = collect(value_near, value_far, responses)
     return (
         grad_hidden[None],
         grad_weight,

time: 160 us -> 161 us (level)
  Pallas kernels: 45 us -> 31.6 us
  waiting for transfers between devices: 50.6 us -> 60.7 us
  starting transfers between devices: 46.4 us -> 53.4 us
  local copies, waits for them, and re-layouts: 9.04 us -> 6.97 us
    pallas_call x3 -> x2, Pallas kernels: 37.1 us -> 23.7 us  [attend(): pl.pallas_call(partial(attend_kernel, len(key_pieces), bool(earlier)), gr...]
    ppermute x44 -> x52, waiting for transfers between devices: 50.6 us -> 60.7 us  [swap(): return lax.ppermute(array, axis, [(i, i ^ distance) for i in range(size)])]
    ppermute x44 -> x52, starting transfers between devices: 46.4 us -> 53.4 us  [swap(): return lax.ppermute(array, axis, [(i, i ^ distance) for i in range(size)])]
    add x3 -> x6, other arithmetic: 2.28 us -> 0.17 us  [the longest x4 0.14 us: pair_sum(): return near + swap(far, 'resp', size, 1)]
    unnamed x68 -> x64, local copies, waits for them, and re-layouts: 3.79 us -> 2.55 us
  transfers between devices with their start and end apart: 44 -> 52, of which waited for: 16 -> 22; matrix products, arithmetic and copies ran while one was open for 6% -> 5% of each run, Pallas kernels for 15% -> 9%
where the time goes in v3:
time: 161 us; the launch traced here: 160 us
  waiting for transfers between devices  60.7 us (38%)
  starting transfers between devices  53.4 us (33%)
  Pallas kernels  31.6 us (20%)
  local copies, waits for them, and re-layouts  6.97 us (4%)
  other arithmetic  4.14 us (3%)
  between operations  1.96 us (1%)
    ppermute x52, waiting for transfers between devices, swap(): return lax.ppermute(array, axis, [(i, i ^ distance) for i in range(size)])  60.7 us
    ppermute x52, starting transfers between devices, swap(): return lax.ppermute(array, axis, [(i, i ^ distance) for i in range(size)])  53.4 us
    pallas_call x2, Pallas kernels, attend(): pl.pallas_call(partial(attend_kernel, len(key_pieces), bool(earlier)), gr...  23.7 us
    pallas_call x1, Pallas kernels, hidden_pass(): pl.pallas_call(partial(hidden_kernel, groups), in_specs=[pl.BlockSpec(mem...  5.02 us
  transfers between devices with their start and end apart: 52, of which 22 were waited for; matrix products, arithmetic and copies ran while one was open for 5% of the time, Pallas kernels for 9%

profile of v3, /device:TPU:0, one launch (start us, length us, event | category | flops | bytes accessed | tf_op | source)
XLA Modules:
  0.0 160.1 jit_solution(9552306563961769787)
XLA Ops:
  2.1 3.0 %collective-permute-start = (bf16[64,1280]{0,1:T(8,128)(2,1)S(1)}, bf16[64,1280]{0,1:T(8,128)(2,1)S(1)}, u32[]{:S(2)}, u32[]{:S(2)}) collective-permute-start(bf16[64,1280]{0,1:T(8,128)(2,1)S(1)} %bitcast.58), channel_id=1, source_target_pairs={{0,8},{8,0},{16,24},{24,16},{1,9},{9,1},{17,25},{25,17},{2,10},{10... | collective-permute-start | bytes 491528 | tf_op jit(solution)/shard_map/ppermute | solution.py:172
  8.4 5.2 %collective-permute-done = bf16[64,1280]{0,1:T(8,128)(2,1)S(1)} collective-permute-done((bf16[64,1280]{0,1:T(8,128)(2,1)S(1)}, bf16[64,1280]{0,1:T(8,128)(2,1)S(1)}, u32[]{:S(2)}, u32[]{:S(2)}) %collective-permute-start) | collective-permute-done | bytes 163872 | tf_op jit(solution)/shard_map/ppermute | solution.py:172
  13.6 8.0 %collective-permute-done.2 = bf16[64,1280]{0,1:T(8,128)(2,1)S(1)} collective-permute-done((bf16[64,1280]{0,1:T(8,128)(2,1)S(1)}, bf16[64,1280]{0,1:T(8,128)(2,1)S(1)}, u32[]{:S(2)}, u32[]{:S(2)}) %collective-permute-start.2) | collective-permute-done | bytes 163872 | tf_op jit(solution)/shard_map/ppermute | solution.py:172
  23.2 2.6 %collective-permute-start.14 = (bf16[64,512]{1,0:T(8,128)(2,1)S(1)}, bf16[64,512]{1,0:T(8,128)(2,1)S(1)}, u32[]{:S(2)}, u32[]{:S(2)}) collective-permute-start(bf16[64,512]{1,0:T(8,128)(2,1)S(1)} %bitcast.74), channel_id=1, source_target_pairs={{0,4},{1,5},{2,6},{3,7},{4,0},{5,1},{6,2},{7,3},{8,12},{9,13},{10,... | collective-permute-start | bytes 196616 | tf_op jit(solution)/shard_map/ppermute | solution.py:172
  32.9 2.0 %collective-permute-done.5 = f32[64,512]{1,0:T(8,128)S(1)} collective-permute-done((f32[64,512]{1,0:T(8,128)S(1)}, f32[64,512]{1,0:T(8,128)S(1)}, u32[]{:S(2)}, u32[]{:S(2)}) %collective-permute-start.5) | collective-permute-done | bytes 131104 | tf_op jit(solution)/shard_map/ppermute | solution.py:172
  36.7 3.3 %collective-permute-start.8 = (bf16[64,512]{1,0:T(8,128)(2,1)S(1)}, bf16[64,512]{1,0:T(8,128)(2,1)S(1)}, u32[]{:S(2)}, u32[]{:S(2)}) collective-permute-start(bf16[64,512]{1,0:T(8,128)(2,1)S(1)} %fusion.4.refs_0_), channel_id=1, source_target_pairs={{0,6},{1,7},{2,4},{3,5},{4,2},{5,3},{6,0},{7,1},{8,14},{9,15},{10,... | collective-permute-start | bytes 196616 | tf_op jit(solution)/shard_map/ppermute | solution.py:172
  41.4 2.1 %collective-permute-done.7.refs_2_ = bf16[64,512]{1,0:T(8,128)(2,1)} collective-permute-done((bf16[64,512]{1,0:T(8,128)(2,1)S(1)}, bf16[64,512]{1,0:T(8,128)(2,1)}, u32[]{:S(2)}, u32[]{:S(2)}) %collective-permute-start.7) | collective-permute-done | bytes 65568 | tf_op jit(solution)/shard_map/ppermute | solution.py:172
  45.6 11.9 %attend.2 = (bf16[256,4096]{1,0:T(8,128)(2,1)}, bf16[256,512]{1,0:T(8,128)(2,1)}, bf16[256,512]{1,0:T(8,128)(2,1)}, f32[256,256]{1,0:T(8,128)}, f32[256,256]{1,0...) custom-call(s32[1,1]{1,0:T(1,128)S(6)} %copy.44.length_ref, bf16[256,4096]{1,0:T(8,128)(2,1)} %bitcast.63, ...), custom_call_target="tpu_custom_call" | custom-call | flops 8053063680 | bytes 5000000 | tf_op jit(solution)/shard_map/attend/pallas_call | solution.py:94
  57.9 11.8 %attend.3 = (bf16[256,4096]{1,0:T(8,128)(2,1)}, bf16[256,512]{1,0:T(8,128)(2,1)}, bf16[256,512]{1,0:T(8,128)(2,1)}, f32[256,256]{1,0:T(8,128)}, f32[256,256]{1,0...) custom-call(s32[1,1]{1,0:T(1,128)S(6)} %copy.44.length_ref, ...), custom_call_target="tpu_custom_call", output_to_operand_aliasing={{0}: (21, {}), {1}: (22, {}), {2}: (23, {})} | custom-call | flops 8053063680 | bytes 5000000 | tf_op jit(solution)/shard_map/attend/pallas_call | solution.py:94
  71.8 2.1 %collective-permute-start.26 = (bf16[320,256]{1,0:T(8,128)(2,1)}, bf16[320,256]{1,0:T(8,128)(2,1)}, u32[]{:S(2)}, u32[]{:S(2)}) collective-permute-start(bf16[320,256]{1,0:T(8,128)(2,1)} %get-tuple-element.47), channel_id=1, source_target_pairs={{0,4},{1,5},{2,6},{3,7},{4,0},{5,1},{6,2},{7,3},{8,12},{9,13},{10,... | collective-permute-start | bytes 491528 | tf_op jit(solution)/shard_map/ppermute | solution.py:172
  73.9 2.0 %collective-permute-start.22 = (f32[64,256]{1,0:T(8,128)S(1)}, f32[64,256]{1,0:T(8,128)S(1)}, u32[]{:S(2)}, u32[]{:S(2)}) collective-permute-start(f32[64,256]{1,0:T(8,128)S(1)} %get-tuple-element.62), channel_id=1, source_target_pairs={{0,4},{1,5},{2,6},{3,7},{4,0},{5,1},{6,2},{7,3},{8,12},{9,13},{10,... | collective-permute-start | bytes 196616 | tf_op jit(solution)/shard_map/ppermute | solution.py:172
  75.9 2.4 %collective-permute-start.23 = (f32[64,256]{1,0:T(8,128)S(1)}, f32[64,256]{1,0:T(8,128)S(1)}, u32[]{:S(2)}, u32[]{:S(2)}) collective-permute-start(f32[64,256]{1,0:T(8,128)S(1)} %get-tuple-element.61), channel_id=1, source_target_pairs={{0,6},{1,7},{2,4},{3,5},{4,2},{5,3},{6,0},{7,1},{8,14},{9,15},{10,... | collective-permute-start | bytes 196616 | tf_op jit(solution)/shard_map/ppermute | solution.py:172
  78.4 3.5 %collective-permute-done.21 = f32[64,256]{1,0:T(8,128)S(1)} collective-permute-done((f32[64,256]{1,0:T(8,128)S(1)}, f32[64,256]{1,0:T(8,128)S(1)}, u32[]{:S(2)}, u32[]{:S(2)}) %collective-permute-start.21) | collective-permute-done | bytes 65568 | tf_op jit(solution)/shard_map/ppermute | solution.py:172
  81.8 2.1 %collective-permute-start.29 = (f32[64,256]{1,0:T(8,128)S(1)}, f32[64,256]{1,0:T(8,128)S(1)}, u32[]{:S(2)}, u32[]{:S(2)}) collective-permute-start(f32[64,256]{1,0:T(8,128)S(1)} %get-tuple-element.63), channel_id=1, source_target_pairs={{0,2},{1,3},{2,0},{3,1},{4,6},{5,7},{6,4},{7,5},{8,10},{9,11},{10,... | collective-permute-start | bytes 196616 | tf_op jit(solution)/shard_map/ppermute | solution.py:172
  84.0 4.4 %collective-permute-done.22 = f32[64,256]{1,0:T(8,128)S(1)} collective-permute-done((f32[64,256]{1,0:T(8,128)S(1)}, f32[64,256]{1,0:T(8,128)S(1)}, u32[]{:S(2)}, u32[]{:S(2)}) %collective-permute-start.22) | collective-permute-done | bytes 65568 | tf_op jit(solution)/shard_map/ppermute | solution.py:172
  89.5 2.8 %collective-permute-start.27 = (bf16[320,256]{1,0:T(8,128)(2,1)}, bf16[320,256]{1,0:T(8,128)(2,1)S(1)}, u32[]{:S(2)}, u32[]{:S(2)}) collective-permute-start(bf16[320,256]{1,0:T(8,128)(2,1)} %get-tuple-element.46), channel_id=1, source_target_pairs={{0,6},{1,7},{2,4},{3,5},{4,2},{5,3},{6,0},{7,1},{8,14},{9,15},{10,... | collective-permute-start | bytes 491528 | tf_op jit(solution)/shard_map/ppermute | solution.py:172
  92.3 5.2 %collective-permute-done.30 = f32[64,256]{1,0:T(8,128)S(1)} collective-permute-done((f32[64,256]{1,0:T(8,128)S(1)}, f32[64,256]{1,0:T(8,128)S(1)}, u32[]{:S(2)}, u32[]{:S(2)}) %collective-permute-start.30) | collective-permute-done | bytes 65568 | tf_op jit(solution)/shard_map/ppermute | solution.py:172
  100.2 1.8 %collective-permute-start.32 = (bf16[1280,256]{1,0:T(8,128)(2,1)S(1)}, bf16[1280,256]{1,0:T(8,128)(2,1)S(1)}, u32[]{:S(2)}, u32[]{:S(2)}) collective-permute-start(bf16[1280,256]{1,0:T(8,128)(2,1)S(1)} %constant_dynamic-slice_fusion), channel_id=1, source_target_pairs={{0,8},{8,0},{16,24},{24,16},{1,9},{9,1},{17,25},{25,17},{2,10},{10... | collective-permute-start | bytes 1966088 | tf_op jit(solution)/shard_map/ppermute | solution.py:172
  104.1 1.8 %collective-permute-start.39 = (bf16[64,512]{1,0:T(8,128)(2,1)S(1)}, bf16[64,512]{1,0:T(8,128)(2,1)S(1)}, u32[]{:S(2)}, u32[]{:S(2)}) collective-permute-start(bf16[64,512]{1,0:T(8,128)(2,1)S(1)} %fusion.2.grad_ref), channel_id=1, source_target_pairs={{0,4},{1,5},{2,6},{3,7},{4,0},{5,1},{6,2},{7,3},{8,12},{9,13},{10,... | collective-permute-start | bytes 196616 | tf_op jit(solution)/shard_map/ppermute | solution.py:172
  107.1 5.0 %collective-permute-done.39 = bf16[64,512]{1,0:T(8,128)(2,1)S(1)} collective-permute-done((bf16[64,512]{1,0:T(8,128)(2,1)S(1)}, bf16[64,512]{1,0:T(8,128)(2,1)S(1)}, u32[]{:S(2)}, u32[]{:S(2)}) %collective-permute-start.39) | collective-permute-done | bytes 65568 | tf_op jit(solution)/shard_map/ppermute | solution.py:172
  112.1 3.0 %collective-permute-start.46 = (f32[64,256]{1,0:T(8,128)S(1)}, f32[64,256]{1,0:T(8,128)S(1)}, u32[]{:S(2)}, u32[]{:S(2)}) collective-permute-start(f32[64,256]{1,0:T(8,128)S(1)} %get-tuple-element.56), channel_id=1, source_target_pairs={{0,4},{1,5},{2,6},{3,7},{4,0},{5,1},{6,2},{7,3},{8,12},{9,13},{10,... | collective-permute-start | bytes 196616 | tf_op jit(solution)/shard_map/ppermute | solution.py:172
  116.3 2.4 %collective-permute-start.47 = (f32[64,256]{1,0:T(8,128)S(1)}, f32[64,256]{1,0:T(8,128)S(1)}, u32[]{:S(2)}, u32[]{:S(2)}) collective-permute-start(f32[64,256]{1,0:T(8,128)S(1)} %get-tuple-element.55), channel_id=1, source_target_pairs={{0,6},{1,7},{2,4},{3,5},{4,2},{5,3},{6,0},{7,1},{8,14},{9,15},{10,... | collective-permute-start | bytes 196616 | tf_op jit(solution)/shard_map/ppermute | solution.py:172
  119.4 3.1 %collective-permute-done.47 = f32[64,256]{1,0:T(8,128)S(1)} collective-permute-done((f32[64,256]{1,0:T(8,128)S(1)}, f32[64,256]{1,0:T(8,128)S(1)}, u32[]{:S(2)}, u32[]{:S(2)}) %collective-permute-start.47) | collective-permute-done | bytes 65568 | tf_op jit(solution)/shard_map/ppermute | solution.py:172
  122.5 4.3 %collective-permute-done.49 = f32[64,256]{1,0:T(8,128)S(1)} collective-permute-done((f32[64,256]{1,0:T(8,128)S(1)}, f32[64,256]{1,0:T(8,128)S(1)}, u32[]{:S(2)}, u32[]{:S(2)}) %collective-permute-start.49) | collective-permute-done | bytes 65568 | tf_op jit(solution)/shard_map/ppermute | solution.py:172
  129.3 2.1 %collective-permute-done.33.refs_1_ = bf16[1280,256]{1,0:T(8,128)(2,1)S(1)} collective-permute-done((bf16[1280,256]{1,0:T(8,128)(2,1)S(1)}, bf16[1280,256]{1,0:T(8,128)(2,1)S(1)}, u32[]{:S(2)}, u32[]{:S(2)}) %collective-permute-start.33) | collective-permute-done | bytes 655392 | tf_op jit(solution)/shard_map/ppermute | solution.py:172
  131.4 2.1 %collective-permute-done.34.refs_2_ = bf16[1280,256]{1,0:T(8,128)(2,1)S(1)} collective-permute-done((bf16[1280,256]{1,0:T(8,128)(2,1)S(1)}, bf16[1280,256]{1,0:T(8,128)(2,1)S(1)}, u32[]{:S(2)}, u32[]{:S(2)}) %collective-permute-start.34) | collective-permute-done | bytes 655392 | tf_op jit(solution)/shard_map/ppermute | solution.py:172
  133.5 4.1 %collective-permute-done.41.refs_5_ = bf16[4,64,512]{2,1,0:T(8,128)(2,1)S(1)} collective-permute-done((bf16[4,64,512]{2,1,0:T(8,128)(2,1)S(1)}, bf16[4,64,512]{2,1,0:T(8,128)(2,1)S(1)}, u32[]{:S(2)}, u32[]{:S(2)}) %collective-permute-start.41) | collective-permute-done | bytes 262176 | tf_op jit(solution)/shard_map/ppermute | solution.py:172
  138.3 4.0 %collective-permute-done.42.refs_6_ = bf16[4,64,512]{2,1,0:T(8,128)(2,1)S(1)} collective-permute-done((bf16[4,64,512]{2,1,0:T(8,128)(2,1)S(1)}, bf16[4,64,512]{2,1,0:T(8,128)(2,1)S(1)}, u32[]{:S(2)}, u32[]{:S(2)}) %collective-permute-start.42) | collective-permute-done | bytes 262176 | tf_op jit(solution)/shard_map/ppermute | solution.py:172
  144.0 2.6 %collective-permute-start.51 = (f32[64,256]{1,0:T(8,128)S(1)}, f32[64,256]{1,0:T(8,128)S(1)}, u32[]{:S(2)}, u32[]{:S(2)}) collective-permute-start(f32[64,256]{1,0:T(8,128)S(1)} %get-tuple-element.58), channel_id=1, source_target_pairs={{0,6},{1,7},{2,4},{3,5},{4,2},{5,3},{6,0},{7,1},{8,14},{9,15},{10,... | collective-permute-start | bytes 196616 | tf_op jit(solution)/shard_map/ppermute | solution.py:172
  146.7 2.8 %weight_grad.1 = (f32[160,512]{1,0:T(8,128)}, f32[160,512]{1,0:T(8,128)}) custom-call(s32[2]{0:T(128)} %pad_add_fusion.place_ref, bf16[320,256]{1,0:T(8,128)(2,1)} %get-tuple-element.49.refs_0_, bf16[320,256]{1,0:T(8,128)(2,1)} %copy-done.16, bf16[320,256]{1,0:T(8,128)(2,1)} %collective-permute-done.26.refs_2_, bf16[320,256]{1,0:T(8,128)(2,1)} %copy-done.17, ...), custom_call_target="tpu_custom_call" | custom-call | flops 335544320 | bytes 3000000 | tf_op jit(solution)/shard_map/weight_grad/pallas_call | solution.py:158
  151.4 1.7 %add.129 = f32[160,512]{1,0:T(8,128)} add(f32[160,512]{1,0:T(8,128)} %get-tuple-element.39, f32[160,512]{1,0:T(8,128)S(1)} %collective-permute-done.44) | non-fusion elementwise | flops 81920 | bytes 983040 | tf_op jit(solution)/shard_map/add | solution.py:261
  155.1 5.0 %hidden_grad.1 = bf16[64,5120]{1,0:T(8,128)(2,1)} custom-call(s32[2]{0:T(128)} %pad_add_fusion.place_ref, bf16[64,512]{1,0:T(8,128)(2,1)} %copy-done.8, bf16[1280,512]{1,0:T(8,128)(2,1)} %own_ref.1, bf16[1280,256]{1,0:T(8,128)(2,1)} %copy-done.2, bf16[1280,256]{1,0:T(8,128)(2,1)} %copy-done.3, bf16[1280,256]{1,0:T(8,128)(2,1)} %copy-done.4, ...), custom_call_target="tpu_custom_call" | custom-call | flops 335544320 | bytes 6000000 | tf_op jit(solution)/shard_map/hidden_grad/pallas_call | solution.py:130
  (185 shorter events, 38.1 us)
Async XLA Ops:
  2.1 11.5 %collective-permute-start = (bf16[64,1280]{0,1:T(8,128)(2,1)S(1)}, bf16[64,1280]{0,1:T(8,128)(2,1)S(1)}, u32[]{:S(2)}, u32[]{:S(2)}) collective-permute-start(bf16[64,1280]{0,1:T(8,128)(2,1)S(1)} %bitcast.58), channel_id=1, source_target_pairs={{0,8},{8,0},{16,24},{24,16},{1,9},{9,1},{17,25},{25,17},{2,10},{10... | collective-permute-start | bytes 491528 | tf_op jit(solution)/shard_map/ppermute | solution.py:172
  5.3 16.3 %collective-permute-start.2 = (bf16[64,1280]{0,1:T(8,128)(2,1)S(1)}, bf16[64,1280]{0,1:T(8,128)(2,1)S(1)}, u32[]{:S(2)}, u32[]{:S(2)}) collective-permute-start(bf16[64,1280]{0,1:T(8,128)(2,1)S(1)} %bitcast.59), channel_id=1, source_target_pairs={{0,16},{8,24},{16,0},{24,8},{1,17},{9,25},{17,1},{25,9},{2,18},{10... | collective-permute-start | bytes 491528 | tf_op jit(solution)/shard_map/ppermute | solution.py:172
  7.8 13.8 %collective-permute-start.4 = (bf16[64,1280]{0,1:T(8,128)(2,1)}, bf16[64,1280]{0,1:T(8,128)(2,1)S(1)}, u32[]{:S(2)}, u32[]{:S(2)}) collective-permute-start(bf16[64,1280]{0,1:T(8,128)(2,1)} %bitcast.9), channel_id=1, source_target_pairs={{0,24},{8,16},{16,8},{24,0},{1,25},{9,17},{17,9},{25,1},{2,26},{10... | collective-permute-start | bytes 491528 | tf_op jit(solution)/shard_map/ppermute | solution.py:172
  21.6 9.0 %collective-permute-start.13 = (bf16[64,512]{1,0:T(8,128)(2,1)S(1)}, bf16[64,512]{1,0:T(8,128)(2,1)S(1)}, u32[]{:S(2)}, u32[]{:S(2)}) collective-permute-start(bf16[64,512]{1,0:T(8,128)(2,1)S(1)} %bitcast.73), channel_id=1, source_target_pairs={{0,2},{1,3},{2,0},{3,1},{4,6},{5,7},{6,4},{7,5},{8,10},{9,11},{10,... | collective-permute-start | bytes 196616 | tf_op jit(solution)/shard_map/ppermute | solution.py:172
  23.2 7.7 %collective-permute-start.14 = (bf16[64,512]{1,0:T(8,128)(2,1)S(1)}, bf16[64,512]{1,0:T(8,128)(2,1)S(1)}, u32[]{:S(2)}, u32[]{:S(2)}) collective-permute-start(bf16[64,512]{1,0:T(8,128)(2,1)S(1)} %bitcast.74), channel_id=1, source_target_pairs={{0,4},{1,5},{2,6},{3,7},{4,0},{5,1},{6,2},{7,3},{8,12},{9,13},{10,... | collective-permute-start | bytes 196616 | tf_op jit(solution)/shard_map/ppermute | solution.py:172
  32.4 8.3 %collective-permute-start.17 = (bf16[64,512]{1,0:T(8,128)(2,1)S(1)}, bf16[64,512]{1,0:T(8,128)(2,1)S(1)}, u32[]{:S(2)}, u32[]{:S(2)}) collective-permute-start(bf16[64,512]{1,0:T(8,128)(2,1)S(1)} %collective-permute-done.13.refs_9_), channel_id=1, source_target_pairs={{0,1},{1,0},{2,3},{3,2},{4,5},{5,4},{6,7},{7,6},{8,9},{9,8},{10,11... | collective-permute-start | bytes 196616 | tf_op jit(solution)/shard_map/ppermute | solution.py:172
  32.9 7.9 %collective-permute-start.18 = (bf16[64,512]{1,0:T(8,128)(2,1)S(1)}, bf16[64,512]{1,0:T(8,128)(2,1)}, u32[]{:S(2)}, u32[]{:S(2)}) collective-permute-start(bf16[64,512]{1,0:T(8,128)(2,1)S(1)} %collective-permute-done.14.refs_10_), channel_id=1, source_target_pairs={{0,1},{1,0},{2,3},{3,2},{4,5},{5,4},{6,7},{7,6},{8,9},{9,8},{10,11... | collective-permute-start | bytes 196616 | tf_op jit(solution)/shard_map/ppermute | solution.py:172
  36.7 6.8 %collective-permute-start.7 = (bf16[64,512]{1,0:T(8,128)(2,1)S(1)}, bf16[64,512]{1,0:T(8,128)(2,1)}, u32[]{:S(2)}, u32[]{:S(2)}) collective-permute-start(bf16[64,512]{1,0:T(8,128)(2,1)S(1)} %fusion.4.refs_0_), channel_id=1, source_target_pairs={{0,4},{1,5},{2,6},{3,7},{4,0},{5,1},{6,2},{7,3},{8,12},{9,13},{10,... | collective-permute-start | bytes 196616 | tf_op jit(solution)/shard_map/ppermute | solution.py:172
  36.7 6.8 %collective-permute-start.8 = (bf16[64,512]{1,0:T(8,128)(2,1)S(1)}, bf16[64,512]{1,0:T(8,128)(2,1)S(1)}, u32[]{:S(2)}, u32[]{:S(2)}) collective-permute-start(bf16[64,512]{1,0:T(8,128)(2,1)S(1)} %fusion.4.refs_0_), channel_id=1, source_target_pairs={{0,6},{1,7},{2,4},{3,5},{4,2},{5,3},{6,0},{7,1},{8,14},{9,15},{10,... | collective-permute-start | bytes 196616 | tf_op jit(solution)/shard_map/ppermute | solution.py:172
  57.5 16.3 %collective-permute-start.20 = (f32[256,256]{1,0:T(8,128)}, f32[256,256]{1,0:T(8,128)S(1)}, u32[]{:S(2)}, u32[]{:S(2)}) collective-permute-start(f32[256,256]{1,0:T(8,128)} %get-tuple-element.28), channel_id=1, source_target_pairs={{0,1},{1,0},{2,3},{3,2},{4,5},{5,4},{6,7},{7,6},{8,9},{9,8},{10,11... | collective-permute-start | bytes 786440 | tf_op jit(solution)/shard_map/ppermute | solution.py:172
  70.8 27.8 %collective-permute-start.25 = (bf16[320,256]{1,0:T(8,128)(2,1)}, bf16[320,256]{1,0:T(8,128)(2,1)S(1)}, u32[]{:S(2)}, u32[]{:S(2)}) collective-permute-start(bf16[320,256]{1,0:T(8,128)(2,1)} %get-tuple-element.48), channel_id=1, source_target_pairs={{0,2},{1,3},{2,0},{3,1},{4,6},{5,7},{6,4},{7,5},{8,10},{9,11},{10,... | collective-permute-start | bytes 491528 | tf_op jit(solution)/shard_map/ppermute | solution.py:172
  71.8 30.3 %collective-permute-start.26 = (bf16[320,256]{1,0:T(8,128)(2,1)}, bf16[320,256]{1,0:T(8,128)(2,1)}, u32[]{:S(2)}, u32[]{:S(2)}) collective-permute-start(bf16[320,256]{1,0:T(8,128)(2,1)} %get-tuple-element.47), channel_id=1, source_target_pairs={{0,4},{1,5},{2,6},{3,7},{4,0},{5,1},{6,2},{7,3},{8,12},{9,13},{10,... | collective-permute-start | bytes 491528 | tf_op jit(solution)/shard_map/ppermute | solution.py:172
  73.9 8.0 %collective-permute-start.21 = (f32[64,256]{1,0:T(8,128)S(1)}, f32[64,256]{1,0:T(8,128)S(1)}, u32[]{:S(2)}, u32[]{:S(2)}) collective-permute-start(f32[64,256]{1,0:T(8,128)S(1)} %get-tuple-element.60), channel_id=1, source_target_pairs={{0,2},{1,3},{2,0},{3,1},{4,6},{5,7},{6,4},{7,5},{8,10},{9,11},{10,... | collective-permute-start | bytes 196616 | tf_op jit(solution)/shard_map/ppermute | solution.py:172
  73.9 14.4 %collective-permute-start.22 = (f32[64,256]{1,0:T(8,128)S(1)}, f32[64,256]{1,0:T(8,128)S(1)}, u32[]{:S(2)}, u32[]{:S(2)}) collective-permute-start(f32[64,256]{1,0:T(8,128)S(1)} %get-tuple-element.62), channel_id=1, source_target_pairs={{0,4},{1,5},{2,6},{3,7},{4,0},{5,1},{6,2},{7,3},{8,12},{9,13},{10,... | collective-permute-start | bytes 196616 | tf_op jit(solution)/shard_map/ppermute | solution.py:172
  75.9 12.5 %collective-permute-start.23 = (f32[64,256]{1,0:T(8,128)S(1)}, f32[64,256]{1,0:T(8,128)S(1)}, u32[]{:S(2)}, u32[]{:S(2)}) collective-permute-start(f32[64,256]{1,0:T(8,128)S(1)} %get-tuple-element.61), channel_id=1, source_target_pairs={{0,6},{1,7},{2,4},{3,5},{4,2},{5,3},{6,0},{7,1},{8,14},{9,15},{10,... | collective-permute-start | bytes 196616 | tf_op jit(solution)/shard_map/ppermute | solution.py:172
  81.8 7.7 %collective-permute-start.29 = (f32[64,256]{1,0:T(8,128)S(1)}, f32[64,256]{1,0:T(8,128)S(1)}, u32[]{:S(2)}, u32[]{:S(2)}) collective-permute-start(f32[64,256]{1,0:T(8,128)S(1)} %get-tuple-element.63), channel_id=1, source_target_pairs={{0,2},{1,3},{2,0},{3,1},{4,6},{5,7},{6,4},{7,5},{8,10},{9,11},{10,... | collective-permute-start | bytes 196616 | tf_op jit(solution)/shard_map/ppermute | solution.py:172
  88.4 9.1 %collective-permute-start.30 = (f32[64,256]{1,0:T(8,128)S(1)}, f32[64,256]{1,0:T(8,128)S(1)}, u32[]{:S(2)}, u32[]{:S(2)}) collective-permute-start(f32[64,256]{1,0:T(8,128)S(1)} %get-tuple-element.65), channel_id=1, source_target_pairs={{0,4},{1,5},{2,6},{3,7},{4,0},{5,1},{6,2},{7,3},{8,12},{9,13},{10,... | collective-permute-start | bytes 196616 | tf_op jit(solution)/shard_map/ppermute | solution.py:172
  88.4 9.1 %collective-permute-start.31 = (f32[64,256]{1,0:T(8,128)S(1)}, f32[64,256]{1,0:T(8,128)S(1)}, u32[]{:S(2)}, u32[]{:S(2)}) collective-permute-start(f32[64,256]{1,0:T(8,128)S(1)} %get-tuple-element.64), channel_id=1, source_target_pairs={{0,6},{1,7},{2,4},{3,5},{4,2},{5,3},{6,0},{7,1},{8,14},{9,15},{10,... | collective-permute-start | bytes 196616 | tf_op jit(solution)/shard_map/ppermute | solution.py:172
  89.5 13.0 %collective-permute-start.27 = (bf16[320,256]{1,0:T(8,128)(2,1)}, bf16[320,256]{1,0:T(8,128)(2,1)S(1)}, u32[]{:S(2)}, u32[]{:S(2)}) collective-permute-start(bf16[320,256]{1,0:T(8,128)(2,1)} %get-tuple-element.46), channel_id=1, source_target_pairs={{0,6},{1,7},{2,4},{3,5},{4,2},{5,3},{6,0},{7,1},{8,14},{9,15},{10,... | collective-permute-start | bytes 491528 | tf_op jit(solution)/shard_map/ppermute | solution.py:172
  98.7 7.2 %collective-permute-start.38 = (bf16[64,512]{1,0:T(8,128)(2,1)S(1)}, bf16[64,512]{1,0:T(8,128)(2,1)S(1)}, u32[]{:S(2)}, u32[]{:S(2)}) collective-permute-start(bf16[64,512]{1,0:T(8,128)(2,1)S(1)} %fusion.2.grad_ref), channel_id=1, source_target_pairs={{0,2},{1,3},{2,0},{3,1},{4,6},{5,7},{6,4},{7,5},{8,10},{9,11},{10,... | collective-permute-start | bytes 196616 | tf_op jit(solution)/shard_map/ppermute | solution.py:172
  100.2 27.7 %collective-permute-start.32 = (bf16[1280,256]{1,0:T(8,128)(2,1)S(1)}, bf16[1280,256]{1,0:T(8,128)(2,1)S(1)}, u32[]{:S(2)}, u32[]{:S(2)}) collective-permute-start(bf16[1280,256]{1,0:T(8,128)(2,1)S(1)} %constant_dynamic-slice_fusion), channel_id=1, source_target_pairs={{0,8},{8,0},{16,24},{24,16},{1,9},{9,1},{17,25},{25,17},{2,10},{10... | collective-permute-start | bytes 1966088 | tf_op jit(solution)/shard_map/ppermute | solution.py:172
  102.1 29.3 %collective-permute-start.33 = (bf16[1280,256]{1,0:T(8,128)(2,1)S(1)}, bf16[1280,256]{1,0:T(8,128)(2,1)S(1)}, u32[]{:S(2)}, u32[]{:S(2)}) collective-permute-start(bf16[1280,256]{1,0:T(8,128)(2,1)S(1)} %constant_dynamic-slice_fusion), channel_id=1, source_target_pairs={{0,16},{8,24},{16,0},{24,8},{1,17},{9,25},{17,1},{25,9},{2,18},{10... | collective-permute-start | bytes 1966088 | tf_op jit(solution)/shard_map/ppermute | solution.py:172
  102.6 30.9 %collective-permute-start.34 = (bf16[1280,256]{1,0:T(8,128)(2,1)S(1)}, bf16[1280,256]{1,0:T(8,128)(2,1)S(1)}, u32[]{:S(2)}, u32[]{:S(2)}) collective-permute-start(bf16[1280,256]{1,0:T(8,128)(2,1)S(1)} %constant_dynamic-slice_fusion), channel_id=1, source_target_pairs={{0,24},{8,16},{16,8},{24,0},{1,25},{9,17},{17,9},{25,1},{2,26},{10... | collective-permute-start | bytes 1966088 | tf_op jit(solution)/shard_map/ppermute | solution.py:172
  104.1 8.0 %collective-permute-start.39 = (bf16[64,512]{1,0:T(8,128)(2,1)S(1)}, bf16[64,512]{1,0:T(8,128)(2,1)S(1)}, u32[]{:S(2)}, u32[]{:S(2)}) collective-permute-start(bf16[64,512]{1,0:T(8,128)(2,1)S(1)} %fusion.2.grad_ref), channel_id=1, source_target_pairs={{0,4},{1,5},{2,6},{3,7},{4,0},{5,1},{6,2},{7,3},{8,12},{9,13},{10,... | collective-permute-start | bytes 196616 | tf_op jit(solution)/shard_map/ppermute | solution.py:172
  112.1 6.7 %collective-permute-start.46 = (f32[64,256]{1,0:T(8,128)S(1)}, f32[64,256]{1,0:T(8,128)S(1)}, u32[]{:S(2)}, u32[]{:S(2)}) collective-permute-start(f32[64,256]{1,0:T(8,128)S(1)} %get-tuple-element.56), channel_id=1, source_target_pairs={{0,4},{1,5},{2,6},{3,7},{4,0},{5,1},{6,2},{7,3},{8,12},{9,13},{10,... | collective-permute-start | bytes 196616 | tf_op jit(solution)/shard_map/ppermute | solution.py:172
  118.8 18.8 %collective-permute-start.41 = (bf16[4,64,512]{2,1,0:T(8,128)(2,1)S(1)}, bf16[4,64,512]{2,1,0:T(8,128)(2,1)S(1)}, u32[]{:S(2)}, u32[]{:S(2)}) collective-permute-start(bf16[4,64,512]{2,1,0:T(8,128)(2,1)S(1)} %pad_maximum_fusion.refs_4_), channel_id=1, source_target_pairs={{0,8},{8,0},{16,24},{24,16},{1,9},{9,1},{17,25},{25,17},{2,10},{10... | collective-permute-start | bytes 786440 | tf_op jit(solution)/shard_map/ppermute | solution.py:172
  126.7 15.5 %collective-permute-start.42 = (bf16[4,64,512]{2,1,0:T(8,128)(2,1)S(1)}, bf16[4,64,512]{2,1,0:T(8,128)(2,1)S(1)}, u32[]{:S(2)}, u32[]{:S(2)}) collective-permute-start(bf16[4,64,512]{2,1,0:T(8,128)(2,1)S(1)} %pad_maximum_fusion.refs_4_), channel_id=1, source_target_pairs={{0,16},{8,24},{16,0},{24,8},{1,17},{9,25},{17,1},{25,9},{2,18},{10... | collective-permute-start | bytes 786440 | tf_op jit(solution)/shard_map/ppermute | solution.py:172
  128.0 16.1 %collective-permute-start.43 = (bf16[4,64,512]{2,1,0:T(8,128)(2,1)S(1)}, bf16[4,64,512]{2,1,0:T(8,128)(2,1)S(1)}, u32[]{:S(2)}, u32[]{:S(2)}) collective-permute-start(bf16[4,64,512]{2,1,0:T(8,128)(2,1)S(1)} %pad_maximum_fusion.refs_4_), channel_id=1, source_target_pairs={{0,24},{8,16},{16,8},{24,0},{1,25},{9,17},{17,9},{25,1},{2,26},{10... | collective-permute-start | bytes 786440 | tf_op jit(solution)/shard_map/ppermute | solution.py:172
  131.4 21.8 %collective-permute-start.35 = (bf16[1280,256]{1,0:T(8,128)(2,1)S(1)}, bf16[1280,256]{1,0:T(8,128)(2,1)S(1)}, u32[]{:S(2)}, u32[]{:S(2)}) collective-permute-start(bf16[1280,256]{1,0:T(8,128)(2,1)S(1)} %collective-permute-done.32.refs_0_), channel_id=1, source_target_pairs={{0,1},{1,0},{2,3},{3,2},{4,5},{5,4},{6,7},{7,6},{8,9},{9,8},{10,11... | collective-permute-start | bytes 1966088 | tf_op jit(solution)/shard_map/ppermute | solution.py:172
  133.5 19.7 %collective-permute-start.36 = (bf16[1280,256]{1,0:T(8,128)(2,1)S(1)}, bf16[1280,256]{1,0:T(8,128)(2,1)S(1)}, u32[]{:S(2)}, u32[]{:S(2)}) collective-permute-start(bf16[1280,256]{1,0:T(8,128)(2,1)S(1)} %collective-permute-done.33.refs_1_), channel_id=1, source_target_pairs={{0,1},{1,0},{2,3},{3,2},{4,5},{5,4},{6,7},{7,6},{8,9},{9,8},{10,11... | collective-permute-start | bytes 1966088 | tf_op jit(solution)/shard_map/ppermute | solution.py:172
  137.6 15.6 %collective-permute-start.37 = (bf16[1280,256]{1,0:T(8,128)(2,1)S(1)}, bf16[1280,256]{1,0:T(8,128)(2,1)S(1)}, u32[]{:S(2)}, u32[]{:S(2)}) collective-permute-start(bf16[1280,256]{1,0:T(8,128)(2,1)S(1)} %collective-permute-done.34.refs_2_), channel_id=1, source_target_pairs={{0,1},{1,0},{2,3},{3,2},{4,5},{5,4},{6,7},{7,6},{8,9},{9,8},{10,11... | collective-permute-start | bytes 1966088 | tf_op jit(solution)/shard_map/ppermute | solution.py:172
  142.2 7.3 %collective-permute-start.50 = (f32[64,256]{1,0:T(8,128)S(1)}, f32[64,256]{1,0:T(8,128)S(1)}, u32[]{:S(2)}, u32[]{:S(2)}) collective-permute-start(f32[64,256]{1,0:T(8,128)S(1)} %get-tuple-element.59), channel_id=1, source_target_pairs={{0,4},{1,5},{2,6},{3,7},{4,0},{5,1},{6,2},{7,3},{8,12},{9,13},{10,... | collective-permute-start | bytes 196616 | tf_op jit(solution)/shard_map/ppermute | solution.py:172
  (52 other events, 392.5 us)

commit v4 on v3

--- a/solution.py
+++ b/solution.py
@@ -107,36 +107,36 @@
     )(length, queries, upstream, keys, values, *key_pieces, *value_pieces, *earlier)
 
 
-def hidden_kernel(groups, place_ref, grad_ref, own_ref, *refs):
+def hidden_kernel(groups, place_ref, first_ref, second_ref, own_ref, *refs):
     near, far, out_ref = refs[: groups - 1], refs[groups - 1 : -1], refs[-1]
     group, core = place_ref[0], place_ref[1]
     depth = own_ref.shape[0]
-    half = near[0].shape[1]
-    near_grad = grad_ref[:, pl.ds(pl.multiple_of(core * half, half), half)]
-    far_grad = grad_ref[:, pl.ds(pl.multiple_of((1 - core) * half, half), half)]
+    first, second = first_ref[...], second_ref[...]
+    near_grad = jnp.where(core == 0, first, second)
+    far_grad = jnp.where(core == 0, second, first)
     for k in range(groups):
         if k:
             block = dot(near_grad, near[k - 1][...], 1, 1) + dot(far_grad, far[k - 1][...], 1, 1)
         else:
-            block = dot(grad_ref[...], own_ref[...], 1, 1)
+            block = dot(jnp.concatenate([first, second], axis=1), own_ref[...], 1, 1)
         start = pl.multiple_of((group ^ k) * depth, depth)
         out_ref[:, pl.ds(start, depth)] = block.astype(BF16)
 
 
-def hidden_pass(place, key_pre_grad, own, near, far):
-    tokens, kv_width = key_pre_grad.shape
+def hidden_pass(place, key_pre_grads, own, near, far):
+    tokens = key_pre_grads[0].shape[0]
     groups = len(near) + 1
     width = groups * own.shape[0]
     return pl.pallas_call(
         partial(hidden_kernel, groups),
         in_specs=[pl.BlockSpec(memory_space=pltpu.SMEM)]
-        + [pl.BlockSpec(memory_space=pltpu.VMEM)] * (2 * groups),
+        + [pl.BlockSpec(memory_space=pltpu.VMEM)] * (2 * groups + 1),
         out_specs=pl.BlockSpec(memory_space=pltpu.VMEM),
         out_shape=jax.ShapeDtypeStruct((tokens, width), BF16),
         compiler_params=PARAMS,
-        cost_estimate=cost(tokens * width * kv_width, 6 * 10**6),
+        cost_estimate=cost(tokens * width * own.shape[1], 6 * 10**6),
         name="hidden_grad",
-    )(place, key_pre_grad, own, *near, *far)
+    )(place, *key_pre_grads, own, *near, *far)
 
 
 def weight_kernel(chips, place_ref, *refs):
@@ -172,8 +172,8 @@
     return lax.ppermute(array, axis, [(i, i ^ distance) for i in range(size)])
 
 
-def after(array, *others):
-    return lax.optimization_barrier((array, *others))[0]
+def together(*arrays):
+    return list(lax.optimization_barrier(arrays))
 
 
 def spread_near(block, size):
@@ -208,63 +208,73 @@
     core = resp % 2
     place = jnp.stack([group, core]).astype(jnp.int32)
 
-    columns = []
-    for k in range(groups):
-        piece = lax.dynamic_slice(hidden, (0, (group ^ k) * depth), (tokens, depth))
-        columns.append(swap(piece, "group", groups, k) if k else piece)
+    pieces = [
+        lax.dynamic_slice(hidden, (0, (group ^ k) * depth), (tokens, depth)) for k in range(groups)
+    ]
+    prompt_value, *pieces = together(prompt_token_value[0], *pieces)
+    columns = [swap(piece, "group", groups, k) if k else piece for k, piece in enumerate(pieces)]
     partials = [dot(piece, key_matrix) for piece in columns]
+    value_near = spread_near(prompt_value, responses)
     key_pre = partials[0]
     for k in range(1, groups):
         key_pre = key_pre + swap(partials[k], "group", groups, k)
-    value_near = spread_near(after(prompt_token_value[0], *columns), responses)
     value_pieces = value_near + spread_far(value_near, responses)
 
+    half_width = kv_width // 2
+    half_weight = lax.dynamic_slice(key_matrix, (0, core * half_width), (depth, half_width))
+    half_weight, key_pre = together(half_weight, key_pre)
     prompt_key = norm_keys(key_pre, key_gain).astype(BF16)
     key_near = spread_near(prompt_key, responses)
-    key_pieces = key_near + spread_far(key_near, responses)
+    weight_near = [swap(half_weight, "group", groups, k) for k in range(1, groups)]
 
     chips = responses // 2
     chip_rows = depth // chips
     hidden_t = jnp.concatenate(columns, axis=0).T
-    hidden_t = after(hidden_t, *key_near)
+    hidden_t, *key_near = together(hidden_t, *key_near)
+    key_pieces = key_near + spread_far(key_near, responses)
     taken = []
     for k in range(0, responses, 2):
         start = ((resp ^ k) // 2) * chip_rows
         piece = lax.dynamic_slice(hidden_t, (start, 0), (chip_rows, hidden_t.shape[1]))
         taken.append(swap(piece, "resp", responses, k) if k else piece)
 
-    half_width = kv_width // 2
-    half_weight = lax.dynamic_slice(key_matrix, (0, core * half_width), (depth, half_width))
-    half_weight = after(half_weight, key_pre)
-    weight_near = [swap(half_weight, "group", groups, k) for k in range(1, groups)]
-
-    queries, upstream = resp_query[0, 0], grad_out[0, 0]
-    rest = (queries, upstream, key_pieces, value_pieces, resp_key[0, 0], response_value[0, 0], head_dim)
+    rest = (
+        resp_query[0, 0], grad_out[0, 0], key_pieces, value_pieces,
+        resp_key[0, 0], response_value[0, 0], head_dim,
+    )
     count = kv_width // head_dim // 2
-    earlier, key_parts, value_parts, length = [], [], [], resp_length
-    for first in (0, count):
-        *earlier, key_near, key_far, value_near, value_far = attend(length, *rest, first, count, earlier)
-        key_near = pair_sum(key_near, key_far, responses)
-        value_near = pair_sum(value_near, value_far, responses)
-        length = after(resp_length, key_near, value_near, *taken)
-        key_parts.append(chip_sum(key_near, responses))
-        value_parts.append(chip_sum(value_near, responses))
-    query_grad, key_grad, value_grad = earlier
-    prompt_key_grad = jnp.concatenate(key_parts, axis=1)
-    prompt_value_grad = jnp.concatenate(value_parts, axis=1)
-    _, pullback = jax.vjp(lambda values: norm_keys(values, key_gain), key_pre)
-    key_pre_grad = pullback(prompt_key_grad)[0].astype(BF16)
-
-    block = jnp.stack(spread_near(key_pre_grad, responses), axis=0)
-    blocks = [block] + [swap(block, "group", groups, k) for k in range(1, groups)]
-    mine, other = weight_pass(place, taken, blocks)
-    grad_weight = mine + swap(other, "resp", responses, 1)
-
+    width = count * head_dim
+    *earlier, near, far, value_near0, value_far0 = attend(resp_length, *rest, 0, count, [])
+    near = pair_sum(near, far, responses)
+    length, near, *taken = together(resp_length, near, *taken)
+    sums0 = chip_sum(near, responses)
+    *outputs, near, far, value_near1, value_far1 = attend(length, *rest, count, count, earlier)
+    query_grad, key_grad, value_grad = outputs
+    sums1 = chip_sum(pair_sum(near, far, responses), responses)
+
+    halves = []
+    for i, sums in enumerate((sums0, sums1)):
+        part = key_pre[:, i * width : (i + 1) * width]
+        _, pullback = jax.vjp(lambda values: norm_keys(values, key_gain), part)
+        halves.append(spread_near(pullback(sums)[0].astype(BF16), responses))
+    value_near = jnp.concatenate([value_near0, value_near1], axis=1)
+    value_far = jnp.concatenate([value_far0, value_far1], axis=1)
+    value_near, value_far, *rest = together(value_near, value_far, *weight_near, *halves[1])
+    weight_near, halves[1] = rest[: groups - 1], rest[groups - 1 :]
     weight_far = [swap(piece, "resp", responses, 1) for piece in weight_near]
-    grad_hidden = hidden_pass(place, key_pre_grad, key_matrix, weight_near, weight_far)
+    grad_hidden = hidden_pass(
+        place, [near[0] for near in halves], key_matrix, weight_near, weight_far
+    )
+    weight_halves = []
+    for near in halves:
+        block = jnp.stack(near, axis=0)
+        blocks = [block] + [swap(block, "group", groups, k) for k in range(1, groups)]
+        mine, other = weight_pass(place, taken, blocks)
+        weight_halves.append(mine + swap(other, "resp", responses, 1))
+    prompt_value_grad = chip_sum(pair_sum(value_near, value_far, responses), responses)
     return (
         grad_hidden[None],
-        grad_weight,
+        jnp.concatenate(weight_halves, axis=1),
         prompt_value_grad.astype(BF16)[None],
         query_grad[None, None],
         key_grad[None, None],

time: 161 us -> 162 us (level)
  waiting for transfers between devices: 60.7 us -> 51.1 us
  local copies, waits for them, and re-layouts: 6.97 us -> 13.6 us
  other arithmetic: 4.14 us -> 6.58 us
  Pallas kernels: 31.6 us -> 33.7 us
    ppermute x52 -> x55, waiting for transfers between devices: 60.7 us -> 51.1 us  [swap(): return lax.ppermute(array, axis, [(i, i ^ distance) for i in range(size)])]
    pallas_call x1 -> x2, Pallas kernels: 2.82 us -> 4.86 us  [weight_pass(): pl.pallas_call(partial(weight_kernel, len(taken)), in_specs=[pl.BlockSpec...]
    unnamed x64 -> x80, local copies, waits for them, and re-layouts: 2.55 us -> 4.46 us
    add x1 -> x2, other arithmetic: 1.74 us -> 0.04 us  [shards(): weight_halves.append(mine + swap(other, 'resp', responses, 1))]
    ppermute x52 -> x55, starting transfers between devices: 53.4 us -> 53.3 us  [swap(): return lax.ppermute(array, axis, [(i, i ^ distance) for i in range(size)])]
  transfers between devices with their start and end apart: 52 -> 55, of which waited for: 22 -> 21; matrix products, arithmetic and copies ran while one was open for 5% -> 8% of each run, Pallas kernels for 9% -> 18%
where the time goes in v4:
time: 162 us
  starting transfers between devices  53.3 us (33%)
  waiting for transfers between devices  51.1 us (32%)
  Pallas kernels  33.7 us (21%)
  local copies, waits for them, and re-layouts  13.6 us (8%)
  other arithmetic  6.58 us (4%)
  between operations  2.1 us (1%)
    ppermute x55, starting transfers between devices, swap(): return lax.ppermute(array, axis, [(i, i ^ distance) for i in range(size)])  53.3 us
    ppermute x55, waiting for transfers between devices, swap(): return lax.ppermute(array, axis, [(i, i ^ distance) for i in range(size)])  51.1 us
    pallas_call x2, Pallas kernels, attend(): pl.pallas_call(partial(attend_kernel, len(key_pieces), bool(earlier)), gr...  23.8 us
    pallas_call x1, Pallas kernels, hidden_pass(): pl.pallas_call(partial(hidden_kernel, groups), in_specs=[pl.BlockSpec(mem...  5.04 us
    pallas_call x2, Pallas kernels, weight_pass(): pl.pallas_call(partial(weight_kernel, len(taken)), in_specs=[pl.BlockSpec...  4.86 us
    unnamed x80, local copies, waits for them, and re-layouts  4.46 us
    dynamic_slice x5, local copies, waits for them, and re-layouts, shards(): lax.dynamic_slice(hidden, (0, (group ^ k) * depth), (tokens, depth))  4.13 us
  transfers between devices with their start and end apart: 55, of which 21 were waited for; matrix products, arithmetic and copies ran while one was open for 8% of the time, Pallas kernels for 18%

profile of v4, /device:TPU:0, one launch (start us, length us, event | category | flops | bytes accessed | tf_op | source)
XLA Modules:
  0.0 161.8 jit_solution(14065064117334467560)
XLA Ops:
  4.8 3.0 %collective-permute-start.13 = (bf16[64,512]{1,0:T(8,128)(2,1)S(1)}, bf16[64,512]{1,0:T(8,128)(2,1)}, u32[]{:S(2)}, u32[]{:S(2)}) collective-permute-start(bf16[64,512]{1,0:T(8,128)(2,1)S(1)} %bitcast.92), channel_id=1, source_target_pairs={{0,2},{1,3},{2,0},{3,1},{4,6},{5,7},{6,4},{7,5},{8,10},{9,11},{10,... | collective-permute-start | bytes 196616 | tf_op jit(solution)/shard_map/ppermute | solution.py:172
  7.8 2.6 %collective-permute-start.14 = (bf16[64,512]{1,0:T(8,128)(2,1)S(1)}, bf16[64,512]{1,0:T(8,128)(2,1)}, u32[]{:S(2)}, u32[]{:S(2)}) collective-permute-start(bf16[64,512]{1,0:T(8,128)(2,1)S(1)} %bitcast.93), channel_id=1, source_target_pairs={{0,4},{1,5},{2,6},{3,7},{4,0},{5,1},{6,2},{7,3},{8,12},{9,13},{10,... | collective-permute-start | bytes 196616 | tf_op jit(solution)/shard_map/ppermute | solution.py:172
  14.3 6.9 %collective-permute-done = bf16[64,1280]{0,1:T(8,128)(2,1)S(1)} collective-permute-done((bf16[64,1280]{0,1:T(8,128)(2,1)}, bf16[64,1280]{0,1:T(8,128)(2,1)S(1)}, u32[]{:S(2)}, u32[]{:S(2)}) %collective-permute-start) | collective-permute-done | bytes 163872 | tf_op jit(solution)/shard_map/ppermute | solution.py:172
  23.2 4.8 %collective-permute-done.1 = bf16[64,1280]{0,1:T(8,128)(2,1)S(1)} collective-permute-done((bf16[64,1280]{0,1:T(8,128)(2,1)}, bf16[64,1280]{0,1:T(8,128)(2,1)S(1)}, u32[]{:S(2)}, u32[]{:S(2)}) %collective-permute-start.1) | collective-permute-done | bytes 163872 | tf_op jit(solution)/shard_map/ppermute | solution.py:172
  28.4 2.4 %collective-permute-start.4 = (f32[64,512]{1,0:T(8,128)S(1)}, f32[64,512]{1,0:T(8,128)S(1)}, u32[]{:S(2)}, u32[]{:S(2)}) collective-permute-start(f32[64,512]{1,0:T(8,128)S(1)} %fusion.18), channel_id=1, source_target_pairs={{0,16},{8,24},{16,0},{24,8},{1,17},{9,25},{17,1},{25,9},{2,18},{10... | collective-permute-start | bytes 393224 | tf_op jit(solution)/shard_map/ppermute | solution.py:172
  31.6 2.1 %collective-permute-done.4 = f32[64,512]{1,0:T(8,128)S(1)} collective-permute-done((f32[64,512]{1,0:T(8,128)S(1)}, f32[64,512]{1,0:T(8,128)S(1)}, u32[]{:S(2)}, u32[]{:S(2)}) %collective-permute-start.4) | collective-permute-done | bytes 131104 | tf_op jit(solution)/shard_map/ppermute | solution.py:172
  33.8 3.3 %collective-permute-done.5 = f32[64,512]{1,0:T(8,128)S(1)} collective-permute-done((f32[64,512]{1,0:T(8,128)S(1)}, f32[64,512]{1,0:T(8,128)S(1)}, u32[]{:S(2)}, u32[]{:S(2)}) %collective-permute-start.5) | collective-permute-done | bytes 131104 | tf_op jit(solution)/shard_map/ppermute | solution.py:172
  39.8 2.2 %collective-permute-done.6.refs_1_ = bf16[64,512]{1,0:T(8,128)(2,1)S(1)} collective-permute-done((bf16[64,512]{1,0:T(8,128)(2,1)S(1)}, bf16[64,512]{1,0:T(8,128)(2,1)S(1)}, u32[]{:S(2)}, u32[]{:S(2)}) %collective-permute-start.6) | collective-permute-done | bytes 65568 | tf_op jit(solution)/shard_map/ppermute | solution.py:172
  43.7 3.4 %collective-permute-done.7.refs_2_ = bf16[64,512]{1,0:T(8,128)(2,1)S(1)} collective-permute-done((bf16[64,512]{1,0:T(8,128)(2,1)S(1)}, bf16[64,512]{1,0:T(8,128)(2,1)S(1)}, u32[]{:S(2)}, u32[]{:S(2)}) %collective-permute-start.7) | collective-permute-done | bytes 65568 | tf_op jit(solution)/shard_map/ppermute | solution.py:172
  52.0 2.5 %collective-permute-start.23 = (bf16[320,256]{1,0:T(8,128)(2,1)}, bf16[320,256]{1,0:T(8,128)(2,1)S(1)}, u32[]{:S(2)}, u32[]{:S(2)}) collective-permute-start(bf16[320,256]{1,0:T(8,128)(2,1)} %get-tuple-element.100), channel_id=1, source_target_pairs={{0,6},{1,7},{2,4},{3,5},{4,2},{5,3},{6,0},{7,1},{8,14},{9,15},{10,... | collective-permute-start | bytes 491528 | tf_op jit(solution)/shard_map/ppermute | solution.py:172
  55.2 12.0 %attend.2 = (bf16[256,4096]{1,0:T(8,128)(2,1)}, bf16[256,512]{1,0:T(8,128)(2,1)}, bf16[256,512]{1,0:T(8,128)(2,1)}, f32[256,256]{1,0:T(8,128)}, f32[256,256]{1,0...) custom-call(s32[1,1]{1,0:T(1,128)S(6)} %copy.59.length_ref, bf16[256,4096]{1,0:T(8,128)(2,1)} %bitcast.82, ...), custom_call_target="tpu_custom_call" | custom-call | flops 8053063680 | bytes 5000000 | tf_op jit(solution)/shard_map/attend/pallas_call | solution.py:94
  67.2 11.9 %attend.3 = (bf16[256,4096]{1,0:T(8,128)(2,1)}, bf16[256,512]{1,0:T(8,128)(2,1)}, bf16[256,512]{1,0:T(8,128)(2,1)}, f32[256,256]{1,0:T(8,128)}, f32[256,256]{1,0...) custom-call(s32[1,1]{1,0:T(1,128)S(6)} %copy.59.length_ref, ...), custom_call_target="tpu_custom_call", output_to_operand_aliasing={{0}: (21, {}), {1}: (22, {}), {2}: (23, {})} | custom-call | flops 8053063680 | bytes 5000000 | tf_op jit(solution)/shard_map/attend/pallas_call | solution.py:94
  81.9 1.8 %collective-permute-start.25 = (f32[64,256]{1,0:T(8,128)S(1)}, f32[64,256]{1,0:T(8,128)S(1)}, u32[]{:S(2)}, u32[]{:S(2)}) collective-permute-start(f32[64,256]{1,0:T(8,128)S(1)} %get-tuple-element.116), channel_id=1, source_target_pairs={{0,4},{1,5},{2,6},{3,7},{4,0},{5,1},{6,2},{7,3},{8,12},{9,13},{10,... | collective-permute-start | bytes 196616 | tf_op jit(solution)/shard_map/ppermute | solution.py:172
  83.6 2.5 %collective-permute-start.26 = (f32[64,256]{1,0:T(8,128)S(1)}, f32[64,256]{1,0:T(8,128)S(1)}, u32[]{:S(2)}, u32[]{:S(2)}) collective-permute-start(f32[64,256]{1,0:T(8,128)S(1)} %get-tuple-element.115), channel_id=1, source_target_pairs={{0,6},{1,7},{2,4},{3,5},{4,2},{5,3},{6,0},{7,1},{8,14},{9,15},{10,... | collective-permute-start | bytes 196616 | tf_op jit(solution)/shard_map/ppermute | solution.py:172
  86.8 2.4 %collective-permute-done.25 = f32[64,256]{1,0:T(8,128)S(1)} collective-permute-done((f32[64,256]{1,0:T(8,128)S(1)}, f32[64,256]{1,0:T(8,128)S(1)}, u32[]{:S(2)}, u32[]{:S(2)}) %collective-permute-start.25) | collective-permute-done | bytes 65568 | tf_op jit(solution)/shard_map/ppermute | solution.py:172
  89.9 2.5 %collective-permute-start.33 = (f32[64,256]{1,0:T(8,128)}, f32[64,256]{1,0:T(8,128)}, u32[]{:S(2)}, u32[]{:S(2)}) collective-permute-start(f32[64,256]{1,0:T(8,128)} %get-tuple-element.112), channel_id=1, source_target_pairs={{0,6},{1,7},{2,4},{3,5},{4,2},{5,3},{6,0},{7,1},{8,14},{9,15},{10,... | collective-permute-start | bytes 196616 | tf_op jit(solution)/shard_map/ppermute | solution.py:172
  93.0 2.9 %collective-permute-start.29 = (bf16[1280,256]{1,0:T(8,128)(2,1)S(1)}, bf16[1280,256]{1,0:T(8,128)(2,1)S(1)}, u32[]{:S(2)}, u32[]{:S(2)}) collective-permute-start(bf16[1280,256]{1,0:T(8,128)(2,1)S(1)} %constant_dynamic-slice_fusion.4), channel_id=1, source_target_pairs={{0,24},{8,16},{16,8},{24,0},{1,25},{9,17},{17,9},{25,1},{2,26},{10... | collective-permute-start | bytes 1966088 | tf_op jit(solution)/shard_map/ppermute | solution.py:172
  101.2 1.8 %collective-permute-start.35 = (bf16[64,256]{1,0:T(8,128)(2,1)S(1)}, bf16[64,256]{1,0:T(8,128)(2,1)S(1)}, u32[]{:S(2)}, u32[]{:S(2)}) collective-permute-start(bf16[64,256]{1,0:T(8,128)(2,1)S(1)} %get-tuple-element.76.second_ref), channel_id=1, source_target_pairs={{0,4},{1,5},{2,6},{3,7},{4,0},{5,1},{6,2},{7,3},{8,12},{9,13},{10,... | collective-permute-start | bytes 98312 | tf_op jit(solution)/shard_map/ppermute | solution.py:172
  104.1 2.3 %collective-permute-start.36 = (bf16[64,256]{1,0:T(8,128)(2,1)S(1)}, bf16[64,256]{1,0:T(8,128)(2,1)S(1)}, u32[]{:S(2)}, u32[]{:S(2)}) collective-permute-start(bf16[64,256]{1,0:T(8,128)(2,1)S(1)} %get-tuple-element.76.second_ref), channel_id=1, source_target_pairs={{0,6},{1,7},{2,4},{3,5},{4,2},{5,3},{6,0},{7,1},{8,14},{9,15},{10,... | collective-permute-start | bytes 98312 | tf_op jit(solution)/shard_map/ppermute | solution.py:172
  107.7 2.1 %collective-permute-done.36 = bf16[64,256]{1,0:T(8,128)(2,1)S(1)} collective-permute-done((bf16[64,256]{1,0:T(8,128)(2,1)S(1)}, bf16[64,256]{1,0:T(8,128)(2,1)S(1)}, u32[]{:S(2)}, u32[]{:S(2)}) %collective-permute-start.36) | collective-permute-done | bytes 32800 | tf_op jit(solution)/shard_map/ppermute | solution.py:172
  109.8 2.0 %collective-permute-done.28.refs_1_ = bf16[1280,256]{1,0:T(8,128)(2,1)S(1)} collective-permute-done((bf16[1280,256]{1,0:T(8,128)(2,1)S(1)}, bf16[1280,256]{1,0:T(8,128)(2,1)S(1)}, u32[]{:S(2)}, u32[]{:S(2)}) %collective-permute-start.28) | collective-permute-done | bytes 655392 | tf_op jit(solution)/shard_map/ppermute | solution.py:172
  113.8 2.5 %collective-permute-start.42 = (bf16[64,256]{1,0:T(8,128)(2,1)S(1)}, bf16[64,256]{1,0:T(8,128)(2,1)S(1)}, u32[]{:S(2)}, u32[]{:S(2)}) collective-permute-start(bf16[64,256]{1,0:T(8,128)(2,1)S(1)} %get-tuple-element.118.first_ref), channel_id=1, source_target_pairs={{0,6},{1,7},{2,4},{3,5},{4,2},{5,3},{6,0},{7,1},{8,14},{9,15},{10,... | collective-permute-start | bytes 98312 | tf_op jit(solution)/shard_map/ppermute | solution.py:172
  116.9 2.6 %collective-permute-done.42 = bf16[64,256]{1,0:T(8,128)(2,1)S(1)} collective-permute-done((bf16[64,256]{1,0:T(8,128)(2,1)S(1)}, bf16[64,256]{1,0:T(8,128)(2,1)S(1)}, u32[]{:S(2)}, u32[]{:S(2)}) %collective-permute-start.42) | collective-permute-done | bytes 32800 | tf_op jit(solution)/shard_map/ppermute | solution.py:172
  119.6 1.8 %collective-permute-start.43 = (bf16[4,64,256]{2,1,0:T(8,128)(2,1)S(1)}, bf16[4,64,256]{2,1,0:T(8,128)(2,1)S(1)}, u32[]{:S(2)}, u32[]{:S(2)}) collective-permute-start(bf16[4,64,256]{2,1,0:T(8,128)(2,1)S(1)} %pad_maximum_fusion.3.refs_4_), channel_id=1, source_target_pairs={{0,8},{8,0},{16,24},{24,16},{1,9},{9,1},{17,25},{25,17},{2,10},{10... | collective-permute-start | bytes 393224 | tf_op jit(solution)/shard_map/ppermute | solution.py:172
  123.2 1.8 %collective-permute-start.47 = (bf16[4,64,256]{2,1,0:T(8,128)(2,1)S(1)}, bf16[4,64,256]{2,1,0:T(8,128)(2,1)S(1)}, u32[]{:S(2)}, u32[]{:S(2)}) collective-permute-start(bf16[4,64,256]{2,1,0:T(8,128)(2,1)S(1)} %pad_maximum_fusion.4.refs_4_), channel_id=1, source_target_pairs={{0,8},{8,0},{16,24},{24,16},{1,9},{9,1},{17,25},{25,17},{2,10},{10... | collective-permute-start | bytes 393224 | tf_op jit(solution)/shard_map/ppermute | solution.py:172
  127.2 3.0 %collective-permute-done.44.refs_6_ = bf16[4,64,256]{2,1,0:T(8,128)(2,1)S(1)} collective-permute-done((bf16[4,64,256]{2,1,0:T(8,128)(2,1)S(1)}, bf16[4,64,256]{2,1,0:T(8,128)(2,1)S(1)}, u32[]{:S(2)}, u32[]{:S(2)}) %collective-permute-start.44) | collective-permute-done | bytes 131104 | tf_op jit(solution)/shard_map/ppermute | solution.py:172
  131.5 2.4 %weight_grad.2 = (f32[160,256]{1,0:T(8,128)}, f32[160,256]{1,0:T(8,128)}) custom-call(s32[2]{0:T(128)} %pad_add_fusion.place_ref, bf16[320,256]{1,0:T(8,128)(2,1)} %get-tuple-element.80.refs_0_, bf16[320,256]{1,0:T(8,128)(2,1)} %copy-done.7, bf16[320,256]{1,0:T(8,128)(2,1)} %copy-done.8, bf16[320,256]{1,0:T(8,128)(2,1)} %copy-done.9, ...), custom_call_target="tpu_custom_call" | custom-call | flops 167772160 | bytes 3000000 | tf_op jit(solution)/shard_map/weight_grad/pallas_call | solution.py:158
  136.7 2.4 %weight_grad.3 = (f32[160,256]{1,0:T(8,128)}, f32[160,256]{1,0:T(8,128)}) custom-call(s32[2]{0:T(128)} %pad_add_fusion.place_ref, bf16[320,256]{1,0:T(8,128)(2,1)} %get-tuple-element.80.refs_0_, bf16[320,256]{1,0:T(8,128)(2,1)} %copy-done.7, bf16[320,256]{1,0:T(8,128)(2,1)} %copy-done.8, bf16[320,256]{1,0:T(8,128)(2,1)} %copy-done.9, ...), custom_call_target="tpu_custom_call" | custom-call | flops 167772160 | bytes 3000000 | tf_op jit(solution)/shard_map/weight_grad/pallas_call | solution.py:158
  140.9 1.8 %collective-permute-start.53 = (f32[64,512]{1,0:T(8,128)S(1)}, f32[64,512]{1,0:T(8,128)S(1)}, u32[]{:S(2)}, u32[]{:S(2)}) collective-permute-start(f32[64,512]{1,0:T(8,128)S(1)} %get-tuple-element.110), channel_id=1, source_target_pairs={{0,4},{1,5},{2,6},{3,7},{4,0},{5,1},{6,2},{7,3},{8,12},{9,13},{10,... | collective-permute-start | bytes 393224 | tf_op jit(solution)/shard_map/ppermute | solution.py:172
  142.6 4.5 %collective-permute-done.52 = f32[64,512]{1,0:T(8,128)S(1)} collective-permute-done((f32[64,512]{1,0:T(8,128)S(1)}, f32[64,512]{1,0:T(8,128)S(1)}, u32[]{:S(2)}, u32[]{:S(2)}) %collective-permute-start.52) | collective-permute-done | bytes 131104 | tf_op jit(solution)/shard_map/ppermute | solution.py:172
  151.0 3.2 %collective-permute-done.54 = f32[64,512]{1,0:T(8,128)S(1)} collective-permute-done((f32[64,512]{1,0:T(8,128)S(1)}, f32[64,512]{1,0:T(8,128)S(1)}, u32[]{:S(2)}, u32[]{:S(2)}) %collective-permute-start.54) | collective-permute-done | bytes 131104 | tf_op jit(solution)/shard_map/ppermute | solution.py:172
  156.8 5.0 %hidden_grad.1 = bf16[64,5120]{1,0:T(8,128)(2,1)} custom-call(s32[2]{0:T(128)} %pad_add_fusion.place_ref, bf16[64,256]{1,0:T(8,128)(2,1)} %copy-done.13, bf16[64,256]{1,0:T(8,128)(2,1)} %copy-done.12, bf16[1280,512]{1,0:T(8,128)(2,1)} %own_ref.1, bf16[1280,256]{1,0:T(8,128)(2,1)} %copy-done.1, bf16[1280,256]{1,0:T(8,128)(2,1)} %copy-done.2, ...), custom_call_target="tpu_custom_call" | custom-call | flops 335544320 | bytes 6000000 | tf_op jit(solution)/shard_map/hidden_grad/pallas_call | solution.py:130
  (221 shorter events, 51.2 us)
Async XLA Ops:
  4.8 34.0 %collective-permute-start.13 = (bf16[64,512]{1,0:T(8,128)(2,1)S(1)}, bf16[64,512]{1,0:T(8,128)(2,1)}, u32[]{:S(2)}, u32[]{:S(2)}) collective-permute-start(bf16[64,512]{1,0:T(8,128)(2,1)S(1)} %bitcast.92), channel_id=1, source_target_pairs={{0,2},{1,3},{2,0},{3,1},{4,6},{5,7},{6,4},{7,5},{8,10},{9,11},{10,... | collective-permute-start | bytes 196616 | tf_op jit(solution)/shard_map/ppermute | solution.py:172
  7.8 31.0 %collective-permute-start.14 = (bf16[64,512]{1,0:T(8,128)(2,1)S(1)}, bf16[64,512]{1,0:T(8,128)(2,1)}, u32[]{:S(2)}, u32[]{:S(2)}) collective-permute-start(bf16[64,512]{1,0:T(8,128)(2,1)S(1)} %bitcast.93), channel_id=1, source_target_pairs={{0,4},{1,5},{2,6},{3,7},{4,0},{5,1},{6,2},{7,3},{8,12},{9,13},{10,... | collective-permute-start | bytes 196616 | tf_op jit(solution)/shard_map/ppermute | solution.py:172
  10.4 10.9 %collective-permute-start = (bf16[64,1280]{0,1:T(8,128)(2,1)}, bf16[64,1280]{0,1:T(8,128)(2,1)S(1)}, u32[]{:S(2)}, u32[]{:S(2)}) collective-permute-start(bf16[64,1280]{0,1:T(8,128)(2,1)} %bitcast.8), channel_id=1, source_target_pairs={{0,8},{8,0},{16,24},{24,16},{1,9},{9,1},{17,25},{25,17},{2,10},{10... | collective-permute-start | bytes 491528 | tf_op jit(solution)/shard_map/ppermute | solution.py:172
  11.9 16.1 %collective-permute-start.1 = (bf16[64,1280]{0,1:T(8,128)(2,1)}, bf16[64,1280]{0,1:T(8,128)(2,1)S(1)}, u32[]{:S(2)}, u32[]{:S(2)}) collective-permute-start(bf16[64,1280]{0,1:T(8,128)(2,1)} %bitcast.9), channel_id=1, source_target_pairs={{0,16},{8,24},{16,0},{24,8},{1,17},{9,25},{17,1},{25,9},{2,18},{10... | collective-permute-start | bytes 491528 | tf_op jit(solution)/shard_map/ppermute | solution.py:172
  13.4 17.4 %collective-permute-start.2 = (bf16[64,1280]{0,1:T(8,128)(2,1)}, bf16[64,1280]{0,1:T(8,128)(2,1)S(1)}, u32[]{:S(2)}, u32[]{:S(2)}) collective-permute-start(bf16[64,1280]{0,1:T(8,128)(2,1)} %bitcast.10), channel_id=1, source_target_pairs={{0,24},{8,16},{16,8},{24,0},{1,25},{9,17},{17,9},{25,1},{2,26},{10... | collective-permute-start | bytes 491528 | tf_op jit(solution)/shard_map/ppermute | solution.py:172
  21.7 9.6 %collective-permute-start.3 = (f32[64,512]{1,0:T(8,128)S(1)}, f32[64,512]{1,0:T(8,128)S(1)}, u32[]{:S(2)}, u32[]{:S(2)}) collective-permute-start(f32[64,512]{1,0:T(8,128)S(1)} %fusion.17), channel_id=1, source_target_pairs={{0,8},{8,0},{16,24},{24,16},{1,9},{9,1},{17,25},{25,17},{2,10},{10... | collective-permute-start | bytes 393224 | tf_op jit(solution)/shard_map/ppermute | solution.py:172
  31.3 8.1 %collective-permute-start.15 = (bf16[64,512]{1,0:T(8,128)(2,1)S(1)}, bf16[64,512]{1,0:T(8,128)(2,1)S(1)}, u32[]{:S(2)}, u32[]{:S(2)}) collective-permute-start(bf16[64,512]{1,0:T(8,128)(2,1)S(1)} %bitcast.94), channel_id=1, source_target_pairs={{0,6},{1,7},{2,4},{3,5},{4,2},{5,3},{6,0},{7,1},{8,14},{9,15},{10,... | collective-permute-start | bytes 196616 | tf_op jit(solution)/shard_map/ppermute | solution.py:172
  33.8 14.3 %collective-permute-start.16 = (bf16[64,512]{1,0:T(8,128)(2,1)S(1)}, bf16[64,512]{1,0:T(8,128)(2,1)S(1)}, u32[]{:S(2)}, u32[]{:S(2)}) collective-permute-start(bf16[64,512]{1,0:T(8,128)(2,1)S(1)} %bitcast.95), channel_id=1, source_target_pairs={{0,1},{1,0},{2,3},{3,2},{4,5},{5,4},{6,7},{7,6},{8,9},{9,8},{10,11... | collective-permute-start | bytes 196616 | tf_op jit(solution)/shard_map/ppermute | solution.py:172
  38.8 9.8 %collective-permute-start.17 = (bf16[64,512]{1,0:T(8,128)(2,1)}, bf16[64,512]{1,0:T(8,128)(2,1)S(1)}, u32[]{:S(2)}, u32[]{:S(2)}) collective-permute-start(bf16[64,512]{1,0:T(8,128)(2,1)} %collective-permute-done.13.refs_9_), channel_id=1, source_target_pairs={{0,1},{1,0},{2,3},{3,2},{4,5},{5,4},{6,7},{7,6},{8,9},{9,8},{10,11... | collective-permute-start | bytes 196616 | tf_op jit(solution)/shard_map/ppermute | solution.py:172
  38.9 9.8 %collective-permute-start.18 = (bf16[64,512]{1,0:T(8,128)(2,1)}, bf16[64,512]{1,0:T(8,128)(2,1)S(1)}, u32[]{:S(2)}, u32[]{:S(2)}) collective-permute-start(bf16[64,512]{1,0:T(8,128)(2,1)} %collective-permute-done.14.refs_10_), channel_id=1, source_target_pairs={{0,1},{1,0},{2,3},{3,2},{4,5},{5,4},{6,7},{7,6},{8,9},{9,8},{10,11... | collective-permute-start | bytes 196616 | tf_op jit(solution)/shard_map/ppermute | solution.py:172
  39.4 7.8 %collective-permute-start.7 = (bf16[64,512]{1,0:T(8,128)(2,1)S(1)}, bf16[64,512]{1,0:T(8,128)(2,1)S(1)}, u32[]{:S(2)}, u32[]{:S(2)}) collective-permute-start(bf16[64,512]{1,0:T(8,128)(2,1)S(1)} %fusion.1.refs_0_), channel_id=1, source_target_pairs={{0,4},{1,5},{2,6},{3,7},{4,0},{5,1},{6,2},{7,3},{8,12},{9,13},{10,... | collective-permute-start | bytes 196616 | tf_op jit(solution)/shard_map/ppermute | solution.py:172
  50.0 30.9 %collective-permute-start.21 = (bf16[320,256]{1,0:T(8,128)(2,1)}, bf16[320,256]{1,0:T(8,128)(2,1)S(1)}, u32[]{:S(2)}, u32[]{:S(2)}) collective-permute-start(bf16[320,256]{1,0:T(8,128)(2,1)} %get-tuple-element.102), channel_id=1, source_target_pairs={{0,2},{1,3},{2,0},{3,1},{4,6},{5,7},{6,4},{7,5},{8,10},{9,11},{10,... | collective-permute-start | bytes 491528 | tf_op jit(solution)/shard_map/ppermute | solution.py:172
  51.1 30.5 %collective-permute-start.22 = (bf16[320,256]{1,0:T(8,128)(2,1)}, bf16[320,256]{1,0:T(8,128)(2,1)S(1)}, u32[]{:S(2)}, u32[]{:S(2)}) collective-permute-start(bf16[320,256]{1,0:T(8,128)(2,1)} %get-tuple-element.101), channel_id=1, source_target_pairs={{0,4},{1,5},{2,6},{3,7},{4,0},{5,1},{6,2},{7,3},{8,12},{9,13},{10,... | collective-permute-start | bytes 491528 | tf_op jit(solution)/shard_map/ppermute | solution.py:172
  52.0 29.6 %collective-permute-start.23 = (bf16[320,256]{1,0:T(8,128)(2,1)}, bf16[320,256]{1,0:T(8,128)(2,1)S(1)}, u32[]{:S(2)}, u32[]{:S(2)}) collective-permute-start(bf16[320,256]{1,0:T(8,128)(2,1)} %get-tuple-element.100), channel_id=1, source_target_pairs={{0,6},{1,7},{2,4},{3,5},{4,2},{5,3},{6,0},{7,1},{8,14},{9,15},{10,... | collective-permute-start | bytes 491528 | tf_op jit(solution)/shard_map/ppermute | solution.py:172
  67.1 13.8 %collective-permute-start.20 = (f32[256,256]{1,0:T(8,128)}, f32[256,256]{1,0:T(8,128)S(1)}, u32[]{:S(2)}, u32[]{:S(2)}) collective-permute-start(f32[256,256]{1,0:T(8,128)} %get-tuple-element.62), channel_id=1, source_target_pairs={{0,1},{1,0},{2,3},{3,2},{4,5},{5,4},{6,7},{7,6},{8,9},{9,8},{10,11... | collective-permute-start | bytes 786440 | tf_op jit(solution)/shard_map/ppermute | solution.py:172
  80.9 28.9 %collective-permute-start.27 = (bf16[1280,256]{1,0:T(8,128)(2,1)S(1)}, bf16[1280,256]{1,0:T(8,128)(2,1)S(1)}, u32[]{:S(2)}, u32[]{:S(2)}) collective-permute-start(bf16[1280,256]{1,0:T(8,128)(2,1)S(1)} %constant_dynamic-slice_fusion.4), channel_id=1, source_target_pairs={{0,8},{8,0},{16,24},{24,16},{1,9},{9,1},{17,25},{25,17},{2,10},{10... | collective-permute-start | bytes 1966088 | tf_op jit(solution)/shard_map/ppermute | solution.py:172
  81.0 30.8 %collective-permute-start.28 = (bf16[1280,256]{1,0:T(8,128)(2,1)S(1)}, bf16[1280,256]{1,0:T(8,128)(2,1)S(1)}, u32[]{:S(2)}, u32[]{:S(2)}) collective-permute-start(bf16[1280,256]{1,0:T(8,128)(2,1)S(1)} %constant_dynamic-slice_fusion.4), channel_id=1, source_target_pairs={{0,16},{8,24},{16,0},{24,8},{1,17},{9,25},{17,1},{25,9},{2,18},{10... | collective-permute-start | bytes 1966088 | tf_op jit(solution)/shard_map/ppermute | solution.py:172
  81.9 7.3 %collective-permute-start.25 = (f32[64,256]{1,0:T(8,128)S(1)}, f32[64,256]{1,0:T(8,128)S(1)}, u32[]{:S(2)}, u32[]{:S(2)}) collective-permute-start(f32[64,256]{1,0:T(8,128)S(1)} %get-tuple-element.116), channel_id=1, source_target_pairs={{0,4},{1,5},{2,6},{3,7},{4,0},{5,1},{6,2},{7,3},{8,12},{9,13},{10,... | collective-permute-start | bytes 196616 | tf_op jit(solution)/shard_map/ppermute | solution.py:172
  89.2 6.7 %collective-permute-start.32 = (f32[64,256]{1,0:T(8,128)}, f32[64,256]{1,0:T(8,128)S(1)}, u32[]{:S(2)}, u32[]{:S(2)}) collective-permute-start(f32[64,256]{1,0:T(8,128)} %get-tuple-element.113), channel_id=1, source_target_pairs={{0,4},{1,5},{2,6},{3,7},{4,0},{5,1},{6,2},{7,3},{8,12},{9,13},{10,... | collective-permute-start | bytes 196616 | tf_op jit(solution)/shard_map/ppermute | solution.py:172
  89.9 6.7 %collective-permute-start.33 = (f32[64,256]{1,0:T(8,128)}, f32[64,256]{1,0:T(8,128)}, u32[]{:S(2)}, u32[]{:S(2)}) collective-permute-start(f32[64,256]{1,0:T(8,128)} %get-tuple-element.112), channel_id=1, source_target_pairs={{0,6},{1,7},{2,4},{3,5},{4,2},{5,3},{6,0},{7,1},{8,14},{9,15},{10,... | collective-permute-start | bytes 196616 | tf_op jit(solution)/shard_map/ppermute | solution.py:172
  93.0 18.8 %collective-permute-start.29 = (bf16[1280,256]{1,0:T(8,128)(2,1)S(1)}, bf16[1280,256]{1,0:T(8,128)(2,1)S(1)}, u32[]{:S(2)}, u32[]{:S(2)}) collective-permute-start(bf16[1280,256]{1,0:T(8,128)(2,1)S(1)} %constant_dynamic-slice_fusion.4), channel_id=1, source_target_pairs={{0,24},{8,16},{16,8},{24,0},{1,25},{9,17},{17,9},{25,1},{2,26},{10... | collective-permute-start | bytes 1966088 | tf_op jit(solution)/shard_map/ppermute | solution.py:172
  111.8 27.4 %collective-permute-start.51 = (f32[256,512]{1,0:T(8,128)S(1)}, f32[256,512]{1,0:T(8,128)S(1)}, u32[]{:S(2)}, u32[]{:S(2)}) collective-permute-start(f32[256,512]{1,0:T(8,128)S(1)} %get-tuple-element.92), channel_id=1, source_target_pairs={{0,1},{1,0},{2,3},{3,2},{4,5},{5,4},{6,7},{7,6},{8,9},{9,8},{10,11... | collective-permute-start | bytes 1572872 | tf_op jit(solution)/shard_map/ppermute | solution.py:172
  121.4 8.8 %collective-permute-start.44 = (bf16[4,64,256]{2,1,0:T(8,128)(2,1)S(1)}, bf16[4,64,256]{2,1,0:T(8,128)(2,1)S(1)}, u32[]{:S(2)}, u32[]{:S(2)}) collective-permute-start(bf16[4,64,256]{2,1,0:T(8,128)(2,1)S(1)} %pad_maximum_fusion.3.refs_4_), channel_id=1, source_target_pairs={{0,16},{8,24},{16,0},{24,8},{1,17},{9,25},{17,1},{25,9},{2,18},{10... | collective-permute-start | bytes 393224 | tf_op jit(solution)/shard_map/ppermute | solution.py:172
  122.1 8.7 %collective-permute-start.45 = (bf16[4,64,256]{2,1,0:T(8,128)(2,1)S(1)}, bf16[4,64,256]{2,1,0:T(8,128)(2,1)S(1)}, u32[]{:S(2)}, u32[]{:S(2)}) collective-permute-start(bf16[4,64,256]{2,1,0:T(8,128)(2,1)S(1)} %pad_maximum_fusion.3.refs_4_), channel_id=1, source_target_pairs={{0,24},{8,16},{16,8},{24,0},{1,25},{9,17},{17,9},{25,1},{2,26},{10... | collective-permute-start | bytes 393224 | tf_op jit(solution)/shard_map/ppermute | solution.py:172
  123.2 10.8 %collective-permute-start.47 = (bf16[4,64,256]{2,1,0:T(8,128)(2,1)S(1)}, bf16[4,64,256]{2,1,0:T(8,128)(2,1)S(1)}, u32[]{:S(2)}, u32[]{:S(2)}) collective-permute-start(bf16[4,64,256]{2,1,0:T(8,128)(2,1)S(1)} %pad_maximum_fusion.4.refs_4_), channel_id=1, source_target_pairs={{0,8},{8,0},{16,24},{24,16},{1,9},{9,1},{17,25},{25,17},{2,10},{10... | collective-permute-start | bytes 393224 | tf_op jit(solution)/shard_map/ppermute | solution.py:172
  125.6 8.9 %collective-permute-start.48 = (bf16[4,64,256]{2,1,0:T(8,128)(2,1)S(1)}, bf16[4,64,256]{2,1,0:T(8,128)(2,1)S(1)}, u32[]{:S(2)}, u32[]{:S(2)}) collective-permute-start(bf16[4,64,256]{2,1,0:T(8,128)(2,1)S(1)} %pad_maximum_fusion.4.refs_4_), channel_id=1, source_target_pairs={{0,16},{8,24},{16,0},{24,8},{1,17},{9,25},{17,1},{25,9},{2,18},{10... | collective-permute-start | bytes 393224 | tf_op jit(solution)/shard_map/ppermute | solution.py:172
  134.0 20.8 %collective-permute-start.37 = (bf16[1280,256]{1,0:T(8,128)(2,1)S(1)}, bf16[1280,256]{1,0:T(8,128)(2,1)S(1)}, u32[]{:S(2)}, u32[]{:S(2)}) collective-permute-start(bf16[1280,256]{1,0:T(8,128)(2,1)S(1)} %collective-permute-done.27.refs_0_), channel_id=1, source_target_pairs={{0,1},{1,0},{2,3},{3,2},{4,5},{5,4},{6,7},{7,6},{8,9},{9,8},{10,11... | collective-permute-start | bytes 1966088 | tf_op jit(solution)/shard_map/ppermute | solution.py:172
  134.5 20.3 %collective-permute-start.38 = (bf16[1280,256]{1,0:T(8,128)(2,1)S(1)}, bf16[1280,256]{1,0:T(8,128)(2,1)S(1)}, u32[]{:S(2)}, u32[]{:S(2)}) collective-permute-start(bf16[1280,256]{1,0:T(8,128)(2,1)S(1)} %collective-permute-done.28.refs_1_), channel_id=1, source_target_pairs={{0,1},{1,0},{2,3},{3,2},{4,5},{5,4},{6,7},{7,6},{8,9},{9,8},{10,11... | collective-permute-start | bytes 1966088 | tf_op jit(solution)/shard_map/ppermute | solution.py:172
  136.1 18.8 %collective-permute-start.39 = (bf16[1280,256]{1,0:T(8,128)(2,1)S(1)}, bf16[1280,256]{1,0:T(8,128)(2,1)S(1)}, u32[]{:S(2)}, u32[]{:S(2)}) collective-permute-start(bf16[1280,256]{1,0:T(8,128)(2,1)S(1)} %collective-permute-done.29.refs_2_), channel_id=1, source_target_pairs={{0,1},{1,0},{2,3},{3,2},{4,5},{5,4},{6,7},{7,6},{8,9},{9,8},{10,11... | collective-permute-start | bytes 1966088 | tf_op jit(solution)/shard_map/ppermute | solution.py:172
  139.4 7.7 %collective-permute-start.52 = (f32[64,512]{1,0:T(8,128)S(1)}, f32[64,512]{1,0:T(8,128)S(1)}, u32[]{:S(2)}, u32[]{:S(2)}) collective-permute-start(f32[64,512]{1,0:T(8,128)S(1)} %get-tuple-element.108), channel_id=1, source_target_pairs={{0,2},{1,3},{2,0},{3,1},{4,6},{5,7},{6,4},{7,5},{8,10},{9,11},{10,... | collective-permute-start | bytes 393224 | tf_op jit(solution)/shard_map/ppermute | solution.py:172
  140.9 10.1 %collective-permute-start.53 = (f32[64,512]{1,0:T(8,128)S(1)}, f32[64,512]{1,0:T(8,128)S(1)}, u32[]{:S(2)}, u32[]{:S(2)}) collective-permute-start(f32[64,512]{1,0:T(8,128)S(1)} %get-tuple-element.110), channel_id=1, source_target_pairs={{0,4},{1,5},{2,6},{3,7},{4,0},{5,1},{6,2},{7,3},{8,12},{9,13},{10,... | collective-permute-start | bytes 393224 | tf_op jit(solution)/shard_map/ppermute | solution.py:172
  147.1 7.0 %collective-permute-start.54 = (f32[64,512]{1,0:T(8,128)S(1)}, f32[64,512]{1,0:T(8,128)S(1)}, u32[]{:S(2)}, u32[]{:S(2)}) collective-permute-start(f32[64,512]{1,0:T(8,128)S(1)} %get-tuple-element.109), channel_id=1, source_target_pairs={{0,6},{1,7},{2,4},{3,5},{4,2},{5,3},{6,0},{7,1},{8,14},{9,15},{10,... | collective-permute-start | bytes 393224 | tf_op jit(solution)/shard_map/ppermute | solution.py:172
  (63 other events, 456.0 us)

commit v5 on v4

--- a/solution.py
+++ b/solution.py
@@ -34,8 +34,7 @@
 
 def attend_kernel(pieces, chained, length_ref, query_ref, upstream_ref, key_ref, value_ref, *refs):
     key_pieces, value_pieces = refs[:pieces], refs[pieces : 2 * pieces]
-    query_grad_ref, key_grad_ref, value_grad_ref, *halves = refs[2 * pieces + 3 * chained :]
-    key_near_ref, key_far_ref, value_near_ref, value_far_ref = halves
+    query_grad_ref, key_grad_ref, value_grad_ref, *sum_refs = refs[2 * pieces + 3 * chained :]
     rows = query_ref.shape[0]
     own_len, head_dim = key_ref.shape
     heads = query_ref.shape[1] // head_dim
@@ -70,8 +69,10 @@
     key_grad = dot(queries.T, dscore).T
     value_grad = dot(upstream.T, weights).T
     half = prompt_len // 2
-    key_near_ref[...], key_far_ref[...] = key_grad[:half], key_grad[half:prompt_len]
-    value_near_ref[...], value_far_ref[...] = value_grad[:half], value_grad[half:prompt_len]
+    per_array = len(sum_refs) // 2
+    for i, grad in enumerate((key_grad, value_grad)):
+        near_ref, far_ref = sum_refs[:2] if per_array == 1 else sum_refs[2 * i : 2 * i + 2]
+        near_ref[i % (3 - per_array)], far_ref[i % (3 - per_array)] = grad[:half], grad[half:prompt_len]
     key_grad_ref[...] = key_grad[prompt_len:].astype(BF16)
     value_grad_ref[...] = value_grad[prompt_len:].astype(BF16)
 
@@ -87,7 +88,9 @@
 
     query_block, own_block = block(rows, width // kv_heads), block(rows, head_dim)
     piece_blocks = [block(piece.shape[0], head_dim) for piece in key_pieces]
-    half = jax.ShapeDtypeStruct((prompt_len // 2, count * head_dim), F32)
+    kinds, arrays = (1, 2) if earlier else (2, 1)
+    half = jax.ShapeDtypeStruct((kinds, prompt_len // 2, count * head_dim), F32)
+    half_block = pl.BlockSpec((kinds, prompt_len // 2, head_dim), lambda i: (0, 0, i))
     own = jax.ShapeDtypeStruct((rows, kv_width), BF16)
     before = 5 + 2 * len(key_pieces)
     macs = 5 * rows * width * (prompt_len + rows) * count // kv_heads
@@ -98,8 +101,8 @@
             pl.BlockSpec(memory_space=pltpu.SMEM), query_block, query_block, own_block, own_block,
             *piece_blocks, *piece_blocks, *[pl.BlockSpec(memory_space=pl.ANY) for _ in earlier],
         ],
-        out_specs=[query_block, own_block, own_block] + [block(prompt_len // 2, head_dim, 0)] * 4,
-        out_shape=[jax.ShapeDtypeStruct((rows, width), BF16), own, own] + [half] * 4,
+        out_specs=[query_block, own_block, own_block] + [half_block] * (2 * arrays),
+        out_shape=[jax.ShapeDtypeStruct((rows, width), BF16), own, own] + [half] * (2 * arrays),
         input_output_aliases={before + i: i for i in range(len(earlier))},
         compiler_params=PARAMS,
         cost_estimate=cost(2 * macs, 5 * 10**6),
@@ -107,36 +110,36 @@
     )(length, queries, upstream, keys, values, *key_pieces, *value_pieces, *earlier)
 
 
-def hidden_kernel(groups, place_ref, first_ref, second_ref, own_ref, *refs):
+def hidden_kernel(groups, place_ref, grad_ref, own_ref, *refs):
     near, far, out_ref = refs[: groups - 1], refs[groups - 1 : -1], refs[-1]
     group, core = place_ref[0], place_ref[1]
     depth = own_ref.shape[0]
-    first, second = first_ref[...], second_ref[...]
-    near_grad = jnp.where(core == 0, first, second)
-    far_grad = jnp.where(core == 0, second, first)
+    half = near[0].shape[1]
+    near_grad = grad_ref[:, pl.ds(pl.multiple_of(core * half, half), half)]
+    far_grad = grad_ref[:, pl.ds(pl.multiple_of((1 - core) * half, half), half)]
     for k in range(groups):
         if k:
             block = dot(near_grad, near[k - 1][...], 1, 1) + dot(far_grad, far[k - 1][...], 1, 1)
         else:
-            block = dot(jnp.concatenate([first, second], axis=1), own_ref[...], 1, 1)
+            block = dot(grad_ref[...], own_ref[...], 1, 1)
         start = pl.multiple_of((group ^ k) * depth, depth)
         out_ref[:, pl.ds(start, depth)] = block.astype(BF16)
 
 
-def hidden_pass(place, key_pre_grads, own, near, far):
-    tokens = key_pre_grads[0].shape[0]
+def hidden_pass(place, key_pre_grad, own, near, far):
+    tokens = key_pre_grad.shape[0]
     groups = len(near) + 1
     width = groups * own.shape[0]
     return pl.pallas_call(
         partial(hidden_kernel, groups),
         in_specs=[pl.BlockSpec(memory_space=pltpu.SMEM)]
-        + [pl.BlockSpec(memory_space=pltpu.VMEM)] * (2 * groups + 1),
+        + [pl.BlockSpec(memory_space=pltpu.VMEM)] * (2 * groups),
         out_specs=pl.BlockSpec(memory_space=pltpu.VMEM),
         out_shape=jax.ShapeDtypeStruct((tokens, width), BF16),
         compiler_params=PARAMS,
         cost_estimate=cost(tokens * width * own.shape[1], 6 * 10**6),
         name="hidden_grad",
-    )(place, *key_pre_grads, own, *near, *far)
+    )(place, key_pre_grad, own, *near, *far)
 
 
 def weight_kernel(chips, place_ref, *refs):
@@ -181,7 +184,7 @@
 
 
 def spread_far(near, size):
-    return [swap(piece, "resp", size, 1) for piece in near]
+    return [swap(jnp.concatenate(near, axis=0), "resp", size, 1)]
 
 
 def pair_sum(near, far, size):
@@ -189,10 +192,10 @@
 
 
 def chip_sum(near, size):
-    rows = near.shape[0] // (size // 2)
-    total = near[:rows]
+    rows = near.shape[1] // (size // 2)
+    total = near[:, :rows]
     for p in range(1, size // 2):
-        total = total + swap(near[p * rows : (p + 1) * rows], "resp", size, 2 * p)
+        total = total + swap(near[:, p * rows : (p + 1) * rows], "resp", size, 2 * p)
     return total
 
 
@@ -211,8 +214,8 @@
     pieces = [
         lax.dynamic_slice(hidden, (0, (group ^ k) * depth), (tokens, depth)) for k in range(groups)
     ]
-    prompt_value, *pieces = together(prompt_token_value[0], *pieces)
     columns = [swap(piece, "group", groups, k) if k else piece for k, piece in enumerate(pieces)]
+    prompt_value, columns[1] = together(prompt_token_value[0], columns[1])
     partials = [dot(piece, key_matrix) for piece in columns]
     value_near = spread_near(prompt_value, responses)
     key_pre = partials[0]
@@ -244,37 +247,38 @@
     )
     count = kv_width // head_dim // 2
     width = count * head_dim
-    *earlier, near, far, value_near0, value_far0 = attend(resp_length, *rest, 0, count, [])
+    *earlier, near, far = attend(resp_length, *rest, 0, count, [])
+    near, far, *rest_taken = together(near, far, *weight_near[:-1], *taken)
+    weight_near[:-1], taken = rest_taken[: groups - 2], rest_taken[groups - 2 :]
     near = pair_sum(near, far, responses)
-    length, near, *taken = together(resp_length, near, *taken)
+    length, near = together(resp_length, near)
     sums0 = chip_sum(near, responses)
-    *outputs, near, far, value_near1, value_far1 = attend(length, *rest, count, count, earlier)
+    *outputs, near, far, value_near, value_far = attend(length, *rest, count, count, earlier)
     query_grad, key_grad, value_grad = outputs
+    sums0, near, far, weight_near[-1] = together(sums0, near, far, weight_near[-1])
     sums1 = chip_sum(pair_sum(near, far, responses), responses)
-
-    halves = []
-    for i, sums in enumerate((sums0, sums1)):
-        part = key_pre[:, i * width : (i + 1) * width]
-        _, pullback = jax.vjp(lambda values: norm_keys(values, key_gain), part)
-        halves.append(spread_near(pullback(sums)[0].astype(BF16), responses))
-    value_near = jnp.concatenate([value_near0, value_near1], axis=1)
-    value_far = jnp.concatenate([value_far0, value_far1], axis=1)
-    value_near, value_far, *rest = together(value_near, value_far, *weight_near, *halves[1])
-    weight_near, halves[1] = rest[: groups - 1], rest[groups - 1 :]
+    value_near = pair_sum(value_near, value_far, responses)
+    _, pullback = jax.vjp(lambda values: norm_keys(values, key_gain), key_pre)
+    key_pre_grad = pullback(jnp.concatenate([sums0[0], sums1[0]], axis=1))[0].astype(BF16)
+
+    key_pre_grad, value_near = together(key_pre_grad, value_near)
+
+    grads = spread_near(key_pre_grad, responses)
+    weight_near[0], *grads = together(weight_near[0], *grads)
+    block = jnp.stack(grads, axis=0)
+    blocks = [block] + [swap(block, "group", groups, k) for k in range(1, groups)]
     weight_far = [swap(piece, "resp", responses, 1) for piece in weight_near]
-    grad_hidden = hidden_pass(
-        place, [near[0] for near in halves], key_matrix, weight_near, weight_far
-    )
-    weight_halves = []
-    for near in halves:
-        block = jnp.stack(near, axis=0)
-        blocks = [block] + [swap(block, "group", groups, k) for k in range(1, groups)]
-        mine, other = weight_pass(place, taken, blocks)
-        weight_halves.append(mine + swap(other, "resp", responses, 1))
-    prompt_value_grad = chip_sum(pair_sum(value_near, value_far, responses), responses)
+    grad_hidden = hidden_pass(place, grads[0], key_matrix, weight_near, weight_far)
+    grad_hidden, value_near = together(grad_hidden, value_near)
+    values1 = chip_sum(value_near, responses)
+    grad_hidden, *blocks = together(grad_hidden, *blocks)
+    mine, other = weight_pass(place, taken, blocks)
+    other, values1 = together(other, values1)
+    grad_weight = mine + swap(other, "resp", responses, 1)
+    prompt_value_grad = jnp.concatenate([sums0[1], values1[0]], axis=1)
     return (
         grad_hidden[None],
-        jnp.concatenate(weight_halves, axis=1),
+        grad_weight,
         prompt_value_grad.astype(BF16)[None],
         query_grad[None, None],
         key_grad[None, None],

time: 162 us -> 130 us (0.80)
  waiting for transfers between devices: 51.1 us -> 29.7 us
  starting transfers between devices: 53.3 us -> 47.5 us
  local copies, waits for them, and re-layouts: 13.6 us -> 9.47 us
  Pallas kernels: 33.7 us -> 31.6 us
    ppermute x55 -> x42, waiting for transfers between devices: 51.1 us -> 29.7 us  [swap(): return lax.ppermute(array, axis, [(i, i ^ distance) for i in range(size)])]
    ppermute x55 -> x42, starting transfers between devices: 53.3 us -> 47.5 us  [swap(): return lax.ppermute(array, axis, [(i, i ^ distance) for i in range(size)])]
    pallas_call x2 -> x1, Pallas kernels: 4.86 us -> 2.83 us  [weight_pass(): pl.pallas_call(partial(weight_kernel, len(taken)), in_specs=[pl.BlockSpec...]
    add x3, other arithmetic: 0.15 us -> 2.13 us  [pair_sum(): return near + swap(far, 'resp', size, 1)]
    unnamed x80 -> x50, local copies, waits for them, and re-layouts: 4.46 us -> 3.77 us
  transfers between devices with their start and end apart: 55 -> 42, of which waited for: 21 -> 16; matrix products, arithmetic and copies ran while one was open for 8% -> 9% of each run, Pallas kernels for 18% -> 24%
where the time goes in v5:
time: 130 us
  starting transfers between devices  47.5 us (37%)
  Pallas kernels  31.6 us (24%)
  waiting for transfers between devices  29.7 us (23%)
  local copies, waits for them, and re-layouts  9.47 us (7%)
  other arithmetic  7.75 us (6%)
  matrix products  2.06 us (2%)
  between operations  1.85 us (1%)
    ppermute x42, starting transfers between devices, swap(): return lax.ppermute(array, axis, [(i, i ^ distance) for i in range(size)])  47.5 us
    ppermute x42, waiting for transfers between devices, swap(): return lax.ppermute(array, axis, [(i, i ^ distance) for i in range(size)])  29.7 us
    pallas_call x2, Pallas kernels, attend(): pl.pallas_call(partial(attend_kernel, len(key_pieces), bool(earlier)), gr...  23.7 us
    pallas_call x1, Pallas kernels, hidden_pass(): pl.pallas_call(partial(hidden_kernel, groups), in_specs=[pl.BlockSpec(mem...  5.03 us
    dynamic_slice x5, local copies, waits for them, and re-layouts, shards(): lax.dynamic_slice(hidden, (0, (group ^ k) * depth), (tokens, depth))  4.13 us
    unnamed x50, local copies, waits for them, and re-layouts  3.77 us
    pallas_call x1, Pallas kernels, weight_pass(): pl.pallas_call(partial(weight_kernel, len(taken)), in_specs=[pl.BlockSpec...  2.83 us
  transfers between devices with their start and end apart: 42, of which 16 were waited for; matrix products, arithmetic and copies ran while one was open for 9% of the time, Pallas kernels for 24%

profile of v5, /device:TPU:0, one launch (start us, length us, event | category | flops | bytes accessed | tf_op | source)
XLA Modules:
  0.0 129.9 jit_solution(2970487279249246464)
XLA Ops:
  0.7 1.2 constant_dynamic-slice_fusion.8
  2.8 3.9 %collective-permute-start.2 = (bf16[64,1280]{0,1:T(8,128)(2,1)}, bf16[64,1280]{0,1:T(8,128)(2,1)S(1)}, u32[]{:S(2)}, u32[]{:S(2)}) collective-permute-start(bf16[64,1280]{0,1:T(8,128)(2,1)} %bitcast.10), channel_id=1, source_target_pairs={{0,24},{8,16},{16,8},{24,0},{1,25},{9,17},{17,9},{25,1},{2,26},{10... | collective-permute-start | bytes 491528 | tf_op jit(solution)/shard_map/ppermute | solution.py:175
  10.4 11.5 %collective-permute-done = bf16[64,1280]{0,1:T(8,128)(2,1)S(1)} collective-permute-done((bf16[64,1280]{0,1:T(8,128)(2,1)}, bf16[64,1280]{0,1:T(8,128)(2,1)S(1)}, u32[]{:S(2)}, u32[]{:S(2)}) %collective-permute-start) | collective-permute-done | bytes 163872 | tf_op jit(solution)/shard_map/ppermute | solution.py:175
  21.9 1.6 %collective-permute-start.10 = (bf16[64,512]{1,0:T(8,128)(2,1)}, bf16[64,512]{1,0:T(8,128)(2,1)}, u32[]{:S(2)}, u32[]{:S(2)}) collective-permute-start(bf16[64,512]{1,0:T(8,128)(2,1)} %bitcast.7.refs_5_), channel_id=1, source_target_pairs={{0,2},{1,3},{2,0},{3,1},{4,6},{5,7},{6,4},{7,5},{8,10},{9,11},{10,... | collective-permute-start | bytes 196616 | tf_op jit(solution)/shard_map/ppermute | solution.py:175
  23.5 2.6 %collective-permute-start.11 = (bf16[64,512]{1,0:T(8,128)(2,1)}, bf16[64,512]{1,0:T(8,128)(2,1)}, u32[]{:S(2)}, u32[]{:S(2)}) collective-permute-start(bf16[64,512]{1,0:T(8,128)(2,1)} %bitcast.7.refs_5_), channel_id=1, source_target_pairs={{0,4},{1,5},{2,6},{3,7},{4,0},{5,1},{6,2},{7,3},{8,12},{9,13},{10,... | collective-permute-start | bytes 196616 | tf_op jit(solution)/shard_map/ppermute | solution.py:175
  26.4 1.5 %collective-permute-start.5 = (f32[64,512]{1,0:T(8,128)S(1)}, f32[64,512]{1,0:T(8,128)S(1)}, u32[]{:S(2)}, u32[]{:S(2)}) collective-permute-start(f32[64,512]{1,0:T(8,128)S(1)} %fusion.14), channel_id=1, source_target_pairs={{0,24},{8,16},{16,8},{24,0},{1,25},{9,17},{17,9},{25,1},{2,26},{10... | collective-permute-start | bytes 393224 | tf_op jit(solution)/shard_map/ppermute | solution.py:175
  28.3 1.6 %collective-permute-start.4 = (f32[64,512]{1,0:T(8,128)S(1)}, f32[64,512]{1,0:T(8,128)S(1)}, u32[]{:S(2)}, u32[]{:S(2)}) collective-permute-start(f32[64,512]{1,0:T(8,128)S(1)} %fusion.13), channel_id=1, source_target_pairs={{0,16},{8,24},{16,0},{24,8},{1,17},{9,25},{17,1},{25,9},{2,18},{10... | collective-permute-start | bytes 393224 | tf_op jit(solution)/shard_map/ppermute | solution.py:175
  31.3 2.3 %collective-permute-done.5 = f32[64,512]{1,0:T(8,128)S(1)} collective-permute-done((f32[64,512]{1,0:T(8,128)S(1)}, f32[64,512]{1,0:T(8,128)S(1)}, u32[]{:S(2)}, u32[]{:S(2)}) %collective-permute-start.5) | collective-permute-done | bytes 131104 | tf_op jit(solution)/shard_map/ppermute | solution.py:175
  36.4 2.3 %collective-permute-start.7 = (bf16[64,512]{1,0:T(8,128)(2,1)S(1)}, bf16[64,512]{1,0:T(8,128)(2,1)S(1)}, u32[]{:S(2)}, u32[]{:S(2)}) collective-permute-start(bf16[64,512]{1,0:T(8,128)(2,1)S(1)} %fusion.5.refs_0_), channel_id=1, source_target_pairs={{0,4},{1,5},{2,6},{3,7},{4,0},{5,1},{6,2},{7,3},{8,12},{9,13},{10,... | collective-permute-start | bytes 196616 | tf_op jit(solution)/shard_map/ppermute | solution.py:175
  38.7 1.7 %collective-permute-start.8 = (bf16[64,512]{1,0:T(8,128)(2,1)S(1)}, bf16[64,512]{1,0:T(8,128)(2,1)S(1)}, u32[]{:S(2)}, u32[]{:S(2)}) collective-permute-start(bf16[64,512]{1,0:T(8,128)(2,1)S(1)} %fusion.5.refs_0_), channel_id=1, source_target_pairs={{0,6},{1,7},{2,4},{3,5},{4,2},{5,3},{6,0},{7,1},{8,14},{9,15},{10,... | collective-permute-start | bytes 196616 | tf_op jit(solution)/shard_map/ppermute | solution.py:175
  42.9 1.9 %collective-permute-done.8.refs_3_ = bf16[64,512]{1,0:T(8,128)(2,1)S(1)} collective-permute-done((bf16[64,512]{1,0:T(8,128)(2,1)S(1)}, bf16[64,512]{1,0:T(8,128)(2,1)S(1)}, u32[]{:S(2)}, u32[]{:S(2)}) %collective-permute-start.8) | collective-permute-done | bytes 65568 | tf_op jit(solution)/shard_map/ppermute | solution.py:175
  46.9 1.4 %collective-permute-start.15 = (bf16[1280,256]{1,0:T(8,128)(2,1)S(1)}, bf16[1280,256]{1,0:T(8,128)(2,1)S(1)}, u32[]{:S(2)}, u32[]{:S(2)}) collective-permute-start(bf16[1280,256]{1,0:T(8,128)(2,1)S(1)} %constant_dynamic-slice_fusion.4), channel_id=1, source_target_pairs={{0,16},{8,24},{16,0},{24,8},{1,17},{9,25},{17,1},{25,9},{2,18},{10... | collective-permute-start | bytes 1966088 | tf_op jit(solution)/shard_map/ppermute | solution.py:175
  49.0 1.3 collective-permute-start.17
  50.3 3.1 %collective-permute-start.18 = (bf16[320,256]{1,0:T(8,128)(2,1)S(1)}, bf16[320,256]{1,0:T(8,128)(2,1)S(1)}, u32[]{:S(2)}, u32[]{:S(2)}) collective-permute-start(bf16[320,256]{1,0:T(8,128)(2,1)S(1)} %get-tuple-element.112), channel_id=1, source_target_pairs={{0,6},{1,7},{2,4},{3,5},{4,2},{5,3},{6,0},{7,1},{8,14},{9,15},{10,... | collective-permute-start | bytes 491528 | tf_op jit(solution)/shard_map/ppermute | solution.py:175
  53.4 12.0 %attend.2 = (bf16[256,4096]{1,0:T(8,128)(2,1)}, bf16[256,512]{1,0:T(8,128)(2,1)}, bf16[256,512]{1,0:T(8,128)(2,1)}, f32[2,256,256]{2,1,0:T(8,128)}, f32[2,256,256]{2,1,0:T(8,128)}) custom-call(s32[1,1]{1,0:T(1,128)S(6)} %copy.46.length_ref, bf16[256,4096]{1,0:T(8,128)(2,1)} %bitcast.63, bf16[256,4096]{1,0:T(8,128)(2,1)} %bitcast.65, ...), custom_call_target="tpu_custom_call" | custom-call | flops 8053063680 | bytes 5000000 | tf_op jit(solution)/shard_map/attend/pallas_call | solution.py:97
  66.2 1.4 %collective-permute-start.23 = (bf16[1280,256]{1,0:T(8,128)(2,1)S(1)}, bf16[1280,256]{1,0:T(8,128)(2,1)S(1)}, u32[]{:S(2)}, u32[]{:S(2)}) collective-permute-start(bf16[1280,256]{1,0:T(8,128)(2,1)S(1)} %copy-done.9), channel_id=1, source_target_pairs={{0,24},{8,16},{16,8},{24,0},{1,25},{9,17},{17,9},{25,1},{2,26},{10... | collective-permute-start | bytes 1966088 | tf_op jit(solution)/shard_map/ppermute | solution.py:175
  70.5 1.6 %collective-permute-start.21 = (f32[2,64,256]{2,1,0:T(8,128)S(1)}, f32[2,64,256]{2,1,0:T(8,128)S(1)}, u32[]{:S(2)}, u32[]{:S(2)}) collective-permute-start(f32[2,64,256]{2,1,0:T(8,128)S(1)} %get-tuple-element.122), channel_id=1, source_target_pairs={{0,4},{1,5},{2,6},{3,7},{4,0},{5,1},{6,2},{7,3},{8,12},{9,13},{10,... | collective-permute-start | bytes 393224 | tf_op jit(solution)/shard_map/ppermute | solution.py:175
  72.1 1.8 %collective-permute-start.20 = (f32[2,64,256]{2,1,0:T(8,128)S(1)}, f32[2,64,256]{2,1,0:T(8,128)S(1)}, u32[]{:S(2)}, u32[]{:S(2)}) collective-permute-start(f32[2,64,256]{2,1,0:T(8,128)S(1)} %get-tuple-element.120), channel_id=1, source_target_pairs={{0,2},{1,3},{2,0},{3,1},{4,6},{5,7},{6,4},{7,5},{8,10},{9,11},{10,... | collective-permute-start | bytes 393224 | tf_op jit(solution)/shard_map/ppermute | solution.py:175
  73.9 11.8 %attend.3 = (bf16[256,4096]{1,0:T(8,128)(2,1)}, bf16[256,512]{1,0:T(8,128)(2,1)}, bf16[256,512]{1,0:T(8,128)(2,1)}, f32[1,256,256]{2,1,0:T(8,128)}, f32[1,256,25...) custom-call(s32[1,1]{1,0:T(1,128)S(6)} %copy.46.length_ref, ...), custom_call_target="tpu_custom_call", output_to_operand_aliasing={{0}: (15, {}), {1}: (16, {}), {2}: (17, {})} | custom-call | flops 8053063680 | bytes 5000000 | tf_op jit(solution)/shard_map/attend/pallas_call | solution.py:97
  86.3 1.2 collective-permute-done.24
  90.4 2.7 %collective-permute-start.25 = (f32[1,64,256]{2,1,0:T(8,128)S(1)}, f32[1,64,256]{2,1,0:T(8,128)S(1)}, u32[]{:S(2)}, u32[]{:S(2)}) collective-permute-start(f32[1,64,256]{2,1,0:T(8,128)S(1)} %get-tuple-element.126), channel_id=1, source_target_pairs={{0,2},{1,3},{2,0},{3,1},{4,6},{5,7},{6,4},{7,5},{8,10},{9,11},{10,... | collective-permute-start | bytes 196616 | tf_op jit(solution)/shard_map/ppermute | solution.py:175
  93.1 2.3 %collective-permute-done.27 = f32[1,64,256]{2,1,0:T(8,128)S(1)} collective-permute-done((f32[1,64,256]{2,1,0:T(8,128)S(1)}, f32[1,64,256]{2,1,0:T(8,128)S(1)}, u32[]{:S(2)}, u32[]{:S(2)}) %collective-permute-start.27) | collective-permute-done | bytes 65568 | tf_op jit(solution)/shard_map/ppermute | solution.py:175
  95.4 1.8 %collective-permute-done.26 = f32[1,64,256]{2,1,0:T(8,128)S(1)} collective-permute-done((f32[1,64,256]{2,1,0:T(8,128)S(1)}, f32[1,64,256]{2,1,0:T(8,128)S(1)}, u32[]{:S(2)}, u32[]{:S(2)}) %collective-permute-start.26) | collective-permute-done | bytes 65568 | tf_op jit(solution)/shard_map/ppermute | solution.py:175
  98.0 1.7 %collective-permute-start.30 = (bf16[64,512]{1,0:T(8,128)(2,1)S(1)}, bf16[64,512]{1,0:T(8,128)(2,1)S(1)}, u32[]{:S(2)}, u32[]{:S(2)}) collective-permute-start(bf16[64,512]{1,0:T(8,128)(2,1)S(1)} %fusion.2.grad_ref), channel_id=1, source_target_pairs={{0,4},{1,5},{2,6},{3,7},{4,0},{5,1},{6,2},{7,3},{8,12},{9,13},{10,... | collective-permute-start | bytes 196616 | tf_op jit(solution)/shard_map/ppermute | solution.py:175
  99.7 2.6 %collective-permute-start.31 = (bf16[64,512]{1,0:T(8,128)(2,1)S(1)}, bf16[64,512]{1,0:T(8,128)(2,1)S(1)}, u32[]{:S(2)}, u32[]{:S(2)}) collective-permute-start(bf16[64,512]{1,0:T(8,128)(2,1)S(1)} %fusion.2.grad_ref), channel_id=1, source_target_pairs={{0,6},{1,7},{2,4},{3,5},{4,2},{5,3},{6,0},{7,1},{8,14},{9,15},{10,... | collective-permute-start | bytes 196616 | tf_op jit(solution)/shard_map/ppermute | solution.py:175
  102.8 3.4 %collective-permute-done.30 = bf16[64,512]{1,0:T(8,128)(2,1)S(1)} collective-permute-done((bf16[64,512]{1,0:T(8,128)(2,1)S(1)}, bf16[64,512]{1,0:T(8,128)(2,1)S(1)}, u32[]{:S(2)}, u32[]{:S(2)}) %collective-permute-start.30) | collective-permute-done | bytes 65568 | tf_op jit(solution)/shard_map/ppermute | solution.py:175
  107.7 1.6 %collective-permute-start.36 = (bf16[4,64,512]{2,1,0:T(8,128)(2,1)S(1)}, bf16[4,64,512]{2,1,0:T(8,128)(2,1)S(1)}, u32[]{:S(2)}, u32[]{:S(2)}) collective-permute-start(bf16[4,64,512]{2,1,0:T(8,128)(2,1)S(1)} %pad_maximum_fusion.2.refs_4_), channel_id=1, source_target_pairs={{0,16},{8,24},{16,0},{24,8},{1,17},{9,25},{17,1},{25,9},{2,18},{10... | collective-permute-start | bytes 786440 | tf_op jit(solution)/shard_map/ppermute | solution.py:175
  112.2 5.0 %hidden_grad.1 = bf16[64,5120]{1,0:T(8,128)(2,1)} custom-call(s32[2]{0:T(128)} %pad_add_fusion.place_ref, bf16[64,512]{1,0:T(8,128)(2,1)} %copy-done.10, bf16[1280,512]{1,0:T(8,128)(2,1)} %own_ref.1, bf16[1280,256]{1,0:T(8,128)(2,1)} %copy-done.2, bf16[1280,256]{1,0:T(8,128)(2,1)} %copy-done.3, bf16[1280,256]{1,0:T(8,128)(2,1)} %copy-done.4, ...), custom_call_target="tpu_custom_call" | custom-call | flops 335544320 | bytes 6000000 | tf_op jit(solution)/shard_map/hidden_grad/pallas_call | solution.py:133
  117.2 2.3 %collective-permute-start.40 = (f32[1,64,256]{2,1,0:T(8,128)S(1)}, f32[1,64,256]{2,1,0:T(8,128)S(1)}, u32[]{:S(2)}, u32[]{:S(2)}) collective-permute-start(f32[1,64,256]{2,1,0:T(8,128)S(1)} %get-tuple-element.124), channel_id=1, source_target_pairs={{0,6},{1,7},{2,4},{3,5},{4,2},{5,3},{6,0},{7,1},{8,14},{9,15},{10,... | collective-permute-start | bytes 196616 | tf_op jit(solution)/shard_map/ppermute | solution.py:175
  120.0 1.7 %collective-permute-start.38 = (f32[1,64,256]{2,1,0:T(8,128)S(1)}, f32[1,64,256]{2,1,0:T(8,128)S(1)}, u32[]{:S(2)}, u32[]{:S(2)}) collective-permute-start(f32[1,64,256]{2,1,0:T(8,128)S(1)} %get-tuple-element.123), channel_id=1, source_target_pairs={{0,2},{1,3},{2,0},{3,1},{4,6},{5,7},{6,4},{7,5},{8,10},{9,11},{10,... | collective-permute-start | bytes 196616 | tf_op jit(solution)/shard_map/ppermute | solution.py:175
  123.1 2.8 %weight_grad.1 = (f32[160,512]{1,0:T(8,128)}, f32[160,512]{1,0:T(8,128)}) custom-call(s32[2]{0:T(128)} %pad_add_fusion.place_ref, bf16[320,256]{1,0:T(8,128)(2,1)} %get-tuple-element.96.refs_0_, bf16[320,256]{1,0:T(8,128)(2,1)} %copy-done.17, bf16[320,256]{1,0:T(8,128)(2,1)} %copy-done.18, bf16[320,256]{1,0:T(8,128)(2,1)} %copy-done.19, ...), custom_call_target="tpu_custom_call" | custom-call | flops 335544320 | bytes 3000000 | tf_op jit(solution)/shard_map/weight_grad/pallas_call | solution.py:161
  128.2 1.7 %add.120 = f32[160,512]{1,0:T(8,128)} add(f32[160,512]{1,0:T(8,128)} %get-tuple-element.104, f32[160,512]{1,0:T(8,128)S(1)} %collective-permute-done.41) | non-fusion elementwise | flops 81920 | bytes 983040 | tf_op jit(solution)/shard_map/add | solution.py:277
  (152 shorter events, 30.8 us)
Async XLA Ops:
  2.8 23.3 %collective-permute-start.2 = (bf16[64,1280]{0,1:T(8,128)(2,1)}, bf16[64,1280]{0,1:T(8,128)(2,1)S(1)}, u32[]{:S(2)}, u32[]{:S(2)}) collective-permute-start(bf16[64,1280]{0,1:T(8,128)(2,1)} %bitcast.10), channel_id=1, source_target_pairs={{0,24},{8,16},{16,8},{24,0},{1,25},{9,17},{17,9},{25,1},{2,26},{10... | collective-permute-start | bytes 491528 | tf_op jit(solution)/shard_map/ppermute | solution.py:175
  7.6 20.4 %collective-permute-start.1 = (bf16[64,1280]{0,1:T(8,128)(2,1)}, bf16[64,1280]{0,1:T(8,128)(2,1)S(1)}, u32[]{:S(2)}, u32[]{:S(2)}) collective-permute-start(bf16[64,1280]{0,1:T(8,128)(2,1)} %bitcast.9), channel_id=1, source_target_pairs={{0,16},{8,24},{16,0},{24,8},{1,17},{9,25},{17,1},{25,9},{2,18},{10... | collective-permute-start | bytes 491528 | tf_op jit(solution)/shard_map/ppermute | solution.py:175
  9.0 12.9 %collective-permute-start = (bf16[64,1280]{0,1:T(8,128)(2,1)}, bf16[64,1280]{0,1:T(8,128)(2,1)S(1)}, u32[]{:S(2)}, u32[]{:S(2)}) collective-permute-start(bf16[64,1280]{0,1:T(8,128)(2,1)} %bitcast.8), channel_id=1, source_target_pairs={{0,8},{8,0},{16,24},{24,16},{1,9},{9,1},{17,25},{25,17},{2,10},{10... | collective-permute-start | bytes 491528 | tf_op jit(solution)/shard_map/ppermute | solution.py:175
  21.9 16.8 %collective-permute-start.10 = (bf16[64,512]{1,0:T(8,128)(2,1)}, bf16[64,512]{1,0:T(8,128)(2,1)}, u32[]{:S(2)}, u32[]{:S(2)}) collective-permute-start(bf16[64,512]{1,0:T(8,128)(2,1)} %bitcast.7.refs_5_), channel_id=1, source_target_pairs={{0,2},{1,3},{2,0},{3,1},{4,6},{5,7},{6,4},{7,5},{8,10},{9,11},{10,... | collective-permute-start | bytes 196616 | tf_op jit(solution)/shard_map/ppermute | solution.py:175
  23.5 16.9 %collective-permute-start.11 = (bf16[64,512]{1,0:T(8,128)(2,1)}, bf16[64,512]{1,0:T(8,128)(2,1)}, u32[]{:S(2)}, u32[]{:S(2)}) collective-permute-start(bf16[64,512]{1,0:T(8,128)(2,1)} %bitcast.7.refs_5_), channel_id=1, source_target_pairs={{0,4},{1,5},{2,6},{3,7},{4,0},{5,1},{6,2},{7,3},{8,12},{9,13},{10,... | collective-permute-start | bytes 196616 | tf_op jit(solution)/shard_map/ppermute | solution.py:175
  26.4 7.2 %collective-permute-start.5 = (f32[64,512]{1,0:T(8,128)S(1)}, f32[64,512]{1,0:T(8,128)S(1)}, u32[]{:S(2)}, u32[]{:S(2)}) collective-permute-start(f32[64,512]{1,0:T(8,128)S(1)} %fusion.14), channel_id=1, source_target_pairs={{0,24},{8,16},{16,8},{24,0},{1,25},{9,17},{17,9},{25,1},{2,26},{10... | collective-permute-start | bytes 393224 | tf_op jit(solution)/shard_map/ppermute | solution.py:175
  33.6 7.0 %collective-permute-start.12 = (bf16[64,512]{1,0:T(8,128)(2,1)}, bf16[64,512]{1,0:T(8,128)(2,1)S(1)}, u32[]{:S(2)}, u32[]{:S(2)}) collective-permute-start(bf16[64,512]{1,0:T(8,128)(2,1)} %bitcast.7.refs_5_), channel_id=1, source_target_pairs={{0,6},{1,7},{2,4},{3,5},{4,2},{5,3},{6,0},{7,1},{8,14},{9,15},{10,... | collective-permute-start | bytes 196616 | tf_op jit(solution)/shard_map/ppermute | solution.py:175
  36.4 6.5 %collective-permute-start.7 = (bf16[64,512]{1,0:T(8,128)(2,1)S(1)}, bf16[64,512]{1,0:T(8,128)(2,1)S(1)}, u32[]{:S(2)}, u32[]{:S(2)}) collective-permute-start(bf16[64,512]{1,0:T(8,128)(2,1)S(1)} %fusion.5.refs_0_), channel_id=1, source_target_pairs={{0,4},{1,5},{2,6},{3,7},{4,0},{5,1},{6,2},{7,3},{8,12},{9,13},{10,... | collective-permute-start | bytes 196616 | tf_op jit(solution)/shard_map/ppermute | solution.py:175
  41.5 7.5 %collective-permute-start.13 = (bf16[256,512]{1,0:T(8,128)(2,1)S(1)}, bf16[256,512]{1,0:T(8,128)(2,1)}, u32[]{:S(2)}, u32[]{:S(2)}) collective-permute-start(bf16[256,512]{1,0:T(8,128)(2,1)S(1)} %pad_maximum_fusion.1), channel_id=1, source_target_pairs={{0,1},{1,0},{2,3},{3,2},{4,5},{5,4},{6,7},{7,6},{8,9},{9,8},{10,11... | collective-permute-start | bytes 786440 | tf_op jit(solution)/shard_map/ppermute | solution.py:175
  46.2 19.3 %collective-permute-start.14 = (bf16[1280,256]{1,0:T(8,128)(2,1)S(1)}, bf16[1280,256]{1,0:T(8,128)(2,1)S(1)}, u32[]{:S(2)}, u32[]{:S(2)}) collective-permute-start(bf16[1280,256]{1,0:T(8,128)(2,1)S(1)} %constant_dynamic-slice_fusion.4), channel_id=1, source_target_pairs={{0,8},{8,0},{16,24},{24,16},{1,9},{9,1},{17,25},{25,17},{2,10},{10... | collective-permute-start | bytes 1966088 | tf_op jit(solution)/shard_map/ppermute | solution.py:175
  46.9 18.6 %collective-permute-start.15 = (bf16[1280,256]{1,0:T(8,128)(2,1)S(1)}, bf16[1280,256]{1,0:T(8,128)(2,1)S(1)}, u32[]{:S(2)}, u32[]{:S(2)}) collective-permute-start(bf16[1280,256]{1,0:T(8,128)(2,1)S(1)} %constant_dynamic-slice_fusion.4), channel_id=1, source_target_pairs={{0,16},{8,24},{16,0},{24,8},{1,17},{9,25},{17,1},{25,9},{2,18},{10... | collective-permute-start | bytes 1966088 | tf_op jit(solution)/shard_map/ppermute | solution.py:175
  49.0 16.4 %collective-permute-start.16 = (bf16[320,256]{1,0:T(8,128)(2,1)S(1)}, bf16[320,256]{1,0:T(8,128)(2,1)S(1)}, u32[]{:S(2)}, u32[]{:S(2)}) collective-permute-start(bf16[320,256]{1,0:T(8,128)(2,1)S(1)} %get-tuple-element.114), channel_id=1, source_target_pairs={{0,2},{1,3},{2,0},{3,1},{4,6},{5,7},{6,4},{7,5},{8,10},{9,11},{10,... | collective-permute-start | bytes 491528 | tf_op jit(solution)/shard_map/ppermute | solution.py:175
  49.0 16.4 %collective-permute-start.17 = (bf16[320,256]{1,0:T(8,128)(2,1)S(1)}, bf16[320,256]{1,0:T(8,128)(2,1)S(1)}, u32[]{:S(2)}, u32[]{:S(2)}) collective-permute-start(bf16[320,256]{1,0:T(8,128)(2,1)S(1)} %get-tuple-element.113), channel_id=1, source_target_pairs={{0,4},{1,5},{2,6},{3,7},{4,0},{5,1},{6,2},{7,3},{8,12},{9,13},{10,... | collective-permute-start | bytes 491528 | tf_op jit(solution)/shard_map/ppermute | solution.py:175
  50.3 15.1 %collective-permute-start.18 = (bf16[320,256]{1,0:T(8,128)(2,1)S(1)}, bf16[320,256]{1,0:T(8,128)(2,1)S(1)}, u32[]{:S(2)}, u32[]{:S(2)}) collective-permute-start(bf16[320,256]{1,0:T(8,128)(2,1)S(1)} %get-tuple-element.112), channel_id=1, source_target_pairs={{0,6},{1,7},{2,4},{3,5},{4,2},{5,3},{6,0},{7,1},{8,14},{9,15},{10,... | collective-permute-start | bytes 491528 | tf_op jit(solution)/shard_map/ppermute | solution.py:175
  66.2 19.6 %collective-permute-start.23 = (bf16[1280,256]{1,0:T(8,128)(2,1)S(1)}, bf16[1280,256]{1,0:T(8,128)(2,1)S(1)}, u32[]{:S(2)}, u32[]{:S(2)}) collective-permute-start(bf16[1280,256]{1,0:T(8,128)(2,1)S(1)} %copy-done.9), channel_id=1, source_target_pairs={{0,24},{8,16},{16,8},{24,0},{1,25},{9,17},{17,9},{25,1},{2,26},{10... | collective-permute-start | bytes 1966088 | tf_op jit(solution)/shard_map/ppermute | solution.py:175
  69.4 16.2 %collective-permute-start.22 = (f32[2,64,256]{2,1,0:T(8,128)S(1)}, f32[2,64,256]{2,1,0:T(8,128)S(1)}, u32[]{:S(2)}, u32[]{:S(2)}) collective-permute-start(f32[2,64,256]{2,1,0:T(8,128)S(1)} %get-tuple-element.121), channel_id=1, source_target_pairs={{0,6},{1,7},{2,4},{3,5},{4,2},{5,3},{6,0},{7,1},{8,14},{9,15},{10,... | collective-permute-start | bytes 393224 | tf_op jit(solution)/shard_map/ppermute | solution.py:175
  70.5 15.2 %collective-permute-start.21 = (f32[2,64,256]{2,1,0:T(8,128)S(1)}, f32[2,64,256]{2,1,0:T(8,128)S(1)}, u32[]{:S(2)}, u32[]{:S(2)}) collective-permute-start(f32[2,64,256]{2,1,0:T(8,128)S(1)} %get-tuple-element.122), channel_id=1, source_target_pairs={{0,4},{1,5},{2,6},{3,7},{4,0},{5,1},{6,2},{7,3},{8,12},{9,13},{10,... | collective-permute-start | bytes 393224 | tf_op jit(solution)/shard_map/ppermute | solution.py:175
  72.1 13.6 %collective-permute-start.20 = (f32[2,64,256]{2,1,0:T(8,128)S(1)}, f32[2,64,256]{2,1,0:T(8,128)S(1)}, u32[]{:S(2)}, u32[]{:S(2)}) collective-permute-start(f32[2,64,256]{2,1,0:T(8,128)S(1)} %get-tuple-element.120), channel_id=1, source_target_pairs={{0,2},{1,3},{2,0},{3,1},{4,6},{5,7},{6,4},{7,5},{8,10},{9,11},{10,... | collective-permute-start | bytes 393224 | tf_op jit(solution)/shard_map/ppermute | solution.py:175
  85.8 7.2 %collective-permute-start.28 = (f32[1,256,256]{2,1,0:T(8,128)}, f32[1,256,256]{2,1,0:T(8,128)S(1)}, u32[]{:S(2)}, u32[]{:S(2)}) collective-permute-start(f32[1,256,256]{2,1,0:T(8,128)} %get-tuple-element.84), channel_id=1, source_target_pairs={{0,1},{1,0},{2,3},{3,2},{4,5},{5,4},{6,7},{7,6},{8,9},{9,8},{10,11... | collective-permute-start | bytes 786440 | tf_op jit(solution)/shard_map/ppermute | solution.py:175
  88.6 6.9 %collective-permute-start.27 = (f32[1,64,256]{2,1,0:T(8,128)S(1)}, f32[1,64,256]{2,1,0:T(8,128)S(1)}, u32[]{:S(2)}, u32[]{:S(2)}) collective-permute-start(f32[1,64,256]{2,1,0:T(8,128)S(1)} %get-tuple-element.127), channel_id=1, source_target_pairs={{0,6},{1,7},{2,4},{3,5},{4,2},{5,3},{6,0},{7,1},{8,14},{9,15},{10,... | collective-permute-start | bytes 196616 | tf_op jit(solution)/shard_map/ppermute | solution.py:175
  89.6 7.6 %collective-permute-start.26 = (f32[1,64,256]{2,1,0:T(8,128)S(1)}, f32[1,64,256]{2,1,0:T(8,128)S(1)}, u32[]{:S(2)}, u32[]{:S(2)}) collective-permute-start(f32[1,64,256]{2,1,0:T(8,128)S(1)} %get-tuple-element.128), channel_id=1, source_target_pairs={{0,4},{1,5},{2,6},{3,7},{4,0},{5,1},{6,2},{7,3},{8,12},{9,13},{10,... | collective-permute-start | bytes 196616 | tf_op jit(solution)/shard_map/ppermute | solution.py:175
  90.4 6.8 %collective-permute-start.25 = (f32[1,64,256]{2,1,0:T(8,128)S(1)}, f32[1,64,256]{2,1,0:T(8,128)S(1)}, u32[]{:S(2)}, u32[]{:S(2)}) collective-permute-start(f32[1,64,256]{2,1,0:T(8,128)S(1)} %get-tuple-element.126), channel_id=1, source_target_pairs={{0,2},{1,3},{2,0},{3,1},{4,6},{5,7},{6,4},{7,5},{8,10},{9,11},{10,... | collective-permute-start | bytes 196616 | tf_op jit(solution)/shard_map/ppermute | solution.py:175
  98.0 8.2 %collective-permute-start.30 = (bf16[64,512]{1,0:T(8,128)(2,1)S(1)}, bf16[64,512]{1,0:T(8,128)(2,1)S(1)}, u32[]{:S(2)}, u32[]{:S(2)}) collective-permute-start(bf16[64,512]{1,0:T(8,128)(2,1)S(1)} %fusion.2.grad_ref), channel_id=1, source_target_pairs={{0,4},{1,5},{2,6},{3,7},{4,0},{5,1},{6,2},{7,3},{8,12},{9,13},{10,... | collective-permute-start | bytes 196616 | tf_op jit(solution)/shard_map/ppermute | solution.py:175
  99.7 6.5 %collective-permute-start.31 = (bf16[64,512]{1,0:T(8,128)(2,1)S(1)}, bf16[64,512]{1,0:T(8,128)(2,1)S(1)}, u32[]{:S(2)}, u32[]{:S(2)}) collective-permute-start(bf16[64,512]{1,0:T(8,128)(2,1)S(1)} %fusion.2.grad_ref), channel_id=1, source_target_pairs={{0,6},{1,7},{2,4},{3,5},{4,2},{5,3},{6,0},{7,1},{8,14},{9,15},{10,... | collective-permute-start | bytes 196616 | tf_op jit(solution)/shard_map/ppermute | solution.py:175
  102.3 7.0 %collective-permute-start.33 = (bf16[1280,256]{1,0:T(8,128)(2,1)S(1)}, bf16[1280,256]{1,0:T(8,128)(2,1)S(1)}, u32[]{:S(2)}, u32[]{:S(2)}) collective-permute-start(bf16[1280,256]{1,0:T(8,128)(2,1)S(1)} %collective-permute-done.15.refs_1_), channel_id=1, source_target_pairs={{0,1},{1,0},{2,3},{3,2},{4,5},{5,4},{6,7},{7,6},{8,9},{9,8},{10,11... | collective-permute-start | bytes 1966088 | tf_op jit(solution)/shard_map/ppermute | solution.py:175
  102.3 8.2 %collective-permute-start.34 = (bf16[1280,256]{1,0:T(8,128)(2,1)S(1)}, bf16[1280,256]{1,0:T(8,128)(2,1)S(1)}, u32[]{:S(2)}, u32[]{:S(2)}) collective-permute-start(bf16[1280,256]{1,0:T(8,128)(2,1)S(1)} %collective-permute-done.23.refs_2_), channel_id=1, source_target_pairs={{0,1},{1,0},{2,3},{3,2},{4,5},{5,4},{6,7},{7,6},{8,9},{9,8},{10,11... | collective-permute-start | bytes 1966088 | tf_op jit(solution)/shard_map/ppermute | solution.py:175
  106.9 13.1 %collective-permute-start.35 = (bf16[4,64,512]{2,1,0:T(8,128)(2,1)S(1)}, bf16[4,64,512]{2,1,0:T(8,128)(2,1)S(1)}, u32[]{:S(2)}, u32[]{:S(2)}) collective-permute-start(bf16[4,64,512]{2,1,0:T(8,128)(2,1)S(1)} %pad_maximum_fusion.2.refs_4_), channel_id=1, source_target_pairs={{0,8},{8,0},{16,24},{24,16},{1,9},{9,1},{17,25},{25,17},{2,10},{10... | collective-permute-start | bytes 786440 | tf_op jit(solution)/shard_map/ppermute | solution.py:175
  107.7 14.0 %collective-permute-start.36 = (bf16[4,64,512]{2,1,0:T(8,128)(2,1)S(1)}, bf16[4,64,512]{2,1,0:T(8,128)(2,1)S(1)}, u32[]{:S(2)}, u32[]{:S(2)}) collective-permute-start(bf16[4,64,512]{2,1,0:T(8,128)(2,1)S(1)} %pad_maximum_fusion.2.refs_4_), channel_id=1, source_target_pairs={{0,16},{8,24},{16,0},{24,8},{1,17},{9,25},{17,1},{25,9},{2,18},{10... | collective-permute-start | bytes 786440 | tf_op jit(solution)/shard_map/ppermute | solution.py:175
  109.3 12.4 %collective-permute-start.37 = (bf16[4,64,512]{2,1,0:T(8,128)(2,1)S(1)}, bf16[4,64,512]{2,1,0:T(8,128)(2,1)S(1)}, u32[]{:S(2)}, u32[]{:S(2)}) collective-permute-start(bf16[4,64,512]{2,1,0:T(8,128)(2,1)S(1)} %pad_maximum_fusion.2.refs_4_), channel_id=1, source_target_pairs={{0,24},{8,16},{16,8},{24,0},{1,25},{9,17},{17,9},{25,1},{2,26},{10... | collective-permute-start | bytes 786440 | tf_op jit(solution)/shard_map/ppermute | solution.py:175
  117.2 8.7 %collective-permute-start.40 = (f32[1,64,256]{2,1,0:T(8,128)S(1)}, f32[1,64,256]{2,1,0:T(8,128)S(1)}, u32[]{:S(2)}, u32[]{:S(2)}) collective-permute-start(f32[1,64,256]{2,1,0:T(8,128)S(1)} %get-tuple-element.124), channel_id=1, source_target_pairs={{0,6},{1,7},{2,4},{3,5},{4,2},{5,3},{6,0},{7,1},{8,14},{9,15},{10,... | collective-permute-start | bytes 196616 | tf_op jit(solution)/shard_map/ppermute | solution.py:175
  119.5 6.7 %collective-permute-start.39 = (f32[1,64,256]{2,1,0:T(8,128)S(1)}, f32[1,64,256]{2,1,0:T(8,128)S(1)}, u32[]{:S(2)}, u32[]{:S(2)}) collective-permute-start(f32[1,64,256]{2,1,0:T(8,128)S(1)} %get-tuple-element.125), channel_id=1, source_target_pairs={{0,4},{1,5},{2,6},{3,7},{4,0},{5,1},{6,2},{7,3},{8,12},{9,13},{10,... | collective-permute-start | bytes 196616 | tf_op jit(solution)/shard_map/ppermute | solution.py:175
  120.0 6.2 %collective-permute-start.38 = (f32[1,64,256]{2,1,0:T(8,128)S(1)}, f32[1,64,256]{2,1,0:T(8,128)S(1)}, u32[]{:S(2)}, u32[]{:S(2)}) collective-permute-start(f32[1,64,256]{2,1,0:T(8,128)S(1)} %get-tuple-element.123), channel_id=1, source_target_pairs={{0,2},{1,3},{2,0},{3,1},{4,6},{5,7},{6,4},{7,5},{8,10},{9,11},{10,... | collective-permute-start | bytes 196616 | tf_op jit(solution)/shard_map/ppermute | solution.py:175
  (35 other events, 277.5 us)

commit v6 on v5

--- a/solution.py
+++ b/solution.py
@@ -32,9 +32,9 @@
     return jnp.concatenate([ref[:, i * head_dim : (i + 1) * head_dim] for i in range(heads)], axis=0)
 
 
-def attend_kernel(pieces, chained, length_ref, query_ref, upstream_ref, key_ref, value_ref, *refs):
+def attend_kernel(pieces, length_ref, query_ref, upstream_ref, key_ref, value_ref, *refs):
     key_pieces, value_pieces = refs[:pieces], refs[pieces : 2 * pieces]
-    query_grad_ref, key_grad_ref, value_grad_ref, *sum_refs = refs[2 * pieces + 3 * chained :]
+    query_grad_ref, key_grad_ref, value_grad_ref, *sum_refs = refs[2 * pieces :]
     rows = query_ref.shape[0]
     own_len, head_dim = key_ref.shape
     heads = query_ref.shape[1] // head_dim
@@ -69,45 +69,81 @@
     key_grad = dot(queries.T, dscore).T
     value_grad = dot(upstream.T, weights).T
     half = prompt_len // 2
-    per_array = len(sum_refs) // 2
     for i, grad in enumerate((key_grad, value_grad)):
-        near_ref, far_ref = sum_refs[:2] if per_array == 1 else sum_refs[2 * i : 2 * i + 2]
-        near_ref[i % (3 - per_array)], far_ref[i % (3 - per_array)] = grad[:half], grad[half:prompt_len]
+        sum_refs[2 * i][...], sum_refs[2 * i + 1][...] = grad[:half], grad[half:prompt_len]
     key_grad_ref[...] = key_grad[prompt_len:].astype(BF16)
     value_grad_ref[...] = value_grad[prompt_len:].astype(BF16)
 
 
-def attend(length, queries, upstream, key_pieces, value_pieces, keys, values, head_dim, first, count, earlier):
+def attend(length, queries, upstream, key_pieces, value_pieces, keys, values, head_dim):
     rows, width = queries.shape
     kv_width = keys.shape[1]
     kv_heads = kv_width // head_dim
     prompt_len = sum(piece.shape[0] for piece in key_pieces)
 
-    def block(rows, columns, offset=first):
-        return pl.BlockSpec((rows, columns), lambda i: (0, i + offset))
+    def block(rows, columns):
+        return pl.BlockSpec((rows, columns), lambda i: (0, i))
 
     query_block, own_block = block(rows, width // kv_heads), block(rows, head_dim)
     piece_blocks = [block(piece.shape[0], head_dim) for piece in key_pieces]
-    kinds, arrays = (1, 2) if earlier else (2, 1)
-    half = jax.ShapeDtypeStruct((kinds, prompt_len // 2, count * head_dim), F32)
-    half_block = pl.BlockSpec((kinds, prompt_len // 2, head_dim), lambda i: (0, 0, i))
+    half = jax.ShapeDtypeStruct((prompt_len // 2, kv_width), F32)
     own = jax.ShapeDtypeStruct((rows, kv_width), BF16)
-    before = 5 + 2 * len(key_pieces)
-    macs = 5 * rows * width * (prompt_len + rows) * count // kv_heads
-    return pl.pallas_call(
-        partial(attend_kernel, len(key_pieces), bool(earlier)),
-        grid=(count,),
+    return pl.pallas_call(
+        partial(attend_kernel, len(key_pieces)),
+        grid=(kv_heads,),
         in_specs=[
             pl.BlockSpec(memory_space=pltpu.SMEM), query_block, query_block, own_block, own_block,
-            *piece_blocks, *piece_blocks, *[pl.BlockSpec(memory_space=pl.ANY) for _ in earlier],
+            *piece_blocks, *piece_blocks,
         ],
-        out_specs=[query_block, own_block, own_block] + [half_block] * (2 * arrays),
-        out_shape=[jax.ShapeDtypeStruct((rows, width), BF16), own, own] + [half] * (2 * arrays),
-        input_output_aliases={before + i: i for i in range(len(earlier))},
-        compiler_params=PARAMS,
-        cost_estimate=cost(2 * macs, 5 * 10**6),
+        out_specs=[query_block, own_block, own_block] + [block(prompt_len // 2, head_dim)] * 4,
+        out_shape=[jax.ShapeDtypeStruct((rows, width), BF16), own, own] + [half] * 4,
+        compiler_params=PARAMS,
+        cost_estimate=cost(10 * rows * width * (prompt_len + rows), 10**7),
         name="attend",
-    )(length, queries, upstream, keys, values, *key_pieces, *value_pieces, *earlier)
+    )(length, queries, upstream, keys, values, *key_pieces, *value_pieces)
+
+
+def split_kernel(place_ref, hidden_ref, *piece_refs):
+    depth = piece_refs[0].shape[1]
+    for k, piece_ref in enumerate(piece_refs):
+        start = pl.multiple_of((place_ref[0] ^ k) * depth, depth)
+        piece_ref[...] = hidden_ref[:, pl.ds(start, depth)]
+
+
+def split_pass(place, hidden, groups):
+    tokens, width = hidden.shape
+    return pl.pallas_call(
+        split_kernel,
+        in_specs=[pl.BlockSpec(memory_space=pltpu.SMEM), pl.BlockSpec(memory_space=pltpu.VMEM)],
+        out_specs=[pl.BlockSpec(memory_space=pltpu.VMEM)] * groups,
+        out_shape=[jax.ShapeDtypeStruct((tokens, width // groups), BF16)] * groups,
+        compiler_params=PARAMS,
+        name="split_hidden",
+    )(place, hidden)
+
+
+def turn_kernel(groups, place_ref, *refs):
+    columns, piece_refs, turned = refs[:groups], refs[groups:-1], refs[-1]
+    rows = piece_refs[0].shape[0]
+    turned[...] = jnp.concatenate([ref[...] for ref in columns], axis=0).T
+    for p, piece_ref in enumerate(piece_refs):
+        start = pl.multiple_of((place_ref[2] ^ p) * rows, 16)
+        piece_ref[...] = turned[pl.ds(start, rows)]
+
+
+def turn_pass(place, columns, chips):
+    tokens, depth = columns[0].shape
+    every = tokens * len(columns)
+    return pl.pallas_call(
+        partial(turn_kernel, len(columns)),
+        in_specs=[pl.BlockSpec(memory_space=pltpu.SMEM)]
+        + [pl.BlockSpec(memory_space=pltpu.VMEM)] * len(columns),
+        out_specs=[pl.BlockSpec(memory_space=pltpu.VMEM)] * chips,
+        out_shape=[jax.ShapeDtypeStruct((depth // chips, every), BF16)] * chips,
+        scratch_shapes=[pltpu.VMEM((depth, every), BF16)],
+        compiler_params=PARAMS,
+        name="turn_hidden",
+    )(place, *columns)
 
 
 def hidden_kernel(groups, place_ref, grad_ref, own_ref, *refs):
@@ -142,33 +178,33 @@
     )(place, key_pre_grad, own, *near, *far)
 
 
-def weight_kernel(chips, place_ref, *refs):
-    taken, blocks = refs[:chips], refs[chips:-3]
+def weight_kernel(chips, groups, place_ref, *refs):
+    taken, first, rest = refs[:chips], refs[chips : chips + groups], refs[chips + groups : -3]
     mine_ref, other_ref, product = refs[-3:]
     half = mine_ref.shape[0]
     core = place_ref[1]
     columns = jnp.concatenate([ref[...] for ref in taken], axis=1)
-    grads = jnp.concatenate([ref[p] for p in range(chips) for ref in blocks], axis=0)
-    product[...] = dot(columns, grads)
+    grads = [ref[...] for ref in first] + [ref[p] for p in range(chips - 1) for ref in rest]
+    product[...] = dot(columns, jnp.concatenate(grads, axis=0))
     mine_ref[...] = product[pl.ds(pl.multiple_of(core * half, 8), half)]
     other_ref[...] = product[pl.ds(pl.multiple_of((1 - core) * half, 8), half)]
 
 
-def weight_pass(place, taken, blocks):
+def weight_pass(place, taken, first, rest):
     rows = taken[0].shape[0]
-    kv_width = blocks[0].shape[-1]
+    kv_width = first[0].shape[-1]
     out = jax.ShapeDtypeStruct((rows // 2, kv_width), F32)
     return pl.pallas_call(
-        partial(weight_kernel, len(taken)),
+        partial(weight_kernel, len(taken), len(first)),
         in_specs=[pl.BlockSpec(memory_space=pltpu.SMEM)]
-        + [pl.BlockSpec(memory_space=pltpu.VMEM)] * (len(taken) + len(blocks)),
+        + [pl.BlockSpec(memory_space=pltpu.VMEM)] * (len(taken) + len(first) + len(rest)),
         out_specs=[pl.BlockSpec(memory_space=pltpu.VMEM)] * 2,
         out_shape=[out, out],
         scratch_shapes=[pltpu.VMEM((rows, kv_width), F32)],
         compiler_params=PARAMS,
         cost_estimate=cost(rows * kv_width * taken[0].shape[1] * len(taken), 3 * 10**6),
         name="weight_grad",
-    )(place, *taken, *blocks)
+    )(place, *taken, *first, *rest)
 
 
 def swap(array, axis, size, distance):
@@ -192,10 +228,11 @@
 
 
 def chip_sum(near, size):
-    rows = near.shape[1] // (size // 2)
-    total = near[:, :rows]
+    rows = near.shape[0] // (size // 2)
+    total = near[:rows]
     for p in range(1, size // 2):
-        total = total + swap(near[:, p * rows : (p + 1) * rows], "resp", size, 2 * p)
+        piece = near[p * rows : (p + 1) * rows].astype(BF16)
+        total = total + swap(piece, "resp", size, 2 * p).astype(F32)
     return total
 
 
@@ -208,78 +245,65 @@
     depth, kv_width = key_matrix.shape
     head_dim = key_gain.shape[0]
     group, resp = lax.axis_index("group"), lax.axis_index("resp")
-    core = resp % 2
-    place = jnp.stack([group, core]).astype(jnp.int32)
-
-    pieces = [
-        lax.dynamic_slice(hidden, (0, (group ^ k) * depth), (tokens, depth)) for k in range(groups)
-    ]
+    core, chip, chips = resp % 2, resp // 2, responses // 2
+    place = jnp.stack([group, core, chip]).astype(jnp.int32)
+
+    pieces = split_pass(place, hidden, groups)
     columns = [swap(piece, "group", groups, k) if k else piece for k, piece in enumerate(pieces)]
-    prompt_value, columns[1] = together(prompt_token_value[0], columns[1])
     partials = [dot(piece, key_matrix) for piece in columns]
+    prompt_value, partials[0] = together(prompt_token_value[0], partials[0])
     value_near = spread_near(prompt_value, responses)
     key_pre = partials[0]
     for k in range(1, groups):
         key_pre = key_pre + swap(partials[k], "group", groups, k)
-    value_pieces = value_near + spread_far(value_near, responses)
+    value_far = spread_far(value_near, responses)
 
     half_width = kv_width // 2
     half_weight = lax.dynamic_slice(key_matrix, (0, core * half_width), (depth, half_width))
-    half_weight, key_pre = together(half_weight, key_pre)
+    half_weight, key_pre, *value_far = together(half_weight, key_pre, *value_far)
+    value_pieces = value_near + value_far
     prompt_key = norm_keys(key_pre, key_gain).astype(BF16)
     key_near = spread_near(prompt_key, responses)
     weight_near = [swap(half_weight, "group", groups, k) for k in range(1, groups)]
 
-    chips = responses // 2
-    chip_rows = depth // chips
-    hidden_t = jnp.concatenate(columns, axis=0).T
-    hidden_t, *key_near = together(hidden_t, *key_near)
+    taken = turn_pass(place, columns, chips)
+    count = len(taken)
+    both = together(*taken, *key_near)
+    taken, key_near = both[:count], both[count:]
     key_pieces = key_near + spread_far(key_near, responses)
-    taken = []
-    for k in range(0, responses, 2):
-        start = ((resp ^ k) // 2) * chip_rows
-        piece = lax.dynamic_slice(hidden_t, (start, 0), (chip_rows, hidden_t.shape[1]))
-        taken.append(swap(piece, "resp", responses, k) if k else piece)
-
-    rest = (
-        resp_query[0, 0], grad_out[0, 0], key_pieces, value_pieces,
+    taken[1:] = [swap(taken[p], "resp", responses, 2 * p) for p in range(1, chips)]
+
+    query_grad, key_grad, value_grad, key_sums, far, value_sums, value_far = attend(
+        resp_length, resp_query[0, 0], grad_out[0, 0], key_pieces, value_pieces,
         resp_key[0, 0], response_value[0, 0], head_dim,
     )
-    count = kv_width // head_dim // 2
-    width = count * head_dim
-    *earlier, near, far = attend(resp_length, *rest, 0, count, [])
-    near, far, *rest_taken = together(near, far, *weight_near[:-1], *taken)
-    weight_near[:-1], taken = rest_taken[: groups - 2], rest_taken[groups - 2 :]
-    near = pair_sum(near, far, responses)
-    length, near = together(resp_length, near)
-    sums0 = chip_sum(near, responses)
-    *outputs, near, far, value_near, value_far = attend(length, *rest, count, count, earlier)
-    query_grad, key_grad, value_grad = outputs
-    sums0, near, far, weight_near[-1] = together(sums0, near, far, weight_near[-1])
-    sums1 = chip_sum(pair_sum(near, far, responses), responses)
-    value_near = pair_sum(value_near, value_far, responses)
+    key_sums, far, *rest = together(key_sums, far, *weight_near[:-1], *taken)
+    weight_near[:-1], taken = rest[: groups - 2], rest[groups - 2 :]
+    key_sums = chip_sum(pair_sum(key_sums, far, responses), responses)
+    value_sums = pair_sum(value_sums, value_far, responses)
+    weight_far = [swap(piece, "resp", responses, 1) for piece in weight_near[:-1]]
+    key_sums, value_sums, weight_near[-1], *weight_far = together(
+        key_sums, value_sums, weight_near[-1], *weight_far
+    )
     _, pullback = jax.vjp(lambda values: norm_keys(values, key_gain), key_pre)
-    key_pre_grad = pullback(jnp.concatenate([sums0[0], sums1[0]], axis=1))[0].astype(BF16)
-
-    key_pre_grad, value_near = together(key_pre_grad, value_near)
-
-    grads = spread_near(key_pre_grad, responses)
-    weight_near[0], *grads = together(weight_near[0], *grads)
-    block = jnp.stack(grads, axis=0)
+    key_pre_grad = pullback(key_sums)[0].astype(BF16)
+
+    first = [key_pre_grad] + [swap(key_pre_grad, "group", groups, k) for k in range(1, groups)]
+    grads = spread_near(key_pre_grad, responses)[1:]
+    weight_far.append(swap(weight_near[-1], "resp", responses, 1))
+    *first, weight_far[-1], block = together(*first, weight_far[-1], jnp.stack(grads, axis=0))
     blocks = [block] + [swap(block, "group", groups, k) for k in range(1, groups)]
-    weight_far = [swap(piece, "resp", responses, 1) for piece in weight_near]
-    grad_hidden = hidden_pass(place, grads[0], key_matrix, weight_near, weight_far)
-    grad_hidden, value_near = together(grad_hidden, value_near)
-    values1 = chip_sum(value_near, responses)
+    grad_hidden = hidden_pass(place, first[0], key_matrix, weight_near, weight_far)
+    grad_hidden, value_sums = together(grad_hidden, value_sums)
+    value_sums = chip_sum(value_sums, responses)
     grad_hidden, *blocks = together(grad_hidden, *blocks)
-    mine, other = weight_pass(place, taken, blocks)
-    other, values1 = together(other, values1)
+    mine, other = weight_pass(place, taken, first, blocks)
+    other, value_sums = together(other, value_sums)
     grad_weight = mine + swap(other, "resp", responses, 1)
-    prompt_value_grad = jnp.concatenate([sums0[1], values1[0]], axis=1)
     return (
         grad_hidden[None],
         grad_weight,
-        prompt_value_grad.astype(BF16)[None],
+        value_sums.astype(BF16)[None],
         query_grad[None, None],
         key_grad[None, None],
         value_grad[None, None],

time: 130 us -> 128 us (0.985)
  local copies, waits for them, and re-layouts: 9.47 us -> 3.93 us
  waiting for transfers between devices: 29.7 us -> 32.7 us
  other arithmetic: 7.75 us -> 4.77 us
  Pallas kernels: 31.6 us -> 33.6 us
    dynamic_slice x6 -> x0, local copies, waits for them, and re-layouts: 4.85 us -> none  [the longest x5 4.13 us: shards(): lax.dynamic_slice(hidden, (0, (group ^ k) * depth), (tokens, depth))]
    ppermute x42 -> x41, waiting for transfers between devices: 29.7 us -> 32.7 us  [swap(): return lax.ppermute(array, axis, [(i, i ^ distance) for i in range(size)])]
    add x3 -> x1, other arithmetic: 2.13 us -> 0.08 us  [pair_sum(): return near + swap(far, 'resp', size, 1)]
    pallas_call x3 -> x4, Pallas kernels: 26.6 us -> 28.6 us  [the longest x1 21.5 us: attend(): pl.pallas_call(partial(attend_kernel, len(key_pieces)), grid=(kv_heads,),...]
    concatenate x2, other arithmetic: 1.67 us -> 0.04 us  [spread_far(): return [swap(jnp.concatenate(near, axis=0), 'resp', size, 1)]]
    unnamed x50 -> x68, local copies, waits for them, and re-layouts: 3.77 us -> 3.15 us
    ppermute x42 -> x41, starting transfers between devices: 47.5 us -> 47.8 us  [swap(): return lax.ppermute(array, axis, [(i, i ^ distance) for i in range(size)])]
  transfers between devices with their start and end apart: 42 -> 41, of which waited for: 16 -> 17; matrix products, arithmetic and copies ran while one was open for 9% -> 3% of each run, Pallas kernels for 24% -> 19%
where the time goes in v6:
time: 128 us; the launch traced here: 127 us
  starting transfers between devices  47.8 us (37%)
  Pallas kernels  33.6 us (26%)
  waiting for transfers between devices  32.7 us (26%)
  other arithmetic  4.77 us (4%)
  local copies, waits for them, and re-layouts  3.93 us (3%)
  matrix products  2.74 us (2%)
  between operations  1.88 us (1%)
    ppermute x41, starting transfers between devices, swap(): return lax.ppermute(array, axis, [(i, i ^ distance) for i in range(size)])  47.8 us
    ppermute x41, waiting for transfers between devices, swap(): return lax.ppermute(array, axis, [(i, i ^ distance) for i in range(size)])  32.7 us
    pallas_call x1, Pallas kernels, attend(): pl.pallas_call(partial(attend_kernel, len(key_pieces)), grid=(kv_heads,),...  21.5 us
    pallas_call x1, Pallas kernels, hidden_pass(): pl.pallas_call(partial(hidden_kernel, groups), in_specs=[pl.BlockSpec(mem...  5.03 us
    unnamed x68, local copies, waits for them, and re-layouts  3.15 us
    pallas_call x1, Pallas kernels, weight_pass(): pl.pallas_call(partial(weight_kernel, len(taken), len(first)), in_specs=[...  2.9 us
    dot_general x4, matrix products, dot(): return lax.dot_general(left, right, dims, preferred_element_type=F32)  2.74 us
  transfers between devices with their start and end apart: 41, of which 17 were waited for; matrix products, arithmetic and copies ran while one was open for 3% of the time, Pallas kernels for 19%

profile of v6, /device:TPU:0, one launch (start us, length us, event | category | flops | bytes accessed | tf_op | source)
XLA Modules:
  0.0 127.4 jit_solution(11388836974130627405)
XLA Ops:
  1.3 2.0 %split_hidden.1 = (bf16[64,1280]{1,0:T(8,128)(2,1)}, bf16[64,1280]{1,0:T(8,128)(2,1)}, bf16[64,1280]{1,0:T(8,128)(2,1)}, bf16[64,1280]{1,0:T(8,128)(2,1)}) custom-call(s32[3]{0:T(128)} %pad_add_fusion.place_ref, bf16[64,5120]{1,0:T(8,128)(2,1)} %bitcast.47), custom_call_target="tpu_custom_call" | custom-call | tf_op jit(solution)/shard_map/split_hidden/pallas_call | solution.py:115
  3.3 1.7 %fusion.9 = f32[64,512]{1,0:T(8,128)S(1)} fusion(bf16[64,1280]{1,0:T(8,128)(2,1)} %get-tuple-element.64.refs_0_, bf16[1280,512]{1,0:T(8,128)(2,1)} %own_ref.1), kind=kOutput, calls=%fused_computation.27 | convolution fusion | flops 83886080 | bytes 1605632 | tf_op jit(solution)/shard_map/dot_general | solution.py:23
  5.0 5.1 %collective-permute-start.8 = (bf16[64,512]{1,0:T(8,128)(2,1)S(1)}, bf16[64,512]{1,0:T(8,128)(2,1)S(1)}, u32[]{:S(2)}, u32[]{:S(2)}) collective-permute-start(bf16[64,512]{1,0:T(8,128)(2,1)S(1)} %bitcast.54), channel_id=1, source_target_pairs={{0,6},{1,7},{2,4},{3,5},{4,2},{5,3},{6,0},{7,1},{8,14},{9,15},{10,... | collective-permute-start | bytes 196616 | tf_op jit(solution)/shard_map/ppermute | solution.py:211
  10.8 1.6 %collective-permute-start = (bf16[64,1280]{1,0:T(8,128)(2,1)}, bf16[64,1280]{1,0:T(8,128)(2,1)S(1)}, u32[]{:S(2)}, u32[]{:S(2)}) collective-permute-start(bf16[64,1280]{1,0:T(8,128)(2,1)} %get-tuple-element.65), channel_id=1, source_target_pairs={{0,8},{8,0},{16,24},{24,16},{1,9},{9,1},{17,25},{25,17},{2,10},{10... | collective-permute-start | bytes 491528 | tf_op jit(solution)/shard_map/ppermute | solution.py:211
  12.4 1.5 %collective-permute-start.1 = (bf16[64,1280]{1,0:T(8,128)(2,1)}, bf16[64,1280]{1,0:T(8,128)(2,1)S(1)}, u32[]{:S(2)}, u32[]{:S(2)}) collective-permute-start(bf16[64,1280]{1,0:T(8,128)(2,1)} %get-tuple-element.66), channel_id=1, source_target_pairs={{0,16},{8,24},{16,0},{24,8},{1,17},{9,25},{17,1},{25,9},{2,18},{10... | collective-permute-start | bytes 491528 | tf_op jit(solution)/shard_map/ppermute | solution.py:211
  17.7 2.0 %collective-permute-start.3 = (f32[64,512]{1,0:T(8,128)S(1)}, f32[64,512]{1,0:T(8,128)S(1)}, u32[]{:S(2)}, u32[]{:S(2)}) collective-permute-start(f32[64,512]{1,0:T(8,128)S(1)} %fusion.10), channel_id=1, source_target_pairs={{0,8},{8,0},{16,24},{24,16},{1,9},{9,1},{17,25},{25,17},{2,10},{10... | collective-permute-start | bytes 393224 | tf_op jit(solution)/shard_map/ppermute | solution.py:211
  19.7 1.9 %collective-permute-done.1.refs_2_ = bf16[64,1280]{1,0:T(8,128)(2,1)S(1)} collective-permute-done((bf16[64,1280]{1,0:T(8,128)(2,1)}, bf16[64,1280]{1,0:T(8,128)(2,1)S(1)}, u32[]{:S(2)}, u32[]{:S(2)}) %collective-permute-start.1) | collective-permute-done | bytes 163872 | tf_op jit(solution)/shard_map/ppermute | solution.py:211
  23.7 3.4 %collective-permute-done.4 = f32[64,512]{1,0:T(8,128)S(1)} collective-permute-done((f32[64,512]{1,0:T(8,128)S(1)}, f32[64,512]{1,0:T(8,128)S(1)}, u32[]{:S(2)}, u32[]{:S(2)}) %collective-permute-start.4) | collective-permute-done | bytes 131104 | tf_op jit(solution)/shard_map/ppermute | solution.py:211
  27.0 2.3 %collective-permute-done.5 = f32[64,512]{1,0:T(8,128)S(1)} collective-permute-done((f32[64,512]{1,0:T(8,128)S(1)}, f32[64,512]{1,0:T(8,128)S(1)}, u32[]{:S(2)}, u32[]{:S(2)}) %collective-permute-start.5) | collective-permute-done | bytes 131104 | tf_op jit(solution)/shard_map/ppermute | solution.py:211
  30.0 4.1 %collective-permute-start.12 = (bf16[64,512]{1,0:T(8,128)(2,1)S(1)}, bf16[64,512]{1,0:T(8,128)(2,1)S(1)}, u32[]{:S(2)}, u32[]{:S(2)}) collective-permute-start(bf16[64,512]{1,0:T(8,128)(2,1)S(1)} %fusion.2.refs_0_), channel_id=1, source_target_pairs={{0,6},{1,7},{2,4},{3,5},{4,2},{5,3},{6,0},{7,1},{8,14},{9,15},{10,... | collective-permute-start | bytes 196616 | tf_op jit(solution)/shard_map/ppermute | solution.py:211
  34.8 2.2 %turn_hidden.1 = (bf16[320,256]{1,0:T(8,128)(2,1)}, bf16[320,256]{1,0:T(8,128)(2,1)}, bf16[320,256]{1,0:T(8,128)(2,1)}, bf16[320,256]{1,0:T(8,128)(2,1)}) custom-call(s32[3]{0:T(128)} %pad_add_fusion.place_ref, bf16[64,1280]{1,0:T(8,128)(2,1)} %get-tuple-element.64.refs_0_, bf16[64,1280]{1,0:T(8,128)(2,1)} %copy-done.9, bf16[64,1280]{1,0:T(8,128)(2,1)} %copy-done.10, ...), custom_call_target="tpu_custom_call" | custom-call | tf_op jit(solution)/shard_map/turn_hidden/pallas_call | solution.py:137
  37.0 2.3 %collective-permute-done.11.refs_2_ = bf16[64,512]{1,0:T(8,128)(2,1)S(1)} collective-permute-done((bf16[64,512]{1,0:T(8,128)(2,1)S(1)}, bf16[64,512]{1,0:T(8,128)(2,1)S(1)}, u32[]{:S(2)}, u32[]{:S(2)}) %collective-permute-start.11) | collective-permute-done | bytes 65568 | tf_op jit(solution)/shard_map/ppermute | solution.py:211
  41.4 1.7 %collective-permute-start.17 = (bf16[320,256]{1,0:T(8,128)(2,1)}, bf16[320,256]{1,0:T(8,128)(2,1)S(1)}, u32[]{:S(2)}, u32[]{:S(2)}) collective-permute-start(bf16[320,256]{1,0:T(8,128)(2,1)} %get-tuple-element.85), channel_id=1, source_target_pairs={{0,4},{1,5},{2,6},{3,7},{4,0},{5,1},{6,2},{7,3},{8,12},{9,13},{10,... | collective-permute-start | bytes 491528 | tf_op jit(solution)/shard_map/ppermute | solution.py:211
  43.1 2.2 %collective-permute-start.18 = (bf16[320,256]{1,0:T(8,128)(2,1)}, bf16[320,256]{1,0:T(8,128)(2,1)S(1)}, u32[]{:S(2)}, u32[]{:S(2)}) collective-permute-start(bf16[320,256]{1,0:T(8,128)(2,1)} %get-tuple-element.86), channel_id=1, source_target_pairs={{0,6},{1,7},{2,4},{3,5},{4,2},{5,3},{6,0},{7,1},{8,14},{9,15},{10,... | collective-permute-start | bytes 491528 | tf_op jit(solution)/shard_map/ppermute | solution.py:211
  45.4 21.5 %attend.1 = (bf16[256,4096]{1,0:T(8,128)(2,1)}, bf16[256,512]{1,0:T(8,128)(2,1)}, bf16[256,512]{1,0:T(8,128)(2,1)}, f32[256,512]{1,0:T(8,128)}, f32[256,512]{1,0...) custom-call(s32[1,1]{1,0:T(1,128)S(6)} %copy.26.length_ref, bf16[256,4096]{1,0:T(8,128)(2,1)} %bitcast.58, ...), custom_call_target="tpu_custom_call" | custom-call | flops 16106127360 | bytes 10000000 | tf_op jit(solution)/shard_map/attend/pallas_call | solution.py:91
  67.0 2.8 %collective-permute-start.24 = (bf16[1280,256]{1,0:T(8,128)(2,1)S(1)}, bf16[1280,256]{1,0:T(8,128)(2,1)S(1)}, u32[]{:S(2)}, u32[]{:S(2)}) collective-permute-start(bf16[1280,256]{1,0:T(8,128)(2,1)S(1)} %copy-done.8), channel_id=1, source_target_pairs={{0,24},{8,16},{16,8},{24,0},{1,25},{9,17},{17,9},{25,1},{2,26},{10... | collective-permute-start | bytes 1966088 | tf_op jit(solution)/shard_map/ppermute | solution.py:211
  72.0 2.3 %collective-permute-start.22 = (bf16[64,512]{1,0:T(8,128)(2,1)S(1)}, bf16[64,512]{1,0:T(8,128)(2,1)S(1)}, u32[]{:S(2)}, u32[]{:S(2)}) collective-permute-start(bf16[64,512]{1,0:T(8,128)(2,1)S(1)} %get-tuple-element.128), channel_id=1, source_target_pairs={{0,6},{1,7},{2,4},{3,5},{4,2},{5,3},{6,0},{7,1},{8,14},{9,15},{10,... | collective-permute-start | bytes 196616 | tf_op jit(solution)/shard_map/ppermute | solution.py:211
  74.3 1.8 %collective-permute-done.20 = bf16[64,512]{1,0:T(8,128)(2,1)S(1)} collective-permute-done((bf16[64,512]{1,0:T(8,128)(2,1)S(1)}, bf16[64,512]{1,0:T(8,128)(2,1)S(1)}, u32[]{:S(2)}, u32[]{:S(2)}) %collective-permute-start.20) | collective-permute-done | bytes 65568 | tf_op jit(solution)/shard_map/ppermute | solution.py:211
  78.1 3.5 %collective-permute-done.21 = bf16[64,512]{1,0:T(8,128)(2,1)S(1)} collective-permute-done((bf16[64,512]{1,0:T(8,128)(2,1)S(1)}, bf16[64,512]{1,0:T(8,128)(2,1)S(1)}, u32[]{:S(2)}, u32[]{:S(2)}) %collective-permute-start.21) | collective-permute-done | bytes 65568 | tf_op jit(solution)/shard_map/ppermute | solution.py:211
  81.7 3.4 %collective-permute-done.24.refs_2_ = bf16[1280,256]{1,0:T(8,128)(2,1)S(1)} collective-permute-done((bf16[1280,256]{1,0:T(8,128)(2,1)S(1)}, bf16[1280,256]{1,0:T(8,128)(2,1)S(1)}, u32[]{:S(2)}, u32[]{:S(2)}) %collective-permute-start.24) | collective-permute-done | bytes 655392 | tf_op jit(solution)/shard_map/ppermute | solution.py:211
  86.6 1.7 %collective-permute-start.33 = (bf16[64,512]{1,0:T(8,128)(2,1)S(1)}, bf16[64,512]{1,0:T(8,128)(2,1)S(1)}, u32[]{:S(2)}, u32[]{:S(2)}) collective-permute-start(bf16[64,512]{1,0:T(8,128)(2,1)S(1)} %fusion.grad_ref.refs_4_), channel_id=1, source_target_pairs={{0,6},{1,7},{2,4},{3,5},{4,2},{5,3},{6,0},{7,1},{8,14},{9,15},{10,... | collective-permute-start | bytes 196616 | tf_op jit(solution)/shard_map/ppermute | solution.py:211
  88.5 2.6 %collective-permute-start.31 = (bf16[64,512]{1,0:T(8,128)(2,1)S(1)}, bf16[64,512]{1,0:T(8,128)(2,1)S(1)}, u32[]{:S(2)}, u32[]{:S(2)}) collective-permute-start(bf16[64,512]{1,0:T(8,128)(2,1)S(1)} %fusion.grad_ref.refs_4_), channel_id=1, source_target_pairs={{0,2},{1,3},{2,0},{3,1},{4,6},{5,7},{6,4},{7,5},{8,10},{9,11},{10,... | collective-permute-start | bytes 196616 | tf_op jit(solution)/shard_map/ppermute | solution.py:211
  91.1 2.7 %collective-permute-start.29 = (bf16[64,512]{1,0:T(8,128)(2,1)S(1)}, bf16[64,512]{1,0:T(8,128)(2,1)S(1)}, u32[]{:S(2)}, u32[]{:S(2)}) collective-permute-start(bf16[64,512]{1,0:T(8,128)(2,1)S(1)} %fusion.grad_ref.refs_4_), channel_id=1, source_target_pairs={{0,24},{8,16},{16,8},{24,0},{1,25},{9,17},{17,9},{25,1},{2,26},{10... | collective-permute-start | bytes 196616 | tf_op jit(solution)/shard_map/ppermute | solution.py:211
  98.0 2.0 %collective-permute-done.27.refs_5_ = bf16[64,512]{1,0:T(8,128)(2,1)S(1)} collective-permute-done((bf16[64,512]{1,0:T(8,128)(2,1)S(1)}, bf16[64,512]{1,0:T(8,128)(2,1)S(1)}, u32[]{:S(2)}, u32[]{:S(2)}) %collective-permute-start.27) | collective-permute-done | bytes 65568 | tf_op jit(solution)/shard_map/ppermute | solution.py:211
  100.9 5.0 %hidden_grad.1 = bf16[64,5120]{1,0:T(8,128)(2,1)} custom-call(s32[3]{0:T(128)} %pad_add_fusion.place_ref, bf16[64,512]{1,0:T(8,128)(2,1)} %copy-done.12, bf16[1280,512]{1,0:T(8,128)(2,1)} %own_ref.1, bf16[1280,256]{1,0:T(8,128)(2,1)} %copy-done.3, bf16[1280,256]{1,0:T(8,128)(2,1)} %copy-done.2, bf16[1280,256]{1,0:T(8,128)(2,1)} %copy-done.4, ...), custom_call_target="tpu_custom_call" | custom-call | flops 335544320 | bytes 6000000 | tf_op jit(solution)/shard_map/hidden_grad/pallas_call | solution.py:169
  106.1 1.7 %collective-permute-start.39 = (bf16[64,512]{1,0:T(8,128)(2,1)S(1)}, bf16[64,512]{1,0:T(8,128)(2,1)S(1)}, u32[]{:S(2)}, u32[]{:S(2)}) collective-permute-start(bf16[64,512]{1,0:T(8,128)(2,1)S(1)} %get-tuple-element.125), channel_id=1, source_target_pairs={{0,6},{1,7},{2,4},{3,5},{4,2},{5,3},{6,0},{7,1},{8,14},{9,15},{10,... | collective-permute-start | bytes 196616 | tf_op jit(solution)/shard_map/ppermute | solution.py:211
  107.8 1.8 %collective-permute-start.38 = (bf16[64,512]{1,0:T(8,128)(2,1)S(1)}, bf16[64,512]{1,0:T(8,128)(2,1)S(1)}, u32[]{:S(2)}, u32[]{:S(2)}) collective-permute-start(bf16[64,512]{1,0:T(8,128)(2,1)S(1)} %get-tuple-element.126), channel_id=1, source_target_pairs={{0,4},{1,5},{2,6},{3,7},{4,0},{5,1},{6,2},{7,3},{8,12},{9,13},{10,... | collective-permute-start | bytes 196616 | tf_op jit(solution)/shard_map/ppermute | solution.py:211
  109.6 2.7 %collective-permute-start.36 = (bf16[3,64,512]{2,1,0:T(8,128)(2,1)S(1)}, bf16[3,64,512]{2,1,0:T(8,128)(2,1)S(1)}, u32[]{:S(2)}, u32[]{:S(2)}) collective-permute-start(bf16[3,64,512]{2,1,0:T(8,128)(2,1)S(1)} %pad_maximum_fusion.2.refs_8_), channel_id=1, source_target_pairs={{0,24},{8,16},{16,8},{24,0},{1,25},{9,17},{17,9},{25,1},{2,26},{10... | collective-permute-start | bytes 589832 | tf_op jit(solution)/shard_map/ppermute | solution.py:211
  115.3 2.9 %collective-permute-done.36.refs_11_ = bf16[3,64,512]{2,1,0:T(8,128)(2,1)S(1)} collective-permute-done((bf16[3,64,512]{2,1,0:T(8,128)(2,1)S(1)}, bf16[3,64,512]{2,1,0:T(8,128)(2,1)S(1)}, u32[]{:S(2)}, u32[]{:S(2)}) %collective-permute-start.36) | collective-permute-done | bytes 196640 | tf_op jit(solution)/shard_map/ppermute | solution.py:211
  120.9 2.9 %weight_grad.1 = (f32[160,512]{1,0:T(8,128)}, f32[160,512]{1,0:T(8,128)}) custom-call(s32[3]{0:T(128)} %pad_add_fusion.place_ref, bf16[320,256]{1,0:T(8,128)(2,1)} %get-tuple-element.103.refs_0_, bf16[320,256]{1,0:T(8,128)(2,1)} %copy-done.18, bf16[320,256]{1,0:T(8,128)(2,1)} %copy-done.19, bf16[320,256]{1,0:T(8,128)(2,1)} %copy-done.20, ...), custom_call_target="tpu_custom_call" | custom-call | flops 335544320 | bytes 3000000 | tf_op jit(solution)/shard_map/weight_grad/pallas_call | solution.py:197
  123.8 1.8 %collective-permute-done.40 = f32[160,512]{1,0:T(8,128)S(1)} collective-permute-done((f32[160,512]{1,0:T(8,128)}, f32[160,512]{1,0:T(8,128)S(1)}, u32[]{:S(2)}, u32[]{:S(2)}) %collective-permute-start.40) | collective-permute-done | bytes 327712 | tf_op jit(solution)/shard_map/ppermute | solution.py:211
  125.7 1.7 %add.69 = f32[160,512]{1,0:T(8,128)} add(f32[160,512]{1,0:T(8,128)} %get-tuple-element.114, f32[160,512]{1,0:T(8,128)S(1)} %collective-permute-done.40) | non-fusion elementwise | flops 81920 | bytes 983040 | tf_op jit(solution)/shard_map/add | solution.py:302
  (156 shorter events, 26.8 us)
Async XLA Ops:
  5.0 9.0 %collective-permute-start.8 = (bf16[64,512]{1,0:T(8,128)(2,1)S(1)}, bf16[64,512]{1,0:T(8,128)(2,1)S(1)}, u32[]{:S(2)}, u32[]{:S(2)}) collective-permute-start(bf16[64,512]{1,0:T(8,128)(2,1)S(1)} %bitcast.54), channel_id=1, source_target_pairs={{0,6},{1,7},{2,4},{3,5},{4,2},{5,3},{6,0},{7,1},{8,14},{9,15},{10,... | collective-permute-start | bytes 196616 | tf_op jit(solution)/shard_map/ppermute | solution.py:211
  10.1 5.6 %collective-permute-start.7 = (bf16[64,512]{1,0:T(8,128)(2,1)S(1)}, bf16[64,512]{1,0:T(8,128)(2,1)S(1)}, u32[]{:S(2)}, u32[]{:S(2)}) collective-permute-start(bf16[64,512]{1,0:T(8,128)(2,1)S(1)} %bitcast.55), channel_id=1, source_target_pairs={{0,4},{1,5},{2,6},{3,7},{4,0},{5,1},{6,2},{7,3},{8,12},{9,13},{10,... | collective-permute-start | bytes 196616 | tf_op jit(solution)/shard_map/ppermute | solution.py:211
  10.1 5.6 %collective-permute-start.6 = (bf16[64,512]{1,0:T(8,128)(2,1)S(1)}, bf16[64,512]{1,0:T(8,128)(2,1)S(1)}, u32[]{:S(2)}, u32[]{:S(2)}) collective-permute-start(bf16[64,512]{1,0:T(8,128)(2,1)S(1)} %bitcast.56), channel_id=1, source_target_pairs={{0,2},{1,3},{2,0},{3,1},{4,6},{5,7},{6,4},{7,5},{8,10},{9,11},{10,... | collective-permute-start | bytes 196616 | tf_op jit(solution)/shard_map/ppermute | solution.py:211
  10.8 6.6 %collective-permute-start = (bf16[64,1280]{1,0:T(8,128)(2,1)}, bf16[64,1280]{1,0:T(8,128)(2,1)S(1)}, u32[]{:S(2)}, u32[]{:S(2)}) collective-permute-start(bf16[64,1280]{1,0:T(8,128)(2,1)} %get-tuple-element.65), channel_id=1, source_target_pairs={{0,8},{8,0},{16,24},{24,16},{1,9},{9,1},{17,25},{25,17},{2,10},{10... | collective-permute-start | bytes 491528 | tf_op jit(solution)/shard_map/ppermute | solution.py:211
  12.4 9.2 %collective-permute-start.1 = (bf16[64,1280]{1,0:T(8,128)(2,1)}, bf16[64,1280]{1,0:T(8,128)(2,1)S(1)}, u32[]{:S(2)}, u32[]{:S(2)}) collective-permute-start(bf16[64,1280]{1,0:T(8,128)(2,1)} %get-tuple-element.66), channel_id=1, source_target_pairs={{0,16},{8,24},{16,0},{24,8},{1,17},{9,25},{17,1},{25,9},{2,18},{10... | collective-permute-start | bytes 491528 | tf_op jit(solution)/shard_map/ppermute | solution.py:211
  14.0 9.0 %collective-permute-start.2 = (bf16[64,1280]{1,0:T(8,128)(2,1)}, bf16[64,1280]{1,0:T(8,128)(2,1)S(1)}, u32[]{:S(2)}, u32[]{:S(2)}) collective-permute-start(bf16[64,1280]{1,0:T(8,128)(2,1)} %get-tuple-element.67), channel_id=1, source_target_pairs={{0,24},{8,16},{16,8},{24,0},{1,25},{9,17},{17,9},{25,1},{2,26},{10... | collective-permute-start | bytes 491528 | tf_op jit(solution)/shard_map/ppermute | solution.py:211
  15.8 13.6 %collective-permute-start.9 = (bf16[256,512]{1,0:T(8,128)(2,1)S(1)}, bf16[256,512]{1,0:T(8,128)(2,1)S(1)}, u32[]{:S(2)}, u32[]{:S(2)}) collective-permute-start(bf16[256,512]{1,0:T(8,128)(2,1)S(1)} %pad_maximum_fusion), channel_id=1, source_target_pairs={{0,1},{1,0},{2,3},{3,2},{4,5},{5,4},{6,7},{7,6},{8,9},{9,8},{10,11... | collective-permute-start | bytes 786440 | tf_op jit(solution)/shard_map/ppermute | solution.py:211
  17.7 5.9 %collective-permute-start.3 = (f32[64,512]{1,0:T(8,128)S(1)}, f32[64,512]{1,0:T(8,128)S(1)}, u32[]{:S(2)}, u32[]{:S(2)}) collective-permute-start(f32[64,512]{1,0:T(8,128)S(1)} %fusion.10), channel_id=1, source_target_pairs={{0,8},{8,0},{16,24},{24,16},{1,9},{9,1},{17,25},{25,17},{2,10},{10... | collective-permute-start | bytes 393224 | tf_op jit(solution)/shard_map/ppermute | solution.py:211
  23.4 5.9 %collective-permute-start.5 = (f32[64,512]{1,0:T(8,128)S(1)}, f32[64,512]{1,0:T(8,128)S(1)}, u32[]{:S(2)}, u32[]{:S(2)}) collective-permute-start(f32[64,512]{1,0:T(8,128)S(1)} %fusion.12), channel_id=1, source_target_pairs={{0,24},{8,16},{16,8},{24,0},{1,25},{9,17},{17,9},{25,1},{2,26},{10... | collective-permute-start | bytes 393224 | tf_op jit(solution)/shard_map/ppermute | solution.py:211
  30.0 7.0 %collective-permute-start.12 = (bf16[64,512]{1,0:T(8,128)(2,1)S(1)}, bf16[64,512]{1,0:T(8,128)(2,1)S(1)}, u32[]{:S(2)}, u32[]{:S(2)}) collective-permute-start(bf16[64,512]{1,0:T(8,128)(2,1)S(1)} %fusion.2.refs_0_), channel_id=1, source_target_pairs={{0,6},{1,7},{2,4},{3,5},{4,2},{5,3},{6,0},{7,1},{8,14},{9,15},{10,... | collective-permute-start | bytes 196616 | tf_op jit(solution)/shard_map/ppermute | solution.py:211
  34.1 5.2 %collective-permute-start.10 = (bf16[64,512]{1,0:T(8,128)(2,1)S(1)}, bf16[64,512]{1,0:T(8,128)(2,1)S(1)}, u32[]{:S(2)}, u32[]{:S(2)}) collective-permute-start(bf16[64,512]{1,0:T(8,128)(2,1)S(1)} %fusion.2.refs_0_), channel_id=1, source_target_pairs={{0,2},{1,3},{2,0},{3,1},{4,6},{5,7},{6,4},{7,5},{8,10},{9,11},{10,... | collective-permute-start | bytes 196616 | tf_op jit(solution)/shard_map/ppermute | solution.py:211
  40.0 26.8 %collective-permute-start.15 = (bf16[1280,256]{1,0:T(8,128)(2,1)S(1)}, bf16[1280,256]{1,0:T(8,128)(2,1)S(1)}, u32[]{:S(2)}, u32[]{:S(2)}) collective-permute-start(bf16[1280,256]{1,0:T(8,128)(2,1)S(1)} %constant_dynamic-slice_fusion), channel_id=1, source_target_pairs={{0,16},{8,24},{16,0},{24,8},{1,17},{9,25},{17,1},{25,9},{2,18},{10... | collective-permute-start | bytes 1966088 | tf_op jit(solution)/shard_map/ppermute | solution.py:211
  40.2 26.7 %collective-permute-start.14 = (bf16[1280,256]{1,0:T(8,128)(2,1)S(1)}, bf16[1280,256]{1,0:T(8,128)(2,1)S(1)}, u32[]{:S(2)}, u32[]{:S(2)}) collective-permute-start(bf16[1280,256]{1,0:T(8,128)(2,1)S(1)} %constant_dynamic-slice_fusion), channel_id=1, source_target_pairs={{0,8},{8,0},{16,24},{24,16},{1,9},{9,1},{17,25},{25,17},{2,10},{10... | collective-permute-start | bytes 1966088 | tf_op jit(solution)/shard_map/ppermute | solution.py:211
  40.9 25.9 %collective-permute-start.16 = (bf16[320,256]{1,0:T(8,128)(2,1)}, bf16[320,256]{1,0:T(8,128)(2,1)S(1)}, u32[]{:S(2)}, u32[]{:S(2)}) collective-permute-start(bf16[320,256]{1,0:T(8,128)(2,1)} %get-tuple-element.84), channel_id=1, source_target_pairs={{0,2},{1,3},{2,0},{3,1},{4,6},{5,7},{6,4},{7,5},{8,10},{9,11},{10,... | collective-permute-start | bytes 491528 | tf_op jit(solution)/shard_map/ppermute | solution.py:211
  41.4 25.4 %collective-permute-start.17 = (bf16[320,256]{1,0:T(8,128)(2,1)}, bf16[320,256]{1,0:T(8,128)(2,1)S(1)}, u32[]{:S(2)}, u32[]{:S(2)}) collective-permute-start(bf16[320,256]{1,0:T(8,128)(2,1)} %get-tuple-element.85), channel_id=1, source_target_pairs={{0,4},{1,5},{2,6},{3,7},{4,0},{5,1},{6,2},{7,3},{8,12},{9,13},{10,... | collective-permute-start | bytes 491528 | tf_op jit(solution)/shard_map/ppermute | solution.py:211
  43.1 23.8 %collective-permute-start.18 = (bf16[320,256]{1,0:T(8,128)(2,1)}, bf16[320,256]{1,0:T(8,128)(2,1)S(1)}, u32[]{:S(2)}, u32[]{:S(2)}) collective-permute-start(bf16[320,256]{1,0:T(8,128)(2,1)} %get-tuple-element.86), channel_id=1, source_target_pairs={{0,6},{1,7},{2,4},{3,5},{4,2},{5,3},{6,0},{7,1},{8,14},{9,15},{10,... | collective-permute-start | bytes 491528 | tf_op jit(solution)/shard_map/ppermute | solution.py:211
  67.0 18.1 %collective-permute-start.24 = (bf16[1280,256]{1,0:T(8,128)(2,1)S(1)}, bf16[1280,256]{1,0:T(8,128)(2,1)S(1)}, u32[]{:S(2)}, u32[]{:S(2)}) collective-permute-start(bf16[1280,256]{1,0:T(8,128)(2,1)S(1)} %copy-done.8), channel_id=1, source_target_pairs={{0,24},{8,16},{16,8},{24,0},{1,25},{9,17},{17,9},{25,1},{2,26},{10... | collective-permute-start | bytes 1966088 | tf_op jit(solution)/shard_map/ppermute | solution.py:211
  69.9 15.2 %collective-permute-start.25 = (bf16[1280,256]{1,0:T(8,128)(2,1)S(1)}, bf16[1280,256]{1,0:T(8,128)(2,1)S(1)}, u32[]{:S(2)}, u32[]{:S(2)}) collective-permute-start(bf16[1280,256]{1,0:T(8,128)(2,1)S(1)} %collective-permute-done.14.refs_0_), channel_id=1, source_target_pairs={{0,1},{1,0},{2,3},{3,2},{4,5},{5,4},{6,7},{7,6},{8,9},{9,8},{10,11... | collective-permute-start | bytes 1966088 | tf_op jit(solution)/shard_map/ppermute | solution.py:211
  70.3 15.7 %collective-permute-start.26 = (bf16[1280,256]{1,0:T(8,128)(2,1)S(1)}, bf16[1280,256]{1,0:T(8,128)(2,1)}, u32[]{:S(2)}, u32[]{:S(2)}) collective-permute-start(bf16[1280,256]{1,0:T(8,128)(2,1)S(1)} %collective-permute-done.15.refs_1_), channel_id=1, source_target_pairs={{0,1},{1,0},{2,3},{3,2},{4,5},{5,4},{6,7},{7,6},{8,9},{9,8},{10,11... | collective-permute-start | bytes 1966088 | tf_op jit(solution)/shard_map/ppermute | solution.py:211
  72.0 6.1 %collective-permute-start.22 = (bf16[64,512]{1,0:T(8,128)(2,1)S(1)}, bf16[64,512]{1,0:T(8,128)(2,1)S(1)}, u32[]{:S(2)}, u32[]{:S(2)}) collective-permute-start(bf16[64,512]{1,0:T(8,128)(2,1)S(1)} %get-tuple-element.128), channel_id=1, source_target_pairs={{0,6},{1,7},{2,4},{3,5},{4,2},{5,3},{6,0},{7,1},{8,14},{9,15},{10,... | collective-permute-start | bytes 196616 | tf_op jit(solution)/shard_map/ppermute | solution.py:211
  76.0 5.6 %collective-permute-start.21 = (bf16[64,512]{1,0:T(8,128)(2,1)S(1)}, bf16[64,512]{1,0:T(8,128)(2,1)S(1)}, u32[]{:S(2)}, u32[]{:S(2)}) collective-permute-start(bf16[64,512]{1,0:T(8,128)(2,1)S(1)} %get-tuple-element.129), channel_id=1, source_target_pairs={{0,4},{1,5},{2,6},{3,7},{4,0},{5,1},{6,2},{7,3},{8,12},{9,13},{10,... | collective-permute-start | bytes 196616 | tf_op jit(solution)/shard_map/ppermute | solution.py:211
  86.0 14.1 %collective-permute-start.30 = (bf16[1280,256]{1,0:T(8,128)(2,1)S(1)}, bf16[1280,256]{1,0:T(8,128)(2,1)S(1)}, u32[]{:S(2)}, u32[]{:S(2)}) collective-permute-start(bf16[1280,256]{1,0:T(8,128)(2,1)S(1)} %collective-permute-done.24.refs_2_), channel_id=1, source_target_pairs={{0,1},{1,0},{2,3},{3,2},{4,5},{5,4},{6,7},{7,6},{8,9},{9,8},{10,11... | collective-permute-start | bytes 1966088 | tf_op jit(solution)/shard_map/ppermute | solution.py:211
  86.6 7.1 %collective-permute-start.33 = (bf16[64,512]{1,0:T(8,128)(2,1)S(1)}, bf16[64,512]{1,0:T(8,128)(2,1)S(1)}, u32[]{:S(2)}, u32[]{:S(2)}) collective-permute-start(bf16[64,512]{1,0:T(8,128)(2,1)S(1)} %fusion.grad_ref.refs_4_), channel_id=1, source_target_pairs={{0,6},{1,7},{2,4},{3,5},{4,2},{5,3},{6,0},{7,1},{8,14},{9,15},{10,... | collective-permute-start | bytes 196616 | tf_op jit(solution)/shard_map/ppermute | solution.py:211
  88.3 7.5 %collective-permute-start.32 = (bf16[64,512]{1,0:T(8,128)(2,1)S(1)}, bf16[64,512]{1,0:T(8,128)(2,1)S(1)}, u32[]{:S(2)}, u32[]{:S(2)}) collective-permute-start(bf16[64,512]{1,0:T(8,128)(2,1)S(1)} %fusion.grad_ref.refs_4_), channel_id=1, source_target_pairs={{0,4},{1,5},{2,6},{3,7},{4,0},{5,1},{6,2},{7,3},{8,12},{9,13},{10,... | collective-permute-start | bytes 196616 | tf_op jit(solution)/shard_map/ppermute | solution.py:211
  88.5 8.6 %collective-permute-start.31 = (bf16[64,512]{1,0:T(8,128)(2,1)S(1)}, bf16[64,512]{1,0:T(8,128)(2,1)S(1)}, u32[]{:S(2)}, u32[]{:S(2)}) collective-permute-start(bf16[64,512]{1,0:T(8,128)(2,1)S(1)} %fusion.grad_ref.refs_4_), channel_id=1, source_target_pairs={{0,2},{1,3},{2,0},{3,1},{4,6},{5,7},{6,4},{7,5},{8,10},{9,11},{10,... | collective-permute-start | bytes 196616 | tf_op jit(solution)/shard_map/ppermute | solution.py:211
  91.1 6.0 %collective-permute-start.29 = (bf16[64,512]{1,0:T(8,128)(2,1)S(1)}, bf16[64,512]{1,0:T(8,128)(2,1)S(1)}, u32[]{:S(2)}, u32[]{:S(2)}) collective-permute-start(bf16[64,512]{1,0:T(8,128)(2,1)S(1)} %fusion.grad_ref.refs_4_), channel_id=1, source_target_pairs={{0,24},{8,16},{16,8},{24,0},{1,25},{9,17},{17,9},{25,1},{2,26},{10... | collective-permute-start | bytes 196616 | tf_op jit(solution)/shard_map/ppermute | solution.py:211
  106.0 6.3 %collective-permute-start.37 = (bf16[64,512]{1,0:T(8,128)(2,1)S(1)}, bf16[64,512]{1,0:T(8,128)(2,1)S(1)}, u32[]{:S(2)}, u32[]{:S(2)}) collective-permute-start(bf16[64,512]{1,0:T(8,128)(2,1)S(1)} %get-tuple-element.124), channel_id=1, source_target_pairs={{0,2},{1,3},{2,0},{3,1},{4,6},{5,7},{6,4},{7,5},{8,10},{9,11},{10,... | collective-permute-start | bytes 196616 | tf_op jit(solution)/shard_map/ppermute | solution.py:211
  106.1 7.0 %collective-permute-start.39 = (bf16[64,512]{1,0:T(8,128)(2,1)S(1)}, bf16[64,512]{1,0:T(8,128)(2,1)S(1)}, u32[]{:S(2)}, u32[]{:S(2)}) collective-permute-start(bf16[64,512]{1,0:T(8,128)(2,1)S(1)} %get-tuple-element.125), channel_id=1, source_target_pairs={{0,6},{1,7},{2,4},{3,5},{4,2},{5,3},{6,0},{7,1},{8,14},{9,15},{10,... | collective-permute-start | bytes 196616 | tf_op jit(solution)/shard_map/ppermute | solution.py:211
  107.8 6.8 %collective-permute-start.38 = (bf16[64,512]{1,0:T(8,128)(2,1)S(1)}, bf16[64,512]{1,0:T(8,128)(2,1)S(1)}, u32[]{:S(2)}, u32[]{:S(2)}) collective-permute-start(bf16[64,512]{1,0:T(8,128)(2,1)S(1)} %get-tuple-element.126), channel_id=1, source_target_pairs={{0,4},{1,5},{2,6},{3,7},{4,0},{5,1},{6,2},{7,3},{8,12},{9,13},{10,... | collective-permute-start | bytes 196616 | tf_op jit(solution)/shard_map/ppermute | solution.py:211
  109.6 8.5 %collective-permute-start.36 = (bf16[3,64,512]{2,1,0:T(8,128)(2,1)S(1)}, bf16[3,64,512]{2,1,0:T(8,128)(2,1)S(1)}, u32[]{:S(2)}, u32[]{:S(2)}) collective-permute-start(bf16[3,64,512]{2,1,0:T(8,128)(2,1)S(1)} %pad_maximum_fusion.2.refs_8_), channel_id=1, source_target_pairs={{0,24},{8,16},{16,8},{24,0},{1,25},{9,17},{17,9},{25,1},{2,26},{10... | collective-permute-start | bytes 589832 | tf_op jit(solution)/shard_map/ppermute | solution.py:211
  112.2 7.3 %collective-permute-start.35 = (bf16[3,64,512]{2,1,0:T(8,128)(2,1)S(1)}, bf16[3,64,512]{2,1,0:T(8,128)(2,1)S(1)}, u32[]{:S(2)}, u32[]{:S(2)}) collective-permute-start(bf16[3,64,512]{2,1,0:T(8,128)(2,1)S(1)} %pad_maximum_fusion.2.refs_8_), channel_id=1, source_target_pairs={{0,16},{8,24},{16,0},{24,8},{1,17},{9,25},{17,1},{25,9},{2,18},{10... | collective-permute-start | bytes 589832 | tf_op jit(solution)/shard_map/ppermute | solution.py:211
  112.3 7.3 %collective-permute-start.34 = (bf16[3,64,512]{2,1,0:T(8,128)(2,1)S(1)}, bf16[3,64,512]{2,1,0:T(8,128)(2,1)S(1)}, u32[]{:S(2)}, u32[]{:S(2)}) collective-permute-start(bf16[3,64,512]{2,1,0:T(8,128)(2,1)S(1)} %pad_maximum_fusion.2.refs_8_), channel_id=1, source_target_pairs={{0,8},{8,0},{16,24},{24,16},{1,9},{9,1},{17,25},{25,17},{2,10},{10... | collective-permute-start | bytes 589832 | tf_op jit(solution)/shard_map/ppermute | solution.py:211
  (43 other events, 358.2 us)

commit v7 on v6

--- a/solution.py
+++ b/solution.py
@@ -103,108 +103,104 @@
     )(length, queries, upstream, keys, values, *key_pieces, *value_pieces)
 
 
-def split_kernel(place_ref, hidden_ref, *piece_refs):
+def in_vmem(kernel, name, outs, arrays, macs=0, scratch=()):
+    whole = pl.BlockSpec(memory_space=pltpu.VMEM)
+    results = pl.pallas_call(
+        kernel,
+        in_specs=[whole] * len(arrays),
+        out_specs=[whole] * len(outs),
+        out_shape=[jax.ShapeDtypeStruct(shape, dtype) for shape, dtype in outs],
+        scratch_shapes=scratch,
+        compiler_params=PARAMS,
+        cost_estimate=cost(macs, 3 * 10**6),
+        name=name,
+    )(*arrays)
+    return list(results)
+
+
+def split_kernel(hidden_ref, *piece_refs):
     depth = piece_refs[0].shape[1]
+    group = lax.axis_index("group")
     for k, piece_ref in enumerate(piece_refs):
-        start = pl.multiple_of((place_ref[0] ^ k) * depth, depth)
+        start = pl.multiple_of((group ^ k) * depth, depth)
         piece_ref[...] = hidden_ref[:, pl.ds(start, depth)]
 
 
-def split_pass(place, hidden, groups):
+def split_pass(hidden, groups):
     tokens, width = hidden.shape
-    return pl.pallas_call(
-        split_kernel,
-        in_specs=[pl.BlockSpec(memory_space=pltpu.SMEM), pl.BlockSpec(memory_space=pltpu.VMEM)],
-        out_specs=[pl.BlockSpec(memory_space=pltpu.VMEM)] * groups,
-        out_shape=[jax.ShapeDtypeStruct((tokens, width // groups), BF16)] * groups,
-        compiler_params=PARAMS,
-        name="split_hidden",
-    )(place, hidden)
-
-
-def turn_kernel(groups, place_ref, *refs):
+    outs = [((tokens, width // groups), hidden.dtype)] * groups
+    return in_vmem(split_kernel, "split_hidden", outs, [hidden])
+
+
+def turn_kernel(groups, *refs):
     columns, piece_refs, turned = refs[:groups], refs[groups:-1], refs[-1]
-    rows = piece_refs[0].shape[0]
-    turned[...] = jnp.concatenate([ref[...] for ref in columns], axis=0).T
+    half = piece_refs[0].shape[0] // 2
+    resp = lax.axis_index("resp")
+    core, chip = resp % 2, resp // 2
+    turned[...] = jnp.concatenate([ref[...] for ref in columns], axis=0).astype(F32).T
     for p, piece_ref in enumerate(piece_refs):
-        start = pl.multiple_of((place_ref[2] ^ p) * rows, 16)
-        piece_ref[...] = turned[pl.ds(start, rows)]
-
-
-def turn_pass(place, columns, chips):
+        start = (chip ^ p) * (2 * half)
+        for i, part in enumerate((core, 1 - core)):
+            rows = turned[pl.ds(pl.multiple_of(start + part * half, 8), half)]
+            piece_ref[i * half : (i + 1) * half] = rows.astype(BF16)
+
+
+def turn_pass(columns, chips):
     tokens, depth = columns[0].shape
     every = tokens * len(columns)
-    return pl.pallas_call(
-        partial(turn_kernel, len(columns)),
-        in_specs=[pl.BlockSpec(memory_space=pltpu.SMEM)]
-        + [pl.BlockSpec(memory_space=pltpu.VMEM)] * len(columns),
-        out_specs=[pl.BlockSpec(memory_space=pltpu.VMEM)] * chips,
-        out_shape=[jax.ShapeDtypeStruct((depth // chips, every), BF16)] * chips,
-        scratch_shapes=[pltpu.VMEM((depth, every), BF16)],
-        compiler_params=PARAMS,
-        name="turn_hidden",
-    )(place, *columns)
-
-
-def hidden_kernel(groups, place_ref, grad_ref, own_ref, *refs):
-    near, far, out_ref = refs[: groups - 1], refs[groups - 1 : -1], refs[-1]
-    group, core = place_ref[0], place_ref[1]
-    depth = own_ref.shape[0]
-    half = near[0].shape[1]
-    near_grad = grad_ref[:, pl.ds(pl.multiple_of(core * half, half), half)]
-    far_grad = grad_ref[:, pl.ds(pl.multiple_of((1 - core) * half, half), half)]
-    for k in range(groups):
-        if k:
-            block = dot(near_grad, near[k - 1][...], 1, 1) + dot(far_grad, far[k - 1][...], 1, 1)
-        else:
-            block = dot(grad_ref[...], own_ref[...], 1, 1)
-        start = pl.multiple_of((group ^ k) * depth, depth)
-        out_ref[:, pl.ds(start, depth)] = block.astype(BF16)
-
-
-def hidden_pass(place, key_pre_grad, own, near, far):
-    tokens = key_pre_grad.shape[0]
-    groups = len(near) + 1
-    width = groups * own.shape[0]
-    return pl.pallas_call(
-        partial(hidden_kernel, groups),
-        in_specs=[pl.BlockSpec(memory_space=pltpu.SMEM)]
-        + [pl.BlockSpec(memory_space=pltpu.VMEM)] * (2 * groups),
-        out_specs=pl.BlockSpec(memory_space=pltpu.VMEM),
-        out_shape=jax.ShapeDtypeStruct((tokens, width), BF16),
-        compiler_params=PARAMS,
-        cost_estimate=cost(tokens * width * own.shape[1], 6 * 10**6),
-        name="hidden_grad",
-    )(place, key_pre_grad, own, *near, *far)
-
-
-def weight_kernel(chips, groups, place_ref, *refs):
-    taken, first, rest = refs[:chips], refs[chips : chips + groups], refs[chips + groups : -3]
-    mine_ref, other_ref, product = refs[-3:]
-    half = mine_ref.shape[0]
-    core = place_ref[1]
-    columns = jnp.concatenate([ref[...] for ref in taken], axis=1)
+    outs = [((depth // chips, every), BF16)] * chips
+    scratch = [pltpu.VMEM((depth, every), F32)]
+    return in_vmem(partial(turn_kernel, len(columns)), "turn_hidden", outs, columns, 0, scratch)
+
+
+def hidden_kernel(beside, across, own_ref, *refs):
+    grads, refs = refs[: len(across) + 1], refs[len(across) + 1 :]
+    near, far = refs[: len(beside)], refs[len(beside) : 2 * len(beside)]
+    out_ref, *part_refs = refs[2 * len(beside) :]
+    group, core = lax.axis_index("group"), lax.axis_index("resp") % 2
+    depth, kv_width = own_ref.shape
+    tokens, half = grads[0].shape[0], kv_width // 2
+    near_grad = grads[0][:, pl.ds(pl.multiple_of(core * half, half), half)]
+    far_grad = grads[0][:, pl.ds(pl.multiple_of((1 - core) * half, half), half)]
+
+    def place(k, block):
+        out_ref[:, pl.ds(pl.multiple_of((group ^ k) * depth, depth), depth)] = block
+
+    own = dot(own_ref[...], jnp.concatenate([ref[...] for ref in grads], axis=0), 1, 1).T.astype(BF16)
+    place(0, own[:tokens])
+    for i, k in enumerate(across):
+        part_refs[i][...] = own[(i + 1) * tokens : (i + 2) * tokens]
+        place(k, jnp.zeros((tokens, depth), BF16))
+    for i, k in enumerate(beside):
+        block = dot(near[i][...], near_grad, 1, 1) + dot(far[i][...], far_grad, 1, 1)
+        place(k, block.T.astype(BF16))
+
+
+def hidden_pass(first, own, near, far, across):
+    tokens, kv_width = first[0].shape
+    depth = own.shape[0]
+    outs = [((tokens, len(first) * depth), BF16)] + [((tokens, depth), BF16)] * len(across)
+    arrays = [own, first[0], *[first[k] for k in across], *near.values(), *far.values()]
+    kernel = partial(hidden_kernel, list(near), across)
+    return in_vmem(kernel, "hidden_grad", outs, arrays, tokens * depth * kv_width * len(first))
+
+
+def weight_kernel(chips, groups, second, *refs):
+    taken, first, rest, out_ref = refs[:chips], refs[chips : chips + groups], refs[chips + groups : -1], refs[-1]
+    half = out_ref.shape[0]
+    start = half if second else 0
+    columns = jnp.concatenate([ref[start : start + half] for ref in taken], axis=1)
     grads = [ref[...] for ref in first] + [ref[p] for p in range(chips - 1) for ref in rest]
-    product[...] = dot(columns, jnp.concatenate(grads, axis=0))
-    mine_ref[...] = product[pl.ds(pl.multiple_of(core * half, 8), half)]
-    other_ref[...] = product[pl.ds(pl.multiple_of((1 - core) * half, 8), half)]
-
-
-def weight_pass(place, taken, first, rest):
-    rows = taken[0].shape[0]
+    out_ref[...] = dot(columns, jnp.concatenate(grads, axis=0))
+
+
+def weight_pass(taken, first, rest, second):
+    rows, tokens = taken[0].shape
     kv_width = first[0].shape[-1]
-    out = jax.ShapeDtypeStruct((rows // 2, kv_width), F32)
-    return pl.pallas_call(
-        partial(weight_kernel, len(taken), len(first)),
-        in_specs=[pl.BlockSpec(memory_space=pltpu.SMEM)]
-        + [pl.BlockSpec(memory_space=pltpu.VMEM)] * (len(taken) + len(first) + len(rest)),
-        out_specs=[pl.BlockSpec(memory_space=pltpu.VMEM)] * 2,
-        out_shape=[out, out],
-        scratch_shapes=[pltpu.VMEM((rows, kv_width), F32)],
-        compiler_params=PARAMS,
-        cost_estimate=cost(rows * kv_width * taken[0].shape[1] * len(taken), 3 * 10**6),
-        name="weight_grad",
-    )(place, *taken, *first, *rest)
+    kernel = partial(weight_kernel, len(taken), len(first), second)
+    macs = rows // 2 * kv_width * tokens * len(taken)
+    outs = [((rows // 2, kv_width), F32)]
+    return in_vmem(kernel, "weight_grad", outs, [*taken, *first, *rest], macs)[0]
 
 
 def swap(array, axis, size, distance):
@@ -244,32 +240,31 @@
     tokens = hidden.shape[0]
     depth, kv_width = key_matrix.shape
     head_dim = key_gain.shape[0]
-    group, resp = lax.axis_index("group"), lax.axis_index("resp")
-    core, chip, chips = resp % 2, resp // 2, responses // 2
-    place = jnp.stack([group, core, chip]).astype(jnp.int32)
-
-    pieces = split_pass(place, hidden, groups)
+    chips = responses // 2
+    beside = [k for k in range(1, groups) if k & (k - 1) == 0]
+    across = [k for k in range(1, groups) if k & (k - 1)]
+
+    pieces = split_pass(hidden, groups)
     columns = [swap(piece, "group", groups, k) if k else piece for k, piece in enumerate(pieces)]
     partials = [dot(piece, key_matrix) for piece in columns]
-    prompt_value, partials[0] = together(prompt_token_value[0], partials[0])
+    prompt_value, partials[-1] = together(prompt_token_value[0], partials[-1])
     value_near = spread_near(prompt_value, responses)
     key_pre = partials[0]
     for k in range(1, groups):
         key_pre = key_pre + swap(partials[k], "group", groups, k)
-    value_far = spread_far(value_near, responses)
-
     half_width = kv_width // 2
-    half_weight = lax.dynamic_slice(key_matrix, (0, core * half_width), (depth, half_width))
-    half_weight, key_pre, *value_far = together(half_weight, key_pre, *value_far)
-    value_pieces = value_near + value_far
+    start = (lax.axis_index("resp") % 2) * half_width
+    half_weight = lax.dynamic_slice(key_matrix, (0, start), (depth, half_width))
+    half_weight, key_pre = together(half_weight, key_pre)
+    weight_near = [swap(half_weight, "group", groups, k) for k in beside]
+
     prompt_key = norm_keys(key_pre, key_gain).astype(BF16)
     key_near = spread_near(prompt_key, responses)
-    weight_near = [swap(half_weight, "group", groups, k) for k in range(1, groups)]
-
-    taken = turn_pass(place, columns, chips)
-    count = len(taken)
+    value_pieces = value_near + spread_far(value_near, responses)
+
+    taken = turn_pass(columns, chips)
     both = together(*taken, *key_near)
-    taken, key_near = both[:count], both[count:]
+    taken, key_near = both[:chips], both[chips:]
     key_pieces = key_near + spread_far(key_near, responses)
     taken[1:] = [swap(taken[p], "resp", responses, 2 * p) for p in range(1, chips)]
 
@@ -277,29 +272,35 @@
         resp_length, resp_query[0, 0], grad_out[0, 0], key_pieces, value_pieces,
         resp_key[0, 0], response_value[0, 0], head_dim,
     )
-    key_sums, far, *rest = together(key_sums, far, *weight_near[:-1], *taken)
-    weight_near[:-1], taken = rest[: groups - 2], rest[groups - 2 :]
+    key_sums, far, *both = together(key_sums, far, *taken, *weight_near)
+    taken, weight_near = both[:chips], both[chips:]
     key_sums = chip_sum(pair_sum(key_sums, far, responses), responses)
     value_sums = pair_sum(value_sums, value_far, responses)
-    weight_far = [swap(piece, "resp", responses, 1) for piece in weight_near[:-1]]
-    key_sums, value_sums, weight_near[-1], *weight_far = together(
-        key_sums, value_sums, weight_near[-1], *weight_far
-    )
+    key_sums, value_sums = together(key_sums, value_sums)
     _, pullback = jax.vjp(lambda values: norm_keys(values, key_gain), key_pre)
     key_pre_grad = pullback(key_sums)[0].astype(BF16)
 
     first = [key_pre_grad] + [swap(key_pre_grad, "group", groups, k) for k in range(1, groups)]
     grads = spread_near(key_pre_grad, responses)[1:]
-    weight_far.append(swap(weight_near[-1], "resp", responses, 1))
-    *first, weight_far[-1], block = together(*first, weight_far[-1], jnp.stack(grads, axis=0))
-    blocks = [block] + [swap(block, "group", groups, k) for k in range(1, groups)]
-    grad_hidden = hidden_pass(place, first[0], key_matrix, weight_near, weight_far)
+    weight_far = [swap(piece, "resp", responses, 1) for piece in weight_near]
+    block, *both = together(jnp.stack(grads, axis=0), *first, *weight_far)
+    first, weight_far = both[:groups], both[groups:]
+    rest = [block] + [swap(block, "group", groups, k) for k in range(1, groups)]
+
+    grad_hidden, *parts = hidden_pass(
+        first, key_matrix, dict(zip(beside, weight_near)), dict(zip(beside, weight_far)), across
+    )
     grad_hidden, value_sums = together(grad_hidden, value_sums)
     value_sums = chip_sum(value_sums, responses)
-    grad_hidden, *blocks = together(grad_hidden, *blocks)
-    mine, other = weight_pass(place, taken, first, blocks)
+    grad_hidden, *both = together(grad_hidden, *parts, *rest)
+    parts, rest = both[: len(parts)], both[len(parts) :]
+    other = weight_pass(taken, first, rest, True)
     other, value_sums = together(other, value_sums)
-    grad_weight = mine + swap(other, "resp", responses, 1)
+    other = swap(other, "resp", responses, 1)
+    grad_weight = weight_pass(taken, first, rest, False) + other
+    for k, part in zip(across, parts):
+        start = (lax.axis_index("group") ^ k) * depth
+        grad_hidden = lax.dynamic_update_slice(grad_hidden, swap(part, "group", groups, k), (0, start))
     return (
         grad_hidden[None],
         grad_weight,

time: 128 us -> 117 us (0.914)
  waiting for transfers between devices: 32.7 us -> 22.6 us
  local copies, waits for them, and re-layouts: 3.93 us -> 1.6 us
  Pallas kernels: 33.6 us -> 35.3 us
    ppermute x41 -> x40, waiting for transfers between devices: 32.7 us -> 22.6 us  [swap(): return lax.ppermute(array, axis, [(i, i ^ distance) for i in range(size)])]
    unnamed x68 -> x66, local copies, waits for them, and re-layouts: 3.15 us -> 0.14 us
    pallas_call x4 -> x5, Pallas kernels: 12.1 us -> 13.7 us  [in_vmem(): pl.pallas_call(kernel, in_specs=[whole] * len(arrays), out_specs=[whole]...]
    ppermute x41 -> x40, starting transfers between devices: 47.8 us -> 48.6 us  [swap(): return lax.ppermute(array, axis, [(i, i ^ distance) for i in range(size)])]
  transfers between devices with their start and end apart: 41 -> 40, of which waited for: 17 -> 14; matrix products, arithmetic and copies ran while one was open for 3% -> 6% of each run, Pallas kernels for 19% -> 28%
where the time goes in v7:
time: 117 us
  starting transfers between devices  48.6 us (42%)
  Pallas kernels  35.3 us (30%)
  waiting for transfers between devices  22.6 us (19%)
  other arithmetic  4.14 us (4%)
  matrix products  2.74 us (2%)
  between operations  1.87 us (2%)
  local copies, waits for them, and re-layouts  1.6 us (1%)
    ppermute x40, starting transfers between devices, swap(): return lax.ppermute(array, axis, [(i, i ^ distance) for i in range(size)])  48.6 us
    ppermute x40, waiting for transfers between devices, swap(): return lax.ppermute(array, axis, [(i, i ^ distance) for i in range(size)])  22.6 us
    pallas_call x1, Pallas kernels, attend(): pl.pallas_call(partial(attend_kernel, len(key_pieces)), grid=(kv_heads,),...  21.6 us
    pallas_call x5, Pallas kernels, in_vmem(): pl.pallas_call(kernel, in_specs=[whole] * len(arrays), out_specs=[whole]...  13.7 us
    dot_general x4, matrix products, dot(): return lax.dot_general(left, right, dims, preferred_element_type=F32)  2.74 us
  transfers between devices with their start and end apart: 40, of which 14 were waited for; matrix products, arithmetic and copies ran while one was open for 6% of the time, Pallas kernels for 28%

profile of v7, /device:TPU:0, one launch (start us, length us, event | category | flops | bytes accessed | tf_op | source)
XLA Modules:
  0.0 116.9 jit_solution(4900669062153444313)
XLA Ops:
  0.6 2.1 %split_hidden.1 = (bf16[64,1280]{1,0:T(8,128)(2,1)}, bf16[64,1280]{1,0:T(8,128)(2,1)}, bf16[64,1280]{1,0:T(8,128)(2,1)}, bf16[64,1280]{1,0:T(8,128)(2,1)}) custom-call(bf16[64,5120]{1,0:T(8,128)(2,1)} %bitcast.45), custom_call_target="tpu_custom_call" | custom-call | bytes 3000000 | tf_op jit(solution)/shard_map/split_hidden/pallas_call | solution.py:108
  2.7 3.9 %collective-permute-start.2 = (bf16[64,1280]{1,0:T(8,128)(2,1)}, bf16[64,1280]{1,0:T(8,128)(2,1)S(1)}, u32[]{:S(2)}, u32[]{:S(2)}) collective-permute-start(bf16[64,1280]{1,0:T(8,128)(2,1)} %get-tuple-element.65), channel_id=1, source_target_pairs={{0,24},{8,16},{16,8},{24,0},{1,25},{9,17},{17,9},{25,1},{2,26},{10... | collective-permute-start | bytes 491528 | tf_op jit(solution)/shard_map/ppermute | solution.py:207
  7.2 1.7 %fusion.9 = f32[64,512]{1,0:T(8,128)S(1)} fusion(bf16[64,1280]{1,0:T(8,128)(2,1)} %get-tuple-element.62.refs_0_, bf16[1280,512]{1,0:T(8,128)(2,1)} %own_ref.1), kind=kOutput, calls=%fused_computation.27 | convolution fusion | flops 83886080 | bytes 1605632 | tf_op jit(solution)/shard_map/dot_general | solution.py:23
  9.0 2.8 %collective-permute-done.2.refs_3_ = bf16[64,1280]{1,0:T(8,128)(2,1)S(1)} collective-permute-done((bf16[64,1280]{1,0:T(8,128)(2,1)}, bf16[64,1280]{1,0:T(8,128)(2,1)S(1)}, u32[]{:S(2)}, u32[]{:S(2)}) %collective-permute-start.2) | collective-permute-done | bytes 163872 | tf_op jit(solution)/shard_map/ppermute | solution.py:207
  12.2 3.1 %collective-permute-start.5 = (f32[64,512]{1,0:T(8,128)S(1)}, f32[64,512]{1,0:T(8,128)S(1)}, u32[]{:S(2)}, u32[]{:S(2)}) collective-permute-start(f32[64,512]{1,0:T(8,128)S(1)} %fusion.12), channel_id=1, source_target_pairs={{0,24},{8,16},{16,8},{24,0},{1,25},{9,17},{17,9},{25,1},{2,26},{10... | collective-permute-start | bytes 393224 | tf_op jit(solution)/shard_map/ppermute | solution.py:207
  15.7 1.6 %collective-permute-start.3 = (f32[64,512]{1,0:T(8,128)S(1)}, f32[64,512]{1,0:T(8,128)S(1)}, u32[]{:S(2)}, u32[]{:S(2)}) collective-permute-start(f32[64,512]{1,0:T(8,128)S(1)} %fusion.10), channel_id=1, source_target_pairs={{0,8},{8,0},{16,24},{24,16},{1,9},{9,1},{17,25},{25,17},{2,10},{10... | collective-permute-start | bytes 393224 | tf_op jit(solution)/shard_map/ppermute | solution.py:207
  18.2 1.6 %collective-permute-start.10 = (bf16[64,512]{1,0:T(8,128)(2,1)S(1)}, bf16[64,512]{1,0:T(8,128)(2,1)S(1)}, u32[]{:S(2)}, u32[]{:S(2)}) collective-permute-start(bf16[64,512]{1,0:T(8,128)(2,1)S(1)} %bitcast.52), channel_id=1, source_target_pairs={{0,2},{1,3},{2,0},{3,1},{4,6},{5,7},{6,4},{7,5},{8,10},{9,11},{10,... | collective-permute-start | bytes 196616 | tf_op jit(solution)/shard_map/ppermute | solution.py:207
  19.7 2.6 %collective-permute-start.11 = (bf16[64,512]{1,0:T(8,128)(2,1)S(1)}, bf16[64,512]{1,0:T(8,128)(2,1)S(1)}, u32[]{:S(2)}, u32[]{:S(2)}) collective-permute-start(bf16[64,512]{1,0:T(8,128)(2,1)S(1)} %bitcast.53), channel_id=1, source_target_pairs={{0,4},{1,5},{2,6},{3,7},{4,0},{5,1},{6,2},{7,3},{8,12},{9,13},{10,... | collective-permute-start | bytes 196616 | tf_op jit(solution)/shard_map/ppermute | solution.py:207
  22.3 2.2 %turn_hidden.1 = (bf16[320,256]{1,0:T(8,128)(2,1)}, bf16[320,256]{1,0:T(8,128)(2,1)}, bf16[320,256]{1,0:T(8,128)(2,1)}, bf16[320,256]{1,0:T(8,128)(2,1)}) custom-call(bf16[64,1280]{1,0:T(8,128)(2,1)} %get-tuple-element.62.refs_0_, bf16[64,1280]{1,0:T(8,128)(2,1)} %copy-done.10, bf16[64,1280]{1,0:T(8,128)(2,1)} %copy-done.11, bf16[64,1280]{1,0:T(8,128)(2,1)} %copy-done.9), custom_call_target="tpu_custom_call" | custom-call | bytes 3000000 | tf_op jit(solution)/shard_map/turn_hidden/pallas_call | solution.py:108
  26.2 3.5 %collective-permute-start.7 = (bf16[64,512]{1,0:T(8,128)(2,1)S(1)}, bf16[64,512]{1,0:T(8,128)(2,1)S(1)}, u32[]{:S(2)}, u32[]{:S(2)}) collective-permute-start(bf16[64,512]{1,0:T(8,128)(2,1)S(1)} %fusion.2.refs_0_), channel_id=1, source_target_pairs={{0,4},{1,5},{2,6},{3,7},{4,0},{5,1},{6,2},{7,3},{8,12},{9,13},{10,... | collective-permute-start | bytes 196616 | tf_op jit(solution)/shard_map/ppermute | solution.py:207
  31.0 2.7 %collective-permute-done.7.refs_2_ = bf16[64,512]{1,0:T(8,128)(2,1)S(1)} collective-permute-done((bf16[64,512]{1,0:T(8,128)(2,1)S(1)}, bf16[64,512]{1,0:T(8,128)(2,1)S(1)}, u32[]{:S(2)}, u32[]{:S(2)}) %collective-permute-start.7) | collective-permute-done | bytes 65568 | tf_op jit(solution)/shard_map/ppermute | solution.py:207
  33.7 2.1 %collective-permute-done.8.refs_3_ = bf16[64,512]{1,0:T(8,128)(2,1)S(1)} collective-permute-done((bf16[64,512]{1,0:T(8,128)(2,1)S(1)}, bf16[64,512]{1,0:T(8,128)(2,1)S(1)}, u32[]{:S(2)}, u32[]{:S(2)}) %collective-permute-start.8) | collective-permute-done | bytes 65568 | tf_op jit(solution)/shard_map/ppermute | solution.py:207
  37.1 1.5 %collective-permute-start.18 = (bf16[1280,256]{1,0:T(8,128)(2,1)S(1)}, bf16[1280,256]{1,0:T(8,128)(2,1)S(1)}, u32[]{:S(2)}, u32[]{:S(2)}) collective-permute-start(bf16[1280,256]{1,0:T(8,128)(2,1)S(1)} %constant_dynamic-slice_fusion), channel_id=1, source_target_pairs={{0,16},{8,24},{16,0},{24,8},{1,17},{9,25},{17,1},{25,9},{2,18},{10... | collective-permute-start | bytes 1966088 | tf_op jit(solution)/shard_map/ppermute | solution.py:207
  38.7 1.4 %collective-permute-start.15 = (bf16[320,256]{1,0:T(8,128)(2,1)S(1)}, bf16[320,256]{1,0:T(8,128)(2,1)S(1)}, u32[]{:S(2)}, u32[]{:S(2)}) collective-permute-start(bf16[320,256]{1,0:T(8,128)(2,1)S(1)} %copy-done.31), channel_id=1, source_target_pairs={{0,4},{1,5},{2,6},{3,7},{4,0},{5,1},{6,2},{7,3},{8,12},{9,13},{10,... | collective-permute-start | bytes 491528 | tf_op jit(solution)/shard_map/ppermute | solution.py:207
  40.1 3.1 %collective-permute-start.16 = (bf16[320,256]{1,0:T(8,128)(2,1)S(1)}, bf16[320,256]{1,0:T(8,128)(2,1)S(1)}, u32[]{:S(2)}, u32[]{:S(2)}) collective-permute-start(bf16[320,256]{1,0:T(8,128)(2,1)S(1)} %copy-done.30), channel_id=1, source_target_pairs={{0,6},{1,7},{2,4},{3,5},{4,2},{5,3},{6,0},{7,1},{8,14},{9,15},{10,... | collective-permute-start | bytes 491528 | tf_op jit(solution)/shard_map/ppermute | solution.py:207
  43.3 21.6 %attend.1 = (bf16[256,4096]{1,0:T(8,128)(2,1)}, bf16[256,512]{1,0:T(8,128)(2,1)}, bf16[256,512]{1,0:T(8,128)(2,1)}, f32[256,512]{1,0:T(8,128)}, f32[256,512]{1,0...) custom-call(s32[1,1]{1,0:T(1,128)S(6)} %copy.27.length_ref, bf16[256,4096]{1,0:T(8,128)(2,1)} %bitcast.56, ...), custom_call_target="tpu_custom_call" | custom-call | flops 16106127360 | bytes 10000000 | tf_op jit(solution)/shard_map/attend/pallas_call | solution.py:91
  65.5 1.6 %collective-permute-done.19 = f32[256,512]{1,0:T(8,128)S(1)} collective-permute-done((f32[256,512]{1,0:T(8,128)}, f32[256,512]{1,0:T(8,128)S(1)}, u32[]{:S(2)}, u32[]{:S(2)}) %collective-permute-start.19) | collective-permute-done | bytes 524320 | tf_op jit(solution)/shard_map/ppermute | solution.py:207
  69.7 3.1 %collective-permute-start.22 = (bf16[64,512]{1,0:T(8,128)(2,1)S(1)}, bf16[64,512]{1,0:T(8,128)(2,1)S(1)}, u32[]{:S(2)}, u32[]{:S(2)}) collective-permute-start(bf16[64,512]{1,0:T(8,128)(2,1)S(1)} %get-tuple-element.124), channel_id=1, source_target_pairs={{0,6},{1,7},{2,4},{3,5},{4,2},{5,3},{6,0},{7,1},{8,14},{9,15},{10,... | collective-permute-start | bytes 196616 | tf_op jit(solution)/shard_map/ppermute | solution.py:207
  73.6 3.5 %collective-permute-done.21 = bf16[64,512]{1,0:T(8,128)(2,1)S(1)} collective-permute-done((bf16[64,512]{1,0:T(8,128)(2,1)S(1)}, bf16[64,512]{1,0:T(8,128)(2,1)S(1)}, u32[]{:S(2)}, u32[]{:S(2)}) %collective-permute-start.21) | collective-permute-done | bytes 65568 | tf_op jit(solution)/shard_map/ppermute | solution.py:207
  80.2 1.9 %collective-permute-start.26 = (bf16[64,512]{1,0:T(8,128)(2,1)S(1)}, bf16[64,512]{1,0:T(8,128)(2,1)S(1)}, u32[]{:S(2)}, u32[]{:S(2)}) collective-permute-start(bf16[64,512]{1,0:T(8,128)(2,1)S(1)} %fusion.refs_0_.refs_4_), channel_id=1, source_target_pairs={{0,6},{1,7},{2,4},{3,5},{4,2},{5,3},{6,0},{7,1},{8,14},{9,15},{10,... | collective-permute-start | bytes 196616 | tf_op jit(solution)/shard_map/ppermute | solution.py:207
  83.2 1.5 %collective-permute-start.27 = (bf16[64,512]{1,0:T(8,128)(2,1)S(1)}, bf16[64,512]{1,0:T(8,128)(2,1)S(1)}, u32[]{:S(2)}, u32[]{:S(2)}) collective-permute-start(bf16[64,512]{1,0:T(8,128)(2,1)S(1)} %fusion.refs_0_.refs_4_), channel_id=1, source_target_pairs={{0,8},{8,0},{16,24},{24,16},{1,9},{9,1},{17,25},{25,17},{2,10},{10... | collective-permute-start | bytes 196616 | tf_op jit(solution)/shard_map/ppermute | solution.py:207
  86.4 1.8 %collective-permute-start.29 = (bf16[64,512]{1,0:T(8,128)(2,1)S(1)}, bf16[64,512]{1,0:T(8,128)(2,1)S(1)}, u32[]{:S(2)}, u32[]{:S(2)}) collective-permute-start(bf16[64,512]{1,0:T(8,128)(2,1)S(1)} %fusion.refs_0_.refs_4_), channel_id=1, source_target_pairs={{0,24},{8,16},{16,8},{24,0},{1,25},{9,17},{17,9},{25,1},{2,26},{10... | collective-permute-start | bytes 196616 | tf_op jit(solution)/shard_map/ppermute | solution.py:207
  89.5 2.7 %collective-permute-done.29.refs_1_.refs_7_ = bf16[64,512]{1,0:T(8,128)(2,1)S(1)} collective-permute-done((bf16[64,512]{1,0:T(8,128)(2,1)S(1)}, bf16[64,512]{1,0:T(8,128)(2,1)S(1)}, u32[]{:S(2)}, u32[]{:S(2)}) %collective-permute-start.29) | collective-permute-done | bytes 65568 | tf_op jit(solution)/shard_map/ppermute | solution.py:207
  92.2 1.5 %collective-permute-start.32 = (bf16[3,64,512]{2,1,0:T(8,128)(2,1)S(1)}, bf16[3,64,512]{2,1,0:T(8,128)(2,1)S(1)}, u32[]{:S(2)}, u32[]{:S(2)}) collective-permute-start(bf16[3,64,512]{2,1,0:T(8,128)(2,1)S(1)} %pad_maximum_fusion.2.refs_8_), channel_id=1, source_target_pairs={{0,8},{8,0},{16,24},{24,16},{1,9},{9,1},{17,25},{25,17},{2,10},{10... | collective-permute-start | bytes 589832 | tf_op jit(solution)/shard_map/ppermute | solution.py:207
  95.7 4.2 %hidden_grad.1 = (bf16[64,5120]{1,0:T(8,128)(2,1)}, bf16[64,1280]{1,0:T(8,128)(2,1)}) custom-call(bf16[1280,512]{1,0:T(8,128)(2,1)} %own_ref.1, bf16[64,512]{1,0:T(8,128)(2,1)} %copy-done.2, bf16[64,512]{1,0:T(8,128)(2,1)} %copy-done.15, bf16[1280,256]{1,0:T(8,128)(2,1)} %copy-done.6, bf16[1280,256]{1,0:T(8,128)(2,1)} %copy-done.7, ...), custom_call_target="tpu_custom_call" | custom-call | flops 335544320 | bytes 3000000 | tf_op jit(solution)/shard_map/hidden_grad/pallas_call | solution.py:108
  100.5 2.0 %collective-permute-start.37 = (bf16[64,512]{1,0:T(8,128)(2,1)S(1)}, bf16[64,512]{1,0:T(8,128)(2,1)S(1)}, u32[]{:S(2)}, u32[]{:S(2)}) collective-permute-start(bf16[64,512]{1,0:T(8,128)(2,1)S(1)} %get-tuple-element.122), channel_id=1, source_target_pairs={{0,4},{1,5},{2,6},{3,7},{4,0},{5,1},{6,2},{7,3},{8,12},{9,13},{10,... | collective-permute-start | bytes 196616 | tf_op jit(solution)/shard_map/ppermute | solution.py:207
  102.5 1.9 %collective-permute-start.38 = (bf16[64,512]{1,0:T(8,128)(2,1)S(1)}, bf16[64,512]{1,0:T(8,128)(2,1)S(1)}, u32[]{:S(2)}, u32[]{:S(2)}) collective-permute-start(bf16[64,512]{1,0:T(8,128)(2,1)S(1)} %get-tuple-element.121), channel_id=1, source_target_pairs={{0,6},{1,7},{2,4},{3,5},{4,2},{5,3},{6,0},{7,1},{8,14},{9,15},{10,... | collective-permute-start | bytes 196616 | tf_op jit(solution)/shard_map/ppermute | solution.py:207
  104.5 1.6 %collective-permute-start.35 = (bf16[64,1280]{1,0:T(8,128)(2,1)}, bf16[64,1280]{1,0:T(8,128)(2,1)S(1)}, u32[]{:S(2)}, u32[]{:S(2)}) collective-permute-start(bf16[64,1280]{1,0:T(8,128)(2,1)} %get-tuple-element.101), channel_id=1, source_target_pairs={{0,24},{8,16},{16,8},{24,0},{1,25},{9,17},{17,9},{25,1},{2,26},{10... | collective-permute-start | bytes 491528 | tf_op jit(solution)/shard_map/ppermute | solution.py:207
  106.1 2.5 %collective-permute-done.38 = bf16[64,512]{1,0:T(8,128)(2,1)S(1)} collective-permute-done((bf16[64,512]{1,0:T(8,128)(2,1)S(1)}, bf16[64,512]{1,0:T(8,128)(2,1)S(1)}, u32[]{:S(2)}, u32[]{:S(2)}) %collective-permute-start.38) | collective-permute-done | bytes 65568 | tf_op jit(solution)/shard_map/ppermute | solution.py:207
  109.3 2.6 %weight_grad.3 = f32[160,512]{1,0:T(8,128)} custom-call(bf16[320,256]{1,0:T(8,128)(2,1)} %get-tuple-element.102.refs_0_, bf16[320,256]{1,0:T(8,128)(2,1)} %copy-done.12, bf16[320,256]{1,0:T(8,128)(2,1)} %copy-done.13, bf16[320,256]{1,0:T(8,128)(2,1)} %copy-done.14, bf16[64,512]{1,0:T(8,128)(2,1)} %copy-done.2, bf16[64,512]{1,0:T(8,128)(2,1)} %copy-done.17, ...), custom_call_target="tpu_custom_call" | custom-call | flops 167772160 | bytes 3000000 | tf_op jit(solution)/shard_map/weight_grad/pallas_call | solution.py:108
  111.9 2.6 %weight_grad.2 = f32[160,512]{1,0:T(8,128)} custom-call(bf16[320,256]{1,0:T(8,128)(2,1)} %get-tuple-element.102.refs_0_, bf16[320,256]{1,0:T(8,128)(2,1)} %copy-done.12, bf16[320,256]{1,0:T(8,128)(2,1)} %copy-done.13, bf16[320,256]{1,0:T(8,128)(2,1)} %copy-done.14, bf16[64,512]{1,0:T(8,128)(2,1)} %copy-done.2, bf16[64,512]{1,0:T(8,128)(2,1)} %copy-done.17, ...), custom_call_target="tpu_custom_call" | custom-call | flops 167772160 | bytes 3000000 | tf_op jit(solution)/shard_map/weight_grad/pallas_call | solution.py:108
  115.1 1.7 %add.72 = f32[160,512]{1,0:T(8,128)} add(f32[160,512]{1,0:T(8,128)} %weight_grad.2, f32[160,512]{1,0:T(8,128)S(1)} %collective-permute-done.39) | non-fusion elementwise | flops 81920 | bytes 983040 | tf_op jit(solution)/shard_map/add | solution.py:300
  (153 shorter events, 20.9 us)
Async XLA Ops:
  2.7 9.1 %collective-permute-start.2 = (bf16[64,1280]{1,0:T(8,128)(2,1)}, bf16[64,1280]{1,0:T(8,128)(2,1)S(1)}, u32[]{:S(2)}, u32[]{:S(2)}) collective-permute-start(bf16[64,1280]{1,0:T(8,128)(2,1)} %get-tuple-element.65), channel_id=1, source_target_pairs={{0,24},{8,16},{16,8},{24,0},{1,25},{9,17},{17,9},{25,1},{2,26},{10... | collective-permute-start | bytes 491528 | tf_op jit(solution)/shard_map/ppermute | solution.py:207
  6.6 8.8 %collective-permute-start = (bf16[64,1280]{1,0:T(8,128)(2,1)}, bf16[64,1280]{1,0:T(8,128)(2,1)S(1)}, u32[]{:S(2)}, u32[]{:S(2)}) collective-permute-start(bf16[64,1280]{1,0:T(8,128)(2,1)} %get-tuple-element.63), channel_id=1, source_target_pairs={{0,8},{8,0},{16,24},{24,16},{1,9},{9,1},{17,25},{25,17},{2,10},{10... | collective-permute-start | bytes 491528 | tf_op jit(solution)/shard_map/ppermute | solution.py:207
  7.1 10.1 %collective-permute-start.1 = (bf16[64,1280]{1,0:T(8,128)(2,1)}, bf16[64,1280]{1,0:T(8,128)(2,1)S(1)}, u32[]{:S(2)}, u32[]{:S(2)}) collective-permute-start(bf16[64,1280]{1,0:T(8,128)(2,1)} %get-tuple-element.64), channel_id=1, source_target_pairs={{0,16},{8,24},{16,0},{24,8},{1,17},{9,25},{17,1},{25,9},{2,18},{10... | collective-permute-start | bytes 491528 | tf_op jit(solution)/shard_map/ppermute | solution.py:207
  12.2 12.4 %collective-permute-start.5 = (f32[64,512]{1,0:T(8,128)S(1)}, f32[64,512]{1,0:T(8,128)S(1)}, u32[]{:S(2)}, u32[]{:S(2)}) collective-permute-start(f32[64,512]{1,0:T(8,128)S(1)} %fusion.12), channel_id=1, source_target_pairs={{0,24},{8,16},{16,8},{24,0},{1,25},{9,17},{17,9},{25,1},{2,26},{10... | collective-permute-start | bytes 393224 | tf_op jit(solution)/shard_map/ppermute | solution.py:207
  15.7 9.1 %collective-permute-start.3 = (f32[64,512]{1,0:T(8,128)S(1)}, f32[64,512]{1,0:T(8,128)S(1)}, u32[]{:S(2)}, u32[]{:S(2)}) collective-permute-start(f32[64,512]{1,0:T(8,128)S(1)} %fusion.10), channel_id=1, source_target_pairs={{0,8},{8,0},{16,24},{24,16},{1,9},{9,1},{17,25},{25,17},{2,10},{10... | collective-permute-start | bytes 393224 | tf_op jit(solution)/shard_map/ppermute | solution.py:207
  17.6 7.2 %collective-permute-start.4 = (f32[64,512]{1,0:T(8,128)S(1)}, f32[64,512]{1,0:T(8,128)S(1)}, u32[]{:S(2)}, u32[]{:S(2)}) collective-permute-start(f32[64,512]{1,0:T(8,128)S(1)} %fusion.11), channel_id=1, source_target_pairs={{0,16},{8,24},{16,0},{24,8},{1,17},{9,25},{17,1},{25,9},{2,18},{10... | collective-permute-start | bytes 393224 | tf_op jit(solution)/shard_map/ppermute | solution.py:207
  18.2 11.5 %collective-permute-start.10 = (bf16[64,512]{1,0:T(8,128)(2,1)S(1)}, bf16[64,512]{1,0:T(8,128)(2,1)S(1)}, u32[]{:S(2)}, u32[]{:S(2)}) collective-permute-start(bf16[64,512]{1,0:T(8,128)(2,1)S(1)} %bitcast.52), channel_id=1, source_target_pairs={{0,2},{1,3},{2,0},{3,1},{4,6},{5,7},{6,4},{7,5},{8,10},{9,11},{10,... | collective-permute-start | bytes 196616 | tf_op jit(solution)/shard_map/ppermute | solution.py:207
  19.7 10.2 %collective-permute-start.11 = (bf16[64,512]{1,0:T(8,128)(2,1)S(1)}, bf16[64,512]{1,0:T(8,128)(2,1)S(1)}, u32[]{:S(2)}, u32[]{:S(2)}) collective-permute-start(bf16[64,512]{1,0:T(8,128)(2,1)S(1)} %bitcast.53), channel_id=1, source_target_pairs={{0,4},{1,5},{2,6},{3,7},{4,0},{5,1},{6,2},{7,3},{8,12},{9,13},{10,... | collective-permute-start | bytes 196616 | tf_op jit(solution)/shard_map/ppermute | solution.py:207
  24.6 6.3 %collective-permute-start.12 = (bf16[64,512]{1,0:T(8,128)(2,1)S(1)}, bf16[64,512]{1,0:T(8,128)(2,1)S(1)}, u32[]{:S(2)}, u32[]{:S(2)}) collective-permute-start(bf16[64,512]{1,0:T(8,128)(2,1)S(1)} %bitcast.54), channel_id=1, source_target_pairs={{0,6},{1,7},{2,4},{3,5},{4,2},{5,3},{6,0},{7,1},{8,14},{9,15},{10,... | collective-permute-start | bytes 196616 | tf_op jit(solution)/shard_map/ppermute | solution.py:207
  26.2 7.5 %collective-permute-start.7 = (bf16[64,512]{1,0:T(8,128)(2,1)S(1)}, bf16[64,512]{1,0:T(8,128)(2,1)S(1)}, u32[]{:S(2)}, u32[]{:S(2)}) collective-permute-start(bf16[64,512]{1,0:T(8,128)(2,1)S(1)} %fusion.2.refs_0_), channel_id=1, source_target_pairs={{0,4},{1,5},{2,6},{3,7},{4,0},{5,1},{6,2},{7,3},{8,12},{9,13},{10,... | collective-permute-start | bytes 196616 | tf_op jit(solution)/shard_map/ppermute | solution.py:207
  29.7 6.1 %collective-permute-start.8 = (bf16[64,512]{1,0:T(8,128)(2,1)S(1)}, bf16[64,512]{1,0:T(8,128)(2,1)S(1)}, u32[]{:S(2)}, u32[]{:S(2)}) collective-permute-start(bf16[64,512]{1,0:T(8,128)(2,1)S(1)} %fusion.2.refs_0_), channel_id=1, source_target_pairs={{0,6},{1,7},{2,4},{3,5},{4,2},{5,3},{6,0},{7,1},{8,14},{9,15},{10,... | collective-permute-start | bytes 196616 | tf_op jit(solution)/shard_map/ppermute | solution.py:207
  30.9 7.8 %collective-permute-start.13 = (bf16[256,512]{1,0:T(8,128)(2,1)S(1)}, bf16[256,512]{1,0:T(8,128)(2,1)S(1)}, u32[]{:S(2)}, u32[]{:S(2)}) collective-permute-start(bf16[256,512]{1,0:T(8,128)(2,1)S(1)} %pad_maximum_fusion.1), channel_id=1, source_target_pairs={{0,1},{1,0},{2,3},{3,2},{4,5},{5,4},{6,7},{7,6},{8,9},{9,8},{10,11... | collective-permute-start | bytes 786440 | tf_op jit(solution)/shard_map/ppermute | solution.py:207
  36.5 28.4 %collective-permute-start.17 = (bf16[1280,256]{1,0:T(8,128)(2,1)S(1)}, bf16[1280,256]{1,0:T(8,128)(2,1)S(1)}, u32[]{:S(2)}, u32[]{:S(2)}) collective-permute-start(bf16[1280,256]{1,0:T(8,128)(2,1)S(1)} %constant_dynamic-slice_fusion), channel_id=1, source_target_pairs={{0,8},{8,0},{16,24},{24,16},{1,9},{9,1},{17,25},{25,17},{2,10},{10... | collective-permute-start | bytes 1966088 | tf_op jit(solution)/shard_map/ppermute | solution.py:207
  37.1 27.8 %collective-permute-start.18 = (bf16[1280,256]{1,0:T(8,128)(2,1)S(1)}, bf16[1280,256]{1,0:T(8,128)(2,1)S(1)}, u32[]{:S(2)}, u32[]{:S(2)}) collective-permute-start(bf16[1280,256]{1,0:T(8,128)(2,1)S(1)} %constant_dynamic-slice_fusion), channel_id=1, source_target_pairs={{0,16},{8,24},{16,0},{24,8},{1,17},{9,25},{17,1},{25,9},{2,18},{10... | collective-permute-start | bytes 1966088 | tf_op jit(solution)/shard_map/ppermute | solution.py:207
  38.7 26.2 %collective-permute-start.14 = (bf16[320,256]{1,0:T(8,128)(2,1)S(1)}, bf16[320,256]{1,0:T(8,128)(2,1)S(1)}, u32[]{:S(2)}, u32[]{:S(2)}) collective-permute-start(bf16[320,256]{1,0:T(8,128)(2,1)S(1)} %copy-done.32), channel_id=1, source_target_pairs={{0,2},{1,3},{2,0},{3,1},{4,6},{5,7},{6,4},{7,5},{8,10},{9,11},{10,... | collective-permute-start | bytes 491528 | tf_op jit(solution)/shard_map/ppermute | solution.py:207
  38.7 26.2 %collective-permute-start.15 = (bf16[320,256]{1,0:T(8,128)(2,1)S(1)}, bf16[320,256]{1,0:T(8,128)(2,1)S(1)}, u32[]{:S(2)}, u32[]{:S(2)}) collective-permute-start(bf16[320,256]{1,0:T(8,128)(2,1)S(1)} %copy-done.31), channel_id=1, source_target_pairs={{0,4},{1,5},{2,6},{3,7},{4,0},{5,1},{6,2},{7,3},{8,12},{9,13},{10,... | collective-permute-start | bytes 491528 | tf_op jit(solution)/shard_map/ppermute | solution.py:207
  40.1 24.8 %collective-permute-start.16 = (bf16[320,256]{1,0:T(8,128)(2,1)S(1)}, bf16[320,256]{1,0:T(8,128)(2,1)S(1)}, u32[]{:S(2)}, u32[]{:S(2)}) collective-permute-start(bf16[320,256]{1,0:T(8,128)(2,1)S(1)} %copy-done.30), channel_id=1, source_target_pairs={{0,6},{1,7},{2,4},{3,5},{4,2},{5,3},{6,0},{7,1},{8,14},{9,15},{10,... | collective-permute-start | bytes 491528 | tf_op jit(solution)/shard_map/ppermute | solution.py:207
  65.0 7.7 %collective-permute-start.23 = (f32[256,512]{1,0:T(8,128)}, f32[256,512]{1,0:T(8,128)S(1)}, u32[]{:S(2)}, u32[]{:S(2)}) collective-permute-start(f32[256,512]{1,0:T(8,128)} %get-tuple-element.87), channel_id=1, source_target_pairs={{0,1},{1,0},{2,3},{3,2},{4,5},{5,4},{6,7},{7,6},{8,9},{9,8},{10,11... | collective-permute-start | bytes 1572872 | tf_op jit(solution)/shard_map/ppermute | solution.py:207
  68.4 8.6 %collective-permute-start.21 = (bf16[64,512]{1,0:T(8,128)(2,1)S(1)}, bf16[64,512]{1,0:T(8,128)(2,1)S(1)}, u32[]{:S(2)}, u32[]{:S(2)}) collective-permute-start(bf16[64,512]{1,0:T(8,128)(2,1)S(1)} %get-tuple-element.125), channel_id=1, source_target_pairs={{0,4},{1,5},{2,6},{3,7},{4,0},{5,1},{6,2},{7,3},{8,12},{9,13},{10,... | collective-permute-start | bytes 196616 | tf_op jit(solution)/shard_map/ppermute | solution.py:207
  69.7 7.3 %collective-permute-start.22 = (bf16[64,512]{1,0:T(8,128)(2,1)S(1)}, bf16[64,512]{1,0:T(8,128)(2,1)S(1)}, u32[]{:S(2)}, u32[]{:S(2)}) collective-permute-start(bf16[64,512]{1,0:T(8,128)(2,1)S(1)} %get-tuple-element.124), channel_id=1, source_target_pairs={{0,6},{1,7},{2,4},{3,5},{4,2},{5,3},{6,0},{7,1},{8,14},{9,15},{10,... | collective-permute-start | bytes 196616 | tf_op jit(solution)/shard_map/ppermute | solution.py:207
  72.8 15.4 %collective-permute-start.30 = (bf16[1280,256]{1,0:T(8,128)(2,1)S(1)}, bf16[1280,256]{1,0:T(8,128)(2,1)S(1)}, u32[]{:S(2)}, u32[]{:S(2)}) collective-permute-start(bf16[1280,256]{1,0:T(8,128)(2,1)S(1)} %collective-permute-done.17.refs_2_), channel_id=1, source_target_pairs={{0,1},{1,0},{2,3},{3,2},{4,5},{5,4},{6,7},{7,6},{8,9},{9,8},{10,11... | collective-permute-start | bytes 1966088 | tf_op jit(solution)/shard_map/ppermute | solution.py:207
  72.8 15.4 %collective-permute-start.31 = (bf16[1280,256]{1,0:T(8,128)(2,1)S(1)}, bf16[1280,256]{1,0:T(8,128)(2,1)}, u32[]{:S(2)}, u32[]{:S(2)}) collective-permute-start(bf16[1280,256]{1,0:T(8,128)(2,1)S(1)} %collective-permute-done.18.refs_3_), channel_id=1, source_target_pairs={{0,1},{1,0},{2,3},{3,2},{4,5},{5,4},{6,7},{7,6},{8,9},{9,8},{10,11... | collective-permute-start | bytes 1966088 | tf_op jit(solution)/shard_map/ppermute | solution.py:207
  79.0 6.2 %collective-permute-start.25 = (bf16[64,512]{1,0:T(8,128)(2,1)S(1)}, bf16[64,512]{1,0:T(8,128)(2,1)S(1)}, u32[]{:S(2)}, u32[]{:S(2)}) collective-permute-start(bf16[64,512]{1,0:T(8,128)(2,1)S(1)} %fusion.refs_0_.refs_4_), channel_id=1, source_target_pairs={{0,4},{1,5},{2,6},{3,7},{4,0},{5,1},{6,2},{7,3},{8,12},{9,13},{10,... | collective-permute-start | bytes 196616 | tf_op jit(solution)/shard_map/ppermute | solution.py:207
  80.2 6.2 %collective-permute-start.26 = (bf16[64,512]{1,0:T(8,128)(2,1)S(1)}, bf16[64,512]{1,0:T(8,128)(2,1)S(1)}, u32[]{:S(2)}, u32[]{:S(2)}) collective-permute-start(bf16[64,512]{1,0:T(8,128)(2,1)S(1)} %fusion.refs_0_.refs_4_), channel_id=1, source_target_pairs={{0,6},{1,7},{2,4},{3,5},{4,2},{5,3},{6,0},{7,1},{8,14},{9,15},{10,... | collective-permute-start | bytes 196616 | tf_op jit(solution)/shard_map/ppermute | solution.py:207
  86.4 5.8 %collective-permute-start.29 = (bf16[64,512]{1,0:T(8,128)(2,1)S(1)}, bf16[64,512]{1,0:T(8,128)(2,1)S(1)}, u32[]{:S(2)}, u32[]{:S(2)}) collective-permute-start(bf16[64,512]{1,0:T(8,128)(2,1)S(1)} %fusion.refs_0_.refs_4_), channel_id=1, source_target_pairs={{0,24},{8,16},{16,8},{24,0},{1,25},{9,17},{17,9},{25,1},{2,26},{10... | collective-permute-start | bytes 196616 | tf_op jit(solution)/shard_map/ppermute | solution.py:207
  92.2 10.3 %collective-permute-start.32 = (bf16[3,64,512]{2,1,0:T(8,128)(2,1)S(1)}, bf16[3,64,512]{2,1,0:T(8,128)(2,1)S(1)}, u32[]{:S(2)}, u32[]{:S(2)}) collective-permute-start(bf16[3,64,512]{2,1,0:T(8,128)(2,1)S(1)} %pad_maximum_fusion.2.refs_8_), channel_id=1, source_target_pairs={{0,8},{8,0},{16,24},{24,16},{1,9},{9,1},{17,25},{25,17},{2,10},{10... | collective-permute-start | bytes 589832 | tf_op jit(solution)/shard_map/ppermute | solution.py:207
  93.7 10.8 %collective-permute-start.33 = (bf16[3,64,512]{2,1,0:T(8,128)(2,1)S(1)}, bf16[3,64,512]{2,1,0:T(8,128)(2,1)S(1)}, u32[]{:S(2)}, u32[]{:S(2)}) collective-permute-start(bf16[3,64,512]{2,1,0:T(8,128)(2,1)S(1)} %pad_maximum_fusion.2.refs_8_), channel_id=1, source_target_pairs={{0,16},{8,24},{16,0},{24,8},{1,17},{9,25},{17,1},{25,9},{2,18},{10... | collective-permute-start | bytes 589832 | tf_op jit(solution)/shard_map/ppermute | solution.py:207
  94.3 10.1 %collective-permute-start.34 = (bf16[3,64,512]{2,1,0:T(8,128)(2,1)S(1)}, bf16[3,64,512]{2,1,0:T(8,128)(2,1)S(1)}, u32[]{:S(2)}, u32[]{:S(2)}) collective-permute-start(bf16[3,64,512]{2,1,0:T(8,128)(2,1)S(1)} %pad_maximum_fusion.2.refs_8_), channel_id=1, source_target_pairs={{0,24},{8,16},{16,8},{24,0},{1,25},{9,17},{17,9},{25,1},{2,26},{10... | collective-permute-start | bytes 589832 | tf_op jit(solution)/shard_map/ppermute | solution.py:207
  100.0 6.1 %collective-permute-start.36 = (bf16[64,512]{1,0:T(8,128)(2,1)S(1)}, bf16[64,512]{1,0:T(8,128)(2,1)S(1)}, u32[]{:S(2)}, u32[]{:S(2)}) collective-permute-start(bf16[64,512]{1,0:T(8,128)(2,1)S(1)} %get-tuple-element.120), channel_id=1, source_target_pairs={{0,2},{1,3},{2,0},{3,1},{4,6},{5,7},{6,4},{7,5},{8,10},{9,11},{10,... | collective-permute-start | bytes 196616 | tf_op jit(solution)/shard_map/ppermute | solution.py:207
  100.5 5.6 %collective-permute-start.37 = (bf16[64,512]{1,0:T(8,128)(2,1)S(1)}, bf16[64,512]{1,0:T(8,128)(2,1)S(1)}, u32[]{:S(2)}, u32[]{:S(2)}) collective-permute-start(bf16[64,512]{1,0:T(8,128)(2,1)S(1)} %get-tuple-element.122), channel_id=1, source_target_pairs={{0,4},{1,5},{2,6},{3,7},{4,0},{5,1},{6,2},{7,3},{8,12},{9,13},{10,... | collective-permute-start | bytes 196616 | tf_op jit(solution)/shard_map/ppermute | solution.py:207
  102.5 6.1 %collective-permute-start.38 = (bf16[64,512]{1,0:T(8,128)(2,1)S(1)}, bf16[64,512]{1,0:T(8,128)(2,1)S(1)}, u32[]{:S(2)}, u32[]{:S(2)}) collective-permute-start(bf16[64,512]{1,0:T(8,128)(2,1)S(1)} %get-tuple-element.121), channel_id=1, source_target_pairs={{0,6},{1,7},{2,4},{3,5},{4,2},{5,3},{6,0},{7,1},{8,14},{9,15},{10,... | collective-permute-start | bytes 196616 | tf_op jit(solution)/shard_map/ppermute | solution.py:207
  104.5 10.0 %collective-permute-start.35 = (bf16[64,1280]{1,0:T(8,128)(2,1)}, bf16[64,1280]{1,0:T(8,128)(2,1)S(1)}, u32[]{:S(2)}, u32[]{:S(2)}) collective-permute-start(bf16[64,1280]{1,0:T(8,128)(2,1)} %get-tuple-element.101), channel_id=1, source_target_pairs={{0,24},{8,16},{16,8},{24,0},{1,25},{9,17},{17,9},{25,1},{2,26},{10... | collective-permute-start | bytes 491528 | tf_op jit(solution)/shard_map/ppermute | solution.py:207
  (41 other events, 352.4 us)

commit v8 on v7

--- a/solution.py
+++ b/solution.py
@@ -118,18 +118,31 @@
     return list(results)
 
 
-def split_kernel(hidden_ref, *piece_refs):
+def split_kernel(hidden_ref, *refs):
+    *piece_refs, arrived = refs
     depth = piece_refs[0].shape[1]
     group = lax.axis_index("group")
+    copies = []
     for k, piece_ref in enumerate(piece_refs):
         start = pl.multiple_of((group ^ k) * depth, depth)
-        piece_ref[...] = hidden_ref[:, pl.ds(start, depth)]
+        copies.append(pltpu.make_async_copy(hidden_ref.at[:, pl.ds(start, depth)], piece_ref, arrived.at[k]))
+        copies[-1].start()
+    for copy in copies:
+        copy.wait()
 
 
 def split_pass(hidden, groups):
     tokens, width = hidden.shape
-    outs = [((tokens, width // groups), hidden.dtype)] * groups
-    return in_vmem(split_kernel, "split_hidden", outs, [hidden])
+    anywhere = pl.BlockSpec(memory_space=pl.ANY)
+    return list(pl.pallas_call(
+        split_kernel,
+        in_specs=[anywhere],
+        out_specs=[anywhere] * groups,
+        out_shape=[jax.ShapeDtypeStruct((tokens, width // groups), hidden.dtype)] * groups,
+        scratch_shapes=[pltpu.SemaphoreType.DMA((groups,))],
+        compiler_params=PARAMS,
+        name="split_hidden",
+    )(hidden))
 
 
 def turn_kernel(groups, *refs):
@@ -176,31 +189,38 @@
         place(k, block.T.astype(BF16))
 
 
-def hidden_pass(first, own, near, far, across):
-    tokens, kv_width = first[0].shape
+def hidden_pass(key_pre_grad, first, own, near, far):
+    tokens, kv_width = key_pre_grad.shape
     depth = own.shape[0]
-    outs = [((tokens, len(first) * depth), BF16)] + [((tokens, depth), BF16)] * len(across)
-    arrays = [own, first[0], *[first[k] for k in across], *near.values(), *far.values()]
-    kernel = partial(hidden_kernel, list(near), across)
-    return in_vmem(kernel, "hidden_grad", outs, arrays, tokens * depth * kv_width * len(first))
-
-
-def weight_kernel(chips, groups, second, *refs):
-    taken, first, rest, out_ref = refs[:chips], refs[chips : chips + groups], refs[chips + groups : -1], refs[-1]
-    half = out_ref.shape[0]
-    start = half if second else 0
-    columns = jnp.concatenate([ref[start : start + half] for ref in taken], axis=1)
-    grads = [ref[...] for ref in first] + [ref[p] for p in range(chips - 1) for ref in rest]
-    out_ref[...] = dot(columns, jnp.concatenate(grads, axis=0))
-
-
-def weight_pass(taken, first, rest, second):
+    groups = 1 + len(first) + len(near)
+    outs = [((tokens, groups * depth), BF16)] + [((tokens, depth), BF16)] * len(first)
+    arrays = [own, key_pre_grad, *first.values(), *near.values(), *far.values()]
+    kernel = partial(hidden_kernel, list(near), list(first))
+    return in_vmem(kernel, "hidden_grad", outs, arrays, tokens * depth * kv_width * groups)
+
+
+def weight_pass(taken, blocks):
     rows, tokens = taken[0].shape
-    kv_width = first[0].shape[-1]
-    kernel = partial(weight_kernel, len(taken), len(first), second)
-    macs = rows // 2 * kv_width * tokens * len(taken)
-    outs = [((rows // 2, kv_width), F32)]
-    return in_vmem(kernel, "weight_grad", outs, [*taken, *first, *rest], macs)[0]
+    chips, groups = len(taken), len(blocks)
+    token_rows = tokens // groups
+    kv_width = blocks[0][0].shape[1]
+    counts = [len(arrays) for arrays in blocks]
+
+    def kernel(*refs):
+        columns = jnp.concatenate([ref[...] for ref in refs[:chips]], axis=1)
+        parts = [jnp.concatenate([ref[...] for ref in arrays], axis=0) for arrays in nested(refs[chips:-2], counts)]
+        grads = [part[p * token_rows : (p + 1) * token_rows] for p in range(chips) for part in parts]
+        product = dot(columns, jnp.concatenate(grads, axis=0))
+        refs[-2][...], refs[-1][...] = product[: rows // 2], product[rows // 2 :]
+
+    outs = [((rows // 2, kv_width), F32)] * 2
+    arrays = [*taken, *[array for arrays in blocks for array in arrays]]
+    return in_vmem(kernel, "weight_grad", outs, arrays, rows * kv_width * tokens * chips)
+
+
+def nested(items, counts):
+    items = iter(items)
+    return [[next(items) for _ in range(count)] for count in counts]
 
 
 def swap(array, axis, size, distance):
@@ -223,13 +243,14 @@
     return near + swap(far, "resp", size, 1)
 
 
-def chip_sum(near, size):
+def chip_parts(near, size):
     rows = near.shape[0] // (size // 2)
-    total = near[:rows]
-    for p in range(1, size // 2):
-        piece = near[p * rows : (p + 1) * rows].astype(BF16)
-        total = total + swap(piece, "resp", size, 2 * p).astype(F32)
-    return total
+    pieces = [near[p * rows : (p + 1) * rows] for p in range(size // 2)]
+    return pieces[:1] + [swap(pieces[p].astype(BF16), "resp", size, 2 * p) for p in range(1, size // 2)]
+
+
+def total(parts):
+    return sum(part.astype(F32) for part in parts[1:]) + parts[0]
 
 
 def shards(
@@ -274,33 +295,38 @@
     )
     key_sums, far, *both = together(key_sums, far, *taken, *weight_near)
     taken, weight_near = both[:chips], both[chips:]
-    key_sums = chip_sum(pair_sum(key_sums, far, responses), responses)
+    key_sums = total(chip_parts(pair_sum(key_sums, far, responses), responses))
     value_sums = pair_sum(value_sums, value_far, responses)
-    key_sums, value_sums = together(key_sums, value_sums)
+    weight_far = [swap(piece, "resp", responses, 1) for piece in weight_near]
+    key_sums, value_sums, *weight_far = together(key_sums, value_sums, *weight_far)
     _, pullback = jax.vjp(lambda values: norm_keys(values, key_gain), key_pre)
     key_pre_grad = pullback(key_sums)[0].astype(BF16)
 
-    first = [key_pre_grad] + [swap(key_pre_grad, "group", groups, k) for k in range(1, groups)]
-    grads = spread_near(key_pre_grad, responses)[1:]
-    weight_far = [swap(piece, "resp", responses, 1) for piece in weight_near]
-    block, *both = together(jnp.stack(grads, axis=0), *first, *weight_far)
-    first, weight_far = both[:groups], both[groups:]
-    rest = [block] + [swap(block, "group", groups, k) for k in range(1, groups)]
-
+    first = {k: swap(key_pre_grad, "group", groups, k) for k in across}
+    grads = spread_near(key_pre_grad, responses)
     grad_hidden, *parts = hidden_pass(
-        first, key_matrix, dict(zip(beside, weight_near)), dict(zip(beside, weight_far)), across
-    )
+        key_pre_grad, first, key_matrix, dict(zip(beside, weight_near)), dict(zip(beside, weight_far))
+    )
+
+    grad_hidden, *both = together(grad_hidden, *parts, *grads)
+    parts, grads = both[: len(parts)], both[len(parts) :]
+    some, every = jnp.concatenate(grads[1:], axis=0), jnp.concatenate(grads, axis=0)
+    blocks = [[every]] + [None] * (groups - 1)
+    for k in beside:
+        blocks[k] = [swap(every, "group", groups, k)]
+    for k in across:
+        blocks[k] = [first[k], swap(some, "group", groups, k)]
     grad_hidden, value_sums = together(grad_hidden, value_sums)
-    value_sums = chip_sum(value_sums, responses)
-    grad_hidden, *both = together(grad_hidden, *parts, *rest)
-    parts, rest = both[: len(parts)], both[len(parts) :]
-    other = weight_pass(taken, first, rest, True)
-    other, value_sums = together(other, value_sums)
-    other = swap(other, "resp", responses, 1)
-    grad_weight = weight_pass(taken, first, rest, False) + other
+    value_parts = chip_parts(value_sums, responses)
+    for k in across:
+        *parts, blocks[k][-1] = together(*parts, blocks[k][-1])
+    parts = [swap(part, "group", groups, k) for k, part in zip(across, parts)]
+    mine, other, *value_parts = together(*weight_pass(taken, blocks), *value_parts)
+    value_sums = total(value_parts)
+    grad_weight = mine + swap(other, "resp", responses, 1)
     for k, part in zip(across, parts):
         start = (lax.axis_index("group") ^ k) * depth
-        grad_hidden = lax.dynamic_update_slice(grad_hidden, swap(part, "group", groups, k), (0, start))
+        grad_hidden = lax.dynamic_update_slice(grad_hidden, part, (0, start))
     return (
         grad_hidden[None],
         grad_weight,

time: 117 us -> 130 us (1.11)
  Pallas kernels: 35.3 us -> 51.6 us
  waiting for transfers between devices: 22.6 us -> 19.5 us
  starting transfers between devices: 48.6 us -> 45.8 us
  local copies, waits for them, and re-layouts: 1.6 us -> 3.83 us
    pallas_call x0 -> x1, Pallas kernels: none -> 21 us  [split_pass(): pl.pallas_call(split_kernel, in_specs=[anywhere], out_specs=[anywhere] *...]
    pallas_call x5 -> x3, Pallas kernels: 13.7 us -> 9.23 us  [in_vmem(): pl.pallas_call(kernel, in_specs=[whole] * len(arrays), out_specs=[whole]...]
    ppermute x40 -> x38, waiting for transfers between devices: 22.6 us -> 19.5 us  [swap(): return lax.ppermute(array, axis, [(i, i ^ distance) for i in range(size)])]
    ppermute x40 -> x38, starting transfers between devices: 48.6 us -> 45.8 us  [swap(): return lax.ppermute(array, axis, [(i, i ^ distance) for i in range(size)])]
    unnamed x66 -> x65, local copies, waits for them, and re-layouts: 0.14 us -> 2.35 us
  transfers between devices with their start and end apart: 40 -> 38, of which waited for: 14 -> 10; matrix products, arithmetic and copies ran while one was open for 6% -> 5% of each run, Pallas kernels for 28% -> 24%
where the time goes in v8:
time: 130 us
  Pallas kernels  51.6 us (40%)
  starting transfers between devices  45.8 us (35%)
  waiting for transfers between devices  19.5 us (15%)
  other arithmetic  4.14 us (3%)
  local copies, waits for them, and re-layouts  3.83 us (3%)
  matrix products  2.74 us (2%)
  between operations  1.92 us (1%)
    ppermute x38, starting transfers between devices, swap(): return lax.ppermute(array, axis, [(i, i ^ distance) for i in range(size)])  45.8 us
    pallas_call x1, Pallas kernels, attend(): pl.pallas_call(partial(attend_kernel, len(key_pieces)), grid=(kv_heads,),...  21.4 us
    pallas_call x1, Pallas kernels, split_pass(): pl.pallas_call(split_kernel, in_specs=[anywhere], out_specs=[anywhere] *...  21 us
    ppermute x38, waiting for transfers between devices, swap(): return lax.ppermute(array, axis, [(i, i ^ distance) for i in range(size)])  19.5 us
    pallas_call x3, Pallas kernels, in_vmem(): pl.pallas_call(kernel, in_specs=[whole] * len(arrays), out_specs=[whole]...  9.23 us
    dot_general x4, matrix products, dot(): return lax.dot_general(left, right, dims, preferred_element_type=F32)  2.74 us
  transfers between devices with their start and end apart: 38, of which 10 were waited for; matrix products, arithmetic and copies ran while one was open for 5% of the time, Pallas kernels for 24%

profile of v8, /device:TPU:0, one launch (start us, length us, event | category | flops | bytes accessed | tf_op | source)
XLA Modules:
  0.0 129.6 jit_solution(11053316168662126192)
XLA Ops:
  0.6 21.0 %split_hidden.1 = (bf16[64,1280]{1,0:T(8,128)(2,1)}, bf16[64,1280]{1,0:T(8,128)(2,1)}, bf16[64,1280]{1,0:T(8,128)(2,1)}, bf16[64,1280]{1,0:T(8,128)(2,1)}) custom-call(bf16[64,5120]{1,0:T(8,128)(2,1)} %bitcast.41), custom_call_target="tpu_custom_call" | custom-call | tf_op jit(solution)/shard_map/split_hidden/pallas_call | solution.py:137
  21.7 4.0 %collective-permute-start.2 = (bf16[64,1280]{1,0:T(8,128)(2,1)}, bf16[64,1280]{1,0:T(8,128)(2,1)S(1)}, u32[]{:S(2)}, u32[]{:S(2)}) collective-permute-start(bf16[64,1280]{1,0:T(8,128)(2,1)} %get-tuple-element.68), channel_id=1, source_target_pairs={{0,24},{8,16},{16,8},{24,0},{1,25},{9,17},{17,9},{25,1},{2,26},{10... | collective-permute-start | bytes 491528 | tf_op jit(solution)/shard_map/ppermute | solution.py:227
  26.3 1.7 %fusion.8 = f32[64,512]{1,0:T(8,128)S(1)} fusion(bf16[64,1280]{1,0:T(8,128)(2,1)} %get-tuple-element.65.refs_0_, bf16[1280,512]{1,0:T(8,128)(2,1)} %own_ref.1), kind=kOutput, calls=%fused_computation.29 | convolution fusion | flops 83886080 | bytes 1605632 | tf_op jit(solution)/shard_map/dot_general | solution.py:23
  28.1 2.8 %collective-permute-done.2.refs_3_ = bf16[64,1280]{1,0:T(8,128)(2,1)S(1)} collective-permute-done((bf16[64,1280]{1,0:T(8,128)(2,1)}, bf16[64,1280]{1,0:T(8,128)(2,1)S(1)}, u32[]{:S(2)}, u32[]{:S(2)}) %collective-permute-start.2) | collective-permute-done | bytes 163872 | tf_op jit(solution)/shard_map/ppermute | solution.py:227
  31.2 3.1 %collective-permute-start.5 = (f32[64,512]{1,0:T(8,128)S(1)}, f32[64,512]{1,0:T(8,128)S(1)}, u32[]{:S(2)}, u32[]{:S(2)}) collective-permute-start(f32[64,512]{1,0:T(8,128)S(1)} %fusion.11), channel_id=1, source_target_pairs={{0,24},{8,16},{16,8},{24,0},{1,25},{9,17},{17,9},{25,1},{2,26},{10... | collective-permute-start | bytes 393224 | tf_op jit(solution)/shard_map/ppermute | solution.py:227
  34.7 1.6 %collective-permute-start.3 = (f32[64,512]{1,0:T(8,128)S(1)}, f32[64,512]{1,0:T(8,128)S(1)}, u32[]{:S(2)}, u32[]{:S(2)}) collective-permute-start(f32[64,512]{1,0:T(8,128)S(1)} %fusion.9), channel_id=1, source_target_pairs={{0,8},{8,0},{16,24},{24,16},{1,9},{9,1},{17,25},{25,17},{2,10},{10... | collective-permute-start | bytes 393224 | tf_op jit(solution)/shard_map/ppermute | solution.py:227
  37.2 1.6 %collective-permute-start.10 = (bf16[64,512]{1,0:T(8,128)(2,1)S(1)}, bf16[64,512]{1,0:T(8,128)(2,1)S(1)}, u32[]{:S(2)}, u32[]{:S(2)}) collective-permute-start(bf16[64,512]{1,0:T(8,128)(2,1)S(1)} %bitcast.44), channel_id=1, source_target_pairs={{0,2},{1,3},{2,0},{3,1},{4,6},{5,7},{6,4},{7,5},{8,10},{9,11},{10,... | collective-permute-start | bytes 196616 | tf_op jit(solution)/shard_map/ppermute | solution.py:227
  38.8 2.6 %collective-permute-start.11 = (bf16[64,512]{1,0:T(8,128)(2,1)S(1)}, bf16[64,512]{1,0:T(8,128)(2,1)S(1)}, u32[]{:S(2)}, u32[]{:S(2)}) collective-permute-start(bf16[64,512]{1,0:T(8,128)(2,1)S(1)} %bitcast.45), channel_id=1, source_target_pairs={{0,4},{1,5},{2,6},{3,7},{4,0},{5,1},{6,2},{7,3},{8,12},{9,13},{10,... | collective-permute-start | bytes 196616 | tf_op jit(solution)/shard_map/ppermute | solution.py:227
  41.3 2.2 %turn_hidden.1 = (bf16[320,256]{1,0:T(8,128)(2,1)}, bf16[320,256]{1,0:T(8,128)(2,1)}, bf16[320,256]{1,0:T(8,128)(2,1)}, bf16[320,256]{1,0:T(8,128)(2,1)}) custom-call(bf16[64,1280]{1,0:T(8,128)(2,1)} %get-tuple-element.65.refs_0_, bf16[64,1280]{1,0:T(8,128)(2,1)} %copy-done.6, bf16[64,1280]{1,0:T(8,128)(2,1)} %copy-done.7, bf16[64,1280]{1,0:T(8,128)(2,1)} %copy-done.5), custom_call_target="tpu_custom_call" | custom-call | bytes 3000000 | tf_op jit(solution)/shard_map/turn_hidden/pallas_call | solution.py:108
  45.2 3.5 %collective-permute-start.7 = (bf16[64,512]{1,0:T(8,128)(2,1)S(1)}, bf16[64,512]{1,0:T(8,128)(2,1)S(1)}, u32[]{:S(2)}, u32[]{:S(2)}) collective-permute-start(bf16[64,512]{1,0:T(8,128)(2,1)S(1)} %fusion.2.refs_0_), channel_id=1, source_target_pairs={{0,4},{1,5},{2,6},{3,7},{4,0},{5,1},{6,2},{7,3},{8,12},{9,13},{10,... | collective-permute-start | bytes 196616 | tf_op jit(solution)/shard_map/ppermute | solution.py:227
  50.0 2.7 %collective-permute-done.7.refs_2_ = bf16[64,512]{1,0:T(8,128)(2,1)S(1)} collective-permute-done((bf16[64,512]{1,0:T(8,128)(2,1)S(1)}, bf16[64,512]{1,0:T(8,128)(2,1)S(1)}, u32[]{:S(2)}, u32[]{:S(2)}) %collective-permute-start.7) | collective-permute-done | bytes 65568 | tf_op jit(solution)/shard_map/ppermute | solution.py:227
  52.7 2.1 %collective-permute-done.8.refs_3_ = bf16[64,512]{1,0:T(8,128)(2,1)S(1)} collective-permute-done((bf16[64,512]{1,0:T(8,128)(2,1)S(1)}, bf16[64,512]{1,0:T(8,128)(2,1)S(1)}, u32[]{:S(2)}, u32[]{:S(2)}) %collective-permute-start.8) | collective-permute-done | bytes 65568 | tf_op jit(solution)/shard_map/ppermute | solution.py:227
  56.2 1.5 %collective-permute-start.18 = (bf16[1280,256]{1,0:T(8,128)(2,1)S(1)}, bf16[1280,256]{1,0:T(8,128)(2,1)S(1)}, u32[]{:S(2)}, u32[]{:S(2)}) collective-permute-start(bf16[1280,256]{1,0:T(8,128)(2,1)S(1)} %constant_dynamic-slice_fusion), channel_id=1, source_target_pairs={{0,16},{8,24},{16,0},{24,8},{1,17},{9,25},{17,1},{25,9},{2,18},{10... | collective-permute-start | bytes 1966088 | tf_op jit(solution)/shard_map/ppermute | solution.py:227
  57.7 1.3 %collective-permute-start.15 = (bf16[320,256]{1,0:T(8,128)(2,1)}, bf16[320,256]{1,0:T(8,128)(2,1)S(1)}, u32[]{:S(2)}, u32[]{:S(2)}) collective-permute-start(bf16[320,256]{1,0:T(8,128)(2,1)} %get-tuple-element.84), channel_id=1, source_target_pairs={{0,4},{1,5},{2,6},{3,7},{4,0},{5,1},{6,2},{7,3},{8,12},{9,13},{10,... | collective-permute-start | bytes 491528 | tf_op jit(solution)/shard_map/ppermute | solution.py:227
  59.0 3.1 %collective-permute-start.16 = (bf16[320,256]{1,0:T(8,128)(2,1)S(1)}, bf16[320,256]{1,0:T(8,128)(2,1)S(1)}, u32[]{:S(2)}, u32[]{:S(2)}) collective-permute-start(bf16[320,256]{1,0:T(8,128)(2,1)S(1)} %copy-done.29), channel_id=1, source_target_pairs={{0,6},{1,7},{2,4},{3,5},{4,2},{5,3},{6,0},{7,1},{8,14},{9,15},{10,... | collective-permute-start | bytes 491528 | tf_op jit(solution)/shard_map/ppermute | solution.py:227
  62.2 21.4 %attend.1 = (bf16[256,4096]{1,0:T(8,128)(2,1)}, bf16[256,512]{1,0:T(8,128)(2,1)}, bf16[256,512]{1,0:T(8,128)(2,1)}, f32[256,512]{1,0:T(8,128)}, f32[256,512]{1,0...) custom-call(s32[1,1]{1,0:T(1,128)S(6)} %copy.30.length_ref, bf16[256,4096]{1,0:T(8,128)(2,1)} %bitcast.48, ...), custom_call_target="tpu_custom_call" | custom-call | flops 16106127360 | bytes 10000000 | tf_op jit(solution)/shard_map/attend/pallas_call | solution.py:91
  85.9 1.1 fusion.5
  87.2 1.3 %collective-permute-start.21 = (bf16[64,512]{1,0:T(8,128)(2,1)S(1)}, bf16[64,512]{1,0:T(8,128)(2,1)S(1)}, u32[]{:S(2)}, u32[]{:S(2)}) collective-permute-start(bf16[64,512]{1,0:T(8,128)(2,1)S(1)} %get-tuple-element.131), channel_id=1, source_target_pairs={{0,4},{1,5},{2,6},{3,7},{4,0},{5,1},{6,2},{7,3},{8,12},{9,13},{10,... | collective-permute-start | bytes 196616 | tf_op jit(solution)/shard_map/ppermute | solution.py:227
  88.5 3.1 %collective-permute-start.22 = (bf16[64,512]{1,0:T(8,128)(2,1)S(1)}, bf16[64,512]{1,0:T(8,128)(2,1)S(1)}, u32[]{:S(2)}, u32[]{:S(2)}) collective-permute-start(bf16[64,512]{1,0:T(8,128)(2,1)S(1)} %get-tuple-element.130), channel_id=1, source_target_pairs={{0,6},{1,7},{2,4},{3,5},{4,2},{5,3},{6,0},{7,1},{8,14},{9,15},{10,... | collective-permute-start | bytes 196616 | tf_op jit(solution)/shard_map/ppermute | solution.py:227
  92.3 3.5 %collective-permute-done.21 = bf16[64,512]{1,0:T(8,128)(2,1)S(1)} collective-permute-done((bf16[64,512]{1,0:T(8,128)(2,1)S(1)}, bf16[64,512]{1,0:T(8,128)(2,1)S(1)}, u32[]{:S(2)}, u32[]{:S(2)}) %collective-permute-start.21) | collective-permute-done | bytes 65568 | tf_op jit(solution)/shard_map/ppermute | solution.py:227
  96.4 1.5 %collective-permute-start.26 = (bf16[64,512]{1,0:T(8,128)(2,1)S(1)}, bf16[64,512]{1,0:T(8,128)(2,1)S(1)}, u32[]{:S(2)}, u32[]{:S(2)}) collective-permute-start(bf16[64,512]{1,0:T(8,128)(2,1)S(1)} %fusion.refs_0_), channel_id=1, source_target_pairs={{0,24},{8,16},{16,8},{24,0},{1,25},{9,17},{17,9},{25,1},{2,26},{10... | collective-permute-start | bytes 196616 | tf_op jit(solution)/shard_map/ppermute | solution.py:227
  97.9 1.3 collective-permute-start.27
  99.2 1.2 collective-permute-start.28
  100.4 1.9 %collective-permute-start.29 = (bf16[64,512]{1,0:T(8,128)(2,1)S(1)}, bf16[64,512]{1,0:T(8,128)(2,1)S(1)}, u32[]{:S(2)}, u32[]{:S(2)}) collective-permute-start(bf16[64,512]{1,0:T(8,128)(2,1)S(1)} %fusion.refs_0_), channel_id=1, source_target_pairs={{0,6},{1,7},{2,4},{3,5},{4,2},{5,3},{6,0},{7,1},{8,14},{9,15},{10,... | collective-permute-start | bytes 196616 | tf_op jit(solution)/shard_map/ppermute | solution.py:227
  102.9 4.2 %hidden_grad.1 = (bf16[64,5120]{1,0:T(8,128)(2,1)}, bf16[64,1280]{1,0:T(8,128)(2,1)}) custom-call(bf16[1280,512]{1,0:T(8,128)(2,1)} %own_ref.1, bf16[64,512]{1,0:T(8,128)(2,1)} %copy-done.8, bf16[64,512]{1,0:T(8,128)(2,1)} %copy-done.11, bf16[1280,256]{1,0:T(8,128)(2,1)} %copy-done.2, bf16[1280,256]{1,0:T(8,128)(2,1)} %copy-done.3, ...), custom_call_target="tpu_custom_call" | custom-call | flops 335544320 | bytes 3000000 | tf_op jit(solution)/shard_map/hidden_grad/pallas_call | solution.py:108
  109.1 1.2 collective-permute-start.33
  110.3 1.5 %collective-permute-start.30 = (bf16[192,512]{1,0:T(8,128)(2,1)S(1)}, bf16[192,512]{1,0:T(8,128)(2,1)S(1)}, u32[]{:S(2)}, u32[]{:S(2)}) collective-permute-start(bf16[192,512]{1,0:T(8,128)(2,1)S(1)} %pad_maximum_fusion.2), channel_id=1, source_target_pairs={{0,24},{8,16},{16,8},{24,0},{1,25},{9,17},{17,9},{25,1},{2,26},{10... | collective-permute-start | bytes 589832 | tf_op jit(solution)/shard_map/ppermute | solution.py:227
  112.5 1.9 %collective-permute-start.35 = (bf16[64,512]{1,0:T(8,128)(2,1)S(1)}, bf16[64,512]{1,0:T(8,128)(2,1)S(1)}, u32[]{:S(2)}, u32[]{:S(2)}) collective-permute-start(bf16[64,512]{1,0:T(8,128)(2,1)S(1)} %get-tuple-element.127), channel_id=1, source_target_pairs={{0,4},{1,5},{2,6},{3,7},{4,0},{5,1},{6,2},{7,3},{8,12},{9,13},{10,... | collective-permute-start | bytes 196616 | tf_op jit(solution)/shard_map/ppermute | solution.py:227
  114.4 4.6 %collective-permute-done.30.refs_8_ = bf16[192,512]{1,0:T(8,128)(2,1)S(1)} collective-permute-done((bf16[192,512]{1,0:T(8,128)(2,1)S(1)}, bf16[192,512]{1,0:T(8,128)(2,1)S(1)}, u32[]{:S(2)}, u32[]{:S(2)}) %collective-permute-start.30) | collective-permute-done | bytes 196640 | tf_op jit(solution)/shard_map/ppermute | solution.py:227
  119.0 1.8 %collective-permute-start.36 = (bf16[64,512]{1,0:T(8,128)(2,1)S(1)}, bf16[64,512]{1,0:T(8,128)(2,1)S(1)}, u32[]{:S(2)}, u32[]{:S(2)}) collective-permute-start(bf16[64,512]{1,0:T(8,128)(2,1)S(1)} %get-tuple-element.126), channel_id=1, source_target_pairs={{0,6},{1,7},{2,4},{3,5},{4,2},{5,3},{6,0},{7,1},{8,14},{9,15},{10,... | collective-permute-start | bytes 196616 | tf_op jit(solution)/shard_map/ppermute | solution.py:227
  122.6 2.8 %weight_grad.1 = (f32[160,512]{1,0:T(8,128)}, f32[160,512]{1,0:T(8,128)}) custom-call(bf16[320,256]{1,0:T(8,128)(2,1)} %get-tuple-element.106.refs_0_, bf16[320,256]{1,0:T(8,128)(2,1)} %copy-done.16, bf16[320,256]{1,0:T(8,128)(2,1)} %copy-done.17, bf16[320,256]{1,0:T(8,128)(2,1)} %copy-done.18, bf16[256,512]{1,0:T(8,128)(2,1)} %copy-done.10, ...), custom_call_target="tpu_custom_call" | custom-call | flops 335544320 | bytes 3000000 | tf_op jit(solution)/shard_map/weight_grad/pallas_call | solution.py:108
  127.8 1.7 %add.69 = f32[160,512]{1,0:T(8,128)} add(f32[160,512]{1,0:T(8,128)} %get-tuple-element.115, f32[160,512]{1,0:T(8,128)S(1)} %collective-permute-done.37) | non-fusion elementwise | flops 81920 | bytes 983040 | tf_op jit(solution)/shard_map/add | solution.py:326
  (150 shorter events, 17.0 us)
Async XLA Ops:
  21.7 9.2 %collective-permute-start.2 = (bf16[64,1280]{1,0:T(8,128)(2,1)}, bf16[64,1280]{1,0:T(8,128)(2,1)S(1)}, u32[]{:S(2)}, u32[]{:S(2)}) collective-permute-start(bf16[64,1280]{1,0:T(8,128)(2,1)} %get-tuple-element.68), channel_id=1, source_target_pairs={{0,24},{8,16},{16,8},{24,0},{1,25},{9,17},{17,9},{25,1},{2,26},{10... | collective-permute-start | bytes 491528 | tf_op jit(solution)/shard_map/ppermute | solution.py:227
  25.6 8.8 %collective-permute-start = (bf16[64,1280]{1,0:T(8,128)(2,1)}, bf16[64,1280]{1,0:T(8,128)(2,1)S(1)}, u32[]{:S(2)}, u32[]{:S(2)}) collective-permute-start(bf16[64,1280]{1,0:T(8,128)(2,1)} %get-tuple-element.66), channel_id=1, source_target_pairs={{0,8},{8,0},{16,24},{24,16},{1,9},{9,1},{17,25},{25,17},{2,10},{10... | collective-permute-start | bytes 491528 | tf_op jit(solution)/shard_map/ppermute | solution.py:227
  26.1 10.1 %collective-permute-start.1 = (bf16[64,1280]{1,0:T(8,128)(2,1)}, bf16[64,1280]{1,0:T(8,128)(2,1)S(1)}, u32[]{:S(2)}, u32[]{:S(2)}) collective-permute-start(bf16[64,1280]{1,0:T(8,128)(2,1)} %get-tuple-element.67), channel_id=1, source_target_pairs={{0,16},{8,24},{16,0},{24,8},{1,17},{9,25},{17,1},{25,9},{2,18},{10... | collective-permute-start | bytes 491528 | tf_op jit(solution)/shard_map/ppermute | solution.py:227
  31.2 12.4 %collective-permute-start.5 = (f32[64,512]{1,0:T(8,128)S(1)}, f32[64,512]{1,0:T(8,128)S(1)}, u32[]{:S(2)}, u32[]{:S(2)}) collective-permute-start(f32[64,512]{1,0:T(8,128)S(1)} %fusion.11), channel_id=1, source_target_pairs={{0,24},{8,16},{16,8},{24,0},{1,25},{9,17},{17,9},{25,1},{2,26},{10... | collective-permute-start | bytes 393224 | tf_op jit(solution)/shard_map/ppermute | solution.py:227
  34.7 9.1 %collective-permute-start.3 = (f32[64,512]{1,0:T(8,128)S(1)}, f32[64,512]{1,0:T(8,128)S(1)}, u32[]{:S(2)}, u32[]{:S(2)}) collective-permute-start(f32[64,512]{1,0:T(8,128)S(1)} %fusion.9), channel_id=1, source_target_pairs={{0,8},{8,0},{16,24},{24,16},{1,9},{9,1},{17,25},{25,17},{2,10},{10... | collective-permute-start | bytes 393224 | tf_op jit(solution)/shard_map/ppermute | solution.py:227
  36.6 7.2 %collective-permute-start.4 = (f32[64,512]{1,0:T(8,128)S(1)}, f32[64,512]{1,0:T(8,128)S(1)}, u32[]{:S(2)}, u32[]{:S(2)}) collective-permute-start(f32[64,512]{1,0:T(8,128)S(1)} %fusion.10), channel_id=1, source_target_pairs={{0,16},{8,24},{16,0},{24,8},{1,17},{9,25},{17,1},{25,9},{2,18},{10... | collective-permute-start | bytes 393224 | tf_op jit(solution)/shard_map/ppermute | solution.py:227
  37.2 11.5 %collective-permute-start.10 = (bf16[64,512]{1,0:T(8,128)(2,1)S(1)}, bf16[64,512]{1,0:T(8,128)(2,1)S(1)}, u32[]{:S(2)}, u32[]{:S(2)}) collective-permute-start(bf16[64,512]{1,0:T(8,128)(2,1)S(1)} %bitcast.44), channel_id=1, source_target_pairs={{0,2},{1,3},{2,0},{3,1},{4,6},{5,7},{6,4},{7,5},{8,10},{9,11},{10,... | collective-permute-start | bytes 196616 | tf_op jit(solution)/shard_map/ppermute | solution.py:227
  38.8 10.2 %collective-permute-start.11 = (bf16[64,512]{1,0:T(8,128)(2,1)S(1)}, bf16[64,512]{1,0:T(8,128)(2,1)S(1)}, u32[]{:S(2)}, u32[]{:S(2)}) collective-permute-start(bf16[64,512]{1,0:T(8,128)(2,1)S(1)} %bitcast.45), channel_id=1, source_target_pairs={{0,4},{1,5},{2,6},{3,7},{4,0},{5,1},{6,2},{7,3},{8,12},{9,13},{10,... | collective-permute-start | bytes 196616 | tf_op jit(solution)/shard_map/ppermute | solution.py:227
  43.6 6.3 %collective-permute-start.12 = (bf16[64,512]{1,0:T(8,128)(2,1)S(1)}, bf16[64,512]{1,0:T(8,128)(2,1)S(1)}, u32[]{:S(2)}, u32[]{:S(2)}) collective-permute-start(bf16[64,512]{1,0:T(8,128)(2,1)S(1)} %bitcast.46), channel_id=1, source_target_pairs={{0,6},{1,7},{2,4},{3,5},{4,2},{5,3},{6,0},{7,1},{8,14},{9,15},{10,... | collective-permute-start | bytes 196616 | tf_op jit(solution)/shard_map/ppermute | solution.py:227
  45.2 7.5 %collective-permute-start.7 = (bf16[64,512]{1,0:T(8,128)(2,1)S(1)}, bf16[64,512]{1,0:T(8,128)(2,1)S(1)}, u32[]{:S(2)}, u32[]{:S(2)}) collective-permute-start(bf16[64,512]{1,0:T(8,128)(2,1)S(1)} %fusion.2.refs_0_), channel_id=1, source_target_pairs={{0,4},{1,5},{2,6},{3,7},{4,0},{5,1},{6,2},{7,3},{8,12},{9,13},{10,... | collective-permute-start | bytes 196616 | tf_op jit(solution)/shard_map/ppermute | solution.py:227
  48.7 6.1 %collective-permute-start.8 = (bf16[64,512]{1,0:T(8,128)(2,1)S(1)}, bf16[64,512]{1,0:T(8,128)(2,1)S(1)}, u32[]{:S(2)}, u32[]{:S(2)}) collective-permute-start(bf16[64,512]{1,0:T(8,128)(2,1)S(1)} %fusion.2.refs_0_), channel_id=1, source_target_pairs={{0,6},{1,7},{2,4},{3,5},{4,2},{5,3},{6,0},{7,1},{8,14},{9,15},{10,... | collective-permute-start | bytes 196616 | tf_op jit(solution)/shard_map/ppermute | solution.py:227
  49.9 7.8 %collective-permute-start.13 = (bf16[256,512]{1,0:T(8,128)(2,1)S(1)}, bf16[256,512]{1,0:T(8,128)(2,1)S(1)}, u32[]{:S(2)}, u32[]{:S(2)}) collective-permute-start(bf16[256,512]{1,0:T(8,128)(2,1)S(1)} %pad_maximum_fusion.1), channel_id=1, source_target_pairs={{0,1},{1,0},{2,3},{3,2},{4,5},{5,4},{6,7},{7,6},{8,9},{9,8},{10,11... | collective-permute-start | bytes 786440 | tf_op jit(solution)/shard_map/ppermute | solution.py:227
  55.5 28.2 %collective-permute-start.17 = (bf16[1280,256]{1,0:T(8,128)(2,1)S(1)}, bf16[1280,256]{1,0:T(8,128)(2,1)S(1)}, u32[]{:S(2)}, u32[]{:S(2)}) collective-permute-start(bf16[1280,256]{1,0:T(8,128)(2,1)S(1)} %constant_dynamic-slice_fusion), channel_id=1, source_target_pairs={{0,8},{8,0},{16,24},{24,16},{1,9},{9,1},{17,25},{25,17},{2,10},{10... | collective-permute-start | bytes 1966088 | tf_op jit(solution)/shard_map/ppermute | solution.py:227
  56.2 27.6 %collective-permute-start.18 = (bf16[1280,256]{1,0:T(8,128)(2,1)S(1)}, bf16[1280,256]{1,0:T(8,128)(2,1)S(1)}, u32[]{:S(2)}, u32[]{:S(2)}) collective-permute-start(bf16[1280,256]{1,0:T(8,128)(2,1)S(1)} %constant_dynamic-slice_fusion), channel_id=1, source_target_pairs={{0,16},{8,24},{16,0},{24,8},{1,17},{9,25},{17,1},{25,9},{2,18},{10... | collective-permute-start | bytes 1966088 | tf_op jit(solution)/shard_map/ppermute | solution.py:227
  57.7 25.9 %collective-permute-start.14 = (bf16[320,256]{1,0:T(8,128)(2,1)}, bf16[320,256]{1,0:T(8,128)(2,1)S(1)}, u32[]{:S(2)}, u32[]{:S(2)}) collective-permute-start(bf16[320,256]{1,0:T(8,128)(2,1)} %get-tuple-element.83), channel_id=1, source_target_pairs={{0,2},{1,3},{2,0},{3,1},{4,6},{5,7},{6,4},{7,5},{8,10},{9,11},{10,... | collective-permute-start | bytes 491528 | tf_op jit(solution)/shard_map/ppermute | solution.py:227
  57.7 26.0 %collective-permute-start.15 = (bf16[320,256]{1,0:T(8,128)(2,1)}, bf16[320,256]{1,0:T(8,128)(2,1)S(1)}, u32[]{:S(2)}, u32[]{:S(2)}) collective-permute-start(bf16[320,256]{1,0:T(8,128)(2,1)} %get-tuple-element.84), channel_id=1, source_target_pairs={{0,4},{1,5},{2,6},{3,7},{4,0},{5,1},{6,2},{7,3},{8,12},{9,13},{10,... | collective-permute-start | bytes 491528 | tf_op jit(solution)/shard_map/ppermute | solution.py:227
  59.0 24.6 %collective-permute-start.16 = (bf16[320,256]{1,0:T(8,128)(2,1)S(1)}, bf16[320,256]{1,0:T(8,128)(2,1)S(1)}, u32[]{:S(2)}, u32[]{:S(2)}) collective-permute-start(bf16[320,256]{1,0:T(8,128)(2,1)S(1)} %copy-done.29), channel_id=1, source_target_pairs={{0,6},{1,7},{2,4},{3,5},{4,2},{5,3},{6,0},{7,1},{8,14},{9,15},{10,... | collective-permute-start | bytes 491528 | tf_op jit(solution)/shard_map/ppermute | solution.py:227
  84.3 11.5 %collective-permute-start.24 = (bf16[1280,256]{1,0:T(8,128)(2,1)S(1)}, bf16[1280,256]{1,0:T(8,128)(2,1)S(1)}, u32[]{:S(2)}, u32[]{:S(2)}) collective-permute-start(bf16[1280,256]{1,0:T(8,128)(2,1)S(1)} %collective-permute-done.17.refs_2_), channel_id=1, source_target_pairs={{0,1},{1,0},{2,3},{3,2},{4,5},{5,4},{6,7},{7,6},{8,9},{9,8},{10,11... | collective-permute-start | bytes 1966088 | tf_op jit(solution)/shard_map/ppermute | solution.py:227
  84.4 11.4 %collective-permute-start.25 = (bf16[1280,256]{1,0:T(8,128)(2,1)S(1)}, bf16[1280,256]{1,0:T(8,128)(2,1)}, u32[]{:S(2)}, u32[]{:S(2)}) collective-permute-start(bf16[1280,256]{1,0:T(8,128)(2,1)S(1)} %collective-permute-done.18.refs_3_), channel_id=1, source_target_pairs={{0,1},{1,0},{2,3},{3,2},{4,5},{5,4},{6,7},{7,6},{8,9},{9,8},{10,11... | collective-permute-start | bytes 1966088 | tf_op jit(solution)/shard_map/ppermute | solution.py:227
  87.2 8.6 %collective-permute-start.21 = (bf16[64,512]{1,0:T(8,128)(2,1)S(1)}, bf16[64,512]{1,0:T(8,128)(2,1)S(1)}, u32[]{:S(2)}, u32[]{:S(2)}) collective-permute-start(bf16[64,512]{1,0:T(8,128)(2,1)S(1)} %get-tuple-element.131), channel_id=1, source_target_pairs={{0,4},{1,5},{2,6},{3,7},{4,0},{5,1},{6,2},{7,3},{8,12},{9,13},{10,... | collective-permute-start | bytes 196616 | tf_op jit(solution)/shard_map/ppermute | solution.py:227
  88.5 7.3 %collective-permute-start.22 = (bf16[64,512]{1,0:T(8,128)(2,1)S(1)}, bf16[64,512]{1,0:T(8,128)(2,1)S(1)}, u32[]{:S(2)}, u32[]{:S(2)}) collective-permute-start(bf16[64,512]{1,0:T(8,128)(2,1)S(1)} %get-tuple-element.130), channel_id=1, source_target_pairs={{0,6},{1,7},{2,4},{3,5},{4,2},{5,3},{6,0},{7,1},{8,14},{9,15},{10,... | collective-permute-start | bytes 196616 | tf_op jit(solution)/shard_map/ppermute | solution.py:227
  96.4 5.8 %collective-permute-start.26 = (bf16[64,512]{1,0:T(8,128)(2,1)S(1)}, bf16[64,512]{1,0:T(8,128)(2,1)S(1)}, u32[]{:S(2)}, u32[]{:S(2)}) collective-permute-start(bf16[64,512]{1,0:T(8,128)(2,1)S(1)} %fusion.refs_0_), channel_id=1, source_target_pairs={{0,24},{8,16},{16,8},{24,0},{1,25},{9,17},{17,9},{25,1},{2,26},{10... | collective-permute-start | bytes 196616 | tf_op jit(solution)/shard_map/ppermute | solution.py:227
  97.9 9.3 %collective-permute-start.27 = (bf16[64,512]{1,0:T(8,128)(2,1)S(1)}, bf16[64,512]{1,0:T(8,128)(2,1)S(1)}, u32[]{:S(2)}, u32[]{:S(2)}) collective-permute-start(bf16[64,512]{1,0:T(8,128)(2,1)S(1)} %fusion.refs_0_), channel_id=1, source_target_pairs={{0,2},{1,3},{2,0},{3,1},{4,6},{5,7},{6,4},{7,5},{8,10},{9,11},{10,... | collective-permute-start | bytes 196616 | tf_op jit(solution)/shard_map/ppermute | solution.py:227
  99.2 8.0 %collective-permute-start.28 = (bf16[64,512]{1,0:T(8,128)(2,1)S(1)}, bf16[64,512]{1,0:T(8,128)(2,1)S(1)}, u32[]{:S(2)}, u32[]{:S(2)}) collective-permute-start(bf16[64,512]{1,0:T(8,128)(2,1)S(1)} %fusion.refs_0_), channel_id=1, source_target_pairs={{0,4},{1,5},{2,6},{3,7},{4,0},{5,1},{6,2},{7,3},{8,12},{9,13},{10,... | collective-permute-start | bytes 196616 | tf_op jit(solution)/shard_map/ppermute | solution.py:227
  100.4 6.8 %collective-permute-start.29 = (bf16[64,512]{1,0:T(8,128)(2,1)S(1)}, bf16[64,512]{1,0:T(8,128)(2,1)S(1)}, u32[]{:S(2)}, u32[]{:S(2)}) collective-permute-start(bf16[64,512]{1,0:T(8,128)(2,1)S(1)} %fusion.refs_0_), channel_id=1, source_target_pairs={{0,6},{1,7},{2,4},{3,5},{4,2},{5,3},{6,0},{7,1},{8,14},{9,15},{10,... | collective-permute-start | bytes 196616 | tf_op jit(solution)/shard_map/ppermute | solution.py:227
  108.1 12.7 %collective-permute-start.32 = (bf16[256,512]{1,0:T(8,128)(2,1)S(1)}, bf16[256,512]{1,0:T(8,128)(2,1)S(1)}, u32[]{:S(2)}, u32[]{:S(2)}) collective-permute-start(bf16[256,512]{1,0:T(8,128)(2,1)S(1)} %constant_dynamic-update-slice_fusion.refs_4_), channel_id=1, source_target_pairs={{0,8},{8,0},{16,24},{24,16},{1,9},{9,1},{17,25},{25,17},{2,10},{10... | collective-permute-start | bytes 786440 | tf_op jit(solution)/shard_map/ppermute | solution.py:227
  109.1 12.8 %collective-permute-start.33 = (bf16[256,512]{1,0:T(8,128)(2,1)S(1)}, bf16[256,512]{1,0:T(8,128)(2,1)S(1)}, u32[]{:S(2)}, u32[]{:S(2)}) collective-permute-start(bf16[256,512]{1,0:T(8,128)(2,1)S(1)} %constant_dynamic-update-slice_fusion.refs_4_), channel_id=1, source_target_pairs={{0,16},{8,24},{16,0},{24,8},{1,17},{9,25},{17,1},{25,9},{2,18},{10... | collective-permute-start | bytes 786440 | tf_op jit(solution)/shard_map/ppermute | solution.py:227
  110.3 8.7 %collective-permute-start.30 = (bf16[192,512]{1,0:T(8,128)(2,1)S(1)}, bf16[192,512]{1,0:T(8,128)(2,1)S(1)}, u32[]{:S(2)}, u32[]{:S(2)}) collective-permute-start(bf16[192,512]{1,0:T(8,128)(2,1)S(1)} %pad_maximum_fusion.2), channel_id=1, source_target_pairs={{0,24},{8,16},{16,8},{24,0},{1,25},{9,17},{17,9},{25,1},{2,26},{10... | collective-permute-start | bytes 589832 | tf_op jit(solution)/shard_map/ppermute | solution.py:227
  111.8 13.5 %collective-permute-start.34 = (bf16[64,512]{1,0:T(8,128)(2,1)S(1)}, bf16[64,512]{1,0:T(8,128)(2,1)S(1)}, u32[]{:S(2)}, u32[]{:S(2)}) collective-permute-start(bf16[64,512]{1,0:T(8,128)(2,1)S(1)} %get-tuple-element.128), channel_id=1, source_target_pairs={{0,2},{1,3},{2,0},{3,1},{4,6},{5,7},{6,4},{7,5},{8,10},{9,11},{10,... | collective-permute-start | bytes 196616 | tf_op jit(solution)/shard_map/ppermute | solution.py:227
  112.5 12.8 %collective-permute-start.35 = (bf16[64,512]{1,0:T(8,128)(2,1)S(1)}, bf16[64,512]{1,0:T(8,128)(2,1)S(1)}, u32[]{:S(2)}, u32[]{:S(2)}) collective-permute-start(bf16[64,512]{1,0:T(8,128)(2,1)S(1)} %get-tuple-element.127), channel_id=1, source_target_pairs={{0,4},{1,5},{2,6},{3,7},{4,0},{5,1},{6,2},{7,3},{8,12},{9,13},{10,... | collective-permute-start | bytes 196616 | tf_op jit(solution)/shard_map/ppermute | solution.py:227
  119.0 6.3 %collective-permute-start.36 = (bf16[64,512]{1,0:T(8,128)(2,1)S(1)}, bf16[64,512]{1,0:T(8,128)(2,1)S(1)}, u32[]{:S(2)}, u32[]{:S(2)}) collective-permute-start(bf16[64,512]{1,0:T(8,128)(2,1)S(1)} %get-tuple-element.126), channel_id=1, source_target_pairs={{0,6},{1,7},{2,4},{3,5},{4,2},{5,3},{6,0},{7,1},{8,14},{9,15},{10,... | collective-permute-start | bytes 196616 | tf_op jit(solution)/shard_map/ppermute | solution.py:227
  120.9 6.3 %collective-permute-start.31 = (bf16[64,1280]{1,0:T(8,128)(2,1)S(1)}, bf16[64,1280]{1,0:T(8,128)(2,1)S(1)}, u32[]{:S(2)}, u32[]{:S(2)}) collective-permute-start(bf16[64,1280]{1,0:T(8,128)(2,1)S(1)} %copy-done.30), channel_id=1, source_target_pairs={{0,24},{8,16},{16,8},{24,0},{1,25},{9,17},{17,9},{25,1},{2,26},{10... | collective-permute-start | bytes 491528 | tf_op jit(solution)/shard_map/ppermute | solution.py:227
  (38 other events, 310.0 us)

commit v9 on v8

--- a/solution.py
+++ b/solution.py
@@ -118,31 +118,18 @@
     return list(results)
 
 
-def split_kernel(hidden_ref, *refs):
-    *piece_refs, arrived = refs
+def split_kernel(hidden_ref, *piece_refs):
     depth = piece_refs[0].shape[1]
     group = lax.axis_index("group")
-    copies = []
     for k, piece_ref in enumerate(piece_refs):
         start = pl.multiple_of((group ^ k) * depth, depth)
-        copies.append(pltpu.make_async_copy(hidden_ref.at[:, pl.ds(start, depth)], piece_ref, arrived.at[k]))
-        copies[-1].start()
-    for copy in copies:
-        copy.wait()
+        piece_ref[...] = hidden_ref[:, pl.ds(start, depth)]
 
 
 def split_pass(hidden, groups):
     tokens, width = hidden.shape
-    anywhere = pl.BlockSpec(memory_space=pl.ANY)
-    return list(pl.pallas_call(
-        split_kernel,
-        in_specs=[anywhere],
-        out_specs=[anywhere] * groups,
-        out_shape=[jax.ShapeDtypeStruct((tokens, width // groups), hidden.dtype)] * groups,
-        scratch_shapes=[pltpu.SemaphoreType.DMA((groups,))],
-        compiler_params=PARAMS,
-        name="split_hidden",
-    )(hidden))
+    outs = [((tokens, width // groups), hidden.dtype)] * groups
+    return in_vmem(split_kernel, "split_hidden", outs, [hidden])
 
 
 def turn_kernel(groups, *refs):

time: 130 us -> 111 us (0.85)
  Pallas kernels: 51.6 us -> 32.7 us
    pallas_call x1 -> x0, Pallas kernels: 21 us -> none  [split_pass(): pl.pallas_call(split_kernel, in_specs=[anywhere], out_specs=[anywhere] *...]
    pallas_call x3 -> x4, Pallas kernels: 9.23 us -> 11.3 us  [in_vmem(): pl.pallas_call(kernel, in_specs=[whole] * len(arrays), out_specs=[whole]...]
  transfers between devices with their start and end apart: 38 -> 38, of which waited for: 10 -> 10; matrix products, arithmetic and copies ran while one was open for 5% -> 5% of each run, Pallas kernels for 24% -> 28%
where the time goes in v9:
time: 111 us
  starting transfers between devices  45.7 us (41%)
  Pallas kernels  32.7 us (29%)
  waiting for transfers between devices  19.6 us (18%)
  other arithmetic  4.14 us (4%)
  local copies, waits for them, and re-layouts  3.83 us (3%)
  matrix products  2.74 us (2%)
  between operations  1.91 us (2%)
    ppermute x38, starting transfers between devices, swap(): return lax.ppermute(array, axis, [(i, i ^ distance) for i in range(size)])  45.7 us
    pallas_call x1, Pallas kernels, attend(): pl.pallas_call(partial(attend_kernel, len(key_pieces)), grid=(kv_heads,),...  21.4 us
    ppermute x38, waiting for transfers between devices, swap(): return lax.ppermute(array, axis, [(i, i ^ distance) for i in range(size)])  19.6 us
    pallas_call x4, Pallas kernels, in_vmem(): pl.pallas_call(kernel, in_specs=[whole] * len(arrays), out_specs=[whole]...  11.3 us
    dot_general x4, matrix products, dot(): return lax.dot_general(left, right, dims, preferred_element_type=F32)  2.74 us
    unnamed x65, local copies, waits for them, and re-layouts  2.35 us
  transfers between devices with their start and end apart: 38, of which 10 were waited for; matrix products, arithmetic and copies ran while one was open for 5% of the time, Pallas kernels for 28%

profile of v9, /device:TPU:0, one launch (start us, length us, event | category | flops | bytes accessed | tf_op | source)
XLA Modules:
  0.0 110.6 jit_solution(3602402822804360051)
XLA Ops:
  0.6 2.1 %split_hidden.1 = (bf16[64,1280]{1,0:T(8,128)(2,1)}, bf16[64,1280]{1,0:T(8,128)(2,1)}, bf16[64,1280]{1,0:T(8,128)(2,1)}, bf16[64,1280]{1,0:T(8,128)(2,1)}) custom-call(bf16[64,5120]{1,0:T(8,128)(2,1)} %bitcast.41), custom_call_target="tpu_custom_call" | custom-call | bytes 3000000 | tf_op jit(solution)/shard_map/split_hidden/pallas_call | solution.py:108
  2.7 3.9 %collective-permute-start.2 = (bf16[64,1280]{1,0:T(8,128)(2,1)}, bf16[64,1280]{1,0:T(8,128)(2,1)S(1)}, u32[]{:S(2)}, u32[]{:S(2)}) collective-permute-start(bf16[64,1280]{1,0:T(8,128)(2,1)} %get-tuple-element.68), channel_id=1, source_target_pairs={{0,24},{8,16},{16,8},{24,0},{1,25},{9,17},{17,9},{25,1},{2,26},{10... | collective-permute-start | bytes 491528 | tf_op jit(solution)/shard_map/ppermute | solution.py:214
  7.2 1.7 %fusion.8 = f32[64,512]{1,0:T(8,128)S(1)} fusion(bf16[64,1280]{1,0:T(8,128)(2,1)} %get-tuple-element.65.refs_0_, bf16[1280,512]{1,0:T(8,128)(2,1)} %own_ref.1), kind=kOutput, calls=%fused_computation.29 | convolution fusion | flops 83886080 | bytes 1605632 | tf_op jit(solution)/shard_map/dot_general | solution.py:23
  9.0 2.8 %collective-permute-done.2.refs_3_ = bf16[64,1280]{1,0:T(8,128)(2,1)S(1)} collective-permute-done((bf16[64,1280]{1,0:T(8,128)(2,1)}, bf16[64,1280]{1,0:T(8,128)(2,1)S(1)}, u32[]{:S(2)}, u32[]{:S(2)}) %collective-permute-start.2) | collective-permute-done | bytes 163872 | tf_op jit(solution)/shard_map/ppermute | solution.py:214
  12.2 3.1 %collective-permute-start.5 = (f32[64,512]{1,0:T(8,128)S(1)}, f32[64,512]{1,0:T(8,128)S(1)}, u32[]{:S(2)}, u32[]{:S(2)}) collective-permute-start(f32[64,512]{1,0:T(8,128)S(1)} %fusion.11), channel_id=1, source_target_pairs={{0,24},{8,16},{16,8},{24,0},{1,25},{9,17},{17,9},{25,1},{2,26},{10... | collective-permute-start | bytes 393224 | tf_op jit(solution)/shard_map/ppermute | solution.py:214
  15.7 1.6 %collective-permute-start.3 = (f32[64,512]{1,0:T(8,128)S(1)}, f32[64,512]{1,0:T(8,128)S(1)}, u32[]{:S(2)}, u32[]{:S(2)}) collective-permute-start(f32[64,512]{1,0:T(8,128)S(1)} %fusion.9), channel_id=1, source_target_pairs={{0,8},{8,0},{16,24},{24,16},{1,9},{9,1},{17,25},{25,17},{2,10},{10... | collective-permute-start | bytes 393224 | tf_op jit(solution)/shard_map/ppermute | solution.py:214
  18.2 1.6 %collective-permute-start.10 = (bf16[64,512]{1,0:T(8,128)(2,1)S(1)}, bf16[64,512]{1,0:T(8,128)(2,1)S(1)}, u32[]{:S(2)}, u32[]{:S(2)}) collective-permute-start(bf16[64,512]{1,0:T(8,128)(2,1)S(1)} %bitcast.44), channel_id=1, source_target_pairs={{0,2},{1,3},{2,0},{3,1},{4,6},{5,7},{6,4},{7,5},{8,10},{9,11},{10,... | collective-permute-start | bytes 196616 | tf_op jit(solution)/shard_map/ppermute | solution.py:214
  19.7 2.6 %collective-permute-start.11 = (bf16[64,512]{1,0:T(8,128)(2,1)S(1)}, bf16[64,512]{1,0:T(8,128)(2,1)S(1)}, u32[]{:S(2)}, u32[]{:S(2)}) collective-permute-start(bf16[64,512]{1,0:T(8,128)(2,1)S(1)} %bitcast.45), channel_id=1, source_target_pairs={{0,4},{1,5},{2,6},{3,7},{4,0},{5,1},{6,2},{7,3},{8,12},{9,13},{10,... | collective-permute-start | bytes 196616 | tf_op jit(solution)/shard_map/ppermute | solution.py:214
  22.3 2.2 %turn_hidden.1 = (bf16[320,256]{1,0:T(8,128)(2,1)}, bf16[320,256]{1,0:T(8,128)(2,1)}, bf16[320,256]{1,0:T(8,128)(2,1)}, bf16[320,256]{1,0:T(8,128)(2,1)}) custom-call(bf16[64,1280]{1,0:T(8,128)(2,1)} %get-tuple-element.65.refs_0_, bf16[64,1280]{1,0:T(8,128)(2,1)} %copy-done.6, bf16[64,1280]{1,0:T(8,128)(2,1)} %copy-done.7, bf16[64,1280]{1,0:T(8,128)(2,1)} %copy-done.5), custom_call_target="tpu_custom_call" | custom-call | bytes 3000000 | tf_op jit(solution)/shard_map/turn_hidden/pallas_call | solution.py:108
  26.2 3.5 %collective-permute-start.7 = (bf16[64,512]{1,0:T(8,128)(2,1)S(1)}, bf16[64,512]{1,0:T(8,128)(2,1)S(1)}, u32[]{:S(2)}, u32[]{:S(2)}) collective-permute-start(bf16[64,512]{1,0:T(8,128)(2,1)S(1)} %fusion.2.refs_0_), channel_id=1, source_target_pairs={{0,4},{1,5},{2,6},{3,7},{4,0},{5,1},{6,2},{7,3},{8,12},{9,13},{10,... | collective-permute-start | bytes 196616 | tf_op jit(solution)/shard_map/ppermute | solution.py:214
  31.0 2.7 %collective-permute-done.7.refs_2_ = bf16[64,512]{1,0:T(8,128)(2,1)S(1)} collective-permute-done((bf16[64,512]{1,0:T(8,128)(2,1)S(1)}, bf16[64,512]{1,0:T(8,128)(2,1)S(1)}, u32[]{:S(2)}, u32[]{:S(2)}) %collective-permute-start.7) | collective-permute-done | bytes 65568 | tf_op jit(solution)/shard_map/ppermute | solution.py:214
  33.7 2.1 %collective-permute-done.8.refs_3_ = bf16[64,512]{1,0:T(8,128)(2,1)S(1)} collective-permute-done((bf16[64,512]{1,0:T(8,128)(2,1)S(1)}, bf16[64,512]{1,0:T(8,128)(2,1)S(1)}, u32[]{:S(2)}, u32[]{:S(2)}) %collective-permute-start.8) | collective-permute-done | bytes 65568 | tf_op jit(solution)/shard_map/ppermute | solution.py:214
  37.1 1.5 %collective-permute-start.18 = (bf16[1280,256]{1,0:T(8,128)(2,1)S(1)}, bf16[1280,256]{1,0:T(8,128)(2,1)S(1)}, u32[]{:S(2)}, u32[]{:S(2)}) collective-permute-start(bf16[1280,256]{1,0:T(8,128)(2,1)S(1)} %constant_dynamic-slice_fusion), channel_id=1, source_target_pairs={{0,16},{8,24},{16,0},{24,8},{1,17},{9,25},{17,1},{25,9},{2,18},{10... | collective-permute-start | bytes 1966088 | tf_op jit(solution)/shard_map/ppermute | solution.py:214
  38.7 1.3 %collective-permute-start.15 = (bf16[320,256]{1,0:T(8,128)(2,1)}, bf16[320,256]{1,0:T(8,128)(2,1)S(1)}, u32[]{:S(2)}, u32[]{:S(2)}) collective-permute-start(bf16[320,256]{1,0:T(8,128)(2,1)} %get-tuple-element.84), channel_id=1, source_target_pairs={{0,4},{1,5},{2,6},{3,7},{4,0},{5,1},{6,2},{7,3},{8,12},{9,13},{10,... | collective-permute-start | bytes 491528 | tf_op jit(solution)/shard_map/ppermute | solution.py:214
  40.0 3.1 %collective-permute-start.16 = (bf16[320,256]{1,0:T(8,128)(2,1)S(1)}, bf16[320,256]{1,0:T(8,128)(2,1)S(1)}, u32[]{:S(2)}, u32[]{:S(2)}) collective-permute-start(bf16[320,256]{1,0:T(8,128)(2,1)S(1)} %copy-done.29), channel_id=1, source_target_pairs={{0,6},{1,7},{2,4},{3,5},{4,2},{5,3},{6,0},{7,1},{8,14},{9,15},{10,... | collective-permute-start | bytes 491528 | tf_op jit(solution)/shard_map/ppermute | solution.py:214
  43.2 21.4 %attend.1 = (bf16[256,4096]{1,0:T(8,128)(2,1)}, bf16[256,512]{1,0:T(8,128)(2,1)}, bf16[256,512]{1,0:T(8,128)(2,1)}, f32[256,512]{1,0:T(8,128)}, f32[256,512]{1,0...) custom-call(s32[1,1]{1,0:T(1,128)S(6)} %copy.30.length_ref, bf16[256,4096]{1,0:T(8,128)(2,1)} %bitcast.48, ...), custom_call_target="tpu_custom_call" | custom-call | flops 16106127360 | bytes 10000000 | tf_op jit(solution)/shard_map/attend/pallas_call | solution.py:91
  66.9 1.1 %fusion.5 = (bf16[256,512]{1,0:T(8,128)(2,1)S(1)}, f32[256,512]{1,0:T(8,128)S(1)}) fusion(f32[256,512]{1,0:T(8,128)} %get-tuple-element.87, f32[256,512]{1,0:T(8,128)S(1)} %collective-permute-done.19), kind=kLoop, calls=%fused_computation.26 | loop fusion | flops 262144 | bytes 1835008 | tf_op jit(solution)/shard_map/convert.5
  68.2 1.3 %collective-permute-start.21 = (bf16[64,512]{1,0:T(8,128)(2,1)S(1)}, bf16[64,512]{1,0:T(8,128)(2,1)S(1)}, u32[]{:S(2)}, u32[]{:S(2)}) collective-permute-start(bf16[64,512]{1,0:T(8,128)(2,1)S(1)} %get-tuple-element.131), channel_id=1, source_target_pairs={{0,4},{1,5},{2,6},{3,7},{4,0},{5,1},{6,2},{7,3},{8,12},{9,13},{10,... | collective-permute-start | bytes 196616 | tf_op jit(solution)/shard_map/ppermute | solution.py:214
  69.5 3.0 %collective-permute-start.22 = (bf16[64,512]{1,0:T(8,128)(2,1)S(1)}, bf16[64,512]{1,0:T(8,128)(2,1)S(1)}, u32[]{:S(2)}, u32[]{:S(2)}) collective-permute-start(bf16[64,512]{1,0:T(8,128)(2,1)S(1)} %get-tuple-element.130), channel_id=1, source_target_pairs={{0,6},{1,7},{2,4},{3,5},{4,2},{5,3},{6,0},{7,1},{8,14},{9,15},{10,... | collective-permute-start | bytes 196616 | tf_op jit(solution)/shard_map/ppermute | solution.py:214
  73.3 3.5 %collective-permute-done.21 = bf16[64,512]{1,0:T(8,128)(2,1)S(1)} collective-permute-done((bf16[64,512]{1,0:T(8,128)(2,1)S(1)}, bf16[64,512]{1,0:T(8,128)(2,1)S(1)}, u32[]{:S(2)}, u32[]{:S(2)}) %collective-permute-start.21) | collective-permute-done | bytes 65568 | tf_op jit(solution)/shard_map/ppermute | solution.py:214
  77.4 1.5 %collective-permute-start.26 = (bf16[64,512]{1,0:T(8,128)(2,1)S(1)}, bf16[64,512]{1,0:T(8,128)(2,1)S(1)}, u32[]{:S(2)}, u32[]{:S(2)}) collective-permute-start(bf16[64,512]{1,0:T(8,128)(2,1)S(1)} %fusion.refs_0_), channel_id=1, source_target_pairs={{0,24},{8,16},{16,8},{24,0},{1,25},{9,17},{17,9},{25,1},{2,26},{10... | collective-permute-start | bytes 196616 | tf_op jit(solution)/shard_map/ppermute | solution.py:214
  78.9 1.3 %collective-permute-start.27 = (bf16[64,512]{1,0:T(8,128)(2,1)S(1)}, bf16[64,512]{1,0:T(8,128)(2,1)S(1)}, u32[]{:S(2)}, u32[]{:S(2)}) collective-permute-start(bf16[64,512]{1,0:T(8,128)(2,1)S(1)} %fusion.refs_0_), channel_id=1, source_target_pairs={{0,2},{1,3},{2,0},{3,1},{4,6},{5,7},{6,4},{7,5},{8,10},{9,11},{10,... | collective-permute-start | bytes 196616 | tf_op jit(solution)/shard_map/ppermute | solution.py:214
  80.2 1.2 %collective-permute-start.28 = (bf16[64,512]{1,0:T(8,128)(2,1)S(1)}, bf16[64,512]{1,0:T(8,128)(2,1)S(1)}, u32[]{:S(2)}, u32[]{:S(2)}) collective-permute-start(bf16[64,512]{1,0:T(8,128)(2,1)S(1)} %fusion.refs_0_), channel_id=1, source_target_pairs={{0,4},{1,5},{2,6},{3,7},{4,0},{5,1},{6,2},{7,3},{8,12},{9,13},{10,... | collective-permute-start | bytes 196616 | tf_op jit(solution)/shard_map/ppermute | solution.py:214
  81.4 1.9 %collective-permute-start.29 = (bf16[64,512]{1,0:T(8,128)(2,1)S(1)}, bf16[64,512]{1,0:T(8,128)(2,1)S(1)}, u32[]{:S(2)}, u32[]{:S(2)}) collective-permute-start(bf16[64,512]{1,0:T(8,128)(2,1)S(1)} %fusion.refs_0_), channel_id=1, source_target_pairs={{0,6},{1,7},{2,4},{3,5},{4,2},{5,3},{6,0},{7,1},{8,14},{9,15},{10,... | collective-permute-start | bytes 196616 | tf_op jit(solution)/shard_map/ppermute | solution.py:214
  83.9 4.2 %hidden_grad.1 = (bf16[64,5120]{1,0:T(8,128)(2,1)}, bf16[64,1280]{1,0:T(8,128)(2,1)}) custom-call(bf16[1280,512]{1,0:T(8,128)(2,1)} %own_ref.1, bf16[64,512]{1,0:T(8,128)(2,1)} %copy-done.8, bf16[64,512]{1,0:T(8,128)(2,1)} %copy-done.11, bf16[1280,256]{1,0:T(8,128)(2,1)} %copy-done.2, bf16[1280,256]{1,0:T(8,128)(2,1)} %copy-done.3, ...), custom_call_target="tpu_custom_call" | custom-call | flops 335544320 | bytes 3000000 | tf_op jit(solution)/shard_map/hidden_grad/pallas_call | solution.py:108
  90.0 1.2 %collective-permute-start.33 = (bf16[256,512]{1,0:T(8,128)(2,1)S(1)}, bf16[256,512]{1,0:T(8,128)(2,1)S(1)}, u32[]{:S(2)}, u32[]{:S(2)}) collective-permute-start(bf16[256,512]{1,0:T(8,128)(2,1)S(1)} %constant_dynamic-update-slice_fusion.refs_4_), channel_id=1, source_target_pairs={{0,16},{8,24},{16,0},{24,8},{1,17},{9,25},{17,1},{25,9},{2,18},{10... | collective-permute-start | bytes 786440 | tf_op jit(solution)/shard_map/ppermute | solution.py:214
  91.3 1.5 %collective-permute-start.30 = (bf16[192,512]{1,0:T(8,128)(2,1)S(1)}, bf16[192,512]{1,0:T(8,128)(2,1)S(1)}, u32[]{:S(2)}, u32[]{:S(2)}) collective-permute-start(bf16[192,512]{1,0:T(8,128)(2,1)S(1)} %pad_maximum_fusion.2), channel_id=1, source_target_pairs={{0,24},{8,16},{16,8},{24,0},{1,25},{9,17},{17,9},{25,1},{2,26},{10... | collective-permute-start | bytes 589832 | tf_op jit(solution)/shard_map/ppermute | solution.py:214
  93.5 1.9 %collective-permute-start.35 = (bf16[64,512]{1,0:T(8,128)(2,1)S(1)}, bf16[64,512]{1,0:T(8,128)(2,1)S(1)}, u32[]{:S(2)}, u32[]{:S(2)}) collective-permute-start(bf16[64,512]{1,0:T(8,128)(2,1)S(1)} %get-tuple-element.127), channel_id=1, source_target_pairs={{0,4},{1,5},{2,6},{3,7},{4,0},{5,1},{6,2},{7,3},{8,12},{9,13},{10,... | collective-permute-start | bytes 196616 | tf_op jit(solution)/shard_map/ppermute | solution.py:214
  95.4 4.6 %collective-permute-done.30.refs_8_ = bf16[192,512]{1,0:T(8,128)(2,1)S(1)} collective-permute-done((bf16[192,512]{1,0:T(8,128)(2,1)S(1)}, bf16[192,512]{1,0:T(8,128)(2,1)S(1)}, u32[]{:S(2)}, u32[]{:S(2)}) %collective-permute-start.30) | collective-permute-done | bytes 196640 | tf_op jit(solution)/shard_map/ppermute | solution.py:214
  100.0 1.8 %collective-permute-start.36 = (bf16[64,512]{1,0:T(8,128)(2,1)S(1)}, bf16[64,512]{1,0:T(8,128)(2,1)S(1)}, u32[]{:S(2)}, u32[]{:S(2)}) collective-permute-start(bf16[64,512]{1,0:T(8,128)(2,1)S(1)} %get-tuple-element.126), channel_id=1, source_target_pairs={{0,6},{1,7},{2,4},{3,5},{4,2},{5,3},{6,0},{7,1},{8,14},{9,15},{10,... | collective-permute-start | bytes 196616 | tf_op jit(solution)/shard_map/ppermute | solution.py:214
  103.6 2.8 %weight_grad.1 = (f32[160,512]{1,0:T(8,128)}, f32[160,512]{1,0:T(8,128)}) custom-call(bf16[320,256]{1,0:T(8,128)(2,1)} %get-tuple-element.106.refs_0_, bf16[320,256]{1,0:T(8,128)(2,1)} %copy-done.16, bf16[320,256]{1,0:T(8,128)(2,1)} %copy-done.17, bf16[320,256]{1,0:T(8,128)(2,1)} %copy-done.18, bf16[256,512]{1,0:T(8,128)(2,1)} %copy-done.10, ...), custom_call_target="tpu_custom_call" | custom-call | flops 335544320 | bytes 3000000 | tf_op jit(solution)/shard_map/weight_grad/pallas_call | solution.py:108
  108.8 1.7 %add.69 = f32[160,512]{1,0:T(8,128)} add(f32[160,512]{1,0:T(8,128)} %get-tuple-element.115, f32[160,512]{1,0:T(8,128)S(1)} %collective-permute-done.37) | non-fusion elementwise | flops 81920 | bytes 983040 | tf_op jit(solution)/shard_map/add | solution.py:313
  (150 shorter events, 16.9 us)
Async XLA Ops:
  2.7 9.1 %collective-permute-start.2 = (bf16[64,1280]{1,0:T(8,128)(2,1)}, bf16[64,1280]{1,0:T(8,128)(2,1)S(1)}, u32[]{:S(2)}, u32[]{:S(2)}) collective-permute-start(bf16[64,1280]{1,0:T(8,128)(2,1)} %get-tuple-element.68), channel_id=1, source_target_pairs={{0,24},{8,16},{16,8},{24,0},{1,25},{9,17},{17,9},{25,1},{2,26},{10... | collective-permute-start | bytes 491528 | tf_op jit(solution)/shard_map/ppermute | solution.py:214
  6.6 8.8 %collective-permute-start = (bf16[64,1280]{1,0:T(8,128)(2,1)}, bf16[64,1280]{1,0:T(8,128)(2,1)S(1)}, u32[]{:S(2)}, u32[]{:S(2)}) collective-permute-start(bf16[64,1280]{1,0:T(8,128)(2,1)} %get-tuple-element.66), channel_id=1, source_target_pairs={{0,8},{8,0},{16,24},{24,16},{1,9},{9,1},{17,25},{25,17},{2,10},{10... | collective-permute-start | bytes 491528 | tf_op jit(solution)/shard_map/ppermute | solution.py:214
  7.1 10.1 %collective-permute-start.1 = (bf16[64,1280]{1,0:T(8,128)(2,1)}, bf16[64,1280]{1,0:T(8,128)(2,1)S(1)}, u32[]{:S(2)}, u32[]{:S(2)}) collective-permute-start(bf16[64,1280]{1,0:T(8,128)(2,1)} %get-tuple-element.67), channel_id=1, source_target_pairs={{0,16},{8,24},{16,0},{24,8},{1,17},{9,25},{17,1},{25,9},{2,18},{10... | collective-permute-start | bytes 491528 | tf_op jit(solution)/shard_map/ppermute | solution.py:214
  12.2 12.4 %collective-permute-start.5 = (f32[64,512]{1,0:T(8,128)S(1)}, f32[64,512]{1,0:T(8,128)S(1)}, u32[]{:S(2)}, u32[]{:S(2)}) collective-permute-start(f32[64,512]{1,0:T(8,128)S(1)} %fusion.11), channel_id=1, source_target_pairs={{0,24},{8,16},{16,8},{24,0},{1,25},{9,17},{17,9},{25,1},{2,26},{10... | collective-permute-start | bytes 393224 | tf_op jit(solution)/shard_map/ppermute | solution.py:214
  15.7 9.1 %collective-permute-start.3 = (f32[64,512]{1,0:T(8,128)S(1)}, f32[64,512]{1,0:T(8,128)S(1)}, u32[]{:S(2)}, u32[]{:S(2)}) collective-permute-start(f32[64,512]{1,0:T(8,128)S(1)} %fusion.9), channel_id=1, source_target_pairs={{0,8},{8,0},{16,24},{24,16},{1,9},{9,1},{17,25},{25,17},{2,10},{10... | collective-permute-start | bytes 393224 | tf_op jit(solution)/shard_map/ppermute | solution.py:214
  17.6 7.2 %collective-permute-start.4 = (f32[64,512]{1,0:T(8,128)S(1)}, f32[64,512]{1,0:T(8,128)S(1)}, u32[]{:S(2)}, u32[]{:S(2)}) collective-permute-start(f32[64,512]{1,0:T(8,128)S(1)} %fusion.10), channel_id=1, source_target_pairs={{0,16},{8,24},{16,0},{24,8},{1,17},{9,25},{17,1},{25,9},{2,18},{10... | collective-permute-start | bytes 393224 | tf_op jit(solution)/shard_map/ppermute | solution.py:214
  18.2 11.5 %collective-permute-start.10 = (bf16[64,512]{1,0:T(8,128)(2,1)S(1)}, bf16[64,512]{1,0:T(8,128)(2,1)S(1)}, u32[]{:S(2)}, u32[]{:S(2)}) collective-permute-start(bf16[64,512]{1,0:T(8,128)(2,1)S(1)} %bitcast.44), channel_id=1, source_target_pairs={{0,2},{1,3},{2,0},{3,1},{4,6},{5,7},{6,4},{7,5},{8,10},{9,11},{10,... | collective-permute-start | bytes 196616 | tf_op jit(solution)/shard_map/ppermute | solution.py:214
  19.7 10.2 %collective-permute-start.11 = (bf16[64,512]{1,0:T(8,128)(2,1)S(1)}, bf16[64,512]{1,0:T(8,128)(2,1)S(1)}, u32[]{:S(2)}, u32[]{:S(2)}) collective-permute-start(bf16[64,512]{1,0:T(8,128)(2,1)S(1)} %bitcast.45), channel_id=1, source_target_pairs={{0,4},{1,5},{2,6},{3,7},{4,0},{5,1},{6,2},{7,3},{8,12},{9,13},{10,... | collective-permute-start | bytes 196616 | tf_op jit(solution)/shard_map/ppermute | solution.py:214
  24.6 6.3 %collective-permute-start.12 = (bf16[64,512]{1,0:T(8,128)(2,1)S(1)}, bf16[64,512]{1,0:T(8,128)(2,1)S(1)}, u32[]{:S(2)}, u32[]{:S(2)}) collective-permute-start(bf16[64,512]{1,0:T(8,128)(2,1)S(1)} %bitcast.46), channel_id=1, source_target_pairs={{0,6},{1,7},{2,4},{3,5},{4,2},{5,3},{6,0},{7,1},{8,14},{9,15},{10,... | collective-permute-start | bytes 196616 | tf_op jit(solution)/shard_map/ppermute | solution.py:214
  26.2 7.5 %collective-permute-start.7 = (bf16[64,512]{1,0:T(8,128)(2,1)S(1)}, bf16[64,512]{1,0:T(8,128)(2,1)S(1)}, u32[]{:S(2)}, u32[]{:S(2)}) collective-permute-start(bf16[64,512]{1,0:T(8,128)(2,1)S(1)} %fusion.2.refs_0_), channel_id=1, source_target_pairs={{0,4},{1,5},{2,6},{3,7},{4,0},{5,1},{6,2},{7,3},{8,12},{9,13},{10,... | collective-permute-start | bytes 196616 | tf_op jit(solution)/shard_map/ppermute | solution.py:214
  29.7 6.1 %collective-permute-start.8 = (bf16[64,512]{1,0:T(8,128)(2,1)S(1)}, bf16[64,512]{1,0:T(8,128)(2,1)S(1)}, u32[]{:S(2)}, u32[]{:S(2)}) collective-permute-start(bf16[64,512]{1,0:T(8,128)(2,1)S(1)} %fusion.2.refs_0_), channel_id=1, source_target_pairs={{0,6},{1,7},{2,4},{3,5},{4,2},{5,3},{6,0},{7,1},{8,14},{9,15},{10,... | collective-permute-start | bytes 196616 | tf_op jit(solution)/shard_map/ppermute | solution.py:214
  30.9 7.8 %collective-permute-start.13 = (bf16[256,512]{1,0:T(8,128)(2,1)S(1)}, bf16[256,512]{1,0:T(8,128)(2,1)S(1)}, u32[]{:S(2)}, u32[]{:S(2)}) collective-permute-start(bf16[256,512]{1,0:T(8,128)(2,1)S(1)} %pad_maximum_fusion.1), channel_id=1, source_target_pairs={{0,1},{1,0},{2,3},{3,2},{4,5},{5,4},{6,7},{7,6},{8,9},{9,8},{10,11... | collective-permute-start | bytes 786440 | tf_op jit(solution)/shard_map/ppermute | solution.py:214
  36.5 28.2 %collective-permute-start.17 = (bf16[1280,256]{1,0:T(8,128)(2,1)S(1)}, bf16[1280,256]{1,0:T(8,128)(2,1)S(1)}, u32[]{:S(2)}, u32[]{:S(2)}) collective-permute-start(bf16[1280,256]{1,0:T(8,128)(2,1)S(1)} %constant_dynamic-slice_fusion), channel_id=1, source_target_pairs={{0,8},{8,0},{16,24},{24,16},{1,9},{9,1},{17,25},{25,17},{2,10},{10... | collective-permute-start | bytes 1966088 | tf_op jit(solution)/shard_map/ppermute | solution.py:214
  37.1 27.6 %collective-permute-start.18 = (bf16[1280,256]{1,0:T(8,128)(2,1)S(1)}, bf16[1280,256]{1,0:T(8,128)(2,1)S(1)}, u32[]{:S(2)}, u32[]{:S(2)}) collective-permute-start(bf16[1280,256]{1,0:T(8,128)(2,1)S(1)} %constant_dynamic-slice_fusion), channel_id=1, source_target_pairs={{0,16},{8,24},{16,0},{24,8},{1,17},{9,25},{17,1},{25,9},{2,18},{10... | collective-permute-start | bytes 1966088 | tf_op jit(solution)/shard_map/ppermute | solution.py:214
  38.7 25.9 %collective-permute-start.14 = (bf16[320,256]{1,0:T(8,128)(2,1)}, bf16[320,256]{1,0:T(8,128)(2,1)S(1)}, u32[]{:S(2)}, u32[]{:S(2)}) collective-permute-start(bf16[320,256]{1,0:T(8,128)(2,1)} %get-tuple-element.83), channel_id=1, source_target_pairs={{0,2},{1,3},{2,0},{3,1},{4,6},{5,7},{6,4},{7,5},{8,10},{9,11},{10,... | collective-permute-start | bytes 491528 | tf_op jit(solution)/shard_map/ppermute | solution.py:214
  38.7 26.0 %collective-permute-start.15 = (bf16[320,256]{1,0:T(8,128)(2,1)}, bf16[320,256]{1,0:T(8,128)(2,1)S(1)}, u32[]{:S(2)}, u32[]{:S(2)}) collective-permute-start(bf16[320,256]{1,0:T(8,128)(2,1)} %get-tuple-element.84), channel_id=1, source_target_pairs={{0,4},{1,5},{2,6},{3,7},{4,0},{5,1},{6,2},{7,3},{8,12},{9,13},{10,... | collective-permute-start | bytes 491528 | tf_op jit(solution)/shard_map/ppermute | solution.py:214
  40.0 24.6 %collective-permute-start.16 = (bf16[320,256]{1,0:T(8,128)(2,1)S(1)}, bf16[320,256]{1,0:T(8,128)(2,1)S(1)}, u32[]{:S(2)}, u32[]{:S(2)}) collective-permute-start(bf16[320,256]{1,0:T(8,128)(2,1)S(1)} %copy-done.29), channel_id=1, source_target_pairs={{0,6},{1,7},{2,4},{3,5},{4,2},{5,3},{6,0},{7,1},{8,14},{9,15},{10,... | collective-permute-start | bytes 491528 | tf_op jit(solution)/shard_map/ppermute | solution.py:214
  65.3 11.5 %collective-permute-start.24 = (bf16[1280,256]{1,0:T(8,128)(2,1)S(1)}, bf16[1280,256]{1,0:T(8,128)(2,1)S(1)}, u32[]{:S(2)}, u32[]{:S(2)}) collective-permute-start(bf16[1280,256]{1,0:T(8,128)(2,1)S(1)} %collective-permute-done.17.refs_2_), channel_id=1, source_target_pairs={{0,1},{1,0},{2,3},{3,2},{4,5},{5,4},{6,7},{7,6},{8,9},{9,8},{10,11... | collective-permute-start | bytes 1966088 | tf_op jit(solution)/shard_map/ppermute | solution.py:214
  65.4 11.4 %collective-permute-start.25 = (bf16[1280,256]{1,0:T(8,128)(2,1)S(1)}, bf16[1280,256]{1,0:T(8,128)(2,1)}, u32[]{:S(2)}, u32[]{:S(2)}) collective-permute-start(bf16[1280,256]{1,0:T(8,128)(2,1)S(1)} %collective-permute-done.18.refs_3_), channel_id=1, source_target_pairs={{0,1},{1,0},{2,3},{3,2},{4,5},{5,4},{6,7},{7,6},{8,9},{9,8},{10,11... | collective-permute-start | bytes 1966088 | tf_op jit(solution)/shard_map/ppermute | solution.py:214
  68.2 8.6 %collective-permute-start.21 = (bf16[64,512]{1,0:T(8,128)(2,1)S(1)}, bf16[64,512]{1,0:T(8,128)(2,1)S(1)}, u32[]{:S(2)}, u32[]{:S(2)}) collective-permute-start(bf16[64,512]{1,0:T(8,128)(2,1)S(1)} %get-tuple-element.131), channel_id=1, source_target_pairs={{0,4},{1,5},{2,6},{3,7},{4,0},{5,1},{6,2},{7,3},{8,12},{9,13},{10,... | collective-permute-start | bytes 196616 | tf_op jit(solution)/shard_map/ppermute | solution.py:214
  69.5 7.3 %collective-permute-start.22 = (bf16[64,512]{1,0:T(8,128)(2,1)S(1)}, bf16[64,512]{1,0:T(8,128)(2,1)S(1)}, u32[]{:S(2)}, u32[]{:S(2)}) collective-permute-start(bf16[64,512]{1,0:T(8,128)(2,1)S(1)} %get-tuple-element.130), channel_id=1, source_target_pairs={{0,6},{1,7},{2,4},{3,5},{4,2},{5,3},{6,0},{7,1},{8,14},{9,15},{10,... | collective-permute-start | bytes 196616 | tf_op jit(solution)/shard_map/ppermute | solution.py:214
  77.4 5.9 %collective-permute-start.26 = (bf16[64,512]{1,0:T(8,128)(2,1)S(1)}, bf16[64,512]{1,0:T(8,128)(2,1)S(1)}, u32[]{:S(2)}, u32[]{:S(2)}) collective-permute-start(bf16[64,512]{1,0:T(8,128)(2,1)S(1)} %fusion.refs_0_), channel_id=1, source_target_pairs={{0,24},{8,16},{16,8},{24,0},{1,25},{9,17},{17,9},{25,1},{2,26},{10... | collective-permute-start | bytes 196616 | tf_op jit(solution)/shard_map/ppermute | solution.py:214
  78.9 9.3 %collective-permute-start.27 = (bf16[64,512]{1,0:T(8,128)(2,1)S(1)}, bf16[64,512]{1,0:T(8,128)(2,1)S(1)}, u32[]{:S(2)}, u32[]{:S(2)}) collective-permute-start(bf16[64,512]{1,0:T(8,128)(2,1)S(1)} %fusion.refs_0_), channel_id=1, source_target_pairs={{0,2},{1,3},{2,0},{3,1},{4,6},{5,7},{6,4},{7,5},{8,10},{9,11},{10,... | collective-permute-start | bytes 196616 | tf_op jit(solution)/shard_map/ppermute | solution.py:214
  80.2 8.0 %collective-permute-start.28 = (bf16[64,512]{1,0:T(8,128)(2,1)S(1)}, bf16[64,512]{1,0:T(8,128)(2,1)S(1)}, u32[]{:S(2)}, u32[]{:S(2)}) collective-permute-start(bf16[64,512]{1,0:T(8,128)(2,1)S(1)} %fusion.refs_0_), channel_id=1, source_target_pairs={{0,4},{1,5},{2,6},{3,7},{4,0},{5,1},{6,2},{7,3},{8,12},{9,13},{10,... | collective-permute-start | bytes 196616 | tf_op jit(solution)/shard_map/ppermute | solution.py:214
  81.4 6.8 %collective-permute-start.29 = (bf16[64,512]{1,0:T(8,128)(2,1)S(1)}, bf16[64,512]{1,0:T(8,128)(2,1)S(1)}, u32[]{:S(2)}, u32[]{:S(2)}) collective-permute-start(bf16[64,512]{1,0:T(8,128)(2,1)S(1)} %fusion.refs_0_), channel_id=1, source_target_pairs={{0,6},{1,7},{2,4},{3,5},{4,2},{5,3},{6,0},{7,1},{8,14},{9,15},{10,... | collective-permute-start | bytes 196616 | tf_op jit(solution)/shard_map/ppermute | solution.py:214
  89.1 12.7 %collective-permute-start.32 = (bf16[256,512]{1,0:T(8,128)(2,1)S(1)}, bf16[256,512]{1,0:T(8,128)(2,1)S(1)}, u32[]{:S(2)}, u32[]{:S(2)}) collective-permute-start(bf16[256,512]{1,0:T(8,128)(2,1)S(1)} %constant_dynamic-update-slice_fusion.refs_4_), channel_id=1, source_target_pairs={{0,8},{8,0},{16,24},{24,16},{1,9},{9,1},{17,25},{25,17},{2,10},{10... | collective-permute-start | bytes 786440 | tf_op jit(solution)/shard_map/ppermute | solution.py:214
  90.0 12.8 %collective-permute-start.33 = (bf16[256,512]{1,0:T(8,128)(2,1)S(1)}, bf16[256,512]{1,0:T(8,128)(2,1)S(1)}, u32[]{:S(2)}, u32[]{:S(2)}) collective-permute-start(bf16[256,512]{1,0:T(8,128)(2,1)S(1)} %constant_dynamic-update-slice_fusion.refs_4_), channel_id=1, source_target_pairs={{0,16},{8,24},{16,0},{24,8},{1,17},{9,25},{17,1},{25,9},{2,18},{10... | collective-permute-start | bytes 786440 | tf_op jit(solution)/shard_map/ppermute | solution.py:214
  91.3 8.7 %collective-permute-start.30 = (bf16[192,512]{1,0:T(8,128)(2,1)S(1)}, bf16[192,512]{1,0:T(8,128)(2,1)S(1)}, u32[]{:S(2)}, u32[]{:S(2)}) collective-permute-start(bf16[192,512]{1,0:T(8,128)(2,1)S(1)} %pad_maximum_fusion.2), channel_id=1, source_target_pairs={{0,24},{8,16},{16,8},{24,0},{1,25},{9,17},{17,9},{25,1},{2,26},{10... | collective-permute-start | bytes 589832 | tf_op jit(solution)/shard_map/ppermute | solution.py:214
  92.8 13.5 %collective-permute-start.34 = (bf16[64,512]{1,0:T(8,128)(2,1)S(1)}, bf16[64,512]{1,0:T(8,128)(2,1)S(1)}, u32[]{:S(2)}, u32[]{:S(2)}) collective-permute-start(bf16[64,512]{1,0:T(8,128)(2,1)S(1)} %get-tuple-element.128), channel_id=1, source_target_pairs={{0,2},{1,3},{2,0},{3,1},{4,6},{5,7},{6,4},{7,5},{8,10},{9,11},{10,... | collective-permute-start | bytes 196616 | tf_op jit(solution)/shard_map/ppermute | solution.py:214
  93.5 12.8 %collective-permute-start.35 = (bf16[64,512]{1,0:T(8,128)(2,1)S(1)}, bf16[64,512]{1,0:T(8,128)(2,1)S(1)}, u32[]{:S(2)}, u32[]{:S(2)}) collective-permute-start(bf16[64,512]{1,0:T(8,128)(2,1)S(1)} %get-tuple-element.127), channel_id=1, source_target_pairs={{0,4},{1,5},{2,6},{3,7},{4,0},{5,1},{6,2},{7,3},{8,12},{9,13},{10,... | collective-permute-start | bytes 196616 | tf_op jit(solution)/shard_map/ppermute | solution.py:214
  100.0 6.3 %collective-permute-start.36 = (bf16[64,512]{1,0:T(8,128)(2,1)S(1)}, bf16[64,512]{1,0:T(8,128)(2,1)S(1)}, u32[]{:S(2)}, u32[]{:S(2)}) collective-permute-start(bf16[64,512]{1,0:T(8,128)(2,1)S(1)} %get-tuple-element.126), channel_id=1, source_target_pairs={{0,6},{1,7},{2,4},{3,5},{4,2},{5,3},{6,0},{7,1},{8,14},{9,15},{10,... | collective-permute-start | bytes 196616 | tf_op jit(solution)/shard_map/ppermute | solution.py:214
  101.9 6.3 %collective-permute-start.31 = (bf16[64,1280]{1,0:T(8,128)(2,1)S(1)}, bf16[64,1280]{1,0:T(8,128)(2,1)S(1)}, u32[]{:S(2)}, u32[]{:S(2)}) collective-permute-start(bf16[64,1280]{1,0:T(8,128)(2,1)S(1)} %copy-done.30), channel_id=1, source_target_pairs={{0,24},{8,16},{16,8},{24,0},{1,25},{9,17},{17,9},{25,1},{2,26},{10... | collective-permute-start | bytes 491528 | tf_op jit(solution)/shard_map/ppermute | solution.py:214
  (38 other events, 291.0 us)

commit v10 on v9

--- a/solution.py
+++ b/solution.py
@@ -223,17 +223,17 @@
 
 
 def spread_far(near, size):
-    return [swap(jnp.concatenate(near, axis=0), "resp", size, 1)]
+    return [swap(piece, "resp", size, 1) for piece in near]
 
 
 def pair_sum(near, far, size):
     return near + swap(far, "resp", size, 1)
 
 
-def chip_parts(near, size):
+def chip_parts(near, size, distances):
     rows = near.shape[0] // (size // 2)
     pieces = [near[p * rows : (p + 1) * rows] for p in range(size // 2)]
-    return pieces[:1] + [swap(pieces[p].astype(BF16), "resp", size, 2 * p) for p in range(1, size // 2)]
+    return pieces[:1] + [swap(pieces[p].astype(BF16), "resp", size, 2 * p) for p in distances]
 
 
 def total(parts):
@@ -282,7 +282,7 @@
     )
     key_sums, far, *both = together(key_sums, far, *taken, *weight_near)
     taken, weight_near = both[:chips], both[chips:]
-    key_sums = total(chip_parts(pair_sum(key_sums, far, responses), responses))
+    key_sums = total(chip_parts(pair_sum(key_sums, far, responses), responses, range(1, chips)))
     value_sums = pair_sum(value_sums, value_far, responses)
     weight_far = [swap(piece, "resp", responses, 1) for piece in weight_near]
     key_sums, value_sums, *weight_far = together(key_sums, value_sums, *weight_far)
@@ -291,20 +291,21 @@
 
     first = {k: swap(key_pre_grad, "group", groups, k) for k in across}
     grads = spread_near(key_pre_grad, responses)
+    value_parts = chip_parts(value_sums, responses, (1,))
+    grads_first = together(*grads, value_parts[1], value_sums, *first.values())
+    grads, value_parts[1], value_sums = grads_first[:chips], grads_first[chips], grads_first[chips + 1]
+    first = dict(zip(first, grads_first[chips + 2 :]))
+    some, every = jnp.concatenate(grads[1:], axis=0), jnp.concatenate(grads, axis=0)
     grad_hidden, *parts = hidden_pass(
         key_pre_grad, first, key_matrix, dict(zip(beside, weight_near)), dict(zip(beside, weight_far))
     )
 
-    grad_hidden, *both = together(grad_hidden, *parts, *grads)
-    parts, grads = both[: len(parts)], both[len(parts) :]
-    some, every = jnp.concatenate(grads[1:], axis=0), jnp.concatenate(grads, axis=0)
     blocks = [[every]] + [None] * (groups - 1)
     for k in beside:
         blocks[k] = [swap(every, "group", groups, k)]
     for k in across:
         blocks[k] = [first[k], swap(some, "group", groups, k)]
-    grad_hidden, value_sums = together(grad_hidden, value_sums)
-    value_parts = chip_parts(value_sums, responses)
+    value_parts += chip_parts(value_sums, responses, range(2, chips))[1:]
     for k in across:
         *parts, blocks[k][-1] = together(*parts, blocks[k][-1])
     parts = [swap(part, "group", groups, k) for k, part in zip(across, parts)]

time: 111 us -> 108 us (0.973)
  waiting for transfers between devices: 19.6 us -> 15.9 us
  starting transfers between devices: 45.7 us -> 47.2 us
    ppermute x38 -> x44, waiting for transfers between devices: 19.6 us -> 15.9 us  [swap(): return lax.ppermute(array, axis, [(i, i ^ distance) for i in range(size)])]
    ppermute x38 -> x44, starting transfers between devices: 45.7 us -> 47.2 us  [swap(): return lax.ppermute(array, axis, [(i, i ^ distance) for i in range(size)])]
    unnamed x65 -> x73, local copies, waits for them, and re-layouts: 2.35 us -> 1.53 us
  transfers between devices with their start and end apart: 38 -> 44, of which waited for: 10 -> 14; matrix products, arithmetic and copies ran while one was open for 5% -> 6% of each run, Pallas kernels for 28% -> 29%
where the time goes in v10:
time: 108 us
  starting transfers between devices  47.2 us (44%)
  Pallas kernels  33 us (31%)
  waiting for transfers between devices  15.9 us (15%)
  other arithmetic  4.1 us (4%)
  local copies, waits for them, and re-layouts  3.01 us (3%)
  matrix products  2.74 us (3%)
  between operations  1.99 us (2%)
    ppermute x44, starting transfers between devices, swap(): return lax.ppermute(array, axis, [(i, i ^ distance) for i in range(size)])  47.2 us
    pallas_call x1, Pallas kernels, attend(): pl.pallas_call(partial(attend_kernel, len(key_pieces)), grid=(kv_heads,),...  21.7 us
    ppermute x44, waiting for transfers between devices, swap(): return lax.ppermute(array, axis, [(i, i ^ distance) for i in range(size)])  15.9 us
    pallas_call x4, Pallas kernels, in_vmem(): pl.pallas_call(kernel, in_specs=[whole] * len(arrays), out_specs=[whole]...  11.3 us
    dot_general x4, matrix products, dot(): return lax.dot_general(left, right, dims, preferred_element_type=F32)  2.74 us
  transfers between devices with their start and end apart: 44, of which 14 were waited for; matrix products, arithmetic and copies ran while one was open for 6% of the time, Pallas kernels for 29%

profile of v10, /device:TPU:0, one launch (start us, length us, event | category | flops | bytes accessed | tf_op | source)
XLA Modules:
  0.0 108.0 jit_solution(3242722538413414925)
XLA Ops:
  0.6 2.1 %split_hidden.1 = (bf16[64,1280]{1,0:T(8,128)(2,1)}, bf16[64,1280]{1,0:T(8,128)(2,1)}, bf16[64,1280]{1,0:T(8,128)(2,1)}, bf16[64,1280]{1,0:T(8,128)(2,1)}) custom-call(bf16[64,5120]{1,0:T(8,128)(2,1)} %bitcast.41), custom_call_target="tpu_custom_call" | custom-call | bytes 3000000 | tf_op jit(solution)/shard_map/split_hidden/pallas_call | solution.py:108
  2.7 3.9 %collective-permute-start.2 = (bf16[64,1280]{1,0:T(8,128)(2,1)}, bf16[64,1280]{1,0:T(8,128)(2,1)S(1)}, u32[]{:S(2)}, u32[]{:S(2)}) collective-permute-start(bf16[64,1280]{1,0:T(8,128)(2,1)} %get-tuple-element.67), channel_id=1, source_target_pairs={{0,24},{8,16},{16,8},{24,0},{1,25},{9,17},{17,9},{25,1},{2,26},{10... | collective-permute-start | bytes 491528 | tf_op jit(solution)/shard_map/ppermute | solution.py:214
  7.2 1.7 %fusion.8 = f32[64,512]{1,0:T(8,128)S(1)} fusion(bf16[64,1280]{1,0:T(8,128)(2,1)} %get-tuple-element.64.refs_0_, bf16[1280,512]{1,0:T(8,128)(2,1)} %own_ref.1), kind=kOutput, calls=%fused_computation.28 | convolution fusion | flops 83886080 | bytes 1605632 | tf_op jit(solution)/shard_map/dot_general | solution.py:23
  9.0 2.8 %collective-permute-done.2.refs_3_ = bf16[64,1280]{1,0:T(8,128)(2,1)S(1)} collective-permute-done((bf16[64,1280]{1,0:T(8,128)(2,1)}, bf16[64,1280]{1,0:T(8,128)(2,1)S(1)}, u32[]{:S(2)}, u32[]{:S(2)}) %collective-permute-start.2) | collective-permute-done | bytes 163872 | tf_op jit(solution)/shard_map/ppermute | solution.py:214
  12.2 3.0 %collective-permute-start.5 = (f32[64,512]{1,0:T(8,128)S(1)}, f32[64,512]{1,0:T(8,128)S(1)}, u32[]{:S(2)}, u32[]{:S(2)}) collective-permute-start(f32[64,512]{1,0:T(8,128)S(1)} %fusion.11), channel_id=1, source_target_pairs={{0,24},{8,16},{16,8},{24,0},{1,25},{9,17},{17,9},{25,1},{2,26},{10... | collective-permute-start | bytes 393224 | tf_op jit(solution)/shard_map/ppermute | solution.py:214
  15.6 1.6 %collective-permute-start.4 = (f32[64,512]{1,0:T(8,128)S(1)}, f32[64,512]{1,0:T(8,128)S(1)}, u32[]{:S(2)}, u32[]{:S(2)}) collective-permute-start(f32[64,512]{1,0:T(8,128)S(1)} %fusion.10), channel_id=1, source_target_pairs={{0,16},{8,24},{16,0},{24,8},{1,17},{9,25},{17,1},{25,9},{2,18},{10... | collective-permute-start | bytes 393224 | tf_op jit(solution)/shard_map/ppermute | solution.py:214
  17.7 1.8 %collective-permute-start.13 = (bf16[64,512]{1,0:T(8,128)(2,1)S(1)}, bf16[64,512]{1,0:T(8,128)(2,1)S(1)}, u32[]{:S(2)}, u32[]{:S(2)}) collective-permute-start(bf16[64,512]{1,0:T(8,128)(2,1)S(1)} %bitcast.49), channel_id=1, source_target_pairs={{0,2},{1,3},{2,0},{3,1},{4,6},{5,7},{6,4},{7,5},{8,10},{9,11},{10,... | collective-permute-start | bytes 196616 | tf_op jit(solution)/shard_map/ppermute | solution.py:214
  19.4 2.6 %collective-permute-start.14 = (bf16[64,512]{1,0:T(8,128)(2,1)S(1)}, bf16[64,512]{1,0:T(8,128)(2,1)S(1)}, u32[]{:S(2)}, u32[]{:S(2)}) collective-permute-start(bf16[64,512]{1,0:T(8,128)(2,1)S(1)} %bitcast.50), channel_id=1, source_target_pairs={{0,4},{1,5},{2,6},{3,7},{4,0},{5,1},{6,2},{7,3},{8,12},{9,13},{10,... | collective-permute-start | bytes 196616 | tf_op jit(solution)/shard_map/ppermute | solution.py:214
  23.2 1.6 %collective-permute-start.6 = (bf16[64,512]{1,0:T(8,128)(2,1)S(1)}, bf16[64,512]{1,0:T(8,128)(2,1)S(1)}, u32[]{:S(2)}, u32[]{:S(2)}) collective-permute-start(bf16[64,512]{1,0:T(8,128)(2,1)S(1)} %fusion.2.refs_0_), channel_id=1, source_target_pairs={{0,2},{1,3},{2,0},{3,1},{4,6},{5,7},{6,4},{7,5},{8,10},{9,11},{10,... | collective-permute-start | bytes 196616 | tf_op jit(solution)/shard_map/ppermute | solution.py:214
  24.9 2.6 %collective-permute-start.7 = (bf16[64,512]{1,0:T(8,128)(2,1)S(1)}, bf16[64,512]{1,0:T(8,128)(2,1)S(1)}, u32[]{:S(2)}, u32[]{:S(2)}) collective-permute-start(bf16[64,512]{1,0:T(8,128)(2,1)S(1)} %fusion.2.refs_0_), channel_id=1, source_target_pairs={{0,4},{1,5},{2,6},{3,7},{4,0},{5,1},{6,2},{7,3},{8,12},{9,13},{10,... | collective-permute-start | bytes 196616 | tf_op jit(solution)/shard_map/ppermute | solution.py:214
  29.4 2.3 %turn_hidden.1 = (bf16[320,256]{1,0:T(8,128)(2,1)}, bf16[320,256]{1,0:T(8,128)(2,1)}, bf16[320,256]{1,0:T(8,128)(2,1)}, bf16[320,256]{1,0:T(8,128)(2,1)}) custom-call(bf16[64,1280]{1,0:T(8,128)(2,1)} %get-tuple-element.64.refs_0_, bf16[64,1280]{1,0:T(8,128)(2,1)} %copy-done.7, bf16[64,1280]{1,0:T(8,128)(2,1)} %copy-done.6, bf16[64,1280]{1,0:T(8,128)(2,1)} %copy-done.5), custom_call_target="tpu_custom_call" | custom-call | bytes 3000000 | tf_op jit(solution)/shard_map/turn_hidden/pallas_call | solution.py:108
  32.0 1.5 %collective-permute-done.8.refs_3_ = bf16[64,512]{1,0:T(8,128)(2,1)S(1)} collective-permute-done((bf16[64,512]{1,0:T(8,128)(2,1)S(1)}, bf16[64,512]{1,0:T(8,128)(2,1)S(1)}, u32[]{:S(2)}, u32[]{:S(2)}) %collective-permute-start.8) | collective-permute-done | bytes 65568 | tf_op jit(solution)/shard_map/ppermute | solution.py:214
  35.2 1.5 %collective-permute-start.23 = (bf16[1280,256]{1,0:T(8,128)(2,1)S(1)}, bf16[1280,256]{1,0:T(8,128)(2,1)S(1)}, u32[]{:S(2)}, u32[]{:S(2)}) collective-permute-start(bf16[1280,256]{1,0:T(8,128)(2,1)S(1)} %constant_dynamic-slice_fusion), channel_id=1, source_target_pairs={{0,8},{8,0},{16,24},{24,16},{1,9},{9,1},{17,25},{25,17},{2,10},{10... | collective-permute-start | bytes 1966088 | tf_op jit(solution)/shard_map/ppermute | solution.py:214
  37.4 2.2 %collective-permute-start.21 = (bf16[320,256]{1,0:T(8,128)(2,1)}, bf16[320,256]{1,0:T(8,128)(2,1)S(1)}, u32[]{:S(2)}, u32[]{:S(2)}) collective-permute-start(bf16[320,256]{1,0:T(8,128)(2,1)} %get-tuple-element.83), channel_id=1, source_target_pairs={{0,4},{1,5},{2,6},{3,7},{4,0},{5,1},{6,2},{7,3},{8,12},{9,13},{10,... | collective-permute-start | bytes 491528 | tf_op jit(solution)/shard_map/ppermute | solution.py:214
  39.7 2.1 %collective-permute-start.22 = (bf16[320,256]{1,0:T(8,128)(2,1)}, bf16[320,256]{1,0:T(8,128)(2,1)S(1)}, u32[]{:S(2)}, u32[]{:S(2)}) collective-permute-start(bf16[320,256]{1,0:T(8,128)(2,1)} %get-tuple-element.84), channel_id=1, source_target_pairs={{0,6},{1,7},{2,4},{3,5},{4,2},{5,3},{6,0},{7,1},{8,14},{9,15},{10,... | collective-permute-start | bytes 491528 | tf_op jit(solution)/shard_map/ppermute | solution.py:214
  41.9 21.7 %attend.1 = (bf16[256,4096]{1,0:T(8,128)(2,1)}, bf16[256,512]{1,0:T(8,128)(2,1)}, bf16[256,512]{1,0:T(8,128)(2,1)}, f32[256,512]{1,0:T(8,128)}, f32[256,512]{1,0...) custom-call(s32[1,1]{1,0:T(1,128)S(6)} %copy.30.length_ref, bf16[256,4096]{1,0:T(8,128)(2,1)} %bitcast.43, ...), custom_call_target="tpu_custom_call" | custom-call | flops 16106127360 | bytes 10000000 | tf_op jit(solution)/shard_map/attend/pallas_call | solution.py:91
  67.1 1.8 %collective-permute-start.28 = (bf16[64,512]{1,0:T(8,128)(2,1)S(1)}, bf16[64,512]{1,0:T(8,128)(2,1)S(1)}, u32[]{:S(2)}, u32[]{:S(2)}) collective-permute-start(bf16[64,512]{1,0:T(8,128)(2,1)S(1)} %get-tuple-element.127), channel_id=1, source_target_pairs={{0,6},{1,7},{2,4},{3,5},{4,2},{5,3},{6,0},{7,1},{8,14},{9,15},{10,... | collective-permute-start | bytes 196616 | tf_op jit(solution)/shard_map/ppermute | solution.py:214
  68.9 2.7 %collective-permute-start.26 = (bf16[64,512]{1,0:T(8,128)(2,1)S(1)}, bf16[64,512]{1,0:T(8,128)(2,1)S(1)}, u32[]{:S(2)}, u32[]{:S(2)}) collective-permute-start(bf16[64,512]{1,0:T(8,128)(2,1)S(1)} %get-tuple-element.126), channel_id=1, source_target_pairs={{0,2},{1,3},{2,0},{3,1},{4,6},{5,7},{6,4},{7,5},{8,10},{9,11},{10,... | collective-permute-start | bytes 196616 | tf_op jit(solution)/shard_map/ppermute | solution.py:214
  71.7 2.2 %collective-permute-done.28 = bf16[64,512]{1,0:T(8,128)(2,1)S(1)} collective-permute-done((bf16[64,512]{1,0:T(8,128)(2,1)S(1)}, bf16[64,512]{1,0:T(8,128)(2,1)S(1)}, u32[]{:S(2)}, u32[]{:S(2)}) %collective-permute-start.28) | collective-permute-done | bytes 65568 | tf_op jit(solution)/shard_map/ppermute | solution.py:214
  73.9 2.0 %collective-permute-done.27 = bf16[64,512]{1,0:T(8,128)(2,1)S(1)} collective-permute-done((bf16[64,512]{1,0:T(8,128)(2,1)S(1)}, bf16[64,512]{1,0:T(8,128)(2,1)S(1)}, u32[]{:S(2)}, u32[]{:S(2)}) %collective-permute-start.27) | collective-permute-done | bytes 65568 | tf_op jit(solution)/shard_map/ppermute | solution.py:214
  76.7 2.2 %collective-permute-start.33 = (bf16[64,512]{1,0:T(8,128)(2,1)S(1)}, bf16[64,512]{1,0:T(8,128)(2,1)S(1)}, u32[]{:S(2)}, u32[]{:S(2)}) collective-permute-start(bf16[64,512]{1,0:T(8,128)(2,1)S(1)} %fusion.refs_0_), channel_id=1, source_target_pairs={{0,4},{1,5},{2,6},{3,7},{4,0},{5,1},{6,2},{7,3},{8,12},{9,13},{10,... | collective-permute-start | bytes 196616 | tf_op jit(solution)/shard_map/ppermute | solution.py:214
  78.9 2.1 %collective-permute-start.34 = (bf16[64,512]{1,0:T(8,128)(2,1)S(1)}, bf16[64,512]{1,0:T(8,128)(2,1)S(1)}, u32[]{:S(2)}, u32[]{:S(2)}) collective-permute-start(bf16[64,512]{1,0:T(8,128)(2,1)S(1)} %fusion.refs_0_), channel_id=1, source_target_pairs={{0,6},{1,7},{2,4},{3,5},{4,2},{5,3},{6,0},{7,1},{8,14},{9,15},{10,... | collective-permute-start | bytes 196616 | tf_op jit(solution)/shard_map/ppermute | solution.py:214
  81.1 1.5 %collective-permute-start.36 = (bf16[64,512]{1,0:T(8,128)(2,1)S(1)}, bf16[64,512]{1,0:T(8,128)(2,1)S(1)}, u32[]{:S(2)}, u32[]{:S(2)}) collective-permute-start(bf16[64,512]{1,0:T(8,128)(2,1)S(1)} %fusion.refs_0_), channel_id=1, source_target_pairs={{0,24},{8,16},{16,8},{24,0},{1,25},{9,17},{17,9},{25,1},{2,26},{10... | collective-permute-start | bytes 196616 | tf_op jit(solution)/shard_map/ppermute | solution.py:214
  82.6 2.0 %collective-permute-done.33 = bf16[64,512]{1,0:T(8,128)(2,1)S(1)} collective-permute-done((bf16[64,512]{1,0:T(8,128)(2,1)S(1)}, bf16[64,512]{1,0:T(8,128)(2,1)S(1)}, u32[]{:S(2)}, u32[]{:S(2)}) %collective-permute-start.33) | collective-permute-done | bytes 65568 | tf_op jit(solution)/shard_map/ppermute | solution.py:214
  86.4 1.4 %collective-permute-start.39 = (bf16[256,512]{1,0:T(8,128)(2,1)S(1)}, bf16[256,512]{1,0:T(8,128)(2,1)S(1)}, u32[]{:S(2)}, u32[]{:S(2)}) collective-permute-start(bf16[256,512]{1,0:T(8,128)(2,1)S(1)} %constant_dynamic-update-slice_fusion.refs_4_), channel_id=1, source_target_pairs={{0,8},{8,0},{16,24},{24,16},{1,9},{9,1},{17,25},{25,17},{2,10},{10... | collective-permute-start | bytes 786440 | tf_op jit(solution)/shard_map/ppermute | solution.py:214
  88.5 1.5 %collective-permute-start.37 = (bf16[192,512]{1,0:T(8,128)(2,1)S(1)}, bf16[192,512]{1,0:T(8,128)(2,1)S(1)}, u32[]{:S(2)}, u32[]{:S(2)}) collective-permute-start(bf16[192,512]{1,0:T(8,128)(2,1)S(1)} %pad_maximum_fusion), channel_id=1, source_target_pairs={{0,24},{8,16},{16,8},{24,0},{1,25},{9,17},{17,9},{25,1},{2,26},{10... | collective-permute-start | bytes 589832 | tf_op jit(solution)/shard_map/ppermute | solution.py:214
  90.1 2.2 %collective-permute-start.41 = (bf16[64,512]{1,0:T(8,128)(2,1)S(1)}, bf16[64,512]{1,0:T(8,128)(2,1)S(1)}, u32[]{:S(2)}, u32[]{:S(2)}) collective-permute-start(bf16[64,512]{1,0:T(8,128)(2,1)S(1)} %get-tuple-element.125), channel_id=1, source_target_pairs={{0,4},{1,5},{2,6},{3,7},{4,0},{5,1},{6,2},{7,3},{8,12},{9,13},{10,... | collective-permute-start | bytes 196616 | tf_op jit(solution)/shard_map/ppermute | solution.py:214
  92.3 2.1 %collective-permute-start.42 = (bf16[64,512]{1,0:T(8,128)(2,1)S(1)}, bf16[64,512]{1,0:T(8,128)(2,1)S(1)}, u32[]{:S(2)}, u32[]{:S(2)}) collective-permute-start(bf16[64,512]{1,0:T(8,128)(2,1)S(1)} %get-tuple-element.124), channel_id=1, source_target_pairs={{0,6},{1,7},{2,4},{3,5},{4,2},{5,3},{6,0},{7,1},{8,14},{9,15},{10,... | collective-permute-start | bytes 196616 | tf_op jit(solution)/shard_map/ppermute | solution.py:214
  94.4 4.2 %hidden_grad.1 = (bf16[64,5120]{1,0:T(8,128)(2,1)}, bf16[64,1280]{1,0:T(8,128)(2,1)}) custom-call(bf16[1280,512]{1,0:T(8,128)(2,1)} %own_ref.1, bf16[64,512]{1,0:T(8,128)(2,1)} %copy-done.8, bf16[64,512]{1,0:T(8,128)(2,1)} %copy-done.11, bf16[1280,256]{1,0:T(8,128)(2,1)} %copy-done.2, bf16[1280,256]{1,0:T(8,128)(2,1)} %copy-done.3, ...), custom_call_target="tpu_custom_call" | custom-call | flops 335544320 | bytes 3000000 | tf_op jit(solution)/shard_map/hidden_grad/pallas_call | solution.py:108
  98.7 1.5 %collective-permute-start.38 = (bf16[64,1280]{1,0:T(8,128)(2,1)}, bf16[64,1280]{1,0:T(8,128)(2,1)S(1)}, u32[]{:S(2)}, u32[]{:S(2)}) collective-permute-start(bf16[64,1280]{1,0:T(8,128)(2,1)} %get-tuple-element.102), channel_id=1, source_target_pairs={{0,24},{8,16},{16,8},{24,0},{1,25},{9,17},{17,9},{25,1},{2,26},{10... | collective-permute-start | bytes 491528 | tf_op jit(solution)/shard_map/ppermute | solution.py:214
  101.6 2.7 %weight_grad.1 = (f32[160,512]{1,0:T(8,128)}, f32[160,512]{1,0:T(8,128)}) custom-call(bf16[320,256]{1,0:T(8,128)(2,1)} %get-tuple-element.103.refs_0_, bf16[320,256]{1,0:T(8,128)(2,1)} %copy-done.15, bf16[320,256]{1,0:T(8,128)(2,1)} %copy-done.16, bf16[320,256]{1,0:T(8,128)(2,1)} %copy-done.17, bf16[256,512]{1,0:T(8,128)(2,1)} %copy-done.10, ...), custom_call_target="tpu_custom_call" | custom-call | flops 335544320 | bytes 3000000 | tf_op jit(solution)/shard_map/weight_grad/pallas_call | solution.py:108
  106.2 1.7 %add.69 = f32[160,512]{1,0:T(8,128)} add(f32[160,512]{1,0:T(8,128)} %get-tuple-element.113, f32[160,512]{1,0:T(8,128)S(1)} %collective-permute-done.43) | non-fusion elementwise | flops 81920 | bytes 983040 | tf_op jit(solution)/shard_map/add | solution.py:314
  (169 shorter events, 16.8 us)
Async XLA Ops:
  2.7 9.1 %collective-permute-start.2 = (bf16[64,1280]{1,0:T(8,128)(2,1)}, bf16[64,1280]{1,0:T(8,128)(2,1)S(1)}, u32[]{:S(2)}, u32[]{:S(2)}) collective-permute-start(bf16[64,1280]{1,0:T(8,128)(2,1)} %get-tuple-element.67), channel_id=1, source_target_pairs={{0,24},{8,16},{16,8},{24,0},{1,25},{9,17},{17,9},{25,1},{2,26},{10... | collective-permute-start | bytes 491528 | tf_op jit(solution)/shard_map/ppermute | solution.py:214
  6.6 8.6 %collective-permute-start.1 = (bf16[64,1280]{1,0:T(8,128)(2,1)}, bf16[64,1280]{1,0:T(8,128)(2,1)S(1)}, u32[]{:S(2)}, u32[]{:S(2)}) collective-permute-start(bf16[64,1280]{1,0:T(8,128)(2,1)} %get-tuple-element.66), channel_id=1, source_target_pairs={{0,16},{8,24},{16,0},{24,8},{1,17},{9,25},{17,1},{25,9},{2,18},{10... | collective-permute-start | bytes 491528 | tf_op jit(solution)/shard_map/ppermute | solution.py:214
  7.1 10.1 %collective-permute-start = (bf16[64,1280]{1,0:T(8,128)(2,1)}, bf16[64,1280]{1,0:T(8,128)(2,1)S(1)}, u32[]{:S(2)}, u32[]{:S(2)}) collective-permute-start(bf16[64,1280]{1,0:T(8,128)(2,1)} %get-tuple-element.65), channel_id=1, source_target_pairs={{0,8},{8,0},{16,24},{24,16},{1,9},{9,1},{17,25},{25,17},{2,10},{10... | collective-permute-start | bytes 491528 | tf_op jit(solution)/shard_map/ppermute | solution.py:214
  12.2 9.8 %collective-permute-start.5 = (f32[64,512]{1,0:T(8,128)S(1)}, f32[64,512]{1,0:T(8,128)S(1)}, u32[]{:S(2)}, u32[]{:S(2)}) collective-permute-start(f32[64,512]{1,0:T(8,128)S(1)} %fusion.11), channel_id=1, source_target_pairs={{0,24},{8,16},{16,8},{24,0},{1,25},{9,17},{17,9},{25,1},{2,26},{10... | collective-permute-start | bytes 393224 | tf_op jit(solution)/shard_map/ppermute | solution.py:214
  15.6 6.6 %collective-permute-start.4 = (f32[64,512]{1,0:T(8,128)S(1)}, f32[64,512]{1,0:T(8,128)S(1)}, u32[]{:S(2)}, u32[]{:S(2)}) collective-permute-start(f32[64,512]{1,0:T(8,128)S(1)} %fusion.10), channel_id=1, source_target_pairs={{0,16},{8,24},{16,0},{24,8},{1,17},{9,25},{17,1},{25,9},{2,18},{10... | collective-permute-start | bytes 393224 | tf_op jit(solution)/shard_map/ppermute | solution.py:214
  17.7 9.8 %collective-permute-start.13 = (bf16[64,512]{1,0:T(8,128)(2,1)S(1)}, bf16[64,512]{1,0:T(8,128)(2,1)S(1)}, u32[]{:S(2)}, u32[]{:S(2)}) collective-permute-start(bf16[64,512]{1,0:T(8,128)(2,1)S(1)} %bitcast.49), channel_id=1, source_target_pairs={{0,2},{1,3},{2,0},{3,1},{4,6},{5,7},{6,4},{7,5},{8,10},{9,11},{10,... | collective-permute-start | bytes 196616 | tf_op jit(solution)/shard_map/ppermute | solution.py:214
  19.4 8.3 %collective-permute-start.14 = (bf16[64,512]{1,0:T(8,128)(2,1)S(1)}, bf16[64,512]{1,0:T(8,128)(2,1)S(1)}, u32[]{:S(2)}, u32[]{:S(2)}) collective-permute-start(bf16[64,512]{1,0:T(8,128)(2,1)S(1)} %bitcast.50), channel_id=1, source_target_pairs={{0,4},{1,5},{2,6},{3,7},{4,0},{5,1},{6,2},{7,3},{8,12},{9,13},{10,... | collective-permute-start | bytes 196616 | tf_op jit(solution)/shard_map/ppermute | solution.py:214
  22.0 6.8 %collective-permute-start.15 = (bf16[64,512]{1,0:T(8,128)(2,1)S(1)}, bf16[64,512]{1,0:T(8,128)(2,1)S(1)}, u32[]{:S(2)}, u32[]{:S(2)}) collective-permute-start(bf16[64,512]{1,0:T(8,128)(2,1)S(1)} %bitcast.51), channel_id=1, source_target_pairs={{0,6},{1,7},{2,4},{3,5},{4,2},{5,3},{6,0},{7,1},{8,14},{9,15},{10,... | collective-permute-start | bytes 196616 | tf_op jit(solution)/shard_map/ppermute | solution.py:214
  23.2 5.6 %collective-permute-start.6 = (bf16[64,512]{1,0:T(8,128)(2,1)S(1)}, bf16[64,512]{1,0:T(8,128)(2,1)S(1)}, u32[]{:S(2)}, u32[]{:S(2)}) collective-permute-start(bf16[64,512]{1,0:T(8,128)(2,1)S(1)} %fusion.2.refs_0_), channel_id=1, source_target_pairs={{0,2},{1,3},{2,0},{3,1},{4,6},{5,7},{6,4},{7,5},{8,10},{9,11},{10,... | collective-permute-start | bytes 196616 | tf_op jit(solution)/shard_map/ppermute | solution.py:214
  24.9 7.1 %collective-permute-start.7 = (bf16[64,512]{1,0:T(8,128)(2,1)S(1)}, bf16[64,512]{1,0:T(8,128)(2,1)S(1)}, u32[]{:S(2)}, u32[]{:S(2)}) collective-permute-start(bf16[64,512]{1,0:T(8,128)(2,1)S(1)} %fusion.2.refs_0_), channel_id=1, source_target_pairs={{0,4},{1,5},{2,6},{3,7},{4,0},{5,1},{6,2},{7,3},{8,12},{9,13},{10,... | collective-permute-start | bytes 196616 | tf_op jit(solution)/shard_map/ppermute | solution.py:214
  27.5 6.1 %collective-permute-start.8 = (bf16[64,512]{1,0:T(8,128)(2,1)S(1)}, bf16[64,512]{1,0:T(8,128)(2,1)S(1)}, u32[]{:S(2)}, u32[]{:S(2)}) collective-permute-start(bf16[64,512]{1,0:T(8,128)(2,1)S(1)} %fusion.2.refs_0_), channel_id=1, source_target_pairs={{0,6},{1,7},{2,4},{3,5},{4,2},{5,3},{6,0},{7,1},{8,14},{9,15},{10,... | collective-permute-start | bytes 196616 | tf_op jit(solution)/shard_map/ppermute | solution.py:214
  27.7 5.8 %collective-permute-start.16 = (bf16[64,512]{1,0:T(8,128)(2,1)S(1)}, bf16[64,512]{1,0:T(8,128)(2,1)S(1)}, u32[]{:S(2)}, u32[]{:S(2)}) collective-permute-start(bf16[64,512]{1,0:T(8,128)(2,1)S(1)} %bitcast.52), channel_id=1, source_target_pairs={{0,1},{1,0},{2,3},{3,2},{4,5},{5,4},{6,7},{7,6},{8,9},{9,8},{10,11... | collective-permute-start | bytes 196616 | tf_op jit(solution)/shard_map/ppermute | solution.py:214
  34.2 5.5 %collective-permute-start.12 = (bf16[64,512]{1,0:T(8,128)(2,1)S(1)}, bf16[64,512]{1,0:T(8,128)(2,1)S(1)}, u32[]{:S(2)}, u32[]{:S(2)}) collective-permute-start(bf16[64,512]{1,0:T(8,128)(2,1)S(1)} %collective-permute-done.8.refs_3_), channel_id=1, source_target_pairs={{0,1},{1,0},{2,3},{3,2},{4,5},{5,4},{6,7},{7,6},{8,9},{9,8},{10,11... | collective-permute-start | bytes 196616 | tf_op jit(solution)/shard_map/ppermute | solution.py:214
  35.2 28.5 %collective-permute-start.23 = (bf16[1280,256]{1,0:T(8,128)(2,1)S(1)}, bf16[1280,256]{1,0:T(8,128)(2,1)S(1)}, u32[]{:S(2)}, u32[]{:S(2)}) collective-permute-start(bf16[1280,256]{1,0:T(8,128)(2,1)S(1)} %constant_dynamic-slice_fusion), channel_id=1, source_target_pairs={{0,8},{8,0},{16,24},{24,16},{1,9},{9,1},{17,25},{25,17},{2,10},{10... | collective-permute-start | bytes 1966088 | tf_op jit(solution)/shard_map/ppermute | solution.py:214
  36.8 27.0 %collective-permute-start.24 = (bf16[1280,256]{1,0:T(8,128)(2,1)S(1)}, bf16[1280,256]{1,0:T(8,128)(2,1)S(1)}, u32[]{:S(2)}, u32[]{:S(2)}) collective-permute-start(bf16[1280,256]{1,0:T(8,128)(2,1)S(1)} %constant_dynamic-slice_fusion), channel_id=1, source_target_pairs={{0,16},{8,24},{16,0},{24,8},{1,17},{9,25},{17,1},{25,9},{2,18},{10... | collective-permute-start | bytes 1966088 | tf_op jit(solution)/shard_map/ppermute | solution.py:214
  37.4 26.3 %collective-permute-start.20 = (bf16[320,256]{1,0:T(8,128)(2,1)}, bf16[320,256]{1,0:T(8,128)(2,1)S(1)}, u32[]{:S(2)}, u32[]{:S(2)}) collective-permute-start(bf16[320,256]{1,0:T(8,128)(2,1)} %get-tuple-element.82), channel_id=1, source_target_pairs={{0,2},{1,3},{2,0},{3,1},{4,6},{5,7},{6,4},{7,5},{8,10},{9,11},{10,... | collective-permute-start | bytes 491528 | tf_op jit(solution)/shard_map/ppermute | solution.py:214
  37.4 26.2 %collective-permute-start.21 = (bf16[320,256]{1,0:T(8,128)(2,1)}, bf16[320,256]{1,0:T(8,128)(2,1)S(1)}, u32[]{:S(2)}, u32[]{:S(2)}) collective-permute-start(bf16[320,256]{1,0:T(8,128)(2,1)} %get-tuple-element.83), channel_id=1, source_target_pairs={{0,4},{1,5},{2,6},{3,7},{4,0},{5,1},{6,2},{7,3},{8,12},{9,13},{10,... | collective-permute-start | bytes 491528 | tf_op jit(solution)/shard_map/ppermute | solution.py:214
  39.7 24.0 %collective-permute-start.22 = (bf16[320,256]{1,0:T(8,128)(2,1)}, bf16[320,256]{1,0:T(8,128)(2,1)S(1)}, u32[]{:S(2)}, u32[]{:S(2)}) collective-permute-start(bf16[320,256]{1,0:T(8,128)(2,1)} %get-tuple-element.84), channel_id=1, source_target_pairs={{0,6},{1,7},{2,4},{3,5},{4,2},{5,3},{6,0},{7,1},{8,14},{9,15},{10,... | collective-permute-start | bytes 491528 | tf_op jit(solution)/shard_map/ppermute | solution.py:214
  64.3 11.6 %collective-permute-start.30 = (bf16[1280,256]{1,0:T(8,128)(2,1)S(1)}, bf16[1280,256]{1,0:T(8,128)(2,1)S(1)}, u32[]{:S(2)}, u32[]{:S(2)}) collective-permute-start(bf16[1280,256]{1,0:T(8,128)(2,1)S(1)} %collective-permute-done.23.refs_2_), channel_id=1, source_target_pairs={{0,1},{1,0},{2,3},{3,2},{4,5},{5,4},{6,7},{7,6},{8,9},{9,8},{10,11... | collective-permute-start | bytes 1966088 | tf_op jit(solution)/shard_map/ppermute | solution.py:214
  64.4 11.6 %collective-permute-start.31 = (bf16[1280,256]{1,0:T(8,128)(2,1)S(1)}, bf16[1280,256]{1,0:T(8,128)(2,1)}, u32[]{:S(2)}, u32[]{:S(2)}) collective-permute-start(bf16[1280,256]{1,0:T(8,128)(2,1)S(1)} %collective-permute-done.24.refs_3_), channel_id=1, source_target_pairs={{0,1},{1,0},{2,3},{3,2},{4,5},{5,4},{6,7},{7,6},{8,9},{9,8},{10,11... | collective-permute-start | bytes 1966088 | tf_op jit(solution)/shard_map/ppermute | solution.py:214
  67.1 6.8 %collective-permute-start.28 = (bf16[64,512]{1,0:T(8,128)(2,1)S(1)}, bf16[64,512]{1,0:T(8,128)(2,1)S(1)}, u32[]{:S(2)}, u32[]{:S(2)}) collective-permute-start(bf16[64,512]{1,0:T(8,128)(2,1)S(1)} %get-tuple-element.127), channel_id=1, source_target_pairs={{0,6},{1,7},{2,4},{3,5},{4,2},{5,3},{6,0},{7,1},{8,14},{9,15},{10,... | collective-permute-start | bytes 196616 | tf_op jit(solution)/shard_map/ppermute | solution.py:214
  68.9 7.1 %collective-permute-start.27 = (bf16[64,512]{1,0:T(8,128)(2,1)S(1)}, bf16[64,512]{1,0:T(8,128)(2,1)S(1)}, u32[]{:S(2)}, u32[]{:S(2)}) collective-permute-start(bf16[64,512]{1,0:T(8,128)(2,1)S(1)} %get-tuple-element.128), channel_id=1, source_target_pairs={{0,4},{1,5},{2,6},{3,7},{4,0},{5,1},{6,2},{7,3},{8,12},{9,13},{10,... | collective-permute-start | bytes 196616 | tf_op jit(solution)/shard_map/ppermute | solution.py:214
  68.9 7.0 %collective-permute-start.26 = (bf16[64,512]{1,0:T(8,128)(2,1)S(1)}, bf16[64,512]{1,0:T(8,128)(2,1)S(1)}, u32[]{:S(2)}, u32[]{:S(2)}) collective-permute-start(bf16[64,512]{1,0:T(8,128)(2,1)S(1)} %get-tuple-element.126), channel_id=1, source_target_pairs={{0,2},{1,3},{2,0},{3,1},{4,6},{5,7},{6,4},{7,5},{8,10},{9,11},{10,... | collective-permute-start | bytes 196616 | tf_op jit(solution)/shard_map/ppermute | solution.py:214
  76.6 6.0 %collective-permute-start.32 = (bf16[64,512]{1,0:T(8,128)(2,1)S(1)}, bf16[64,512]{1,0:T(8,128)(2,1)S(1)}, u32[]{:S(2)}, u32[]{:S(2)}) collective-permute-start(bf16[64,512]{1,0:T(8,128)(2,1)S(1)} %fusion.refs_0_), channel_id=1, source_target_pairs={{0,2},{1,3},{2,0},{3,1},{4,6},{5,7},{6,4},{7,5},{8,10},{9,11},{10,... | collective-permute-start | bytes 196616 | tf_op jit(solution)/shard_map/ppermute | solution.py:214
  76.7 7.9 %collective-permute-start.33 = (bf16[64,512]{1,0:T(8,128)(2,1)S(1)}, bf16[64,512]{1,0:T(8,128)(2,1)S(1)}, u32[]{:S(2)}, u32[]{:S(2)}) collective-permute-start(bf16[64,512]{1,0:T(8,128)(2,1)S(1)} %fusion.refs_0_), channel_id=1, source_target_pairs={{0,4},{1,5},{2,6},{3,7},{4,0},{5,1},{6,2},{7,3},{8,12},{9,13},{10,... | collective-permute-start | bytes 196616 | tf_op jit(solution)/shard_map/ppermute | solution.py:214
  78.9 6.5 %collective-permute-start.34 = (bf16[64,512]{1,0:T(8,128)(2,1)S(1)}, bf16[64,512]{1,0:T(8,128)(2,1)S(1)}, u32[]{:S(2)}, u32[]{:S(2)}) collective-permute-start(bf16[64,512]{1,0:T(8,128)(2,1)S(1)} %fusion.refs_0_), channel_id=1, source_target_pairs={{0,6},{1,7},{2,4},{3,5},{4,2},{5,3},{6,0},{7,1},{8,14},{9,15},{10,... | collective-permute-start | bytes 196616 | tf_op jit(solution)/shard_map/ppermute | solution.py:214
  86.4 13.7 %collective-permute-start.39 = (bf16[256,512]{1,0:T(8,128)(2,1)S(1)}, bf16[256,512]{1,0:T(8,128)(2,1)S(1)}, u32[]{:S(2)}, u32[]{:S(2)}) collective-permute-start(bf16[256,512]{1,0:T(8,128)(2,1)S(1)} %constant_dynamic-update-slice_fusion.refs_4_), channel_id=1, source_target_pairs={{0,8},{8,0},{16,24},{24,16},{1,9},{9,1},{17,25},{25,17},{2,10},{10... | collective-permute-start | bytes 786440 | tf_op jit(solution)/shard_map/ppermute | solution.py:214
  87.9 12.3 %collective-permute-start.40 = (bf16[256,512]{1,0:T(8,128)(2,1)S(1)}, bf16[256,512]{1,0:T(8,128)(2,1)S(1)}, u32[]{:S(2)}, u32[]{:S(2)}) collective-permute-start(bf16[256,512]{1,0:T(8,128)(2,1)S(1)} %constant_dynamic-update-slice_fusion.refs_4_), channel_id=1, source_target_pairs={{0,16},{8,24},{16,0},{24,8},{1,17},{9,25},{17,1},{25,9},{2,18},{10... | collective-permute-start | bytes 786440 | tf_op jit(solution)/shard_map/ppermute | solution.py:214
  88.5 10.2 %collective-permute-start.37 = (bf16[192,512]{1,0:T(8,128)(2,1)S(1)}, bf16[192,512]{1,0:T(8,128)(2,1)S(1)}, u32[]{:S(2)}, u32[]{:S(2)}) collective-permute-start(bf16[192,512]{1,0:T(8,128)(2,1)S(1)} %pad_maximum_fusion), channel_id=1, source_target_pairs={{0,24},{8,16},{16,8},{24,0},{1,25},{9,17},{17,9},{25,1},{2,26},{10... | collective-permute-start | bytes 589832 | tf_op jit(solution)/shard_map/ppermute | solution.py:214
  90.1 14.3 %collective-permute-start.41 = (bf16[64,512]{1,0:T(8,128)(2,1)S(1)}, bf16[64,512]{1,0:T(8,128)(2,1)S(1)}, u32[]{:S(2)}, u32[]{:S(2)}) collective-permute-start(bf16[64,512]{1,0:T(8,128)(2,1)S(1)} %get-tuple-element.125), channel_id=1, source_target_pairs={{0,4},{1,5},{2,6},{3,7},{4,0},{5,1},{6,2},{7,3},{8,12},{9,13},{10,... | collective-permute-start | bytes 196616 | tf_op jit(solution)/shard_map/ppermute | solution.py:214
  92.3 12.0 %collective-permute-start.42 = (bf16[64,512]{1,0:T(8,128)(2,1)S(1)}, bf16[64,512]{1,0:T(8,128)(2,1)S(1)}, u32[]{:S(2)}, u32[]{:S(2)}) collective-permute-start(bf16[64,512]{1,0:T(8,128)(2,1)S(1)} %get-tuple-element.124), channel_id=1, source_target_pairs={{0,6},{1,7},{2,4},{3,5},{4,2},{5,3},{6,0},{7,1},{8,14},{9,15},{10,... | collective-permute-start | bytes 196616 | tf_op jit(solution)/shard_map/ppermute | solution.py:214
  98.7 6.5 %collective-permute-start.38 = (bf16[64,1280]{1,0:T(8,128)(2,1)}, bf16[64,1280]{1,0:T(8,128)(2,1)S(1)}, u32[]{:S(2)}, u32[]{:S(2)}) collective-permute-start(bf16[64,1280]{1,0:T(8,128)(2,1)} %get-tuple-element.102), channel_id=1, source_target_pairs={{0,24},{8,16},{16,8},{24,0},{1,25},{9,17},{17,9},{25,1},{2,26},{10... | collective-permute-start | bytes 491528 | tf_op jit(solution)/shard_map/ppermute | solution.py:214
  (48 other events, 348.8 us)

commit v11 on v10

--- a/solution.py
+++ b/solution.py
@@ -186,23 +186,41 @@
     return in_vmem(kernel, "hidden_grad", outs, arrays, tokens * depth * kv_width * groups)
 
 
-def weight_pass(taken, blocks):
+def order_kernel(chips, widths, *refs):
+    taken, out_refs = refs[:chips], nested(refs[chips:], [len(parts) for parts in widths for _ in range(2)])
+    half = taken[0].shape[0] // 2
+    tokens = taken[0].shape[1] // len(widths)
+    for k, parts in enumerate(widths):
+        for i in range(2):
+            rows = slice(i * half, (i + 1) * half)
+            columns = [ref[rows, k * tokens : (k + 1) * tokens] for ref in taken]
+            for out_ref, count in zip(out_refs[2 * k + i], parts):
+                out_ref[...] = jnp.concatenate(columns[:count], axis=1)
+                columns = columns[count:]
+
+
+def order_pass(taken, parts):
     rows, tokens = taken[0].shape
-    chips, groups = len(taken), len(blocks)
-    token_rows = tokens // groups
-    kv_width = blocks[0][0].shape[1]
-    counts = [len(arrays) for arrays in blocks]
-
-    def kernel(*refs):
-        columns = jnp.concatenate([ref[...] for ref in refs[:chips]], axis=1)
-        parts = [jnp.concatenate([ref[...] for ref in arrays], axis=0) for arrays in nested(refs[chips:-2], counts)]
-        grads = [part[p * token_rows : (p + 1) * token_rows] for p in range(chips) for part in parts]
-        product = dot(columns, jnp.concatenate(grads, axis=0))
-        refs[-2][...], refs[-1][...] = product[: rows // 2], product[rows // 2 :]
-
-    outs = [((rows // 2, kv_width), F32)] * 2
-    arrays = [*taken, *[array for arrays in blocks for array in arrays]]
-    return in_vmem(kernel, "weight_grad", outs, arrays, rows * kv_width * tokens * chips)
+    groups = len(parts)
+    outs = [
+        ((rows // 2, tokens // groups * count), BF16)
+        for counts in parts for _ in range(2) for count in counts
+    ]
+    arrays = in_vmem(partial(order_kernel, len(taken), parts), "order_columns", outs, taken)
+    halves = nested(arrays, [len(counts) for counts in parts for _ in range(2)])
+    return halves[0::2], halves[1::2]
+
+
+def weight_sum(columns, blocks, order):
+    total = None
+    for k, i in order:
+        product = dot(columns[k][i], blocks[k][i])
+        total = product if total is None else total + product
+    return total
+
+
+def flat(lists):
+    return [item for items in lists for item in items]
 
 
 def nested(items, counts):
@@ -285,16 +303,22 @@
     key_sums = total(chip_parts(pair_sum(key_sums, far, responses), responses, range(1, chips)))
     value_sums = pair_sum(value_sums, value_far, responses)
     weight_far = [swap(piece, "resp", responses, 1) for piece in weight_near]
-    key_sums, value_sums, *weight_far = together(key_sums, value_sums, *weight_far)
+    value_parts = chip_parts(value_sums, responses, (1,))
+    parts = [[1, chips - 1] if k in across else [chips] for k in range(groups)]
+    mine, other = order_pass(taken, parts)
+    count = len(weight_far)
+    key_sums, value_sums, value_parts[1], *both = together(
+        key_sums, value_sums, value_parts[1], *weight_far, *flat(mine), *flat(other)
+    )
+    weight_far, halves = both[:count], nested(both[count:], [len(counts) for counts in parts + parts])
+    mine, other = halves[:groups], halves[groups:]
     _, pullback = jax.vjp(lambda values: norm_keys(values, key_gain), key_pre)
     key_pre_grad = pullback(key_sums)[0].astype(BF16)
 
     first = {k: swap(key_pre_grad, "group", groups, k) for k in across}
     grads = spread_near(key_pre_grad, responses)
-    value_parts = chip_parts(value_sums, responses, (1,))
-    grads_first = together(*grads, value_parts[1], value_sums, *first.values())
-    grads, value_parts[1], value_sums = grads_first[:chips], grads_first[chips], grads_first[chips + 1]
-    first = dict(zip(first, grads_first[chips + 2 :]))
+    both = together(*grads, value_sums, *first.values())
+    grads, value_sums, first = both[:chips], both[chips], dict(zip(first, both[chips + 1 :]))
     some, every = jnp.concatenate(grads[1:], axis=0), jnp.concatenate(grads, axis=0)
     grad_hidden, *parts = hidden_pass(
         key_pre_grad, first, key_matrix, dict(zip(beside, weight_near)), dict(zip(beside, weight_far))
@@ -309,9 +333,10 @@
     for k in across:
         *parts, blocks[k][-1] = together(*parts, blocks[k][-1])
     parts = [swap(part, "group", groups, k) for k, part in zip(across, parts)]
-    mine, other, *value_parts = together(*weight_pass(taken, blocks), *value_parts)
+    order = [(0, 0)] + [(k, 0) for k in across] + [(k, 0) for k in beside] + [(k, 1) for k in across]
+    other, *value_parts = together(weight_sum(other, blocks, order), *value_parts)
     value_sums = total(value_parts)
-    grad_weight = mine + swap(other, "resp", responses, 1)
+    grad_weight = weight_sum(mine, blocks, order) + swap(other, "resp", responses, 1)
     for k, part in zip(across, parts):
         start = (lax.axis_index("group") ^ k) * depth
         grad_hidden = lax.dynamic_update_slice(grad_hidden, part, (0, start))

time: 108 us -> 109 us (level)
  matrix products: 2.74 us -> 6.28 us
  starting transfers between devices: 47.2 us -> 44.5 us
  waiting for transfers between devices: 15.9 us -> 18 us
  other arithmetic: 4.1 us -> 2.36 us
    dot_general x4 -> x14, matrix products: 2.74 us -> 6.28 us  [dot(): return lax.dot_general(left, right, dims, preferred_element_type=F32)]
    ppermute x44, starting transfers between devices: 47.2 us -> 44.5 us  [swap(): return lax.ppermute(array, axis, [(i, i ^ distance) for i in range(size)])]
    ppermute x44, waiting for transfers between devices: 15.9 us -> 18 us  [swap(): return lax.ppermute(array, axis, [(i, i ^ distance) for i in range(size)])]
    add x1 -> x0, other arithmetic: 1.74 us -> none  [shards(): grad_weight = mine + swap(other, 'resp', responses, 1)]
  transfers between devices with their start and end apart: 44 -> 44, of which waited for: 14 -> 11; matrix products, arithmetic and copies ran while one was open for 6% -> 8% of each run, Pallas kernels for 29% -> 28%
where the time goes in v11:
time: 109 us
  starting transfers between devices  44.5 us (41%)
  Pallas kernels  32.6 us (30%)
  waiting for transfers between devices  18 us (17%)
  matrix products  6.28 us (6%)
  local copies, waits for them, and re-layouts  2.9 us (3%)
  other arithmetic  2.36 us (2%)
  between operations  2.14 us (2%)
    ppermute x44, starting transfers between devices, swap(): return lax.ppermute(array, axis, [(i, i ^ distance) for i in range(size)])  44.5 us
    pallas_call x1, Pallas kernels, attend(): pl.pallas_call(partial(attend_kernel, len(key_pieces)), grid=(kv_heads,),...  21.7 us
    ppermute x44, waiting for transfers between devices, swap(): return lax.ppermute(array, axis, [(i, i ^ distance) for i in range(size)])  18 us
    pallas_call x4, Pallas kernels, in_vmem(): pl.pallas_call(kernel, in_specs=[whole] * len(arrays), out_specs=[whole]...  11 us
    dot_general x14, matrix products, dot(): return lax.dot_general(left, right, dims, preferred_element_type=F32)  6.28 us
  transfers between devices with their start and end apart: 44, of which 11 were waited for; matrix products, arithmetic and copies ran while one was open for 8% of the time, Pallas kernels for 28%

profile of v11, /device:TPU:0, one launch (start us, length us, event | category | flops | bytes accessed | tf_op | source)
XLA Modules:
  0.0 108.8 jit_solution(5691280553843582561)
XLA Ops:
  0.6 2.1 %split_hidden.1 = (bf16[64,1280]{1,0:T(8,128)(2,1)}, bf16[64,1280]{1,0:T(8,128)(2,1)}, bf16[64,1280]{1,0:T(8,128)(2,1)}, bf16[64,1280]{1,0:T(8,128)(2,1)}) custom-call(bf16[64,5120]{1,0:T(8,128)(2,1)} %bitcast.61), custom_call_target="tpu_custom_call" | custom-call | bytes 3000000 | tf_op jit(solution)/shard_map/split_hidden/pallas_call | solution.py:108
  2.7 3.9 %collective-permute-start.2 = (bf16[64,1280]{1,0:T(8,128)(2,1)}, bf16[64,1280]{1,0:T(8,128)(2,1)S(1)}, u32[]{:S(2)}, u32[]{:S(2)}) collective-permute-start(bf16[64,1280]{1,0:T(8,128)(2,1)} %get-tuple-element.84), channel_id=1, source_target_pairs={{0,24},{8,16},{16,8},{24,0},{1,25},{9,17},{17,9},{25,1},{2,26},{10... | collective-permute-start | bytes 491528 | tf_op jit(solution)/shard_map/ppermute | solution.py:232
  7.2 1.7 %fusion.15 = f32[64,512]{1,0:T(8,128)S(1)} fusion(bf16[64,1280]{1,0:T(8,128)(2,1)} %get-tuple-element.81.refs_0_, bf16[1280,512]{1,0:T(8,128)(2,1)} %own_ref.1), kind=kOutput, calls=%fused_computation.37 | convolution fusion | flops 83886080 | bytes 1605632 | tf_op jit(solution)/shard_map/dot_general | solution.py:23
  9.0 2.8 %collective-permute-done.2.refs_3_ = bf16[64,1280]{1,0:T(8,128)(2,1)S(1)} collective-permute-done((bf16[64,1280]{1,0:T(8,128)(2,1)}, bf16[64,1280]{1,0:T(8,128)(2,1)S(1)}, u32[]{:S(2)}, u32[]{:S(2)}) %collective-permute-start.2) | collective-permute-done | bytes 163872 | tf_op jit(solution)/shard_map/ppermute | solution.py:232
  12.2 3.0 %collective-permute-start.5 = (f32[64,512]{1,0:T(8,128)S(1)}, f32[64,512]{1,0:T(8,128)S(1)}, u32[]{:S(2)}, u32[]{:S(2)}) collective-permute-start(f32[64,512]{1,0:T(8,128)S(1)} %fusion.18), channel_id=1, source_target_pairs={{0,24},{8,16},{16,8},{24,0},{1,25},{9,17},{17,9},{25,1},{2,26},{10... | collective-permute-start | bytes 393224 | tf_op jit(solution)/shard_map/ppermute | solution.py:232
  15.6 1.6 %collective-permute-start.4 = (f32[64,512]{1,0:T(8,128)S(1)}, f32[64,512]{1,0:T(8,128)S(1)}, u32[]{:S(2)}, u32[]{:S(2)}) collective-permute-start(f32[64,512]{1,0:T(8,128)S(1)} %fusion.17), channel_id=1, source_target_pairs={{0,16},{8,24},{16,0},{24,8},{1,17},{9,25},{17,1},{25,9},{2,18},{10... | collective-permute-start | bytes 393224 | tf_op jit(solution)/shard_map/ppermute | solution.py:232
  17.7 1.8 %collective-permute-start.13 = (bf16[64,512]{1,0:T(8,128)(2,1)S(1)}, bf16[64,512]{1,0:T(8,128)(2,1)S(1)}, u32[]{:S(2)}, u32[]{:S(2)}) collective-permute-start(bf16[64,512]{1,0:T(8,128)(2,1)S(1)} %bitcast.69), channel_id=1, source_target_pairs={{0,2},{1,3},{2,0},{3,1},{4,6},{5,7},{6,4},{7,5},{8,10},{9,11},{10,... | collective-permute-start | bytes 196616 | tf_op jit(solution)/shard_map/ppermute | solution.py:232
  19.4 2.6 %collective-permute-start.14 = (bf16[64,512]{1,0:T(8,128)(2,1)S(1)}, bf16[64,512]{1,0:T(8,128)(2,1)S(1)}, u32[]{:S(2)}, u32[]{:S(2)}) collective-permute-start(bf16[64,512]{1,0:T(8,128)(2,1)S(1)} %bitcast.70), channel_id=1, source_target_pairs={{0,4},{1,5},{2,6},{3,7},{4,0},{5,1},{6,2},{7,3},{8,12},{9,13},{10,... | collective-permute-start | bytes 196616 | tf_op jit(solution)/shard_map/ppermute | solution.py:232
  23.2 1.6 %collective-permute-start.6 = (bf16[64,512]{1,0:T(8,128)(2,1)S(1)}, bf16[64,512]{1,0:T(8,128)(2,1)S(1)}, u32[]{:S(2)}, u32[]{:S(2)}) collective-permute-start(bf16[64,512]{1,0:T(8,128)(2,1)S(1)} %fusion.9.refs_0_), channel_id=1, source_target_pairs={{0,2},{1,3},{2,0},{3,1},{4,6},{5,7},{6,4},{7,5},{8,10},{9,11},{10,... | collective-permute-start | bytes 196616 | tf_op jit(solution)/shard_map/ppermute | solution.py:232
  24.9 2.6 %collective-permute-start.7 = (bf16[64,512]{1,0:T(8,128)(2,1)S(1)}, bf16[64,512]{1,0:T(8,128)(2,1)S(1)}, u32[]{:S(2)}, u32[]{:S(2)}) collective-permute-start(bf16[64,512]{1,0:T(8,128)(2,1)S(1)} %fusion.9.refs_0_), channel_id=1, source_target_pairs={{0,4},{1,5},{2,6},{3,7},{4,0},{5,1},{6,2},{7,3},{8,12},{9,13},{10,... | collective-permute-start | bytes 196616 | tf_op jit(solution)/shard_map/ppermute | solution.py:232
  29.4 2.3 %turn_hidden.1 = (bf16[320,256]{1,0:T(8,128)(2,1)}, bf16[320,256]{1,0:T(8,128)(2,1)}, bf16[320,256]{1,0:T(8,128)(2,1)}, bf16[320,256]{1,0:T(8,128)(2,1)}) custom-call(bf16[64,1280]{1,0:T(8,128)(2,1)} %get-tuple-element.81.refs_0_, bf16[64,1280]{1,0:T(8,128)(2,1)} %copy-done.8, bf16[64,1280]{1,0:T(8,128)(2,1)} %copy-done.7, bf16[64,1280]{1,0:T(8,128)(2,1)} %copy-done.6), custom_call_target="tpu_custom_call" | custom-call | bytes 3000000 | tf_op jit(solution)/shard_map/turn_hidden/pallas_call | solution.py:108
  32.0 1.5 %collective-permute-done.8.refs_3_ = bf16[64,512]{1,0:T(8,128)(2,1)S(1)} collective-permute-done((bf16[64,512]{1,0:T(8,128)(2,1)S(1)}, bf16[64,512]{1,0:T(8,128)(2,1)S(1)}, u32[]{:S(2)}, u32[]{:S(2)}) %collective-permute-start.8) | collective-permute-done | bytes 65568 | tf_op jit(solution)/shard_map/ppermute | solution.py:232
  35.2 1.5 %collective-permute-start.23 = (bf16[1280,256]{1,0:T(8,128)(2,1)S(1)}, bf16[1280,256]{1,0:T(8,128)(2,1)S(1)}, u32[]{:S(2)}, u32[]{:S(2)}) collective-permute-start(bf16[1280,256]{1,0:T(8,128)(2,1)S(1)} %constant_dynamic-slice_fusion), channel_id=1, source_target_pairs={{0,8},{8,0},{16,24},{24,16},{1,9},{9,1},{17,25},{25,17},{2,10},{10... | collective-permute-start | bytes 1966088 | tf_op jit(solution)/shard_map/ppermute | solution.py:232
  37.4 2.2 %collective-permute-start.21 = (bf16[320,256]{1,0:T(8,128)(2,1)}, bf16[320,256]{1,0:T(8,128)(2,1)S(1)}, u32[]{:S(2)}, u32[]{:S(2)}) collective-permute-start(bf16[320,256]{1,0:T(8,128)(2,1)} %get-tuple-element.100), channel_id=1, source_target_pairs={{0,4},{1,5},{2,6},{3,7},{4,0},{5,1},{6,2},{7,3},{8,12},{9,13},{10,... | collective-permute-start | bytes 491528 | tf_op jit(solution)/shard_map/ppermute | solution.py:232
  39.7 2.1 %collective-permute-start.22 = (bf16[320,256]{1,0:T(8,128)(2,1)}, bf16[320,256]{1,0:T(8,128)(2,1)S(1)}, u32[]{:S(2)}, u32[]{:S(2)}) collective-permute-start(bf16[320,256]{1,0:T(8,128)(2,1)} %get-tuple-element.101), channel_id=1, source_target_pairs={{0,6},{1,7},{2,4},{3,5},{4,2},{5,3},{6,0},{7,1},{8,14},{9,15},{10,... | collective-permute-start | bytes 491528 | tf_op jit(solution)/shard_map/ppermute | solution.py:232
  41.9 21.7 %attend.1 = (bf16[256,4096]{1,0:T(8,128)(2,1)}, bf16[256,512]{1,0:T(8,128)(2,1)}, bf16[256,512]{1,0:T(8,128)(2,1)}, f32[256,512]{1,0:T(8,128)}, f32[256,512]{1,0...) custom-call(s32[1,1]{1,0:T(1,128)S(6)} %copy.30.length_ref, bf16[256,4096]{1,0:T(8,128)(2,1)} %bitcast.63, ...), custom_call_target="tpu_custom_call" | custom-call | flops 16106127360 | bytes 10000000 | tf_op jit(solution)/shard_map/attend/pallas_call | solution.py:91
  67.1 1.7 %collective-permute-start.28 = (bf16[64,512]{1,0:T(8,128)(2,1)S(1)}, bf16[64,512]{1,0:T(8,128)(2,1)S(1)}, u32[]{:S(2)}, u32[]{:S(2)}) collective-permute-start(bf16[64,512]{1,0:T(8,128)(2,1)S(1)} %get-tuple-element.161), channel_id=1, source_target_pairs={{0,6},{1,7},{2,4},{3,5},{4,2},{5,3},{6,0},{7,1},{8,14},{9,15},{10,... | collective-permute-start | bytes 196616 | tf_op jit(solution)/shard_map/ppermute | solution.py:232
  68.8 2.7 %collective-permute-start.26 = (bf16[64,512]{1,0:T(8,128)(2,1)S(1)}, bf16[64,512]{1,0:T(8,128)(2,1)S(1)}, u32[]{:S(2)}, u32[]{:S(2)}) collective-permute-start(bf16[64,512]{1,0:T(8,128)(2,1)S(1)} %get-tuple-element.160), channel_id=1, source_target_pairs={{0,2},{1,3},{2,0},{3,1},{4,6},{5,7},{6,4},{7,5},{8,10},{9,11},{10,... | collective-permute-start | bytes 196616 | tf_op jit(solution)/shard_map/ppermute | solution.py:232
  71.7 2.3 %order_columns.1 = (bf16[160,256]{1,0:T(8,128)(2,1)}, bf16[160,256]{1,0:T(8,128)(2,1)}, bf16[160,256]{1,0:T(8,128)(2,1)}, bf16[160,256]{1,0:T(8,128)(2,1)}, bf16...) custom-call(bf16[320,256]{1,0:T(8,128)(2,1)} %get-tuple-element.109., ...), custom_call_target="tpu_custom_call" | custom-call | bytes 3000000 | tf_op jit(solution)/shard_map/order_columns/pallas_call | solution.py:108
  74.1 1.8 %collective-permute-done.27 = bf16[64,512]{1,0:T(8,128)(2,1)S(1)} collective-permute-done((bf16[64,512]{1,0:T(8,128)(2,1)S(1)}, bf16[64,512]{1,0:T(8,128)(2,1)S(1)}, u32[]{:S(2)}, u32[]{:S(2)}) %collective-permute-start.27) | collective-permute-done | bytes 65568 | tf_op jit(solution)/shard_map/ppermute | solution.py:232
  75.9 2.4 %collective-permute-done.30 = bf16[64,512]{1,0:T(8,128)(2,1)S(1)} collective-permute-done((bf16[64,512]{1,0:T(8,128)(2,1)S(1)}, bf16[64,512]{1,0:T(8,128)(2,1)S(1)}, u32[]{:S(2)}, u32[]{:S(2)}) %collective-permute-start.30) | collective-permute-done | bytes 65568 | tf_op jit(solution)/shard_map/ppermute | solution.py:232
  79.9 2.2 %collective-permute-start.34 = (bf16[64,512]{1,0:T(8,128)(2,1)S(1)}, bf16[64,512]{1,0:T(8,128)(2,1)S(1)}, u32[]{:S(2)}, u32[]{:S(2)}) collective-permute-start(bf16[64,512]{1,0:T(8,128)(2,1)S(1)} %fusion.7.refs_0_), channel_id=1, source_target_pairs={{0,4},{1,5},{2,6},{3,7},{4,0},{5,1},{6,2},{7,3},{8,12},{9,13},{10,... | collective-permute-start | bytes 196616 | tf_op jit(solution)/shard_map/ppermute | solution.py:232
  82.2 2.1 %collective-permute-start.35 = (bf16[64,512]{1,0:T(8,128)(2,1)S(1)}, bf16[64,512]{1,0:T(8,128)(2,1)S(1)}, u32[]{:S(2)}, u32[]{:S(2)}) collective-permute-start(bf16[64,512]{1,0:T(8,128)(2,1)S(1)} %fusion.7.refs_0_), channel_id=1, source_target_pairs={{0,6},{1,7},{2,4},{3,5},{4,2},{5,3},{6,0},{7,1},{8,14},{9,15},{10,... | collective-permute-start | bytes 196616 | tf_op jit(solution)/shard_map/ppermute | solution.py:232
  84.3 1.4 %collective-permute-start.36 = (bf16[64,512]{1,0:T(8,128)(2,1)S(1)}, bf16[64,512]{1,0:T(8,128)(2,1)S(1)}, u32[]{:S(2)}, u32[]{:S(2)}) collective-permute-start(bf16[64,512]{1,0:T(8,128)(2,1)S(1)} %fusion.7.refs_0_), channel_id=1, source_target_pairs={{0,24},{8,16},{16,8},{24,0},{1,25},{9,17},{17,9},{25,1},{2,26},{10... | collective-permute-start | bytes 196616 | tf_op jit(solution)/shard_map/ppermute | solution.py:232
  85.7 2.5 %collective-permute-done.35 = bf16[64,512]{1,0:T(8,128)(2,1)S(1)} collective-permute-done((bf16[64,512]{1,0:T(8,128)(2,1)S(1)}, bf16[64,512]{1,0:T(8,128)(2,1)S(1)}, u32[]{:S(2)}, u32[]{:S(2)}) %collective-permute-start.35) | collective-permute-done | bytes 65568 | tf_op jit(solution)/shard_map/ppermute | solution.py:232
  88.2 1.4 %collective-permute-done.36.refs_1_ = bf16[64,512]{1,0:T(8,128)(2,1)S(1)} collective-permute-done((bf16[64,512]{1,0:T(8,128)(2,1)S(1)}, bf16[64,512]{1,0:T(8,128)(2,1)S(1)}, u32[]{:S(2)}, u32[]{:S(2)}) %collective-permute-start.36) | collective-permute-done | bytes 65568 | tf_op jit(solution)/shard_map/ppermute | solution.py:232
  89.7 1.5 %collective-permute-start.40 = (bf16[256,512]{1,0:T(8,128)(2,1)S(1)}, bf16[256,512]{1,0:T(8,128)(2,1)S(1)}, u32[]{:S(2)}, u32[]{:S(2)}) collective-permute-start(bf16[256,512]{1,0:T(8,128)(2,1)S(1)} %constant_dynamic-update-slice_fusion), channel_id=1, source_target_pairs={{0,16},{8,24},{16,0},{24,8},{1,17},{9,25},{17,1},{25,9},{2,18},{10... | collective-permute-start | bytes 786440 | tf_op jit(solution)/shard_map/ppermute | solution.py:232
  91.7 1.5 %collective-permute-start.37 = (bf16[192,512]{1,0:T(8,128)(2,1)S(1)}, bf16[192,512]{1,0:T(8,128)(2,1)S(1)}, u32[]{:S(2)}, u32[]{:S(2)}) collective-permute-start(bf16[192,512]{1,0:T(8,128)(2,1)S(1)} %pad_maximum_fusion), channel_id=1, source_target_pairs={{0,24},{8,16},{16,8},{24,0},{1,25},{9,17},{17,9},{25,1},{2,26},{10... | collective-permute-start | bytes 589832 | tf_op jit(solution)/shard_map/ppermute | solution.py:232
  93.4 1.7 %collective-permute-start.42 = (bf16[64,512]{1,0:T(8,128)(2,1)S(1)}, bf16[64,512]{1,0:T(8,128)(2,1)S(1)}, u32[]{:S(2)}, u32[]{:S(2)}) collective-permute-start(bf16[64,512]{1,0:T(8,128)(2,1)S(1)} %get-tuple-element.158), channel_id=1, source_target_pairs={{0,6},{1,7},{2,4},{3,5},{4,2},{5,3},{6,0},{7,1},{8,14},{9,15},{10,... | collective-permute-start | bytes 196616 | tf_op jit(solution)/shard_map/ppermute | solution.py:232
  95.3 4.3 %hidden_grad.1 = (bf16[64,5120]{1,0:T(8,128)(2,1)}, bf16[64,1280]{1,0:T(8,128)(2,1)}) custom-call(bf16[1280,512]{1,0:T(8,128)(2,1)} %own_ref.1, bf16[64,512]{1,0:T(8,128)(2,1)} %copy-done.9, bf16[64,512]{1,0:T(8,128)(2,1)} %copy-done.10, bf16[1280,256]{1,0:T(8,128)(2,1)} %copy-done.2, bf16[1280,256]{1,0:T(8,128)(2,1)} %copy-done.3, ...), custom_call_target="tpu_custom_call" | custom-call | flops 335544320 | bytes 3000000 | tf_op jit(solution)/shard_map/hidden_grad/pallas_call | solution.py:108
  100.7 1.5 %collective-permute-start.38 = (bf16[64,1280]{1,0:T(8,128)(2,1)}, bf16[64,1280]{1,0:T(8,128)(2,1)S(1)}, u32[]{:S(2)}, u32[]{:S(2)}) collective-permute-start(bf16[64,1280]{1,0:T(8,128)(2,1)} %get-tuple-element.133), channel_id=1, source_target_pairs={{0,24},{8,16},{16,8},{24,0},{1,25},{9,17},{17,9},{25,1},{2,26},{10... | collective-permute-start | bytes 491528 | tf_op jit(solution)/shard_map/ppermute | solution.py:232
  104.8 2.4 %collective-permute-done.38 = bf16[64,1280]{1,0:T(8,128)(2,1)S(1)} collective-permute-done((bf16[64,1280]{1,0:T(8,128)(2,1)}, bf16[64,1280]{1,0:T(8,128)(2,1)S(1)}, u32[]{:S(2)}, u32[]{:S(2)}) %collective-permute-start.38) | collective-permute-done | bytes 163872 | tf_op jit(solution)/shard_map/ppermute | solution.py:232
  (192 shorter events, 18.0 us)
Async XLA Ops:
  2.7 9.1 %collective-permute-start.2 = (bf16[64,1280]{1,0:T(8,128)(2,1)}, bf16[64,1280]{1,0:T(8,128)(2,1)S(1)}, u32[]{:S(2)}, u32[]{:S(2)}) collective-permute-start(bf16[64,1280]{1,0:T(8,128)(2,1)} %get-tuple-element.84), channel_id=1, source_target_pairs={{0,24},{8,16},{16,8},{24,0},{1,25},{9,17},{17,9},{25,1},{2,26},{10... | collective-permute-start | bytes 491528 | tf_op jit(solution)/shard_map/ppermute | solution.py:232
  6.6 8.6 %collective-permute-start.1 = (bf16[64,1280]{1,0:T(8,128)(2,1)}, bf16[64,1280]{1,0:T(8,128)(2,1)S(1)}, u32[]{:S(2)}, u32[]{:S(2)}) collective-permute-start(bf16[64,1280]{1,0:T(8,128)(2,1)} %get-tuple-element.83), channel_id=1, source_target_pairs={{0,16},{8,24},{16,0},{24,8},{1,17},{9,25},{17,1},{25,9},{2,18},{10... | collective-permute-start | bytes 491528 | tf_op jit(solution)/shard_map/ppermute | solution.py:232
  7.1 10.1 %collective-permute-start = (bf16[64,1280]{1,0:T(8,128)(2,1)}, bf16[64,1280]{1,0:T(8,128)(2,1)S(1)}, u32[]{:S(2)}, u32[]{:S(2)}) collective-permute-start(bf16[64,1280]{1,0:T(8,128)(2,1)} %get-tuple-element.82), channel_id=1, source_target_pairs={{0,8},{8,0},{16,24},{24,16},{1,9},{9,1},{17,25},{25,17},{2,10},{10... | collective-permute-start | bytes 491528 | tf_op jit(solution)/shard_map/ppermute | solution.py:232
  12.2 9.8 %collective-permute-start.5 = (f32[64,512]{1,0:T(8,128)S(1)}, f32[64,512]{1,0:T(8,128)S(1)}, u32[]{:S(2)}, u32[]{:S(2)}) collective-permute-start(f32[64,512]{1,0:T(8,128)S(1)} %fusion.18), channel_id=1, source_target_pairs={{0,24},{8,16},{16,8},{24,0},{1,25},{9,17},{17,9},{25,1},{2,26},{10... | collective-permute-start | bytes 393224 | tf_op jit(solution)/shard_map/ppermute | solution.py:232
  15.6 6.6 %collective-permute-start.4 = (f32[64,512]{1,0:T(8,128)S(1)}, f32[64,512]{1,0:T(8,128)S(1)}, u32[]{:S(2)}, u32[]{:S(2)}) collective-permute-start(f32[64,512]{1,0:T(8,128)S(1)} %fusion.17), channel_id=1, source_target_pairs={{0,16},{8,24},{16,0},{24,8},{1,17},{9,25},{17,1},{25,9},{2,18},{10... | collective-permute-start | bytes 393224 | tf_op jit(solution)/shard_map/ppermute | solution.py:232
  17.7 9.8 %collective-permute-start.13 = (bf16[64,512]{1,0:T(8,128)(2,1)S(1)}, bf16[64,512]{1,0:T(8,128)(2,1)S(1)}, u32[]{:S(2)}, u32[]{:S(2)}) collective-permute-start(bf16[64,512]{1,0:T(8,128)(2,1)S(1)} %bitcast.69), channel_id=1, source_target_pairs={{0,2},{1,3},{2,0},{3,1},{4,6},{5,7},{6,4},{7,5},{8,10},{9,11},{10,... | collective-permute-start | bytes 196616 | tf_op jit(solution)/shard_map/ppermute | solution.py:232
  19.4 8.3 %collective-permute-start.14 = (bf16[64,512]{1,0:T(8,128)(2,1)S(1)}, bf16[64,512]{1,0:T(8,128)(2,1)S(1)}, u32[]{:S(2)}, u32[]{:S(2)}) collective-permute-start(bf16[64,512]{1,0:T(8,128)(2,1)S(1)} %bitcast.70), channel_id=1, source_target_pairs={{0,4},{1,5},{2,6},{3,7},{4,0},{5,1},{6,2},{7,3},{8,12},{9,13},{10,... | collective-permute-start | bytes 196616 | tf_op jit(solution)/shard_map/ppermute | solution.py:232
  22.0 6.8 %collective-permute-start.15 = (bf16[64,512]{1,0:T(8,128)(2,1)S(1)}, bf16[64,512]{1,0:T(8,128)(2,1)S(1)}, u32[]{:S(2)}, u32[]{:S(2)}) collective-permute-start(bf16[64,512]{1,0:T(8,128)(2,1)S(1)} %bitcast.71), channel_id=1, source_target_pairs={{0,6},{1,7},{2,4},{3,5},{4,2},{5,3},{6,0},{7,1},{8,14},{9,15},{10,... | collective-permute-start | bytes 196616 | tf_op jit(solution)/shard_map/ppermute | solution.py:232
  23.2 5.6 %collective-permute-start.6 = (bf16[64,512]{1,0:T(8,128)(2,1)S(1)}, bf16[64,512]{1,0:T(8,128)(2,1)S(1)}, u32[]{:S(2)}, u32[]{:S(2)}) collective-permute-start(bf16[64,512]{1,0:T(8,128)(2,1)S(1)} %fusion.9.refs_0_), channel_id=1, source_target_pairs={{0,2},{1,3},{2,0},{3,1},{4,6},{5,7},{6,4},{7,5},{8,10},{9,11},{10,... | collective-permute-start | bytes 196616 | tf_op jit(solution)/shard_map/ppermute | solution.py:232
  24.9 7.1 %collective-permute-start.7 = (bf16[64,512]{1,0:T(8,128)(2,1)S(1)}, bf16[64,512]{1,0:T(8,128)(2,1)S(1)}, u32[]{:S(2)}, u32[]{:S(2)}) collective-permute-start(bf16[64,512]{1,0:T(8,128)(2,1)S(1)} %fusion.9.refs_0_), channel_id=1, source_target_pairs={{0,4},{1,5},{2,6},{3,7},{4,0},{5,1},{6,2},{7,3},{8,12},{9,13},{10,... | collective-permute-start | bytes 196616 | tf_op jit(solution)/shard_map/ppermute | solution.py:232
  27.5 6.1 %collective-permute-start.8 = (bf16[64,512]{1,0:T(8,128)(2,1)S(1)}, bf16[64,512]{1,0:T(8,128)(2,1)S(1)}, u32[]{:S(2)}, u32[]{:S(2)}) collective-permute-start(bf16[64,512]{1,0:T(8,128)(2,1)S(1)} %fusion.9.refs_0_), channel_id=1, source_target_pairs={{0,6},{1,7},{2,4},{3,5},{4,2},{5,3},{6,0},{7,1},{8,14},{9,15},{10,... | collective-permute-start | bytes 196616 | tf_op jit(solution)/shard_map/ppermute | solution.py:232
  27.7 5.8 %collective-permute-start.16 = (bf16[64,512]{1,0:T(8,128)(2,1)S(1)}, bf16[64,512]{1,0:T(8,128)(2,1)S(1)}, u32[]{:S(2)}, u32[]{:S(2)}) collective-permute-start(bf16[64,512]{1,0:T(8,128)(2,1)S(1)} %bitcast.72), channel_id=1, source_target_pairs={{0,1},{1,0},{2,3},{3,2},{4,5},{5,4},{6,7},{7,6},{8,9},{9,8},{10,11... | collective-permute-start | bytes 196616 | tf_op jit(solution)/shard_map/ppermute | solution.py:232
  34.2 5.5 %collective-permute-start.12 = (bf16[64,512]{1,0:T(8,128)(2,1)S(1)}, bf16[64,512]{1,0:T(8,128)(2,1)S(1)}, u32[]{:S(2)}, u32[]{:S(2)}) collective-permute-start(bf16[64,512]{1,0:T(8,128)(2,1)S(1)} %collective-permute-done.8.refs_3_), channel_id=1, source_target_pairs={{0,1},{1,0},{2,3},{3,2},{4,5},{5,4},{6,7},{7,6},{8,9},{9,8},{10,11... | collective-permute-start | bytes 196616 | tf_op jit(solution)/shard_map/ppermute | solution.py:232
  35.2 28.4 %collective-permute-start.23 = (bf16[1280,256]{1,0:T(8,128)(2,1)S(1)}, bf16[1280,256]{1,0:T(8,128)(2,1)S(1)}, u32[]{:S(2)}, u32[]{:S(2)}) collective-permute-start(bf16[1280,256]{1,0:T(8,128)(2,1)S(1)} %constant_dynamic-slice_fusion), channel_id=1, source_target_pairs={{0,8},{8,0},{16,24},{24,16},{1,9},{9,1},{17,25},{25,17},{2,10},{10... | collective-permute-start | bytes 1966088 | tf_op jit(solution)/shard_map/ppermute | solution.py:232
  36.8 26.9 %collective-permute-start.24 = (bf16[1280,256]{1,0:T(8,128)(2,1)S(1)}, bf16[1280,256]{1,0:T(8,128)(2,1)S(1)}, u32[]{:S(2)}, u32[]{:S(2)}) collective-permute-start(bf16[1280,256]{1,0:T(8,128)(2,1)S(1)} %constant_dynamic-slice_fusion), channel_id=1, source_target_pairs={{0,16},{8,24},{16,0},{24,8},{1,17},{9,25},{17,1},{25,9},{2,18},{10... | collective-permute-start | bytes 1966088 | tf_op jit(solution)/shard_map/ppermute | solution.py:232
  37.4 26.2 %collective-permute-start.20 = (bf16[320,256]{1,0:T(8,128)(2,1)}, bf16[320,256]{1,0:T(8,128)(2,1)S(1)}, u32[]{:S(2)}, u32[]{:S(2)}) collective-permute-start(bf16[320,256]{1,0:T(8,128)(2,1)} %get-tuple-element.99), channel_id=1, source_target_pairs={{0,2},{1,3},{2,0},{3,1},{4,6},{5,7},{6,4},{7,5},{8,10},{9,11},{10,... | collective-permute-start | bytes 491528 | tf_op jit(solution)/shard_map/ppermute | solution.py:232
  37.4 26.2 %collective-permute-start.21 = (bf16[320,256]{1,0:T(8,128)(2,1)}, bf16[320,256]{1,0:T(8,128)(2,1)S(1)}, u32[]{:S(2)}, u32[]{:S(2)}) collective-permute-start(bf16[320,256]{1,0:T(8,128)(2,1)} %get-tuple-element.100), channel_id=1, source_target_pairs={{0,4},{1,5},{2,6},{3,7},{4,0},{5,1},{6,2},{7,3},{8,12},{9,13},{10,... | collective-permute-start | bytes 491528 | tf_op jit(solution)/shard_map/ppermute | solution.py:232
  39.7 24.0 %collective-permute-start.22 = (bf16[320,256]{1,0:T(8,128)(2,1)}, bf16[320,256]{1,0:T(8,128)(2,1)S(1)}, u32[]{:S(2)}, u32[]{:S(2)}) collective-permute-start(bf16[320,256]{1,0:T(8,128)(2,1)} %get-tuple-element.101), channel_id=1, source_target_pairs={{0,6},{1,7},{2,4},{3,5},{4,2},{5,3},{6,0},{7,1},{8,14},{9,15},{10,... | collective-permute-start | bytes 491528 | tf_op jit(solution)/shard_map/ppermute | solution.py:232
  64.3 14.0 %collective-permute-start.31 = (bf16[1280,256]{1,0:T(8,128)(2,1)S(1)}, bf16[1280,256]{1,0:T(8,128)(2,1)S(1)}, u32[]{:S(2)}, u32[]{:S(2)}) collective-permute-start(bf16[1280,256]{1,0:T(8,128)(2,1)S(1)} %collective-permute-done.23.refs_2_), channel_id=1, source_target_pairs={{0,1},{1,0},{2,3},{3,2},{4,5},{5,4},{6,7},{7,6},{8,9},{9,8},{10,11... | collective-permute-start | bytes 1966088 | tf_op jit(solution)/shard_map/ppermute | solution.py:232
  64.4 14.0 %collective-permute-start.32 = (bf16[1280,256]{1,0:T(8,128)(2,1)S(1)}, bf16[1280,256]{1,0:T(8,128)(2,1)S(1)}, u32[]{:S(2)}, u32[]{:S(2)}) collective-permute-start(bf16[1280,256]{1,0:T(8,128)(2,1)S(1)} %collective-permute-done.24.refs_3_), channel_id=1, source_target_pairs={{0,1},{1,0},{2,3},{3,2},{4,5},{5,4},{6,7},{7,6},{8,9},{9,8},{10,11... | collective-permute-start | bytes 1966088 | tf_op jit(solution)/shard_map/ppermute | solution.py:232
  67.1 6.9 %collective-permute-start.28 = (bf16[64,512]{1,0:T(8,128)(2,1)S(1)}, bf16[64,512]{1,0:T(8,128)(2,1)S(1)}, u32[]{:S(2)}, u32[]{:S(2)}) collective-permute-start(bf16[64,512]{1,0:T(8,128)(2,1)S(1)} %get-tuple-element.161), channel_id=1, source_target_pairs={{0,6},{1,7},{2,4},{3,5},{4,2},{5,3},{6,0},{7,1},{8,14},{9,15},{10,... | collective-permute-start | bytes 196616 | tf_op jit(solution)/shard_map/ppermute | solution.py:232
  68.8 7.1 %collective-permute-start.27 = (bf16[64,512]{1,0:T(8,128)(2,1)S(1)}, bf16[64,512]{1,0:T(8,128)(2,1)S(1)}, u32[]{:S(2)}, u32[]{:S(2)}) collective-permute-start(bf16[64,512]{1,0:T(8,128)(2,1)S(1)} %get-tuple-element.162), channel_id=1, source_target_pairs={{0,4},{1,5},{2,6},{3,7},{4,0},{5,1},{6,2},{7,3},{8,12},{9,13},{10,... | collective-permute-start | bytes 196616 | tf_op jit(solution)/shard_map/ppermute | solution.py:232
  68.8 7.1 %collective-permute-start.26 = (bf16[64,512]{1,0:T(8,128)(2,1)S(1)}, bf16[64,512]{1,0:T(8,128)(2,1)S(1)}, u32[]{:S(2)}, u32[]{:S(2)}) collective-permute-start(bf16[64,512]{1,0:T(8,128)(2,1)S(1)} %get-tuple-element.160), channel_id=1, source_target_pairs={{0,2},{1,3},{2,0},{3,1},{4,6},{5,7},{6,4},{7,5},{8,10},{9,11},{10,... | collective-permute-start | bytes 196616 | tf_op jit(solution)/shard_map/ppermute | solution.py:232
  79.8 5.9 %collective-permute-start.33 = (bf16[64,512]{1,0:T(8,128)(2,1)S(1)}, bf16[64,512]{1,0:T(8,128)(2,1)S(1)}, u32[]{:S(2)}, u32[]{:S(2)}) collective-permute-start(bf16[64,512]{1,0:T(8,128)(2,1)S(1)} %fusion.7.refs_0_), channel_id=1, source_target_pairs={{0,2},{1,3},{2,0},{3,1},{4,6},{5,7},{6,4},{7,5},{8,10},{9,11},{10,... | collective-permute-start | bytes 196616 | tf_op jit(solution)/shard_map/ppermute | solution.py:232
  79.9 5.8 %collective-permute-start.34 = (bf16[64,512]{1,0:T(8,128)(2,1)S(1)}, bf16[64,512]{1,0:T(8,128)(2,1)S(1)}, u32[]{:S(2)}, u32[]{:S(2)}) collective-permute-start(bf16[64,512]{1,0:T(8,128)(2,1)S(1)} %fusion.7.refs_0_), channel_id=1, source_target_pairs={{0,4},{1,5},{2,6},{3,7},{4,0},{5,1},{6,2},{7,3},{8,12},{9,13},{10,... | collective-permute-start | bytes 196616 | tf_op jit(solution)/shard_map/ppermute | solution.py:232
  82.2 6.1 %collective-permute-start.35 = (bf16[64,512]{1,0:T(8,128)(2,1)S(1)}, bf16[64,512]{1,0:T(8,128)(2,1)S(1)}, u32[]{:S(2)}, u32[]{:S(2)}) collective-permute-start(bf16[64,512]{1,0:T(8,128)(2,1)S(1)} %fusion.7.refs_0_), channel_id=1, source_target_pairs={{0,6},{1,7},{2,4},{3,5},{4,2},{5,3},{6,0},{7,1},{8,14},{9,15},{10,... | collective-permute-start | bytes 196616 | tf_op jit(solution)/shard_map/ppermute | solution.py:232
  89.7 12.9 %collective-permute-start.40 = (bf16[256,512]{1,0:T(8,128)(2,1)S(1)}, bf16[256,512]{1,0:T(8,128)(2,1)S(1)}, u32[]{:S(2)}, u32[]{:S(2)}) collective-permute-start(bf16[256,512]{1,0:T(8,128)(2,1)S(1)} %constant_dynamic-update-slice_fusion), channel_id=1, source_target_pairs={{0,16},{8,24},{16,0},{24,8},{1,17},{9,25},{17,1},{25,9},{2,18},{10... | collective-permute-start | bytes 786440 | tf_op jit(solution)/shard_map/ppermute | solution.py:232
  91.1 11.7 %collective-permute-start.39 = (bf16[256,512]{1,0:T(8,128)(2,1)S(1)}, bf16[256,512]{1,0:T(8,128)(2,1)S(1)}, u32[]{:S(2)}, u32[]{:S(2)}) collective-permute-start(bf16[256,512]{1,0:T(8,128)(2,1)S(1)} %constant_dynamic-update-slice_fusion), channel_id=1, source_target_pairs={{0,8},{8,0},{16,24},{24,16},{1,9},{9,1},{17,25},{25,17},{2,10},{10... | collective-permute-start | bytes 786440 | tf_op jit(solution)/shard_map/ppermute | solution.py:232
  91.7 9.0 %collective-permute-start.37 = (bf16[192,512]{1,0:T(8,128)(2,1)S(1)}, bf16[192,512]{1,0:T(8,128)(2,1)S(1)}, u32[]{:S(2)}, u32[]{:S(2)}) collective-permute-start(bf16[192,512]{1,0:T(8,128)(2,1)S(1)} %pad_maximum_fusion), channel_id=1, source_target_pairs={{0,24},{8,16},{16,8},{24,0},{1,25},{9,17},{17,9},{25,1},{2,26},{10... | collective-permute-start | bytes 589832 | tf_op jit(solution)/shard_map/ppermute | solution.py:232
  93.3 10.0 %collective-permute-start.41 = (bf16[64,512]{1,0:T(8,128)(2,1)S(1)}, bf16[64,512]{1,0:T(8,128)(2,1)S(1)}, u32[]{:S(2)}, u32[]{:S(2)}) collective-permute-start(bf16[64,512]{1,0:T(8,128)(2,1)S(1)} %get-tuple-element.159), channel_id=1, source_target_pairs={{0,4},{1,5},{2,6},{3,7},{4,0},{5,1},{6,2},{7,3},{8,12},{9,13},{10,... | collective-permute-start | bytes 196616 | tf_op jit(solution)/shard_map/ppermute | solution.py:232
  93.4 9.9 %collective-permute-start.42 = (bf16[64,512]{1,0:T(8,128)(2,1)S(1)}, bf16[64,512]{1,0:T(8,128)(2,1)S(1)}, u32[]{:S(2)}, u32[]{:S(2)}) collective-permute-start(bf16[64,512]{1,0:T(8,128)(2,1)S(1)} %get-tuple-element.158), channel_id=1, source_target_pairs={{0,6},{1,7},{2,4},{3,5},{4,2},{5,3},{6,0},{7,1},{8,14},{9,15},{10,... | collective-permute-start | bytes 196616 | tf_op jit(solution)/shard_map/ppermute | solution.py:232
  100.7 6.5 %collective-permute-start.38 = (bf16[64,1280]{1,0:T(8,128)(2,1)}, bf16[64,1280]{1,0:T(8,128)(2,1)S(1)}, u32[]{:S(2)}, u32[]{:S(2)}) collective-permute-start(bf16[64,1280]{1,0:T(8,128)(2,1)} %get-tuple-element.133), channel_id=1, source_target_pairs={{0,24},{8,16},{16,8},{24,0},{1,25},{9,17},{17,9},{25,1},{2,26},{10... | collective-permute-start | bytes 491528 | tf_op jit(solution)/shard_map/ppermute | solution.py:232
  (55 other events, 375.3 us)

commit v12 on v11

--- a/solution.py
+++ b/solution.py
@@ -303,12 +303,11 @@
     key_sums = total(chip_parts(pair_sum(key_sums, far, responses), responses, range(1, chips)))
     value_sums = pair_sum(value_sums, value_far, responses)
     weight_far = [swap(piece, "resp", responses, 1) for piece in weight_near]
-    value_parts = chip_parts(value_sums, responses, (1,))
     parts = [[1, chips - 1] if k in across else [chips] for k in range(groups)]
     mine, other = order_pass(taken, parts)
     count = len(weight_far)
-    key_sums, value_sums, value_parts[1], *both = together(
-        key_sums, value_sums, value_parts[1], *weight_far, *flat(mine), *flat(other)
+    key_sums, value_sums, *both = together(
+        key_sums, value_sums, *weight_far, *flat(mine), *flat(other)
     )
     weight_far, halves = both[:count], nested(both[count:], [len(counts) for counts in parts + parts])
     mine, other = halves[:groups], halves[groups:]
@@ -317,8 +316,9 @@
 
     first = {k: swap(key_pre_grad, "group", groups, k) for k in across}
     grads = spread_near(key_pre_grad, responses)
-    both = together(*grads, value_sums, *first.values())
-    grads, value_sums, first = both[:chips], both[chips], dict(zip(first, both[chips + 1 :]))
+    value_parts = chip_parts(value_sums, responses, (1,))
+    value_parts[1], value_sums, *both = together(value_parts[1], value_sums, *grads, *first.values())
+    grads, first = both[:chips], dict(zip(first, both[chips:]))
     some, every = jnp.concatenate(grads[1:], axis=0), jnp.concatenate(grads, axis=0)
     grad_hidden, *parts = hidden_pass(
         key_pre_grad, first, key_matrix, dict(zip(beside, weight_near)), dict(zip(beside, weight_far))

time: 109 us -> 109 us (level)
  waiting for transfers between devices: 18 us -> 16 us
  starting transfers between devices: 44.5 us -> 46.4 us
    ppermute x44, waiting for transfers between devices: 18 us -> 16 us  [swap(): return lax.ppermute(array, axis, [(i, i ^ distance) for i in range(size)])]
    ppermute x44, starting transfers between devices: 44.5 us -> 46.4 us  [swap(): return lax.ppermute(array, axis, [(i, i ^ distance) for i in range(size)])]
  transfers between devices with their start and end apart: 44 -> 44, of which waited for: 11 -> 10; matrix products, arithmetic and copies ran while one was open for 8% -> 8% of each run, Pallas kernels for 28% -> 28%
where the time goes in v12:
time: 109 us
  starting transfers between devices  46.4 us (43%)
  Pallas kernels  32.4 us (30%)
  waiting for transfers between devices  16 us (15%)
  matrix products  6.29 us (6%)
  local copies, waits for them, and re-layouts  2.89 us (3%)
  other arithmetic  2.36 us (2%)
  between operations  2.14 us (2%)
    ppermute x44, starting transfers between devices, swap(): return lax.ppermute(array, axis, [(i, i ^ distance) for i in range(size)])  46.4 us
    pallas_call x1, Pallas kernels, attend(): pl.pallas_call(partial(attend_kernel, len(key_pieces)), grid=(kv_heads,),...  21.7 us
    ppermute x44, waiting for transfers between devices, swap(): return lax.ppermute(array, axis, [(i, i ^ distance) for i in range(size)])  16 us
    pallas_call x4, Pallas kernels, in_vmem(): pl.pallas_call(kernel, in_specs=[whole] * len(arrays), out_specs=[whole]...  10.8 us
    dot_general x14, matrix products, dot(): return lax.dot_general(left, right, dims, preferred_element_type=F32)  6.29 us
  transfers between devices with their start and end apart: 44, of which 10 were waited for; matrix products, arithmetic and copies ran while one was open for 8% of the time, Pallas kernels for 28%

profile of v12, /device:TPU:0, one launch (start us, length us, event | category | flops | bytes accessed | tf_op | source)
XLA Modules:
  0.0 108.5 jit_solution(7720795447010473402)
XLA Ops:
  0.6 2.1 %split_hidden.1 = (bf16[64,1280]{1,0:T(8,128)(2,1)}, bf16[64,1280]{1,0:T(8,128)(2,1)}, bf16[64,1280]{1,0:T(8,128)(2,1)}, bf16[64,1280]{1,0:T(8,128)(2,1)}) custom-call(bf16[64,5120]{1,0:T(8,128)(2,1)} %bitcast.61), custom_call_target="tpu_custom_call" | custom-call | bytes 3000000 | tf_op jit(solution)/shard_map/split_hidden/pallas_call | solution.py:108
  2.7 3.9 %collective-permute-start.2 = (bf16[64,1280]{1,0:T(8,128)(2,1)}, bf16[64,1280]{1,0:T(8,128)(2,1)S(1)}, u32[]{:S(2)}, u32[]{:S(2)}) collective-permute-start(bf16[64,1280]{1,0:T(8,128)(2,1)} %get-tuple-element.84), channel_id=1, source_target_pairs={{0,24},{8,16},{16,8},{24,0},{1,25},{9,17},{17,9},{25,1},{2,26},{10... | collective-permute-start | bytes 491528 | tf_op jit(solution)/shard_map/ppermute | solution.py:232
  7.2 1.7 %fusion.15 = f32[64,512]{1,0:T(8,128)S(1)} fusion(bf16[64,1280]{1,0:T(8,128)(2,1)} %get-tuple-element.81.refs_0_, bf16[1280,512]{1,0:T(8,128)(2,1)} %own_ref.1), kind=kOutput, calls=%fused_computation.37 | convolution fusion | flops 83886080 | bytes 1605632 | tf_op jit(solution)/shard_map/dot_general | solution.py:23
  9.0 2.8 %collective-permute-done.2.refs_3_ = bf16[64,1280]{1,0:T(8,128)(2,1)S(1)} collective-permute-done((bf16[64,1280]{1,0:T(8,128)(2,1)}, bf16[64,1280]{1,0:T(8,128)(2,1)S(1)}, u32[]{:S(2)}, u32[]{:S(2)}) %collective-permute-start.2) | collective-permute-done | bytes 163872 | tf_op jit(solution)/shard_map/ppermute | solution.py:232
  12.2 3.0 %collective-permute-start.5 = (f32[64,512]{1,0:T(8,128)S(1)}, f32[64,512]{1,0:T(8,128)S(1)}, u32[]{:S(2)}, u32[]{:S(2)}) collective-permute-start(f32[64,512]{1,0:T(8,128)S(1)} %fusion.18), channel_id=1, source_target_pairs={{0,24},{8,16},{16,8},{24,0},{1,25},{9,17},{17,9},{25,1},{2,26},{10... | collective-permute-start | bytes 393224 | tf_op jit(solution)/shard_map/ppermute | solution.py:232
  15.6 1.6 %collective-permute-start.4 = (f32[64,512]{1,0:T(8,128)S(1)}, f32[64,512]{1,0:T(8,128)S(1)}, u32[]{:S(2)}, u32[]{:S(2)}) collective-permute-start(f32[64,512]{1,0:T(8,128)S(1)} %fusion.17), channel_id=1, source_target_pairs={{0,16},{8,24},{16,0},{24,8},{1,17},{9,25},{17,1},{25,9},{2,18},{10... | collective-permute-start | bytes 393224 | tf_op jit(solution)/shard_map/ppermute | solution.py:232
  17.7 1.8 %collective-permute-start.13 = (bf16[64,512]{1,0:T(8,128)(2,1)S(1)}, bf16[64,512]{1,0:T(8,128)(2,1)S(1)}, u32[]{:S(2)}, u32[]{:S(2)}) collective-permute-start(bf16[64,512]{1,0:T(8,128)(2,1)S(1)} %bitcast.69), channel_id=1, source_target_pairs={{0,2},{1,3},{2,0},{3,1},{4,6},{5,7},{6,4},{7,5},{8,10},{9,11},{10,... | collective-permute-start | bytes 196616 | tf_op jit(solution)/shard_map/ppermute | solution.py:232
  19.4 2.6 %collective-permute-start.14 = (bf16[64,512]{1,0:T(8,128)(2,1)S(1)}, bf16[64,512]{1,0:T(8,128)(2,1)S(1)}, u32[]{:S(2)}, u32[]{:S(2)}) collective-permute-start(bf16[64,512]{1,0:T(8,128)(2,1)S(1)} %bitcast.70), channel_id=1, source_target_pairs={{0,4},{1,5},{2,6},{3,7},{4,0},{5,1},{6,2},{7,3},{8,12},{9,13},{10,... | collective-permute-start | bytes 196616 | tf_op jit(solution)/shard_map/ppermute | solution.py:232
  23.2 1.6 %collective-permute-start.6 = (bf16[64,512]{1,0:T(8,128)(2,1)S(1)}, bf16[64,512]{1,0:T(8,128)(2,1)S(1)}, u32[]{:S(2)}, u32[]{:S(2)}) collective-permute-start(bf16[64,512]{1,0:T(8,128)(2,1)S(1)} %fusion.9.refs_0_), channel_id=1, source_target_pairs={{0,2},{1,3},{2,0},{3,1},{4,6},{5,7},{6,4},{7,5},{8,10},{9,11},{10,... | collective-permute-start | bytes 196616 | tf_op jit(solution)/shard_map/ppermute | solution.py:232
  24.9 2.6 %collective-permute-start.7 = (bf16[64,512]{1,0:T(8,128)(2,1)S(1)}, bf16[64,512]{1,0:T(8,128)(2,1)S(1)}, u32[]{:S(2)}, u32[]{:S(2)}) collective-permute-start(bf16[64,512]{1,0:T(8,128)(2,1)S(1)} %fusion.9.refs_0_), channel_id=1, source_target_pairs={{0,4},{1,5},{2,6},{3,7},{4,0},{5,1},{6,2},{7,3},{8,12},{9,13},{10,... | collective-permute-start | bytes 196616 | tf_op jit(solution)/shard_map/ppermute | solution.py:232
  27.7 1.2 %collective-permute-done.15.refs_11_ = bf16[64,512]{1,0:T(8,128)(2,1)S(1)} collective-permute-done((bf16[64,512]{1,0:T(8,128)(2,1)S(1)}, bf16[64,512]{1,0:T(8,128)(2,1)S(1)}, u32[]{:S(2)}, u32[]{:S(2)}) %collective-permute-start.15) | collective-permute-done | bytes 65568 | tf_op jit(solution)/shard_map/ppermute | solution.py:232
  29.4 2.3 %turn_hidden.1 = (bf16[320,256]{1,0:T(8,128)(2,1)}, bf16[320,256]{1,0:T(8,128)(2,1)}, bf16[320,256]{1,0:T(8,128)(2,1)}, bf16[320,256]{1,0:T(8,128)(2,1)}) custom-call(bf16[64,1280]{1,0:T(8,128)(2,1)} %get-tuple-element.81.refs_0_, bf16[64,1280]{1,0:T(8,128)(2,1)} %copy-done.8, bf16[64,1280]{1,0:T(8,128)(2,1)} %copy-done.7, bf16[64,1280]{1,0:T(8,128)(2,1)} %copy-done.6), custom_call_target="tpu_custom_call" | custom-call | bytes 3000000 | tf_op jit(solution)/shard_map/turn_hidden/pallas_call | solution.py:108
  32.0 1.5 %collective-permute-done.8.refs_3_ = bf16[64,512]{1,0:T(8,128)(2,1)S(1)} collective-permute-done((bf16[64,512]{1,0:T(8,128)(2,1)S(1)}, bf16[64,512]{1,0:T(8,128)(2,1)S(1)}, u32[]{:S(2)}, u32[]{:S(2)}) %collective-permute-start.8) | collective-permute-done | bytes 65568 | tf_op jit(solution)/shard_map/ppermute | solution.py:232
  35.2 1.5 %collective-permute-start.23 = (bf16[1280,256]{1,0:T(8,128)(2,1)S(1)}, bf16[1280,256]{1,0:T(8,128)(2,1)S(1)}, u32[]{:S(2)}, u32[]{:S(2)}) collective-permute-start(bf16[1280,256]{1,0:T(8,128)(2,1)S(1)} %constant_dynamic-slice_fusion), channel_id=1, source_target_pairs={{0,8},{8,0},{16,24},{24,16},{1,9},{9,1},{17,25},{25,17},{2,10},{10... | collective-permute-start | bytes 1966088 | tf_op jit(solution)/shard_map/ppermute | solution.py:232
  37.4 2.2 %collective-permute-start.21 = (bf16[320,256]{1,0:T(8,128)(2,1)}, bf16[320,256]{1,0:T(8,128)(2,1)S(1)}, u32[]{:S(2)}, u32[]{:S(2)}) collective-permute-start(bf16[320,256]{1,0:T(8,128)(2,1)} %get-tuple-element.100), channel_id=1, source_target_pairs={{0,4},{1,5},{2,6},{3,7},{4,0},{5,1},{6,2},{7,3},{8,12},{9,13},{10,... | collective-permute-start | bytes 491528 | tf_op jit(solution)/shard_map/ppermute | solution.py:232
  39.7 2.1 %collective-permute-start.22 = (bf16[320,256]{1,0:T(8,128)(2,1)}, bf16[320,256]{1,0:T(8,128)(2,1)S(1)}, u32[]{:S(2)}, u32[]{:S(2)}) collective-permute-start(bf16[320,256]{1,0:T(8,128)(2,1)} %get-tuple-element.101), channel_id=1, source_target_pairs={{0,6},{1,7},{2,4},{3,5},{4,2},{5,3},{6,0},{7,1},{8,14},{9,15},{10,... | collective-permute-start | bytes 491528 | tf_op jit(solution)/shard_map/ppermute | solution.py:232
  41.9 21.7 %attend.1 = (bf16[256,4096]{1,0:T(8,128)(2,1)}, bf16[256,512]{1,0:T(8,128)(2,1)}, bf16[256,512]{1,0:T(8,128)(2,1)}, f32[256,512]{1,0:T(8,128)}, f32[256,512]{1,0...) custom-call(s32[1,1]{1,0:T(1,128)S(6)} %copy.30.length_ref, bf16[256,4096]{1,0:T(8,128)(2,1)} %bitcast.63, ...), custom_call_target="tpu_custom_call" | custom-call | flops 16106127360 | bytes 10000000 | tf_op jit(solution)/shard_map/attend/pallas_call | solution.py:91
  67.1 1.8 %collective-permute-start.28 = (bf16[64,512]{1,0:T(8,128)(2,1)S(1)}, bf16[64,512]{1,0:T(8,128)(2,1)S(1)}, u32[]{:S(2)}, u32[]{:S(2)}) collective-permute-start(bf16[64,512]{1,0:T(8,128)(2,1)S(1)} %get-tuple-element.161), channel_id=1, source_target_pairs={{0,6},{1,7},{2,4},{3,5},{4,2},{5,3},{6,0},{7,1},{8,14},{9,15},{10,... | collective-permute-start | bytes 196616 | tf_op jit(solution)/shard_map/ppermute | solution.py:232
  68.8 2.7 %collective-permute-start.26 = (bf16[64,512]{1,0:T(8,128)(2,1)S(1)}, bf16[64,512]{1,0:T(8,128)(2,1)S(1)}, u32[]{:S(2)}, u32[]{:S(2)}) collective-permute-start(bf16[64,512]{1,0:T(8,128)(2,1)S(1)} %get-tuple-element.160), channel_id=1, source_target_pairs={{0,2},{1,3},{2,0},{3,1},{4,6},{5,7},{6,4},{7,5},{8,10},{9,11},{10,... | collective-permute-start | bytes 196616 | tf_op jit(solution)/shard_map/ppermute | solution.py:232
  71.5 2.1 %order_columns.1 = (bf16[160,256]{1,0:T(8,128)(2,1)}, bf16[160,256]{1,0:T(8,128)(2,1)}, bf16[160,256]{1,0:T(8,128)(2,1)}, bf16[160,256]{1,0:T(8,128)(2,1)}, bf16...) custom-call(bf16[320,256]{1,0:T(8,128)(2,1)} %get-tuple-element.109., ...), custom_call_target="tpu_custom_call" | custom-call | bytes 3000000 | tf_op jit(solution)/shard_map/order_columns/pallas_call | solution.py:108
  73.9 2.0 %collective-permute-done.27 = bf16[64,512]{1,0:T(8,128)(2,1)S(1)} collective-permute-done((bf16[64,512]{1,0:T(8,128)(2,1)S(1)}, bf16[64,512]{1,0:T(8,128)(2,1)S(1)}, u32[]{:S(2)}, u32[]{:S(2)}) %collective-permute-start.27) | collective-permute-done | bytes 65568 | tf_op jit(solution)/shard_map/ppermute | solution.py:232
  77.5 2.0 %collective-permute-start.33 = (bf16[64,512]{1,0:T(8,128)(2,1)S(1)}, bf16[64,512]{1,0:T(8,128)(2,1)S(1)}, u32[]{:S(2)}, u32[]{:S(2)}) collective-permute-start(bf16[64,512]{1,0:T(8,128)(2,1)S(1)} %fusion.7.refs_0_), channel_id=1, source_target_pairs={{0,2},{1,3},{2,0},{3,1},{4,6},{5,7},{6,4},{7,5},{8,10},{9,11},{10,... | collective-permute-start | bytes 196616 | tf_op jit(solution)/shard_map/ppermute | solution.py:232
  80.1 1.9 %collective-permute-start.35 = (bf16[64,512]{1,0:T(8,128)(2,1)S(1)}, bf16[64,512]{1,0:T(8,128)(2,1)S(1)}, u32[]{:S(2)}, u32[]{:S(2)}) collective-permute-start(bf16[64,512]{1,0:T(8,128)(2,1)S(1)} %fusion.7.refs_0_), channel_id=1, source_target_pairs={{0,6},{1,7},{2,4},{3,5},{4,2},{5,3},{6,0},{7,1},{8,14},{9,15},{10,... | collective-permute-start | bytes 196616 | tf_op jit(solution)/shard_map/ppermute | solution.py:232
  82.0 1.4 %collective-permute-start.36 = (bf16[64,512]{1,0:T(8,128)(2,1)S(1)}, bf16[64,512]{1,0:T(8,128)(2,1)S(1)}, u32[]{:S(2)}, u32[]{:S(2)}) collective-permute-start(bf16[64,512]{1,0:T(8,128)(2,1)S(1)} %fusion.7.refs_0_), channel_id=1, source_target_pairs={{0,24},{8,16},{16,8},{24,0},{1,25},{9,17},{17,9},{25,1},{2,26},{10... | collective-permute-start | bytes 196616 | tf_op jit(solution)/shard_map/ppermute | solution.py:232
  83.4 4.0 %collective-permute-done.34 = bf16[64,512]{1,0:T(8,128)(2,1)S(1)} collective-permute-done((bf16[64,512]{1,0:T(8,128)(2,1)S(1)}, bf16[64,512]{1,0:T(8,128)(2,1)S(1)}, u32[]{:S(2)}, u32[]{:S(2)}) %collective-permute-start.34) | collective-permute-done | bytes 65568 | tf_op jit(solution)/shard_map/ppermute | solution.py:232
  87.5 1.5 %collective-permute-start.40 = (bf16[256,512]{1,0:T(8,128)(2,1)S(1)}, bf16[256,512]{1,0:T(8,128)(2,1)S(1)}, u32[]{:S(2)}, u32[]{:S(2)}) collective-permute-start(bf16[256,512]{1,0:T(8,128)(2,1)S(1)} %constant_dynamic-update-slice_fusion), channel_id=1, source_target_pairs={{0,16},{8,24},{16,0},{24,8},{1,17},{9,25},{17,1},{25,9},{2,18},{10... | collective-permute-start | bytes 786440 | tf_op jit(solution)/shard_map/ppermute | solution.py:232
  89.5 1.5 %collective-permute-start.37 = (bf16[192,512]{1,0:T(8,128)(2,1)S(1)}, bf16[192,512]{1,0:T(8,128)(2,1)S(1)}, u32[]{:S(2)}, u32[]{:S(2)}) collective-permute-start(bf16[192,512]{1,0:T(8,128)(2,1)S(1)} %pad_maximum_fusion), channel_id=1, source_target_pairs={{0,24},{8,16},{16,8},{24,0},{1,25},{9,17},{17,9},{25,1},{2,26},{10... | collective-permute-start | bytes 589832 | tf_op jit(solution)/shard_map/ppermute | solution.py:232
  91.1 1.6 %collective-permute-start.41 = (bf16[64,512]{1,0:T(8,128)(2,1)S(1)}, bf16[64,512]{1,0:T(8,128)(2,1)S(1)}, u32[]{:S(2)}, u32[]{:S(2)}) collective-permute-start(bf16[64,512]{1,0:T(8,128)(2,1)S(1)} %get-tuple-element.159), channel_id=1, source_target_pairs={{0,4},{1,5},{2,6},{3,7},{4,0},{5,1},{6,2},{7,3},{8,12},{9,13},{10,... | collective-permute-start | bytes 196616 | tf_op jit(solution)/shard_map/ppermute | solution.py:232
  92.7 2.1 %collective-permute-start.42 = (bf16[64,512]{1,0:T(8,128)(2,1)S(1)}, bf16[64,512]{1,0:T(8,128)(2,1)S(1)}, u32[]{:S(2)}, u32[]{:S(2)}) collective-permute-start(bf16[64,512]{1,0:T(8,128)(2,1)S(1)} %get-tuple-element.158), channel_id=1, source_target_pairs={{0,6},{1,7},{2,4},{3,5},{4,2},{5,3},{6,0},{7,1},{8,14},{9,15},{10,... | collective-permute-start | bytes 196616 | tf_op jit(solution)/shard_map/ppermute | solution.py:232
  95.0 4.3 %hidden_grad.1 = (bf16[64,5120]{1,0:T(8,128)(2,1)}, bf16[64,1280]{1,0:T(8,128)(2,1)}) custom-call(bf16[1280,512]{1,0:T(8,128)(2,1)} %own_ref.1, bf16[64,512]{1,0:T(8,128)(2,1)} %copy-done.9, bf16[64,512]{1,0:T(8,128)(2,1)} %copy-done.10, bf16[1280,256]{1,0:T(8,128)(2,1)} %copy-done.2, bf16[1280,256]{1,0:T(8,128)(2,1)} %copy-done.3, ...), custom_call_target="tpu_custom_call" | custom-call | flops 335544320 | bytes 3000000 | tf_op jit(solution)/shard_map/hidden_grad/pallas_call | solution.py:108
  100.4 1.5 %collective-permute-start.38 = (bf16[64,1280]{1,0:T(8,128)(2,1)}, bf16[64,1280]{1,0:T(8,128)(2,1)S(1)}, u32[]{:S(2)}, u32[]{:S(2)}) collective-permute-start(bf16[64,1280]{1,0:T(8,128)(2,1)} %get-tuple-element.133), channel_id=1, source_target_pairs={{0,24},{8,16},{16,8},{24,0},{1,25},{9,17},{17,9},{25,1},{2,26},{10... | collective-permute-start | bytes 491528 | tf_op jit(solution)/shard_map/ppermute | solution.py:232
  104.5 2.4 %collective-permute-done.38 = bf16[64,1280]{1,0:T(8,128)(2,1)S(1)} collective-permute-done((bf16[64,1280]{1,0:T(8,128)(2,1)}, bf16[64,1280]{1,0:T(8,128)(2,1)S(1)}, u32[]{:S(2)}, u32[]{:S(2)}) %collective-permute-start.38) | collective-permute-done | bytes 163872 | tf_op jit(solution)/shard_map/ppermute | solution.py:232
  (192 shorter events, 17.4 us)
Async XLA Ops:
  2.7 9.1 %collective-permute-start.2 = (bf16[64,1280]{1,0:T(8,128)(2,1)}, bf16[64,1280]{1,0:T(8,128)(2,1)S(1)}, u32[]{:S(2)}, u32[]{:S(2)}) collective-permute-start(bf16[64,1280]{1,0:T(8,128)(2,1)} %get-tuple-element.84), channel_id=1, source_target_pairs={{0,24},{8,16},{16,8},{24,0},{1,25},{9,17},{17,9},{25,1},{2,26},{10... | collective-permute-start | bytes 491528 | tf_op jit(solution)/shard_map/ppermute | solution.py:232
  6.6 8.6 %collective-permute-start.1 = (bf16[64,1280]{1,0:T(8,128)(2,1)}, bf16[64,1280]{1,0:T(8,128)(2,1)S(1)}, u32[]{:S(2)}, u32[]{:S(2)}) collective-permute-start(bf16[64,1280]{1,0:T(8,128)(2,1)} %get-tuple-element.83), channel_id=1, source_target_pairs={{0,16},{8,24},{16,0},{24,8},{1,17},{9,25},{17,1},{25,9},{2,18},{10... | collective-permute-start | bytes 491528 | tf_op jit(solution)/shard_map/ppermute | solution.py:232
  7.1 10.1 %collective-permute-start = (bf16[64,1280]{1,0:T(8,128)(2,1)}, bf16[64,1280]{1,0:T(8,128)(2,1)S(1)}, u32[]{:S(2)}, u32[]{:S(2)}) collective-permute-start(bf16[64,1280]{1,0:T(8,128)(2,1)} %get-tuple-element.82), channel_id=1, source_target_pairs={{0,8},{8,0},{16,24},{24,16},{1,9},{9,1},{17,25},{25,17},{2,10},{10... | collective-permute-start | bytes 491528 | tf_op jit(solution)/shard_map/ppermute | solution.py:232
  12.2 9.8 %collective-permute-start.5 = (f32[64,512]{1,0:T(8,128)S(1)}, f32[64,512]{1,0:T(8,128)S(1)}, u32[]{:S(2)}, u32[]{:S(2)}) collective-permute-start(f32[64,512]{1,0:T(8,128)S(1)} %fusion.18), channel_id=1, source_target_pairs={{0,24},{8,16},{16,8},{24,0},{1,25},{9,17},{17,9},{25,1},{2,26},{10... | collective-permute-start | bytes 393224 | tf_op jit(solution)/shard_map/ppermute | solution.py:232
  15.6 6.6 %collective-permute-start.4 = (f32[64,512]{1,0:T(8,128)S(1)}, f32[64,512]{1,0:T(8,128)S(1)}, u32[]{:S(2)}, u32[]{:S(2)}) collective-permute-start(f32[64,512]{1,0:T(8,128)S(1)} %fusion.17), channel_id=1, source_target_pairs={{0,16},{8,24},{16,0},{24,8},{1,17},{9,25},{17,1},{25,9},{2,18},{10... | collective-permute-start | bytes 393224 | tf_op jit(solution)/shard_map/ppermute | solution.py:232
  17.7 9.8 %collective-permute-start.13 = (bf16[64,512]{1,0:T(8,128)(2,1)S(1)}, bf16[64,512]{1,0:T(8,128)(2,1)S(1)}, u32[]{:S(2)}, u32[]{:S(2)}) collective-permute-start(bf16[64,512]{1,0:T(8,128)(2,1)S(1)} %bitcast.69), channel_id=1, source_target_pairs={{0,2},{1,3},{2,0},{3,1},{4,6},{5,7},{6,4},{7,5},{8,10},{9,11},{10,... | collective-permute-start | bytes 196616 | tf_op jit(solution)/shard_map/ppermute | solution.py:232
  19.4 8.3 %collective-permute-start.14 = (bf16[64,512]{1,0:T(8,128)(2,1)S(1)}, bf16[64,512]{1,0:T(8,128)(2,1)S(1)}, u32[]{:S(2)}, u32[]{:S(2)}) collective-permute-start(bf16[64,512]{1,0:T(8,128)(2,1)S(1)} %bitcast.70), channel_id=1, source_target_pairs={{0,4},{1,5},{2,6},{3,7},{4,0},{5,1},{6,2},{7,3},{8,12},{9,13},{10,... | collective-permute-start | bytes 196616 | tf_op jit(solution)/shard_map/ppermute | solution.py:232
  22.0 6.8 %collective-permute-start.15 = (bf16[64,512]{1,0:T(8,128)(2,1)S(1)}, bf16[64,512]{1,0:T(8,128)(2,1)S(1)}, u32[]{:S(2)}, u32[]{:S(2)}) collective-permute-start(bf16[64,512]{1,0:T(8,128)(2,1)S(1)} %bitcast.71), channel_id=1, source_target_pairs={{0,6},{1,7},{2,4},{3,5},{4,2},{5,3},{6,0},{7,1},{8,14},{9,15},{10,... | collective-permute-start | bytes 196616 | tf_op jit(solution)/shard_map/ppermute | solution.py:232
  23.2 5.6 %collective-permute-start.6 = (bf16[64,512]{1,0:T(8,128)(2,1)S(1)}, bf16[64,512]{1,0:T(8,128)(2,1)S(1)}, u32[]{:S(2)}, u32[]{:S(2)}) collective-permute-start(bf16[64,512]{1,0:T(8,128)(2,1)S(1)} %fusion.9.refs_0_), channel_id=1, source_target_pairs={{0,2},{1,3},{2,0},{3,1},{4,6},{5,7},{6,4},{7,5},{8,10},{9,11},{10,... | collective-permute-start | bytes 196616 | tf_op jit(solution)/shard_map/ppermute | solution.py:232
  24.9 7.1 %collective-permute-start.7 = (bf16[64,512]{1,0:T(8,128)(2,1)S(1)}, bf16[64,512]{1,0:T(8,128)(2,1)S(1)}, u32[]{:S(2)}, u32[]{:S(2)}) collective-permute-start(bf16[64,512]{1,0:T(8,128)(2,1)S(1)} %fusion.9.refs_0_), channel_id=1, source_target_pairs={{0,4},{1,5},{2,6},{3,7},{4,0},{5,1},{6,2},{7,3},{8,12},{9,13},{10,... | collective-permute-start | bytes 196616 | tf_op jit(solution)/shard_map/ppermute | solution.py:232
  27.5 6.1 %collective-permute-start.8 = (bf16[64,512]{1,0:T(8,128)(2,1)S(1)}, bf16[64,512]{1,0:T(8,128)(2,1)S(1)}, u32[]{:S(2)}, u32[]{:S(2)}) collective-permute-start(bf16[64,512]{1,0:T(8,128)(2,1)S(1)} %fusion.9.refs_0_), channel_id=1, source_target_pairs={{0,6},{1,7},{2,4},{3,5},{4,2},{5,3},{6,0},{7,1},{8,14},{9,15},{10,... | collective-permute-start | bytes 196616 | tf_op jit(solution)/shard_map/ppermute | solution.py:232
  27.7 5.8 %collective-permute-start.16 = (bf16[64,512]{1,0:T(8,128)(2,1)S(1)}, bf16[64,512]{1,0:T(8,128)(2,1)S(1)}, u32[]{:S(2)}, u32[]{:S(2)}) collective-permute-start(bf16[64,512]{1,0:T(8,128)(2,1)S(1)} %bitcast.72), channel_id=1, source_target_pairs={{0,1},{1,0},{2,3},{3,2},{4,5},{5,4},{6,7},{7,6},{8,9},{9,8},{10,11... | collective-permute-start | bytes 196616 | tf_op jit(solution)/shard_map/ppermute | solution.py:232
  35.2 28.4 %collective-permute-start.23 = (bf16[1280,256]{1,0:T(8,128)(2,1)S(1)}, bf16[1280,256]{1,0:T(8,128)(2,1)S(1)}, u32[]{:S(2)}, u32[]{:S(2)}) collective-permute-start(bf16[1280,256]{1,0:T(8,128)(2,1)S(1)} %constant_dynamic-slice_fusion), channel_id=1, source_target_pairs={{0,8},{8,0},{16,24},{24,16},{1,9},{9,1},{17,25},{25,17},{2,10},{10... | collective-permute-start | bytes 1966088 | tf_op jit(solution)/shard_map/ppermute | solution.py:232
  36.8 26.9 %collective-permute-start.24 = (bf16[1280,256]{1,0:T(8,128)(2,1)S(1)}, bf16[1280,256]{1,0:T(8,128)(2,1)S(1)}, u32[]{:S(2)}, u32[]{:S(2)}) collective-permute-start(bf16[1280,256]{1,0:T(8,128)(2,1)S(1)} %constant_dynamic-slice_fusion), channel_id=1, source_target_pairs={{0,16},{8,24},{16,0},{24,8},{1,17},{9,25},{17,1},{25,9},{2,18},{10... | collective-permute-start | bytes 1966088 | tf_op jit(solution)/shard_map/ppermute | solution.py:232
  37.4 26.2 %collective-permute-start.20 = (bf16[320,256]{1,0:T(8,128)(2,1)}, bf16[320,256]{1,0:T(8,128)(2,1)S(1)}, u32[]{:S(2)}, u32[]{:S(2)}) collective-permute-start(bf16[320,256]{1,0:T(8,128)(2,1)} %get-tuple-element.99), channel_id=1, source_target_pairs={{0,2},{1,3},{2,0},{3,1},{4,6},{5,7},{6,4},{7,5},{8,10},{9,11},{10,... | collective-permute-start | bytes 491528 | tf_op jit(solution)/shard_map/ppermute | solution.py:232
  37.4 26.2 %collective-permute-start.21 = (bf16[320,256]{1,0:T(8,128)(2,1)}, bf16[320,256]{1,0:T(8,128)(2,1)S(1)}, u32[]{:S(2)}, u32[]{:S(2)}) collective-permute-start(bf16[320,256]{1,0:T(8,128)(2,1)} %get-tuple-element.100), channel_id=1, source_target_pairs={{0,4},{1,5},{2,6},{3,7},{4,0},{5,1},{6,2},{7,3},{8,12},{9,13},{10,... | collective-permute-start | bytes 491528 | tf_op jit(solution)/shard_map/ppermute | solution.py:232
  39.7 24.0 %collective-permute-start.22 = (bf16[320,256]{1,0:T(8,128)(2,1)}, bf16[320,256]{1,0:T(8,128)(2,1)S(1)}, u32[]{:S(2)}, u32[]{:S(2)}) collective-permute-start(bf16[320,256]{1,0:T(8,128)(2,1)} %get-tuple-element.101), channel_id=1, source_target_pairs={{0,6},{1,7},{2,4},{3,5},{4,2},{5,3},{6,0},{7,1},{8,14},{9,15},{10,... | collective-permute-start | bytes 491528 | tf_op jit(solution)/shard_map/ppermute | solution.py:232
  64.3 11.6 %collective-permute-start.30 = (bf16[1280,256]{1,0:T(8,128)(2,1)S(1)}, bf16[1280,256]{1,0:T(8,128)(2,1)S(1)}, u32[]{:S(2)}, u32[]{:S(2)}) collective-permute-start(bf16[1280,256]{1,0:T(8,128)(2,1)S(1)} %collective-permute-done.23.refs_2_), channel_id=1, source_target_pairs={{0,1},{1,0},{2,3},{3,2},{4,5},{5,4},{6,7},{7,6},{8,9},{9,8},{10,11... | collective-permute-start | bytes 1966088 | tf_op jit(solution)/shard_map/ppermute | solution.py:232
  64.4 11.6 %collective-permute-start.31 = (bf16[1280,256]{1,0:T(8,128)(2,1)S(1)}, bf16[1280,256]{1,0:T(8,128)(2,1)S(1)}, u32[]{:S(2)}, u32[]{:S(2)}) collective-permute-start(bf16[1280,256]{1,0:T(8,128)(2,1)S(1)} %collective-permute-done.24.refs_3_), channel_id=1, source_target_pairs={{0,1},{1,0},{2,3},{3,2},{4,5},{5,4},{6,7},{7,6},{8,9},{9,8},{10,11... | collective-permute-start | bytes 1966088 | tf_op jit(solution)/shard_map/ppermute | solution.py:232
  67.1 6.8 %collective-permute-start.28 = (bf16[64,512]{1,0:T(8,128)(2,1)S(1)}, bf16[64,512]{1,0:T(8,128)(2,1)S(1)}, u32[]{:S(2)}, u32[]{:S(2)}) collective-permute-start(bf16[64,512]{1,0:T(8,128)(2,1)S(1)} %get-tuple-element.161), channel_id=1, source_target_pairs={{0,6},{1,7},{2,4},{3,5},{4,2},{5,3},{6,0},{7,1},{8,14},{9,15},{10,... | collective-permute-start | bytes 196616 | tf_op jit(solution)/shard_map/ppermute | solution.py:232
  68.8 7.1 %collective-permute-start.27 = (bf16[64,512]{1,0:T(8,128)(2,1)S(1)}, bf16[64,512]{1,0:T(8,128)(2,1)S(1)}, u32[]{:S(2)}, u32[]{:S(2)}) collective-permute-start(bf16[64,512]{1,0:T(8,128)(2,1)S(1)} %get-tuple-element.162), channel_id=1, source_target_pairs={{0,4},{1,5},{2,6},{3,7},{4,0},{5,1},{6,2},{7,3},{8,12},{9,13},{10,... | collective-permute-start | bytes 196616 | tf_op jit(solution)/shard_map/ppermute | solution.py:232
  68.8 7.0 %collective-permute-start.26 = (bf16[64,512]{1,0:T(8,128)(2,1)S(1)}, bf16[64,512]{1,0:T(8,128)(2,1)S(1)}, u32[]{:S(2)}, u32[]{:S(2)}) collective-permute-start(bf16[64,512]{1,0:T(8,128)(2,1)S(1)} %get-tuple-element.160), channel_id=1, source_target_pairs={{0,2},{1,3},{2,0},{3,1},{4,6},{5,7},{6,4},{7,5},{8,10},{9,11},{10,... | collective-permute-start | bytes 196616 | tf_op jit(solution)/shard_map/ppermute | solution.py:232
  77.4 5.9 %collective-permute-start.32 = (bf16[64,512]{1,0:T(8,128)(2,1)S(1)}, bf16[64,512]{1,0:T(8,128)(2,1)S(1)}, u32[]{:S(2)}, u32[]{:S(2)}) collective-permute-start(bf16[64,512]{1,0:T(8,128)(2,1)S(1)} %slice.47), channel_id=1, source_target_pairs={{0,2},{1,3},{2,0},{3,1},{4,6},{5,7},{6,4},{7,5},{8,10},{9,11},{10,... | collective-permute-start | bytes 196616 | tf_op jit(solution)/shard_map/ppermute | solution.py:232
  77.5 5.9 %collective-permute-start.33 = (bf16[64,512]{1,0:T(8,128)(2,1)S(1)}, bf16[64,512]{1,0:T(8,128)(2,1)S(1)}, u32[]{:S(2)}, u32[]{:S(2)}) collective-permute-start(bf16[64,512]{1,0:T(8,128)(2,1)S(1)} %fusion.7.refs_0_), channel_id=1, source_target_pairs={{0,2},{1,3},{2,0},{3,1},{4,6},{5,7},{6,4},{7,5},{8,10},{9,11},{10,... | collective-permute-start | bytes 196616 | tf_op jit(solution)/shard_map/ppermute | solution.py:232
  79.5 7.9 %collective-permute-start.34 = (bf16[64,512]{1,0:T(8,128)(2,1)S(1)}, bf16[64,512]{1,0:T(8,128)(2,1)S(1)}, u32[]{:S(2)}, u32[]{:S(2)}) collective-permute-start(bf16[64,512]{1,0:T(8,128)(2,1)S(1)} %fusion.7.refs_0_), channel_id=1, source_target_pairs={{0,4},{1,5},{2,6},{3,7},{4,0},{5,1},{6,2},{7,3},{8,12},{9,13},{10,... | collective-permute-start | bytes 196616 | tf_op jit(solution)/shard_map/ppermute | solution.py:232
  80.1 7.3 %collective-permute-start.35 = (bf16[64,512]{1,0:T(8,128)(2,1)S(1)}, bf16[64,512]{1,0:T(8,128)(2,1)S(1)}, u32[]{:S(2)}, u32[]{:S(2)}) collective-permute-start(bf16[64,512]{1,0:T(8,128)(2,1)S(1)} %fusion.7.refs_0_), channel_id=1, source_target_pairs={{0,6},{1,7},{2,4},{3,5},{4,2},{5,3},{6,0},{7,1},{8,14},{9,15},{10,... | collective-permute-start | bytes 196616 | tf_op jit(solution)/shard_map/ppermute | solution.py:232
  87.5 14.7 %collective-permute-start.40 = (bf16[256,512]{1,0:T(8,128)(2,1)S(1)}, bf16[256,512]{1,0:T(8,128)(2,1)S(1)}, u32[]{:S(2)}, u32[]{:S(2)}) collective-permute-start(bf16[256,512]{1,0:T(8,128)(2,1)S(1)} %constant_dynamic-update-slice_fusion), channel_id=1, source_target_pairs={{0,16},{8,24},{16,0},{24,8},{1,17},{9,25},{17,1},{25,9},{2,18},{10... | collective-permute-start | bytes 786440 | tf_op jit(solution)/shard_map/ppermute | solution.py:232
  89.0 13.5 %collective-permute-start.39 = (bf16[256,512]{1,0:T(8,128)(2,1)S(1)}, bf16[256,512]{1,0:T(8,128)(2,1)S(1)}, u32[]{:S(2)}, u32[]{:S(2)}) collective-permute-start(bf16[256,512]{1,0:T(8,128)(2,1)S(1)} %constant_dynamic-update-slice_fusion), channel_id=1, source_target_pairs={{0,8},{8,0},{16,24},{24,16},{1,9},{9,1},{17,25},{25,17},{2,10},{10... | collective-permute-start | bytes 786440 | tf_op jit(solution)/shard_map/ppermute | solution.py:232
  89.5 10.9 %collective-permute-start.37 = (bf16[192,512]{1,0:T(8,128)(2,1)S(1)}, bf16[192,512]{1,0:T(8,128)(2,1)S(1)}, u32[]{:S(2)}, u32[]{:S(2)}) collective-permute-start(bf16[192,512]{1,0:T(8,128)(2,1)S(1)} %pad_maximum_fusion), channel_id=1, source_target_pairs={{0,24},{8,16},{16,8},{24,0},{1,25},{9,17},{17,9},{25,1},{2,26},{10... | collective-permute-start | bytes 589832 | tf_op jit(solution)/shard_map/ppermute | solution.py:232
  91.1 11.9 %collective-permute-start.41 = (bf16[64,512]{1,0:T(8,128)(2,1)S(1)}, bf16[64,512]{1,0:T(8,128)(2,1)S(1)}, u32[]{:S(2)}, u32[]{:S(2)}) collective-permute-start(bf16[64,512]{1,0:T(8,128)(2,1)S(1)} %get-tuple-element.159), channel_id=1, source_target_pairs={{0,4},{1,5},{2,6},{3,7},{4,0},{5,1},{6,2},{7,3},{8,12},{9,13},{10,... | collective-permute-start | bytes 196616 | tf_op jit(solution)/shard_map/ppermute | solution.py:232
  92.7 10.3 %collective-permute-start.42 = (bf16[64,512]{1,0:T(8,128)(2,1)S(1)}, bf16[64,512]{1,0:T(8,128)(2,1)S(1)}, u32[]{:S(2)}, u32[]{:S(2)}) collective-permute-start(bf16[64,512]{1,0:T(8,128)(2,1)S(1)} %get-tuple-element.158), channel_id=1, source_target_pairs={{0,6},{1,7},{2,4},{3,5},{4,2},{5,3},{6,0},{7,1},{8,14},{9,15},{10,... | collective-permute-start | bytes 196616 | tf_op jit(solution)/shard_map/ppermute | solution.py:232
  100.4 6.5 %collective-permute-start.38 = (bf16[64,1280]{1,0:T(8,128)(2,1)}, bf16[64,1280]{1,0:T(8,128)(2,1)S(1)}, u32[]{:S(2)}, u32[]{:S(2)}) collective-permute-start(bf16[64,1280]{1,0:T(8,128)(2,1)} %get-tuple-element.133), channel_id=1, source_target_pairs={{0,24},{8,16},{16,8},{24,0},{1,25},{9,17},{17,9},{25,1},{2,26},{10... | collective-permute-start | bytes 491528 | tf_op jit(solution)/shard_map/ppermute | solution.py:232
  (55 other events, 380.8 us)

commit v13 on v12

--- a/solution.py
+++ b/solution.py
@@ -153,39 +153,6 @@
     return in_vmem(partial(turn_kernel, len(columns)), "turn_hidden", outs, columns, 0, scratch)
 
 
-def hidden_kernel(beside, across, own_ref, *refs):
-    grads, refs = refs[: len(across) + 1], refs[len(across) + 1 :]
-    near, far = refs[: len(beside)], refs[len(beside) : 2 * len(beside)]
-    out_ref, *part_refs = refs[2 * len(beside) :]
-    group, core = lax.axis_index("group"), lax.axis_index("resp") % 2
-    depth, kv_width = own_ref.shape
-    tokens, half = grads[0].shape[0], kv_width // 2
-    near_grad = grads[0][:, pl.ds(pl.multiple_of(core * half, half), half)]
-    far_grad = grads[0][:, pl.ds(pl.multiple_of((1 - core) * half, half), half)]
-
-    def place(k, block):
-        out_ref[:, pl.ds(pl.multiple_of((group ^ k) * depth, depth), depth)] = block
-
-    own = dot(own_ref[...], jnp.concatenate([ref[...] for ref in grads], axis=0), 1, 1).T.astype(BF16)
-    place(0, own[:tokens])
-    for i, k in enumerate(across):
-        part_refs[i][...] = own[(i + 1) * tokens : (i + 2) * tokens]
-        place(k, jnp.zeros((tokens, depth), BF16))
-    for i, k in enumerate(beside):
-        block = dot(near[i][...], near_grad, 1, 1) + dot(far[i][...], far_grad, 1, 1)
-        place(k, block.T.astype(BF16))
-
-
-def hidden_pass(key_pre_grad, first, own, near, far):
-    tokens, kv_width = key_pre_grad.shape
-    depth = own.shape[0]
-    groups = 1 + len(first) + len(near)
-    outs = [((tokens, groups * depth), BF16)] + [((tokens, depth), BF16)] * len(first)
-    arrays = [own, key_pre_grad, *first.values(), *near.values(), *far.values()]
-    kernel = partial(hidden_kernel, list(near), list(first))
-    return in_vmem(kernel, "hidden_grad", outs, arrays, tokens * depth * kv_width * groups)
-
-
 def order_kernel(chips, widths, *refs):
     taken, out_refs = refs[:chips], nested(refs[chips:], [len(parts) for parts in widths for _ in range(2)])
     half = taken[0].shape[0] // 2
@@ -320,9 +287,16 @@
     value_parts[1], value_sums, *both = together(value_parts[1], value_sums, *grads, *first.values())
     grads, first = both[:chips], dict(zip(first, both[chips:]))
     some, every = jnp.concatenate(grads[1:], axis=0), jnp.concatenate(grads, axis=0)
-    grad_hidden, *parts = hidden_pass(
-        key_pre_grad, first, key_matrix, dict(zip(beside, weight_near)), dict(zip(beside, weight_far))
-    )
+    group, core = lax.axis_index("group"), lax.axis_index("resp") % 2
+    grad_hidden = jnp.zeros((tokens, groups * depth), BF16)
+    own = dot(jnp.concatenate([key_pre_grad, *first.values()], axis=0), key_matrix, 1, 1).astype(BF16)
+    parts = [own[(i + 1) * tokens : (i + 2) * tokens] for i in range(len(across))]
+    grad_hidden = lax.dynamic_update_slice(grad_hidden, own[:tokens], (0, group * depth))
+    near_grad = lax.dynamic_slice(key_pre_grad, (0, core * half_width), (tokens, half_width))
+    far_grad = lax.dynamic_slice(key_pre_grad, (0, (1 - core) * half_width), (tokens, half_width))
+    for k, near, far in zip(beside, weight_near, weight_far):
+        block = (dot(near_grad, near, 1, 1) + dot(far_grad, far, 1, 1)).astype(BF16)
+        grad_hidden = lax.dynamic_update_slice(grad_hidden, block, (0, (group ^ k) * depth))
 
     blocks = [[every]] + [None] * (groups - 1)
     for k in beside:
@@ -338,8 +312,7 @@
     value_sums = total(value_parts)
     grad_weight = weight_sum(mine, blocks, order) + swap(other, "resp", responses, 1)
     for k, part in zip(across, parts):
-        start = (lax.axis_index("group") ^ k) * depth
-        grad_hidden = lax.dynamic_update_slice(grad_hidden, part, (0, start))
+        grad_hidden = lax.dynamic_update_slice(grad_hidden, part, (0, (group ^ k) * depth))
     return (
         grad_hidden[None],
         grad_weight,

time: 109 us -> 111 us (1.018)
  Pallas kernels: 32.4 us -> 28.2 us
  matrix products: 6.29 us -> 10.1 us
  other arithmetic: 2.36 us -> 4.46 us
    pallas_call x4 -> x3, Pallas kernels: 10.8 us -> 6.49 us  [in_vmem(): pl.pallas_call(kernel, in_specs=[whole] * len(arrays), out_specs=[whole]...]
    dot_general x14 -> x19, matrix products: 6.29 us -> 10.1 us  [dot(): return lax.dot_general(left, right, dims, preferred_element_type=F32)]
    add x1, other arithmetic: 0.08 us -> 1.28 us  [pair_sum(): return near + swap(far, 'resp', size, 1)]
  transfers between devices with their start and end apart: 44 -> 44, of which waited for: 10 -> 7; matrix products, arithmetic and copies ran while one was open for 8% -> 13% of each run, Pallas kernels for 28% -> 24%
where the time goes in v13:
time: 111 us; the launch traced here: 110 us
  starting transfers between devices  46.6 us (42%)
  Pallas kernels  28.2 us (25%)
  waiting for transfers between devices  16 us (14%)
  matrix products  10.1 us (9%)
  other arithmetic  4.46 us (4%)
  local copies, waits for them, and re-layouts  2.7 us (2%)
  between operations  2.14 us (2%)
    ppermute x44, starting transfers between devices, swap(): return lax.ppermute(array, axis, [(i, i ^ distance) for i in range(size)])  46.6 us
    pallas_call x1, Pallas kernels, attend(): pl.pallas_call(partial(attend_kernel, len(key_pieces)), grid=(kv_heads,),...  21.7 us
    ppermute x44, waiting for transfers between devices, swap(): return lax.ppermute(array, axis, [(i, i ^ distance) for i in range(size)])  16 us
    dot_general x19, matrix products, dot(): return lax.dot_general(left, right, dims, preferred_element_type=F32)  10.1 us
    pallas_call x3, Pallas kernels, in_vmem(): pl.pallas_call(kernel, in_specs=[whole] * len(arrays), out_specs=[whole]...  6.49 us
  transfers between devices with their start and end apart: 44, of which 7 were waited for; matrix products, arithmetic and copies ran while one was open for 13% of the time, Pallas kernels for 24%

profile of v13, /device:TPU:0, one launch (start us, length us, event | category | flops | bytes accessed | tf_op | source)
XLA Modules:
  0.0 110.3 jit_solution(15130579375727726723)
XLA Ops:
  0.6 2.1 %split_hidden.1 = (bf16[64,1280]{1,0:T(8,128)(2,1)}, bf16[64,1280]{1,0:T(8,128)(2,1)}, bf16[64,1280]{1,0:T(8,128)(2,1)}, bf16[64,1280]{1,0:T(8,128)(2,1)}) custom-call(bf16[64,5120]{1,0:T(8,128)(2,1)} %bitcast.77), custom_call_target="tpu_custom_call" | custom-call | bytes 3000000 | tf_op jit(solution)/shard_map/split_hidden/pallas_call | solution.py:108
  2.7 2.9 %collective-permute-start = (bf16[64,1280]{1,0:T(8,128)(2,1)}, bf16[64,1280]{1,0:T(8,128)(2,1)S(1)}, u32[]{:S(2)}, u32[]{:S(2)}) collective-permute-start(bf16[64,1280]{1,0:T(8,128)(2,1)} %get-tuple-element.80), channel_id=1, source_target_pairs={{0,8},{8,0},{16,24},{24,16},{1,9},{9,1},{17,25},{25,17},{2,10},{10... | collective-permute-start | bytes 491528 | tf_op jit(solution)/shard_map/ppermute | solution.py:199
  5.6 1.5 %collective-permute-start.1 = (bf16[64,1280]{1,0:T(8,128)(2,1)}, bf16[64,1280]{1,0:T(8,128)(2,1)S(1)}, u32[]{:S(2)}, u32[]{:S(2)}) collective-permute-start(bf16[64,1280]{1,0:T(8,128)(2,1)} %get-tuple-element.81), channel_id=1, source_target_pairs={{0,16},{8,24},{16,0},{24,8},{1,17},{9,25},{17,1},{25,9},{2,18},{10... | collective-permute-start | bytes 491528 | tf_op jit(solution)/shard_map/ppermute | solution.py:199
  8.5 6.4 %collective-permute-done.2.refs_3_ = bf16[64,1280]{1,0:T(8,128)(2,1)S(1)} collective-permute-done((bf16[64,1280]{1,0:T(8,128)(2,1)}, bf16[64,1280]{1,0:T(8,128)(2,1)S(1)}, u32[]{:S(2)}, u32[]{:S(2)}) %collective-permute-start.2) | collective-permute-done | bytes 163872 | tf_op jit(solution)/shard_map/ppermute | solution.py:199
  15.2 1.5 %collective-permute-start.5 = (f32[64,512]{1,0:T(8,128)S(1)}, f32[64,512]{1,0:T(8,128)S(1)}, u32[]{:S(2)}, u32[]{:S(2)}) collective-permute-start(f32[64,512]{1,0:T(8,128)S(1)} %fusion.39), channel_id=1, source_target_pairs={{0,24},{8,16},{16,8},{24,0},{1,25},{9,17},{17,9},{25,1},{2,26},{10... | collective-permute-start | bytes 393224 | tf_op jit(solution)/shard_map/ppermute | solution.py:199
  17.1 1.5 %collective-permute-start.4 = (f32[64,512]{1,0:T(8,128)S(1)}, f32[64,512]{1,0:T(8,128)S(1)}, u32[]{:S(2)}, u32[]{:S(2)}) collective-permute-start(f32[64,512]{1,0:T(8,128)S(1)} %fusion.38), channel_id=1, source_target_pairs={{0,16},{8,24},{16,0},{24,8},{1,17},{9,25},{17,1},{25,9},{2,18},{10... | collective-permute-start | bytes 393224 | tf_op jit(solution)/shard_map/ppermute | solution.py:199
  19.7 1.6 %collective-permute-start.13 = (bf16[64,512]{1,0:T(8,128)(2,1)S(1)}, bf16[64,512]{1,0:T(8,128)(2,1)S(1)}, u32[]{:S(2)}, u32[]{:S(2)}) collective-permute-start(bf16[64,512]{1,0:T(8,128)(2,1)S(1)} %bitcast.84), channel_id=1, source_target_pairs={{0,2},{1,3},{2,0},{3,1},{4,6},{5,7},{6,4},{7,5},{8,10},{9,11},{10,... | collective-permute-start | bytes 196616 | tf_op jit(solution)/shard_map/ppermute | solution.py:199
  21.2 2.6 %collective-permute-start.14 = (bf16[64,512]{1,0:T(8,128)(2,1)S(1)}, bf16[64,512]{1,0:T(8,128)(2,1)S(1)}, u32[]{:S(2)}, u32[]{:S(2)}) collective-permute-start(bf16[64,512]{1,0:T(8,128)(2,1)S(1)} %bitcast.85), channel_id=1, source_target_pairs={{0,4},{1,5},{2,6},{3,7},{4,0},{5,1},{6,2},{7,3},{8,12},{9,13},{10,... | collective-permute-start | bytes 196616 | tf_op jit(solution)/shard_map/ppermute | solution.py:199
  23.8 2.2 %collective-permute-start.15 = (bf16[64,512]{1,0:T(8,128)(2,1)S(1)}, bf16[64,512]{1,0:T(8,128)(2,1)S(1)}, u32[]{:S(2)}, u32[]{:S(2)}) collective-permute-start(bf16[64,512]{1,0:T(8,128)(2,1)S(1)} %bitcast.86), channel_id=1, source_target_pairs={{0,6},{1,7},{2,4},{3,5},{4,2},{5,3},{6,0},{7,1},{8,14},{9,15},{10,... | collective-permute-start | bytes 196616 | tf_op jit(solution)/shard_map/ppermute | solution.py:199
  26.7 2.2 %collective-permute-start.7 = (bf16[64,512]{1,0:T(8,128)(2,1)S(1)}, bf16[64,512]{1,0:T(8,128)(2,1)S(1)}, u32[]{:S(2)}, u32[]{:S(2)}) collective-permute-start(bf16[64,512]{1,0:T(8,128)(2,1)S(1)} %fusion.16.refs_0_), channel_id=1, source_target_pairs={{0,4},{1,5},{2,6},{3,7},{4,0},{5,1},{6,2},{7,3},{8,12},{9,13},{10,... | collective-permute-start | bytes 196616 | tf_op jit(solution)/shard_map/ppermute | solution.py:199
  28.9 2.2 %collective-permute-start.8 = (bf16[64,512]{1,0:T(8,128)(2,1)S(1)}, bf16[64,512]{1,0:T(8,128)(2,1)S(1)}, u32[]{:S(2)}, u32[]{:S(2)}) collective-permute-start(bf16[64,512]{1,0:T(8,128)(2,1)S(1)} %fusion.16.refs_0_), channel_id=1, source_target_pairs={{0,6},{1,7},{2,4},{3,5},{4,2},{5,3},{6,0},{7,1},{8,14},{9,15},{10,... | collective-permute-start | bytes 196616 | tf_op jit(solution)/shard_map/ppermute | solution.py:199
  31.7 2.3 %turn_hidden.1 = (bf16[320,256]{1,0:T(8,128)(2,1)}, bf16[320,256]{1,0:T(8,128)(2,1)}, bf16[320,256]{1,0:T(8,128)(2,1)}, bf16[320,256]{1,0:T(8,128)(2,1)}) custom-call(bf16[64,1280]{1,0:T(8,128)(2,1)} %get-tuple-element.79.refs_0_, bf16[64,1280]{1,0:T(8,128)(2,1)} %copy-done.2, bf16[64,1280]{1,0:T(8,128)(2,1)} %copy-done.3, bf16[64,1280]{1,0:T(8,128)(2,1)} %copy-done.4), custom_call_target="tpu_custom_call" | custom-call | bytes 3000000 | tf_op jit(solution)/shard_map/turn_hidden/pallas_call | solution.py:108
  36.7 1.4 %collective-permute-start.23 = (bf16[1280,256]{1,0:T(8,128)(2,1)S(1)}, bf16[1280,256]{1,0:T(8,128)(2,1)}, u32[]{:S(2)}, u32[]{:S(2)}) collective-permute-start(bf16[1280,256]{1,0:T(8,128)(2,1)S(1)} %constant_dynamic-slice_fusion), channel_id=1, source_target_pairs={{0,8},{8,0},{16,24},{24,16},{1,9},{9,1},{17,25},{25,17},{2,10},{10... | collective-permute-start | bytes 1966088 | tf_op jit(solution)/shard_map/ppermute | solution.py:199
  38.8 2.6 %collective-permute-start.21 = (bf16[320,256]{1,0:T(8,128)(2,1)}, bf16[320,256]{1,0:T(8,128)(2,1)S(1)}, u32[]{:S(2)}, u32[]{:S(2)}) collective-permute-start(bf16[320,256]{1,0:T(8,128)(2,1)} %get-tuple-element.98), channel_id=1, source_target_pairs={{0,4},{1,5},{2,6},{3,7},{4,0},{5,1},{6,2},{7,3},{8,12},{9,13},{10,... | collective-permute-start | bytes 491528 | tf_op jit(solution)/shard_map/ppermute | solution.py:199
  41.4 1.8 %collective-permute-start.22 = (bf16[320,256]{1,0:T(8,128)(2,1)}, bf16[320,256]{1,0:T(8,128)(2,1)S(1)}, u32[]{:S(2)}, u32[]{:S(2)}) collective-permute-start(bf16[320,256]{1,0:T(8,128)(2,1)} %get-tuple-element.99), channel_id=1, source_target_pairs={{0,6},{1,7},{2,4},{3,5},{4,2},{5,3},{6,0},{7,1},{8,14},{9,15},{10,... | collective-permute-start | bytes 491528 | tf_op jit(solution)/shard_map/ppermute | solution.py:199
  43.3 21.7 %attend.1 = (bf16[256,4096]{1,0:T(8,128)(2,1)}, bf16[256,512]{1,0:T(8,128)(2,1)}, bf16[256,512]{1,0:T(8,128)(2,1)}, f32[256,512]{1,0:T(8,128)}, f32[256,512]{1,0...) custom-call(s32[1,1]{1,0:T(1,128)S(6)} %copy.33.length_ref, bf16[256,4096]{1,0:T(8,128)(2,1)} %bitcast.79, ...), custom_call_target="tpu_custom_call" | custom-call | flops 16106127360 | bytes 10000000 | tf_op jit(solution)/shard_map/attend/pallas_call | solution.py:91
  69.0 2.0 %collective-permute-start.28 = (bf16[64,512]{1,0:T(8,128)(2,1)}, bf16[64,512]{1,0:T(8,128)(2,1)S(1)}, u32[]{:S(2)}, u32[]{:S(2)}) collective-permute-start(bf16[64,512]{1,0:T(8,128)(2,1)} %get-tuple-element.157), channel_id=1, source_target_pairs={{0,6},{1,7},{2,4},{3,5},{4,2},{5,3},{6,0},{7,1},{8,14},{9,15},{10,... | collective-permute-start | bytes 196616 | tf_op jit(solution)/shard_map/ppermute | solution.py:199
  71.1 2.4 %collective-permute-start.26 = (bf16[64,512]{1,0:T(8,128)(2,1)}, bf16[64,512]{1,0:T(8,128)(2,1)}, u32[]{:S(2)}, u32[]{:S(2)}) collective-permute-start(bf16[64,512]{1,0:T(8,128)(2,1)} %get-tuple-element.156), channel_id=1, source_target_pairs={{0,2},{1,3},{2,0},{3,1},{4,6},{5,7},{6,4},{7,5},{8,10},{9,11},{10,... | collective-permute-start | bytes 196616 | tf_op jit(solution)/shard_map/ppermute | solution.py:199
  73.4 2.2 %order_columns.1 = (bf16[160,256]{1,0:T(8,128)(2,1)}, bf16[160,256]{1,0:T(8,128)(2,1)}, bf16[160,256]{1,0:T(8,128)(2,1)}, bf16[160,256]{1,0:T(8,128)(2,1)}, bf16...) custom-call(bf16[320,256]{1,0:T(8,128)(2,1)} %get-tuple-element.107., ...), custom_call_target="tpu_custom_call" | custom-call | bytes 3000000 | tf_op jit(solution)/shard_map/order_columns/pallas_call | solution.py:108
  75.6 1.3 %add.111 = f32[256,512]{1,0:T(8,128)S(1)} add(f32[256,512]{1,0:T(8,128)} %get-tuple-element.103, f32[256,512]{1,0:T(8,128)} %collective-permute-done.29) | non-fusion elementwise | flops 131072 | bytes 1572864 | tf_op jit(solution)/shard_map/add | solution.py:215
  80.2 2.6 %collective-permute-start.34 = (bf16[64,512]{1,0:T(8,128)(2,1)S(1)}, bf16[64,512]{1,0:T(8,128)(2,1)S(1)}, u32[]{:S(2)}, u32[]{:S(2)}) collective-permute-start(bf16[64,512]{1,0:T(8,128)(2,1)S(1)} %fusion.14), channel_id=1, source_target_pairs={{0,4},{1,5},{2,6},{3,7},{4,0},{5,1},{6,2},{7,3},{8,12},{9,13},{10,... | collective-permute-start | bytes 196616 | tf_op jit(solution)/shard_map/ppermute | solution.py:199
  82.8 1.8 %collective-permute-start.35 = (bf16[64,512]{1,0:T(8,128)(2,1)S(1)}, bf16[64,512]{1,0:T(8,128)(2,1)S(1)}, u32[]{:S(2)}, u32[]{:S(2)}) collective-permute-start(bf16[64,512]{1,0:T(8,128)(2,1)S(1)} %fusion.14), channel_id=1, source_target_pairs={{0,6},{1,7},{2,4},{3,5},{4,2},{5,3},{6,0},{7,1},{8,14},{9,15},{10,... | collective-permute-start | bytes 196616 | tf_op jit(solution)/shard_map/ppermute | solution.py:199
  84.6 1.5 %collective-permute-start.36 = (bf16[64,512]{1,0:T(8,128)(2,1)S(1)}, bf16[64,512]{1,0:T(8,128)(2,1)S(1)}, u32[]{:S(2)}, u32[]{:S(2)}) collective-permute-start(bf16[64,512]{1,0:T(8,128)(2,1)S(1)} %fusion.14), channel_id=1, source_target_pairs={{0,24},{8,16},{16,8},{24,0},{1,25},{9,17},{17,9},{25,1},{2,26},{10... | collective-permute-start | bytes 196616 | tf_op jit(solution)/shard_map/ppermute | solution.py:199
  86.5 1.4 %fusion.21 = f32[64,1280]{1,0:T(8,128)S(1)} fusion(bf16[1280,256]{1,0:T(8,128)(2,1)} %collective-permute-done.31, bf16[64,512]{1,0:T(8,128)(2,1)S(1)} %fusion.14, s32[]{:T(128)S(6)} %select_n.31), kind=kOutput, calls=%fused_computation.39 | convolution fusion | flops 41943040 | bytes 1015812 | tf_op jit(solution)/shard_map/dot_general | solution.py:23
  88.0 2.5 %collective-permute-done.32 = bf16[64,512]{1,0:T(8,128)(2,1)S(1)} collective-permute-done((bf16[64,512]{1,0:T(8,128)(2,1)S(1)}, bf16[64,512]{1,0:T(8,128)(2,1)S(1)}, u32[]{:S(2)}, u32[]{:S(2)}) %collective-permute-start.32) | collective-permute-done | bytes 65568 | tf_op jit(solution)/shard_map/ppermute | solution.py:199
  93.2 1.6 %collective-permute-start.37 = (bf16[192,512]{1,0:T(8,128)(2,1)S(1)}, bf16[192,512]{1,0:T(8,128)(2,1)S(1)}, u32[]{:S(2)}, u32[]{:S(2)}) collective-permute-start(bf16[192,512]{1,0:T(8,128)(2,1)S(1)} %pad_maximum_fusion), channel_id=1, source_target_pairs={{0,24},{8,16},{16,8},{24,0},{1,25},{9,17},{17,9},{25,1},{2,26},{10... | collective-permute-start | bytes 589832 | tf_op jit(solution)/shard_map/ppermute | solution.py:199
  95.7 1.7 %collective-permute-start.42 = (bf16[64,512]{1,0:T(8,128)(2,1)S(1)}, bf16[64,512]{1,0:T(8,128)(2,1)S(1)}, u32[]{:S(2)}, u32[]{:S(2)}) collective-permute-start(bf16[64,512]{1,0:T(8,128)(2,1)S(1)} %get-tuple-element.154), channel_id=1, source_target_pairs={{0,6},{1,7},{2,4},{3,5},{4,2},{5,3},{6,0},{7,1},{8,14},{9,15},{10,... | collective-permute-start | bytes 196616 | tf_op jit(solution)/shard_map/ppermute | solution.py:199
  97.5 1.5 %fusion.5 = bf16[1,64,5120]{2,1,0:T(8,128)(2,1)S(1)} fusion(bf16[1,64,5120]{2,1,0:T(8,128)(2,1)S(1)} %fusion.13, s32[]{:T(128)S(6)} %select_n.32, f32[64,1280]{1,0:T(8,128)S(1)} %fusion.23, bf16[1280,256]{1,0:T(8,128)(2,1)} %collective-permute-done.23, bf16[64,512]{1,0:T(8,128)(2,1)S(1)} %fusion.14, s32[]{:T(128)S(6)} %select_n.29), kind=kOutput, calls=%fused_computation.8 | convolution fusion | flops 42106880 | bytes 1179656 | tf_op jit(solution)/shard_map/dot_general | solution.py:23
  99.0 1.5 %fusion.3 = bf16[1,64,5120]{2,1,0:T(8,128)(2,1)S(1)} fusion(bf16[1,64,5120]{2,1,0:T(8,128)(2,1)S(1)} %fusion.5, s32[]{:T(128)S(6)} %select_n.33, f32[64,1280]{1,0:T(8,128)S(1)} %fusion.21, bf16[1280,256]{1,0:T(8,128)(2,1)} %collective-permute-done.24, bf16[64,512]{1,0:T(8,128)(2,1)S(1)} %fusion.14, s32[]{:T(128)S(6)} %select_n.29), kind=kOutput, calls=%fused_computation.6 | convolution fusion | flops 42106880 | bytes 1179656 | tf_op jit(solution)/shard_map/dot_general | solution.py:23
  100.7 2.4 %collective-permute-done.37 = bf16[192,512]{1,0:T(8,128)(2,1)S(1)} collective-permute-done((bf16[192,512]{1,0:T(8,128)(2,1)S(1)}, bf16[192,512]{1,0:T(8,128)(2,1)S(1)}, u32[]{:S(2)}, u32[]{:S(2)}) %collective-permute-start.37) | collective-permute-done | bytes 196640 | tf_op jit(solution)/shard_map/ppermute | solution.py:199
  103.1 1.6 %collective-permute-start.38 = (bf16[64,1280]{1,0:T(8,128)(2,1)S(1)}, bf16[64,1280]{1,0:T(8,128)(2,1)S(1)}, u32[]{:S(2)}, u32[]{:S(2)}) collective-permute-start(bf16[64,1280]{1,0:T(8,128)(2,1)S(1)} %slice.52), channel_id=1, source_target_pairs={{0,24},{8,16},{16,8},{24,0},{1,25},{9,17},{17,9},{25,1},{2,26},{10... | collective-permute-start | bytes 491528 | tf_op jit(solution)/shard_map/ppermute | solution.py:199
  107.3 2.0 %collective-permute-done.38 = bf16[64,1280]{1,0:T(8,128)(2,1)S(1)} collective-permute-done((bf16[64,1280]{1,0:T(8,128)(2,1)S(1)}, bf16[64,1280]{1,0:T(8,128)(2,1)S(1)}, u32[]{:S(2)}, u32[]{:S(2)}) %collective-permute-start.38) | collective-permute-done | bytes 163872 | tf_op jit(solution)/shard_map/ppermute | solution.py:199
  (191 shorter events, 22.1 us)
Async XLA Ops:
  2.7 15.9 %collective-permute-start = (bf16[64,1280]{1,0:T(8,128)(2,1)}, bf16[64,1280]{1,0:T(8,128)(2,1)S(1)}, u32[]{:S(2)}, u32[]{:S(2)}) collective-permute-start(bf16[64,1280]{1,0:T(8,128)(2,1)} %get-tuple-element.80), channel_id=1, source_target_pairs={{0,8},{8,0},{16,24},{24,16},{1,9},{9,1},{17,25},{25,17},{2,10},{10... | collective-permute-start | bytes 491528 | tf_op jit(solution)/shard_map/ppermute | solution.py:199
  5.6 11.1 %collective-permute-start.1 = (bf16[64,1280]{1,0:T(8,128)(2,1)}, bf16[64,1280]{1,0:T(8,128)(2,1)S(1)}, u32[]{:S(2)}, u32[]{:S(2)}) collective-permute-start(bf16[64,1280]{1,0:T(8,128)(2,1)} %get-tuple-element.81), channel_id=1, source_target_pairs={{0,16},{8,24},{16,0},{24,8},{1,17},{9,25},{17,1},{25,9},{2,18},{10... | collective-permute-start | bytes 491528 | tf_op jit(solution)/shard_map/ppermute | solution.py:199
  7.2 7.7 %collective-permute-start.2 = (bf16[64,1280]{1,0:T(8,128)(2,1)}, bf16[64,1280]{1,0:T(8,128)(2,1)S(1)}, u32[]{:S(2)}, u32[]{:S(2)}) collective-permute-start(bf16[64,1280]{1,0:T(8,128)(2,1)} %get-tuple-element.82), channel_id=1, source_target_pairs={{0,24},{8,16},{16,8},{24,0},{1,25},{9,17},{17,9},{25,1},{2,26},{10... | collective-permute-start | bytes 491528 | tf_op jit(solution)/shard_map/ppermute | solution.py:199
  15.2 8.6 %collective-permute-start.5 = (f32[64,512]{1,0:T(8,128)S(1)}, f32[64,512]{1,0:T(8,128)S(1)}, u32[]{:S(2)}, u32[]{:S(2)}) collective-permute-start(f32[64,512]{1,0:T(8,128)S(1)} %fusion.39), channel_id=1, source_target_pairs={{0,24},{8,16},{16,8},{24,0},{1,25},{9,17},{17,9},{25,1},{2,26},{10... | collective-permute-start | bytes 393224 | tf_op jit(solution)/shard_map/ppermute | solution.py:199
  17.1 8.9 %collective-permute-start.4 = (f32[64,512]{1,0:T(8,128)S(1)}, f32[64,512]{1,0:T(8,128)S(1)}, u32[]{:S(2)}, u32[]{:S(2)}) collective-permute-start(f32[64,512]{1,0:T(8,128)S(1)} %fusion.38), channel_id=1, source_target_pairs={{0,16},{8,24},{16,0},{24,8},{1,17},{9,25},{17,1},{25,9},{2,18},{10... | collective-permute-start | bytes 393224 | tf_op jit(solution)/shard_map/ppermute | solution.py:199
  18.9 7.0 %collective-permute-start.3 = (f32[64,512]{1,0:T(8,128)S(1)}, f32[64,512]{1,0:T(8,128)S(1)}, u32[]{:S(2)}, u32[]{:S(2)}) collective-permute-start(f32[64,512]{1,0:T(8,128)S(1)} %fusion.37), channel_id=1, source_target_pairs={{0,8},{8,0},{16,24},{24,16},{1,9},{9,1},{17,25},{25,17},{2,10},{10... | collective-permute-start | bytes 393224 | tf_op jit(solution)/shard_map/ppermute | solution.py:199
  19.7 9.3 %collective-permute-start.13 = (bf16[64,512]{1,0:T(8,128)(2,1)S(1)}, bf16[64,512]{1,0:T(8,128)(2,1)S(1)}, u32[]{:S(2)}, u32[]{:S(2)}) collective-permute-start(bf16[64,512]{1,0:T(8,128)(2,1)S(1)} %bitcast.84), channel_id=1, source_target_pairs={{0,2},{1,3},{2,0},{3,1},{4,6},{5,7},{6,4},{7,5},{8,10},{9,11},{10,... | collective-permute-start | bytes 196616 | tf_op jit(solution)/shard_map/ppermute | solution.py:199
  21.2 9.8 %collective-permute-start.14 = (bf16[64,512]{1,0:T(8,128)(2,1)S(1)}, bf16[64,512]{1,0:T(8,128)(2,1)S(1)}, u32[]{:S(2)}, u32[]{:S(2)}) collective-permute-start(bf16[64,512]{1,0:T(8,128)(2,1)S(1)} %bitcast.85), channel_id=1, source_target_pairs={{0,4},{1,5},{2,6},{3,7},{4,0},{5,1},{6,2},{7,3},{8,12},{9,13},{10,... | collective-permute-start | bytes 196616 | tf_op jit(solution)/shard_map/ppermute | solution.py:199
  23.8 7.3 %collective-permute-start.15 = (bf16[64,512]{1,0:T(8,128)(2,1)S(1)}, bf16[64,512]{1,0:T(8,128)(2,1)S(1)}, u32[]{:S(2)}, u32[]{:S(2)}) collective-permute-start(bf16[64,512]{1,0:T(8,128)(2,1)S(1)} %bitcast.86), channel_id=1, source_target_pairs={{0,6},{1,7},{2,4},{3,5},{4,2},{5,3},{6,0},{7,1},{8,14},{9,15},{10,... | collective-permute-start | bytes 196616 | tf_op jit(solution)/shard_map/ppermute | solution.py:199
  26.7 7.3 %collective-permute-start.7 = (bf16[64,512]{1,0:T(8,128)(2,1)S(1)}, bf16[64,512]{1,0:T(8,128)(2,1)S(1)}, u32[]{:S(2)}, u32[]{:S(2)}) collective-permute-start(bf16[64,512]{1,0:T(8,128)(2,1)S(1)} %fusion.16.refs_0_), channel_id=1, source_target_pairs={{0,4},{1,5},{2,6},{3,7},{4,0},{5,1},{6,2},{7,3},{8,12},{9,13},{10,... | collective-permute-start | bytes 196616 | tf_op jit(solution)/shard_map/ppermute | solution.py:199
  28.9 6.1 %collective-permute-start.8 = (bf16[64,512]{1,0:T(8,128)(2,1)S(1)}, bf16[64,512]{1,0:T(8,128)(2,1)S(1)}, u32[]{:S(2)}, u32[]{:S(2)}) collective-permute-start(bf16[64,512]{1,0:T(8,128)(2,1)S(1)} %fusion.16.refs_0_), channel_id=1, source_target_pairs={{0,6},{1,7},{2,4},{3,5},{4,2},{5,3},{6,0},{7,1},{8,14},{9,15},{10,... | collective-permute-start | bytes 196616 | tf_op jit(solution)/shard_map/ppermute | solution.py:199
  36.7 28.3 %collective-permute-start.23 = (bf16[1280,256]{1,0:T(8,128)(2,1)S(1)}, bf16[1280,256]{1,0:T(8,128)(2,1)}, u32[]{:S(2)}, u32[]{:S(2)}) collective-permute-start(bf16[1280,256]{1,0:T(8,128)(2,1)S(1)} %constant_dynamic-slice_fusion), channel_id=1, source_target_pairs={{0,8},{8,0},{16,24},{24,16},{1,9},{9,1},{17,25},{25,17},{2,10},{10... | collective-permute-start | bytes 1966088 | tf_op jit(solution)/shard_map/ppermute | solution.py:199
  38.1 26.9 %collective-permute-start.24 = (bf16[1280,256]{1,0:T(8,128)(2,1)S(1)}, bf16[1280,256]{1,0:T(8,128)(2,1)}, u32[]{:S(2)}, u32[]{:S(2)}) collective-permute-start(bf16[1280,256]{1,0:T(8,128)(2,1)S(1)} %constant_dynamic-slice_fusion), channel_id=1, source_target_pairs={{0,16},{8,24},{16,0},{24,8},{1,17},{9,25},{17,1},{25,9},{2,18},{10... | collective-permute-start | bytes 1966088 | tf_op jit(solution)/shard_map/ppermute | solution.py:199
  38.8 26.2 %collective-permute-start.20 = (bf16[320,256]{1,0:T(8,128)(2,1)}, bf16[320,256]{1,0:T(8,128)(2,1)S(1)}, u32[]{:S(2)}, u32[]{:S(2)}) collective-permute-start(bf16[320,256]{1,0:T(8,128)(2,1)} %get-tuple-element.97), channel_id=1, source_target_pairs={{0,2},{1,3},{2,0},{3,1},{4,6},{5,7},{6,4},{7,5},{8,10},{9,11},{10,... | collective-permute-start | bytes 491528 | tf_op jit(solution)/shard_map/ppermute | solution.py:199
  38.8 26.2 %collective-permute-start.21 = (bf16[320,256]{1,0:T(8,128)(2,1)}, bf16[320,256]{1,0:T(8,128)(2,1)S(1)}, u32[]{:S(2)}, u32[]{:S(2)}) collective-permute-start(bf16[320,256]{1,0:T(8,128)(2,1)} %get-tuple-element.98), channel_id=1, source_target_pairs={{0,4},{1,5},{2,6},{3,7},{4,0},{5,1},{6,2},{7,3},{8,12},{9,13},{10,... | collective-permute-start | bytes 491528 | tf_op jit(solution)/shard_map/ppermute | solution.py:199
  41.4 23.6 %collective-permute-start.22 = (bf16[320,256]{1,0:T(8,128)(2,1)}, bf16[320,256]{1,0:T(8,128)(2,1)S(1)}, u32[]{:S(2)}, u32[]{:S(2)}) collective-permute-start(bf16[320,256]{1,0:T(8,128)(2,1)} %get-tuple-element.99), channel_id=1, source_target_pairs={{0,6},{1,7},{2,4},{3,5},{4,2},{5,3},{6,0},{7,1},{8,14},{9,15},{10,... | collective-permute-start | bytes 491528 | tf_op jit(solution)/shard_map/ppermute | solution.py:199
  65.1 6.0 %collective-permute-start.29 = (f32[256,512]{1,0:T(8,128)}, f32[256,512]{1,0:T(8,128)}, u32[]{:S(2)}, u32[]{:S(2)}) collective-permute-start(f32[256,512]{1,0:T(8,128)} %get-tuple-element.104), channel_id=1, source_target_pairs={{0,1},{1,0},{2,3},{3,2},{4,5},{5,4},{6,7},{7,6},{8,9},{9,8},{10,11... | collective-permute-start | bytes 1572872 | tf_op jit(solution)/shard_map/ppermute | solution.py:199
  65.6 13.9 %collective-permute-start.30 = (bf16[1280,256]{1,0:T(8,128)(2,1)}, bf16[1280,256]{1,0:T(8,128)(2,1)S(1)}, u32[]{:S(2)}, u32[]{:S(2)}) collective-permute-start(bf16[1280,256]{1,0:T(8,128)(2,1)} %collective-permute-done.23), channel_id=1, source_target_pairs={{0,1},{1,0},{2,3},{3,2},{4,5},{5,4},{6,7},{7,6},{8,9},{9,8},{10,11... | collective-permute-start | bytes 1966088 | tf_op jit(solution)/shard_map/ppermute | solution.py:199
  65.7 13.9 %collective-permute-start.31 = (bf16[1280,256]{1,0:T(8,128)(2,1)}, bf16[1280,256]{1,0:T(8,128)(2,1)}, u32[]{:S(2)}, u32[]{:S(2)}) collective-permute-start(bf16[1280,256]{1,0:T(8,128)(2,1)} %collective-permute-done.24), channel_id=1, source_target_pairs={{0,1},{1,0},{2,3},{3,2},{4,5},{5,4},{6,7},{7,6},{8,9},{9,8},{10,11... | collective-permute-start | bytes 1966088 | tf_op jit(solution)/shard_map/ppermute | solution.py:199
  69.0 7.8 %collective-permute-start.28 = (bf16[64,512]{1,0:T(8,128)(2,1)}, bf16[64,512]{1,0:T(8,128)(2,1)S(1)}, u32[]{:S(2)}, u32[]{:S(2)}) collective-permute-start(bf16[64,512]{1,0:T(8,128)(2,1)} %get-tuple-element.157), channel_id=1, source_target_pairs={{0,6},{1,7},{2,4},{3,5},{4,2},{5,3},{6,0},{7,1},{8,14},{9,15},{10,... | collective-permute-start | bytes 196616 | tf_op jit(solution)/shard_map/ppermute | solution.py:199
  71.1 6.9 %collective-permute-start.27 = (bf16[64,512]{1,0:T(8,128)(2,1)}, bf16[64,512]{1,0:T(8,128)(2,1)S(1)}, u32[]{:S(2)}, u32[]{:S(2)}) collective-permute-start(bf16[64,512]{1,0:T(8,128)(2,1)} %get-tuple-element.158), channel_id=1, source_target_pairs={{0,4},{1,5},{2,6},{3,7},{4,0},{5,1},{6,2},{7,3},{8,12},{9,13},{10,... | collective-permute-start | bytes 196616 | tf_op jit(solution)/shard_map/ppermute | solution.py:199
  71.1 6.9 %collective-permute-start.26 = (bf16[64,512]{1,0:T(8,128)(2,1)}, bf16[64,512]{1,0:T(8,128)(2,1)}, u32[]{:S(2)}, u32[]{:S(2)}) collective-permute-start(bf16[64,512]{1,0:T(8,128)(2,1)} %get-tuple-element.156), channel_id=1, source_target_pairs={{0,2},{1,3},{2,0},{3,1},{4,6},{5,7},{6,4},{7,5},{8,10},{9,11},{10,... | collective-permute-start | bytes 196616 | tf_op jit(solution)/shard_map/ppermute | solution.py:199
  80.1 10.3 %collective-permute-start.33 = (bf16[64,512]{1,0:T(8,128)(2,1)S(1)}, bf16[64,512]{1,0:T(8,128)(2,1)S(1)}, u32[]{:S(2)}, u32[]{:S(2)}) collective-permute-start(bf16[64,512]{1,0:T(8,128)(2,1)S(1)} %fusion.14), channel_id=1, source_target_pairs={{0,2},{1,3},{2,0},{3,1},{4,6},{5,7},{6,4},{7,5},{8,10},{9,11},{10,... | collective-permute-start | bytes 196616 | tf_op jit(solution)/shard_map/ppermute | solution.py:199
  80.2 10.2 %collective-permute-start.34 = (bf16[64,512]{1,0:T(8,128)(2,1)S(1)}, bf16[64,512]{1,0:T(8,128)(2,1)S(1)}, u32[]{:S(2)}, u32[]{:S(2)}) collective-permute-start(bf16[64,512]{1,0:T(8,128)(2,1)S(1)} %fusion.14), channel_id=1, source_target_pairs={{0,4},{1,5},{2,6},{3,7},{4,0},{5,1},{6,2},{7,3},{8,12},{9,13},{10,... | collective-permute-start | bytes 196616 | tf_op jit(solution)/shard_map/ppermute | solution.py:199
  82.8 7.6 %collective-permute-start.35 = (bf16[64,512]{1,0:T(8,128)(2,1)S(1)}, bf16[64,512]{1,0:T(8,128)(2,1)S(1)}, u32[]{:S(2)}, u32[]{:S(2)}) collective-permute-start(bf16[64,512]{1,0:T(8,128)(2,1)S(1)} %fusion.14), channel_id=1, source_target_pairs={{0,6},{1,7},{2,4},{3,5},{4,2},{5,3},{6,0},{7,1},{8,14},{9,15},{10,... | collective-permute-start | bytes 196616 | tf_op jit(solution)/shard_map/ppermute | solution.py:199
  84.6 5.9 %collective-permute-start.36 = (bf16[64,512]{1,0:T(8,128)(2,1)S(1)}, bf16[64,512]{1,0:T(8,128)(2,1)S(1)}, u32[]{:S(2)}, u32[]{:S(2)}) collective-permute-start(bf16[64,512]{1,0:T(8,128)(2,1)S(1)} %fusion.14), channel_id=1, source_target_pairs={{0,24},{8,16},{16,8},{24,0},{1,25},{9,17},{17,9},{25,1},{2,26},{10... | collective-permute-start | bytes 196616 | tf_op jit(solution)/shard_map/ppermute | solution.py:199
  90.5 14.5 %collective-permute-start.40 = (bf16[256,512]{1,0:T(8,128)(2,1)S(1)}, bf16[256,512]{1,0:T(8,128)(2,1)S(1)}, u32[]{:S(2)}, u32[]{:S(2)}) collective-permute-start(bf16[256,512]{1,0:T(8,128)(2,1)S(1)} %constant_dynamic-update-slice_fusion), channel_id=1, source_target_pairs={{0,16},{8,24},{16,0},{24,8},{1,17},{9,25},{17,1},{25,9},{2,18},{10... | collective-permute-start | bytes 786440 | tf_op jit(solution)/shard_map/ppermute | solution.py:199
  91.4 13.9 %collective-permute-start.39 = (bf16[256,512]{1,0:T(8,128)(2,1)S(1)}, bf16[256,512]{1,0:T(8,128)(2,1)S(1)}, u32[]{:S(2)}, u32[]{:S(2)}) collective-permute-start(bf16[256,512]{1,0:T(8,128)(2,1)S(1)} %constant_dynamic-update-slice_fusion), channel_id=1, source_target_pairs={{0,8},{8,0},{16,24},{24,16},{1,9},{9,1},{17,25},{25,17},{2,10},{10... | collective-permute-start | bytes 786440 | tf_op jit(solution)/shard_map/ppermute | solution.py:199
  93.2 9.9 %collective-permute-start.37 = (bf16[192,512]{1,0:T(8,128)(2,1)S(1)}, bf16[192,512]{1,0:T(8,128)(2,1)S(1)}, u32[]{:S(2)}, u32[]{:S(2)}) collective-permute-start(bf16[192,512]{1,0:T(8,128)(2,1)S(1)} %pad_maximum_fusion), channel_id=1, source_target_pairs={{0,24},{8,16},{16,8},{24,0},{1,25},{9,17},{17,9},{25,1},{2,26},{10... | collective-permute-start | bytes 589832 | tf_op jit(solution)/shard_map/ppermute | solution.py:199
  95.0 10.8 %collective-permute-start.41 = (bf16[64,512]{1,0:T(8,128)(2,1)S(1)}, bf16[64,512]{1,0:T(8,128)(2,1)S(1)}, u32[]{:S(2)}, u32[]{:S(2)}) collective-permute-start(bf16[64,512]{1,0:T(8,128)(2,1)S(1)} %get-tuple-element.155), channel_id=1, source_target_pairs={{0,4},{1,5},{2,6},{3,7},{4,0},{5,1},{6,2},{7,3},{8,12},{9,13},{10,... | collective-permute-start | bytes 196616 | tf_op jit(solution)/shard_map/ppermute | solution.py:199
  95.7 10.0 %collective-permute-start.42 = (bf16[64,512]{1,0:T(8,128)(2,1)S(1)}, bf16[64,512]{1,0:T(8,128)(2,1)S(1)}, u32[]{:S(2)}, u32[]{:S(2)}) collective-permute-start(bf16[64,512]{1,0:T(8,128)(2,1)S(1)} %get-tuple-element.154), channel_id=1, source_target_pairs={{0,6},{1,7},{2,4},{3,5},{4,2},{5,3},{6,0},{7,1},{8,14},{9,15},{10,... | collective-permute-start | bytes 196616 | tf_op jit(solution)/shard_map/ppermute | solution.py:199
  103.1 6.2 %collective-permute-start.38 = (bf16[64,1280]{1,0:T(8,128)(2,1)S(1)}, bf16[64,1280]{1,0:T(8,128)(2,1)S(1)}, u32[]{:S(2)}, u32[]{:S(2)}) collective-permute-start(bf16[64,1280]{1,0:T(8,128)(2,1)S(1)} %slice.52), channel_id=1, source_target_pairs={{0,24},{8,16},{16,8},{24,0},{1,25},{9,17},{17,9},{25,1},{2,26},{10... | collective-permute-start | bytes 491528 | tf_op jit(solution)/shard_map/ppermute | solution.py:199
  (51 other events, 280.5 us)

commit v14 on v12

--- a/solution.py
+++ b/solution.py
@@ -9,7 +9,8 @@
 
 F32, BF16 = jnp.float32, jnp.bfloat16
 LOG2E = 1.4426950408889634
-PARAMS = pltpu.CompilerParams(vmem_limit_bytes=56 * 2**20)
+SMALL = pltpu.CompilerParams(vmem_limit_bytes=16 * 2**20)
+LARGE = pltpu.CompilerParams(vmem_limit_bytes=40 * 2**20)
 
 
 def norm_keys(key_pre, key_gain):
@@ -97,7 +98,7 @@
         ],
         out_specs=[query_block, own_block, own_block] + [block(prompt_len // 2, head_dim)] * 4,
         out_shape=[jax.ShapeDtypeStruct((rows, width), BF16), own, own] + [half] * 4,
-        compiler_params=PARAMS,
+        compiler_params=LARGE,
         cost_estimate=cost(10 * rows * width * (prompt_len + rows), 10**7),
         name="attend",
     )(length, queries, upstream, keys, values, *key_pieces, *value_pieces)
@@ -111,7 +112,7 @@
         out_specs=[whole] * len(outs),
         out_shape=[jax.ShapeDtypeStruct(shape, dtype) for shape, dtype in outs],
         scratch_shapes=scratch,
-        compiler_params=PARAMS,
+        compiler_params=SMALL,
         cost_estimate=cost(macs, 3 * 10**6),
         name=name,
     )(*arrays)

time: 109 us -> 117 us (1.073)
  local copies, waits for them, and re-layouts: 2.89 us -> 13.6 us
  Pallas kernels: 32.4 us -> 23.6 us
  other arithmetic: 2.36 us -> 7.63 us
  waiting for transfers between devices: 16 us -> 17.6 us
    pallas_call x4, Pallas kernels: 10.8 us -> 2.72 us  [in_vmem(): pl.pallas_call(kernel, in_specs=[whole] * len(arrays), out_specs=[whole]...]
    unnamed x87 -> x61, local copies, waits for them, and re-layouts: 1.41 us -> 7.36 us
    ppermute x44, waiting for transfers between devices: 16 us -> 17.6 us  [swap(): return lax.ppermute(array, axis, [(i, i ^ distance) for i in range(size)])]
    reshape x1, local copies, waits for them, and re-layouts: 0.05 us -> 1.6 us  [norm_keys(): return (shaped * inverse * key_gain).reshape(key_pre.shape)]
    slice x5, local copies, waits for them, and re-layouts: 0.04 us -> 1.58 us  [chip_parts(): pieces = [near[p * rows:(p + 1) * rows] for p in range(size // 2)]]
  transfers between devices with their start and end apart: 44 -> 44, of which waited for: 10 -> 12; matrix products, arithmetic and copies ran while one was open for 8% -> 9% of each run, Pallas kernels for 28% -> 20%
where the time goes in v14:
time: 117 us; the launch traced here: 116 us
  starting transfers between devices  46.5 us (40%)
  Pallas kernels  23.6 us (20%)
  waiting for transfers between devices  17.6 us (15%)
  local copies, waits for them, and re-layouts  13.6 us (12%)
  other arithmetic  7.63 us (7%)
  matrix products  5.31 us (5%)
  between operations  1.86 us (2%)
    ppermute x44, starting transfers between devices, swap(): return lax.ppermute(array, axis, [(i, i ^ distance) for i in range(size)])  46.5 us
    pallas_call x1, Pallas kernels, attend(): pl.pallas_call(partial(attend_kernel, len(key_pieces)), grid=(kv_heads,),...  20.9 us
    ppermute x44, waiting for transfers between devices, swap(): return lax.ppermute(array, axis, [(i, i ^ distance) for i in range(size)])  17.6 us
    unnamed x61, local copies, waits for them, and re-layouts  7.36 us
    dot_general x14, matrix products, dot(): return lax.dot_general(left, right, dims, preferred_element_type=F32)  5.31 us
    pallas_call x4, Pallas kernels, in_vmem(): pl.pallas_call(kernel, in_specs=[whole] * len(arrays), out_specs=[whole]...  2.72 us
  transfers between devices with their start and end apart: 44, of which 12 were waited for; matrix products, arithmetic and copies ran while one was open for 9% of the time, Pallas kernels for 20%

profile of v14, /device:TPU:0, one launch (start us, length us, event | category | flops | bytes accessed | tf_op | source)
XLA Modules:
  0.0 116.1 jit_solution(9698295212176894861)
XLA Ops:
  1.9 4.0 %collective-permute-start.2 = (bf16[64,1280]{1,0:T(8,128)(2,1)S(1)}, bf16[64,1280]{1,0:T(8,128)(2,1)S(1)}, u32[]{:S(2)}, u32[]{:S(2)}) collective-permute-start(bf16[64,1280]{1,0:T(8,128)(2,1)S(1)} %get-tuple-element.84), channel_id=1, source_target_pairs={{0,24},{8,16},{16,8},{24,0},{1,25},{9,17},{17,9},{25,1},{2,26},{10... | collective-permute-start | bytes 491528 | tf_op jit(solution)/shard_map/ppermute | solution.py:233
  6.5 1.6 %fusion.15 = f32[64,512]{1,0:T(8,128)S(1)} fusion(bf16[64,1280]{1,0:T(8,128)(2,1)S(1)} %get-tuple-element.81.refs_0_, bf16[1280,512]{1,0:T(8,128)(2,1)} %own_ref.1), kind=kOutput, calls=%fused_computation.37 | convolution fusion | flops 83886080 | bytes 1605632 | tf_op jit(solution)/shard_map/dot_general | solution.py:24
  9.0 1.8 %collective-permute-done.2.refs_3_ = bf16[64,1280]{1,0:T(8,128)(2,1)S(1)} collective-permute-done((bf16[64,1280]{1,0:T(8,128)(2,1)S(1)}, bf16[64,1280]{1,0:T(8,128)(2,1)S(1)}, u32[]{:S(2)}, u32[]{:S(2)}) %collective-permute-start.2) | collective-permute-done | bytes 163872 | tf_op jit(solution)/shard_map/ppermute | solution.py:233
  11.2 3.0 %collective-permute-start.5 = (f32[64,512]{1,0:T(8,128)S(1)}, f32[64,512]{1,0:T(8,128)S(1)}, u32[]{:S(2)}, u32[]{:S(2)}) collective-permute-start(f32[64,512]{1,0:T(8,128)S(1)} %fusion.18), channel_id=1, source_target_pairs={{0,24},{8,16},{16,8},{24,0},{1,25},{9,17},{17,9},{25,1},{2,26},{10... | collective-permute-start | bytes 393224 | tf_op jit(solution)/shard_map/ppermute | solution.py:233
  14.6 1.6 %collective-permute-start.4 = (f32[64,512]{1,0:T(8,128)S(1)}, f32[64,512]{1,0:T(8,128)S(1)}, u32[]{:S(2)}, u32[]{:S(2)}) collective-permute-start(f32[64,512]{1,0:T(8,128)S(1)} %fusion.17), channel_id=1, source_target_pairs={{0,16},{8,24},{16,0},{24,8},{1,17},{9,25},{17,1},{25,9},{2,18},{10... | collective-permute-start | bytes 393224 | tf_op jit(solution)/shard_map/ppermute | solution.py:233
  16.8 1.7 %collective-permute-start.13 = (bf16[64,512]{1,0:T(8,128)(2,1)S(1)}, bf16[64,512]{1,0:T(8,128)(2,1)S(1)}, u32[]{:S(2)}, u32[]{:S(2)}) collective-permute-start(bf16[64,512]{1,0:T(8,128)(2,1)S(1)} %bitcast.64), channel_id=1, source_target_pairs={{0,2},{1,3},{2,0},{3,1},{4,6},{5,7},{6,4},{7,5},{8,10},{9,11},{10,... | collective-permute-start | bytes 196616 | tf_op jit(solution)/shard_map/ppermute | solution.py:233
  18.5 2.6 %collective-permute-start.14 = (bf16[64,512]{1,0:T(8,128)(2,1)S(1)}, bf16[64,512]{1,0:T(8,128)(2,1)S(1)}, u32[]{:S(2)}, u32[]{:S(2)}) collective-permute-start(bf16[64,512]{1,0:T(8,128)(2,1)S(1)} %bitcast.65), channel_id=1, source_target_pairs={{0,4},{1,5},{2,6},{3,7},{4,0},{5,1},{6,2},{7,3},{8,12},{9,13},{10,... | collective-permute-start | bytes 196616 | tf_op jit(solution)/shard_map/ppermute | solution.py:233
  22.3 1.6 %collective-permute-start.6 = (bf16[64,512]{1,0:T(8,128)(2,1)S(1)}, bf16[64,512]{1,0:T(8,128)(2,1)S(1)}, u32[]{:S(2)}, u32[]{:S(2)}) collective-permute-start(bf16[64,512]{1,0:T(8,128)(2,1)S(1)} %fusion.9.refs_0_), channel_id=1, source_target_pairs={{0,2},{1,3},{2,0},{3,1},{4,6},{5,7},{6,4},{7,5},{8,10},{9,11},{10,... | collective-permute-start | bytes 196616 | tf_op jit(solution)/shard_map/ppermute | solution.py:233
  23.9 2.6 %collective-permute-start.7 = (bf16[64,512]{1,0:T(8,128)(2,1)S(1)}, bf16[64,512]{1,0:T(8,128)(2,1)S(1)}, u32[]{:S(2)}, u32[]{:S(2)}) collective-permute-start(bf16[64,512]{1,0:T(8,128)(2,1)S(1)} %fusion.9.refs_0_), channel_id=1, source_target_pairs={{0,4},{1,5},{2,6},{3,7},{4,0},{5,1},{6,2},{7,3},{8,12},{9,13},{10,... | collective-permute-start | bytes 196616 | tf_op jit(solution)/shard_map/ppermute | solution.py:233
  28.7 2.3 %collective-permute-done.7.refs_2_ = bf16[64,512]{1,0:T(8,128)(2,1)S(1)} collective-permute-done((bf16[64,512]{1,0:T(8,128)(2,1)S(1)}, bf16[64,512]{1,0:T(8,128)(2,1)S(1)}, u32[]{:S(2)}, u32[]{:S(2)}) %collective-permute-start.7) | collective-permute-done | bytes 65568 | tf_op jit(solution)/shard_map/ppermute | solution.py:233
  31.0 1.6 %collective-permute-done.8.refs_3_ = bf16[64,512]{1,0:T(8,128)(2,1)S(1)} collective-permute-done((bf16[64,512]{1,0:T(8,128)(2,1)S(1)}, bf16[64,512]{1,0:T(8,128)(2,1)S(1)}, u32[]{:S(2)}, u32[]{:S(2)}) %collective-permute-start.8) | collective-permute-done | bytes 65568 | tf_op jit(solution)/shard_map/ppermute | solution.py:233
  34.3 1.5 %collective-permute-start.23 = (bf16[1280,256]{1,0:T(8,128)(2,1)}, bf16[1280,256]{1,0:T(8,128)(2,1)S(1)}, u32[]{:S(2)}, u32[]{:S(2)}) collective-permute-start(bf16[1280,256]{1,0:T(8,128)(2,1)} %constant_dynamic-slice_fusion), channel_id=1, source_target_pairs={{0,8},{8,0},{16,24},{24,16},{1,9},{9,1},{17,25},{25,17},{2,10},{10... | collective-permute-start | bytes 1966088 | tf_op jit(solution)/shard_map/ppermute | solution.py:233
  36.5 2.2 %collective-permute-start.21 = (bf16[320,256]{1,0:T(8,128)(2,1)S(1)}, bf16[320,256]{1,0:T(8,128)(2,1)S(1)}, u32[]{:S(2)}, u32[]{:S(2)}) collective-permute-start(bf16[320,256]{1,0:T(8,128)(2,1)S(1)} %get-tuple-element.100), channel_id=1, source_target_pairs={{0,4},{1,5},{2,6},{3,7},{4,0},{5,1},{6,2},{7,3},{8,12},{9,13},{10,... | collective-permute-start | bytes 491528 | tf_op jit(solution)/shard_map/ppermute | solution.py:233
  38.8 2.1 %collective-permute-start.22 = (bf16[320,256]{1,0:T(8,128)(2,1)S(1)}, bf16[320,256]{1,0:T(8,128)(2,1)S(1)}, u32[]{:S(2)}, u32[]{:S(2)}) collective-permute-start(bf16[320,256]{1,0:T(8,128)(2,1)S(1)} %get-tuple-element.101), channel_id=1, source_target_pairs={{0,6},{1,7},{2,4},{3,5},{4,2},{5,3},{6,0},{7,1},{8,14},{9,15},{10,... | collective-permute-start | bytes 491528 | tf_op jit(solution)/shard_map/ppermute | solution.py:233
  40.9 1.6 %copy-done.20 = bf16[1,1,256,4096]{3,2,1,0:T(8,128)(2,1)S(1)} copy-done((bf16[1,1,256,4096]{3,2,1,0:T(8,128)(2,1)S(1)}, bf16[1,1,256,4096]{3,2,1,0:T(8,128)(2,1)}, u32[]{:S(2)}) %copy-start.20) | copy-done | bytes 2097176
  42.5 1.6 %copy-done.21 = bf16[1,1,256,4096]{3,2,1,0:T(8,128)(2,1)S(1)} copy-done((bf16[1,1,256,4096]{3,2,1,0:T(8,128)(2,1)S(1)}, bf16[1,1,256,4096]{3,2,1,0:T(8,128)(2,1)}, u32[]{:S(2)}) %copy-start.21) | copy-done | bytes 2097176
  44.1 20.9 %attend.1 = (bf16[256,4096]{1,0:T(8,128)(2,1)}, bf16[256,512]{1,0:T(8,128)(2,1)}, bf16[256,512]{1,0:T(8,128)(2,1)}, f32[256,512]{1,0:T(8,128)S(1)}, f32[256,512]...) custom-call(s32[1,1]{1,0:T(1,128)S(6)} %copy.30.length_ref, bf16[256,4096]{1,0:T(8,128)(2,1)S(1)} %bitcast.60, ...), custom_call_target="tpu_custom_call" | custom-call | flops 16106127360 | bytes 10000000 | tf_op jit(solution)/shard_map/attend/pallas_call | solution.py:92
  67.1 1.8 %collective-permute-start.28 = (bf16[64,512]{1,0:T(8,128)(2,1)S(1)}, bf16[64,512]{1,0:T(8,128)(2,1)S(1)}, u32[]{:S(2)}, u32[]{:S(2)}) collective-permute-start(bf16[64,512]{1,0:T(8,128)(2,1)S(1)} %get-tuple-element.161), channel_id=1, source_target_pairs={{0,6},{1,7},{2,4},{3,5},{4,2},{5,3},{6,0},{7,1},{8,14},{9,15},{10,... | collective-permute-start | bytes 196616 | tf_op jit(solution)/shard_map/ppermute | solution.py:233
  68.8 2.7 %collective-permute-start.26 = (bf16[64,512]{1,0:T(8,128)(2,1)S(1)}, bf16[64,512]{1,0:T(8,128)(2,1)S(1)}, u32[]{:S(2)}, u32[]{:S(2)}) collective-permute-start(bf16[64,512]{1,0:T(8,128)(2,1)S(1)} %get-tuple-element.160), channel_id=1, source_target_pairs={{0,2},{1,3},{2,0},{3,1},{4,6},{5,7},{6,4},{7,5},{8,10},{9,11},{10,... | collective-permute-start | bytes 196616 | tf_op jit(solution)/shard_map/ppermute | solution.py:233
  73.9 2.0 %collective-permute-done.27 = bf16[64,512]{1,0:T(8,128)(2,1)S(1)} collective-permute-done((bf16[64,512]{1,0:T(8,128)(2,1)S(1)}, bf16[64,512]{1,0:T(8,128)(2,1)S(1)}, u32[]{:S(2)}, u32[]{:S(2)}) %collective-permute-start.27) | collective-permute-done | bytes 65568 | tf_op jit(solution)/shard_map/ppermute | solution.py:233
  77.5 1.6 %reshape.46 = f32[64,4,128]{2,1,0:T(4,128)} reshape(f32[64,512]{1,0:T(8,128)} %slice_add_fusion) | data formatting | bytes 262144 | tf_op jit(solution)/shard_map/transpose(jvp())/reshape | solution.py:19
  81.6 1.5 %slice.47 = bf16[64,512]{1,0:T(8,128)(2,1)} slice(f32[256,512]{1,0:T(8,128)} %add.91), slice={[64:128], [0:512]} | slice | bytes 131072 | tf_op jit(solution)/shard_map/slice | solution.py:254
  83.1 2.0 %collective-permute-start.33 = (bf16[64,512]{1,0:T(8,128)(2,1)S(1)}, bf16[64,512]{1,0:T(8,128)(2,1)}, u32[]{:S(2)}, u32[]{:S(2)}) collective-permute-start(bf16[64,512]{1,0:T(8,128)(2,1)S(1)} %fusion.7.refs_0_), channel_id=1, source_target_pairs={{0,2},{1,3},{2,0},{3,1},{4,6},{5,7},{6,4},{7,5},{8,10},{9,11},{10,... | collective-permute-start | bytes 196616 | tf_op jit(solution)/shard_map/ppermute | solution.py:233
  85.7 1.8 %collective-permute-start.35 = (bf16[64,512]{1,0:T(8,128)(2,1)S(1)}, bf16[64,512]{1,0:T(8,128)(2,1)}, u32[]{:S(2)}, u32[]{:S(2)}) collective-permute-start(bf16[64,512]{1,0:T(8,128)(2,1)S(1)} %fusion.7.refs_0_), channel_id=1, source_target_pairs={{0,6},{1,7},{2,4},{3,5},{4,2},{5,3},{6,0},{7,1},{8,14},{9,15},{10,... | collective-permute-start | bytes 196616 | tf_op jit(solution)/shard_map/ppermute | solution.py:233
  87.6 1.4 %collective-permute-start.36 = (bf16[64,512]{1,0:T(8,128)(2,1)S(1)}, bf16[64,512]{1,0:T(8,128)(2,1)S(1)}, u32[]{:S(2)}, u32[]{:S(2)}) collective-permute-start(bf16[64,512]{1,0:T(8,128)(2,1)S(1)} %fusion.7.refs_0_), channel_id=1, source_target_pairs={{0,24},{8,16},{16,8},{24,0},{1,25},{9,17},{17,9},{25,1},{2,26},{10... | collective-permute-start | bytes 196616 | tf_op jit(solution)/shard_map/ppermute | solution.py:233
  89.6 3.6 %collective-permute-done.34 = bf16[64,512]{1,0:T(8,128)(2,1)} collective-permute-done((bf16[64,512]{1,0:T(8,128)(2,1)S(1)}, bf16[64,512]{1,0:T(8,128)(2,1)}, u32[]{:S(2)}, u32[]{:S(2)}) %collective-permute-start.34) | collective-permute-done | bytes 65568 | tf_op jit(solution)/shard_map/ppermute | solution.py:233
  98.6 1.5 %collective-permute-start.37 = (bf16[192,512]{1,0:T(8,128)(2,1)S(1)}, bf16[192,512]{1,0:T(8,128)(2,1)S(1)}, u32[]{:S(2)}, u32[]{:S(2)}) collective-permute-start(bf16[192,512]{1,0:T(8,128)(2,1)S(1)} %pad_maximum_fusion), channel_id=1, source_target_pairs={{0,24},{8,16},{16,8},{24,0},{1,25},{9,17},{17,9},{25,1},{2,26},{10... | collective-permute-start | bytes 589832 | tf_op jit(solution)/shard_map/ppermute | solution.py:233
  101.2 1.6 %collective-permute-start.41 = (bf16[64,512]{1,0:T(8,128)(2,1)S(1)}, bf16[64,512]{1,0:T(8,128)(2,1)S(1)}, u32[]{:S(2)}, u32[]{:S(2)}) collective-permute-start(bf16[64,512]{1,0:T(8,128)(2,1)S(1)} %get-tuple-element.159), channel_id=1, source_target_pairs={{0,4},{1,5},{2,6},{3,7},{4,0},{5,1},{6,2},{7,3},{8,12},{9,13},{10,... | collective-permute-start | bytes 196616 | tf_op jit(solution)/shard_map/ppermute | solution.py:233
  102.7 2.1 %collective-permute-start.42 = (bf16[64,512]{1,0:T(8,128)(2,1)S(1)}, bf16[64,512]{1,0:T(8,128)(2,1)S(1)}, u32[]{:S(2)}, u32[]{:S(2)}) collective-permute-start(bf16[64,512]{1,0:T(8,128)(2,1)S(1)} %get-tuple-element.158), channel_id=1, source_target_pairs={{0,6},{1,7},{2,4},{3,5},{4,2},{5,3},{6,0},{7,1},{8,14},{9,15},{10,... | collective-permute-start | bytes 196616 | tf_op jit(solution)/shard_map/ppermute | solution.py:233
  105.1 2.1 %hidden_grad.1 = (bf16[64,5120]{1,0:T(8,128)(2,1)}, bf16[64,1280]{1,0:T(8,128)(2,1)S(1)}) custom-call(bf16[1280,512]{1,0:T(8,128)(2,1)S(1)} %copy-done, bf16[64,512]{1,0:T(8,128)(2,1)S(1)} %fusion.7.refs_0_, bf16[64,512]{1,0:T(8,128)(2,1)S(1)} %collective-permute-done.36.refs_1_, bf16[1280,256]{1,0:T(8,128)(2,1)S(1)} %collective-permute-done.23.refs_2_, ...), custom_call_target="tpu_custom_call" | custom-call | flops 335544320 | bytes 3000000 | tf_op jit(solution)/shard_map/hidden_grad/pallas_call | solution.py:109
  108.2 1.4 %collective-permute-start.38 = (bf16[64,1280]{1,0:T(8,128)(2,1)S(1)}, bf16[64,1280]{1,0:T(8,128)(2,1)S(1)}, u32[]{:S(2)}, u32[]{:S(2)}) collective-permute-start(bf16[64,1280]{1,0:T(8,128)(2,1)S(1)} %get-tuple-element.133), channel_id=1, source_target_pairs={{0,24},{8,16},{16,8},{24,0},{1,25},{9,17},{17,9},{25,1},{2,26},{10... | collective-permute-start | bytes 491528 | tf_op jit(solution)/shard_map/ppermute | solution.py:233
  111.6 1.5 %fusion.10 = bf16[1,64,512]{2,1,0:T(8,128)(2,1)} fusion(f32[64,512]{1,0:T(8,128)S(1)} %slice-done, bf16[64,512]{1,0:T(8,128)(2,1)S(1)} %collective-permute-done.42, bf16[64,512]{1,0:T(8,128)(2,1)S(1)} %collective-permute-done.41, bf16[64,512]{1,0:T(8,128)(2,1)} %collective-permute-done.32), kind=kLoop, calls=%fused_computation.24 | loop fusion | flops 229376 | bytes 393216 | tf_op jit(solution)/shard_map/broadcast_in_dim | solution.py:347
  (166 shorter events, 31.2 us)
Async XLA Ops:
  1.9 9.0 %collective-permute-start.2 = (bf16[64,1280]{1,0:T(8,128)(2,1)S(1)}, bf16[64,1280]{1,0:T(8,128)(2,1)S(1)}, u32[]{:S(2)}, u32[]{:S(2)}) collective-permute-start(bf16[64,1280]{1,0:T(8,128)(2,1)S(1)} %get-tuple-element.84), channel_id=1, source_target_pairs={{0,24},{8,16},{16,8},{24,0},{1,25},{9,17},{17,9},{25,1},{2,26},{10... | collective-permute-start | bytes 491528 | tf_op jit(solution)/shard_map/ppermute | solution.py:233
  5.8 8.4 %collective-permute-start.1 = (bf16[64,1280]{1,0:T(8,128)(2,1)S(1)}, bf16[64,1280]{1,0:T(8,128)(2,1)S(1)}, u32[]{:S(2)}, u32[]{:S(2)}) collective-permute-start(bf16[64,1280]{1,0:T(8,128)(2,1)S(1)} %get-tuple-element.83), channel_id=1, source_target_pairs={{0,16},{8,24},{16,0},{24,8},{1,17},{9,25},{17,1},{25,9},{2,18},{10... | collective-permute-start | bytes 491528 | tf_op jit(solution)/shard_map/ppermute | solution.py:233
  6.3 9.8 %collective-permute-start = (bf16[64,1280]{1,0:T(8,128)(2,1)S(1)}, bf16[64,1280]{1,0:T(8,128)(2,1)S(1)}, u32[]{:S(2)}, u32[]{:S(2)}) collective-permute-start(bf16[64,1280]{1,0:T(8,128)(2,1)S(1)} %get-tuple-element.82), channel_id=1, source_target_pairs={{0,8},{8,0},{16,24},{24,16},{1,9},{9,1},{17,25},{25,17},{2,10},{10... | collective-permute-start | bytes 491528 | tf_op jit(solution)/shard_map/ppermute | solution.py:233
  11.2 9.8 %collective-permute-start.5 = (f32[64,512]{1,0:T(8,128)S(1)}, f32[64,512]{1,0:T(8,128)S(1)}, u32[]{:S(2)}, u32[]{:S(2)}) collective-permute-start(f32[64,512]{1,0:T(8,128)S(1)} %fusion.18), channel_id=1, source_target_pairs={{0,24},{8,16},{16,8},{24,0},{1,25},{9,17},{17,9},{25,1},{2,26},{10... | collective-permute-start | bytes 393224 | tf_op jit(solution)/shard_map/ppermute | solution.py:233
  14.6 6.6 %collective-permute-start.4 = (f32[64,512]{1,0:T(8,128)S(1)}, f32[64,512]{1,0:T(8,128)S(1)}, u32[]{:S(2)}, u32[]{:S(2)}) collective-permute-start(f32[64,512]{1,0:T(8,128)S(1)} %fusion.17), channel_id=1, source_target_pairs={{0,16},{8,24},{16,0},{24,8},{1,17},{9,25},{17,1},{25,9},{2,18},{10... | collective-permute-start | bytes 393224 | tf_op jit(solution)/shard_map/ppermute | solution.py:233
  16.8 9.7 %collective-permute-start.13 = (bf16[64,512]{1,0:T(8,128)(2,1)S(1)}, bf16[64,512]{1,0:T(8,128)(2,1)S(1)}, u32[]{:S(2)}, u32[]{:S(2)}) collective-permute-start(bf16[64,512]{1,0:T(8,128)(2,1)S(1)} %bitcast.64), channel_id=1, source_target_pairs={{0,2},{1,3},{2,0},{3,1},{4,6},{5,7},{6,4},{7,5},{8,10},{9,11},{10,... | collective-permute-start | bytes 196616 | tf_op jit(solution)/shard_map/ppermute | solution.py:233
  18.5 8.3 %collective-permute-start.14 = (bf16[64,512]{1,0:T(8,128)(2,1)S(1)}, bf16[64,512]{1,0:T(8,128)(2,1)S(1)}, u32[]{:S(2)}, u32[]{:S(2)}) collective-permute-start(bf16[64,512]{1,0:T(8,128)(2,1)S(1)} %bitcast.65), channel_id=1, source_target_pairs={{0,4},{1,5},{2,6},{3,7},{4,0},{5,1},{6,2},{7,3},{8,12},{9,13},{10,... | collective-permute-start | bytes 196616 | tf_op jit(solution)/shard_map/ppermute | solution.py:233
  21.1 6.8 %collective-permute-start.15 = (bf16[64,512]{1,0:T(8,128)(2,1)S(1)}, bf16[64,512]{1,0:T(8,128)(2,1)S(1)}, u32[]{:S(2)}, u32[]{:S(2)}) collective-permute-start(bf16[64,512]{1,0:T(8,128)(2,1)S(1)} %bitcast.66), channel_id=1, source_target_pairs={{0,6},{1,7},{2,4},{3,5},{4,2},{5,3},{6,0},{7,1},{8,14},{9,15},{10,... | collective-permute-start | bytes 196616 | tf_op jit(solution)/shard_map/ppermute | solution.py:233
  22.3 5.6 %collective-permute-start.6 = (bf16[64,512]{1,0:T(8,128)(2,1)S(1)}, bf16[64,512]{1,0:T(8,128)(2,1)S(1)}, u32[]{:S(2)}, u32[]{:S(2)}) collective-permute-start(bf16[64,512]{1,0:T(8,128)(2,1)S(1)} %fusion.9.refs_0_), channel_id=1, source_target_pairs={{0,2},{1,3},{2,0},{3,1},{4,6},{5,7},{6,4},{7,5},{8,10},{9,11},{10,... | collective-permute-start | bytes 196616 | tf_op jit(solution)/shard_map/ppermute | solution.py:233
  23.9 7.1 %collective-permute-start.7 = (bf16[64,512]{1,0:T(8,128)(2,1)S(1)}, bf16[64,512]{1,0:T(8,128)(2,1)S(1)}, u32[]{:S(2)}, u32[]{:S(2)}) collective-permute-start(bf16[64,512]{1,0:T(8,128)(2,1)S(1)} %fusion.9.refs_0_), channel_id=1, source_target_pairs={{0,4},{1,5},{2,6},{3,7},{4,0},{5,1},{6,2},{7,3},{8,12},{9,13},{10,... | collective-permute-start | bytes 196616 | tf_op jit(solution)/shard_map/ppermute | solution.py:233
  26.5 6.1 %collective-permute-start.8 = (bf16[64,512]{1,0:T(8,128)(2,1)S(1)}, bf16[64,512]{1,0:T(8,128)(2,1)S(1)}, u32[]{:S(2)}, u32[]{:S(2)}) collective-permute-start(bf16[64,512]{1,0:T(8,128)(2,1)S(1)} %fusion.9.refs_0_), channel_id=1, source_target_pairs={{0,6},{1,7},{2,4},{3,5},{4,2},{5,3},{6,0},{7,1},{8,14},{9,15},{10,... | collective-permute-start | bytes 196616 | tf_op jit(solution)/shard_map/ppermute | solution.py:233
  26.7 5.8 %collective-permute-start.16 = (bf16[64,512]{1,0:T(8,128)(2,1)S(1)}, bf16[64,512]{1,0:T(8,128)(2,1)S(1)}, u32[]{:S(2)}, u32[]{:S(2)}) collective-permute-start(bf16[64,512]{1,0:T(8,128)(2,1)S(1)} %bitcast.67), channel_id=1, source_target_pairs={{0,1},{1,0},{2,3},{3,2},{4,5},{5,4},{6,7},{7,6},{8,9},{9,8},{10,11... | collective-permute-start | bytes 196616 | tf_op jit(solution)/shard_map/ppermute | solution.py:233
  34.3 30.7 %collective-permute-start.23 = (bf16[1280,256]{1,0:T(8,128)(2,1)}, bf16[1280,256]{1,0:T(8,128)(2,1)S(1)}, u32[]{:S(2)}, u32[]{:S(2)}) collective-permute-start(bf16[1280,256]{1,0:T(8,128)(2,1)} %constant_dynamic-slice_fusion), channel_id=1, source_target_pairs={{0,8},{8,0},{16,24},{24,16},{1,9},{9,1},{17,25},{25,17},{2,10},{10... | collective-permute-start | bytes 1966088 | tf_op jit(solution)/shard_map/ppermute | solution.py:233
  35.8 29.2 %collective-permute-start.24 = (bf16[1280,256]{1,0:T(8,128)(2,1)}, bf16[1280,256]{1,0:T(8,128)(2,1)S(1)}, u32[]{:S(2)}, u32[]{:S(2)}) collective-permute-start(bf16[1280,256]{1,0:T(8,128)(2,1)} %constant_dynamic-slice_fusion), channel_id=1, source_target_pairs={{0,16},{8,24},{16,0},{24,8},{1,17},{9,25},{17,1},{25,9},{2,18},{10... | collective-permute-start | bytes 1966088 | tf_op jit(solution)/shard_map/ppermute | solution.py:233
  36.5 28.5 %collective-permute-start.20 = (bf16[320,256]{1,0:T(8,128)(2,1)S(1)}, bf16[320,256]{1,0:T(8,128)(2,1)S(1)}, u32[]{:S(2)}, u32[]{:S(2)}) collective-permute-start(bf16[320,256]{1,0:T(8,128)(2,1)S(1)} %get-tuple-element.99), channel_id=1, source_target_pairs={{0,2},{1,3},{2,0},{3,1},{4,6},{5,7},{6,4},{7,5},{8,10},{9,11},{10,... | collective-permute-start | bytes 491528 | tf_op jit(solution)/shard_map/ppermute | solution.py:233
  36.5 28.5 %collective-permute-start.21 = (bf16[320,256]{1,0:T(8,128)(2,1)S(1)}, bf16[320,256]{1,0:T(8,128)(2,1)S(1)}, u32[]{:S(2)}, u32[]{:S(2)}) collective-permute-start(bf16[320,256]{1,0:T(8,128)(2,1)S(1)} %get-tuple-element.100), channel_id=1, source_target_pairs={{0,4},{1,5},{2,6},{3,7},{4,0},{5,1},{6,2},{7,3},{8,12},{9,13},{10,... | collective-permute-start | bytes 491528 | tf_op jit(solution)/shard_map/ppermute | solution.py:233
  38.8 26.2 %collective-permute-start.22 = (bf16[320,256]{1,0:T(8,128)(2,1)S(1)}, bf16[320,256]{1,0:T(8,128)(2,1)S(1)}, u32[]{:S(2)}, u32[]{:S(2)}) collective-permute-start(bf16[320,256]{1,0:T(8,128)(2,1)S(1)} %get-tuple-element.101), channel_id=1, source_target_pairs={{0,6},{1,7},{2,4},{3,5},{4,2},{5,3},{6,0},{7,1},{8,14},{9,15},{10,... | collective-permute-start | bytes 491528 | tf_op jit(solution)/shard_map/ppermute | solution.py:233
  65.6 11.0 %collective-permute-start.30 = (bf16[1280,256]{1,0:T(8,128)(2,1)S(1)}, bf16[1280,256]{1,0:T(8,128)(2,1)S(1)}, u32[]{:S(2)}, u32[]{:S(2)}) collective-permute-start(bf16[1280,256]{1,0:T(8,128)(2,1)S(1)} %collective-permute-done.23.refs_2_), channel_id=1, source_target_pairs={{0,1},{1,0},{2,3},{3,2},{4,5},{5,4},{6,7},{7,6},{8,9},{9,8},{10,11... | collective-permute-start | bytes 1966088 | tf_op jit(solution)/shard_map/ppermute | solution.py:233
  65.6 10.9 %collective-permute-start.31 = (bf16[1280,256]{1,0:T(8,128)(2,1)S(1)}, bf16[1280,256]{1,0:T(8,128)(2,1)S(1)}, u32[]{:S(2)}, u32[]{:S(2)}) collective-permute-start(bf16[1280,256]{1,0:T(8,128)(2,1)S(1)} %collective-permute-done.24.refs_3_), channel_id=1, source_target_pairs={{0,1},{1,0},{2,3},{3,2},{4,5},{5,4},{6,7},{7,6},{8,9},{9,8},{10,11... | collective-permute-start | bytes 1966088 | tf_op jit(solution)/shard_map/ppermute | solution.py:233
  67.1 6.8 %collective-permute-start.28 = (bf16[64,512]{1,0:T(8,128)(2,1)S(1)}, bf16[64,512]{1,0:T(8,128)(2,1)S(1)}, u32[]{:S(2)}, u32[]{:S(2)}) collective-permute-start(bf16[64,512]{1,0:T(8,128)(2,1)S(1)} %get-tuple-element.161), channel_id=1, source_target_pairs={{0,6},{1,7},{2,4},{3,5},{4,2},{5,3},{6,0},{7,1},{8,14},{9,15},{10,... | collective-permute-start | bytes 196616 | tf_op jit(solution)/shard_map/ppermute | solution.py:233
  68.8 7.0 %collective-permute-start.27 = (bf16[64,512]{1,0:T(8,128)(2,1)S(1)}, bf16[64,512]{1,0:T(8,128)(2,1)S(1)}, u32[]{:S(2)}, u32[]{:S(2)}) collective-permute-start(bf16[64,512]{1,0:T(8,128)(2,1)S(1)} %get-tuple-element.162), channel_id=1, source_target_pairs={{0,4},{1,5},{2,6},{3,7},{4,0},{5,1},{6,2},{7,3},{8,12},{9,13},{10,... | collective-permute-start | bytes 196616 | tf_op jit(solution)/shard_map/ppermute | solution.py:233
  68.8 7.0 %collective-permute-start.26 = (bf16[64,512]{1,0:T(8,128)(2,1)S(1)}, bf16[64,512]{1,0:T(8,128)(2,1)S(1)}, u32[]{:S(2)}, u32[]{:S(2)}) collective-permute-start(bf16[64,512]{1,0:T(8,128)(2,1)S(1)} %get-tuple-element.160), channel_id=1, source_target_pairs={{0,2},{1,3},{2,0},{3,1},{4,6},{5,7},{6,4},{7,5},{8,10},{9,11},{10,... | collective-permute-start | bytes 196616 | tf_op jit(solution)/shard_map/ppermute | solution.py:233
  83.1 5.9 %collective-permute-start.32 = (bf16[64,512]{1,0:T(8,128)(2,1)}, bf16[64,512]{1,0:T(8,128)(2,1)}, u32[]{:S(2)}, u32[]{:S(2)}) collective-permute-start(bf16[64,512]{1,0:T(8,128)(2,1)} %slice.47), channel_id=1, source_target_pairs={{0,2},{1,3},{2,0},{3,1},{4,6},{5,7},{6,4},{7,5},{8,10},{9,11},{10,... | collective-permute-start | bytes 196616 | tf_op jit(solution)/shard_map/ppermute | solution.py:233
  83.1 6.4 %collective-permute-start.33 = (bf16[64,512]{1,0:T(8,128)(2,1)S(1)}, bf16[64,512]{1,0:T(8,128)(2,1)}, u32[]{:S(2)}, u32[]{:S(2)}) collective-permute-start(bf16[64,512]{1,0:T(8,128)(2,1)S(1)} %fusion.7.refs_0_), channel_id=1, source_target_pairs={{0,2},{1,3},{2,0},{3,1},{4,6},{5,7},{6,4},{7,5},{8,10},{9,11},{10,... | collective-permute-start | bytes 196616 | tf_op jit(solution)/shard_map/ppermute | solution.py:233
  85.2 8.0 %collective-permute-start.34 = (bf16[64,512]{1,0:T(8,128)(2,1)S(1)}, bf16[64,512]{1,0:T(8,128)(2,1)}, u32[]{:S(2)}, u32[]{:S(2)}) collective-permute-start(bf16[64,512]{1,0:T(8,128)(2,1)S(1)} %fusion.7.refs_0_), channel_id=1, source_target_pairs={{0,4},{1,5},{2,6},{3,7},{4,0},{5,1},{6,2},{7,3},{8,12},{9,13},{10,... | collective-permute-start | bytes 196616 | tf_op jit(solution)/shard_map/ppermute | solution.py:233
  85.7 7.4 %collective-permute-start.35 = (bf16[64,512]{1,0:T(8,128)(2,1)S(1)}, bf16[64,512]{1,0:T(8,128)(2,1)}, u32[]{:S(2)}, u32[]{:S(2)}) collective-permute-start(bf16[64,512]{1,0:T(8,128)(2,1)S(1)} %fusion.7.refs_0_), channel_id=1, source_target_pairs={{0,6},{1,7},{2,4},{3,5},{4,2},{5,3},{6,0},{7,1},{8,14},{9,15},{10,... | collective-permute-start | bytes 196616 | tf_op jit(solution)/shard_map/ppermute | solution.py:233
  96.6 13.4 %collective-permute-start.40 = (bf16[256,512]{1,0:T(8,128)(2,1)S(1)}, bf16[256,512]{1,0:T(8,128)(2,1)S(1)}, u32[]{:S(2)}, u32[]{:S(2)}) collective-permute-start(bf16[256,512]{1,0:T(8,128)(2,1)S(1)} %constant_dynamic-update-slice_fusion), channel_id=1, source_target_pairs={{0,16},{8,24},{16,0},{24,8},{1,17},{9,25},{17,1},{25,9},{2,18},{10... | collective-permute-start | bytes 786440 | tf_op jit(solution)/shard_map/ppermute | solution.py:233
  98.0 12.3 %collective-permute-start.39 = (bf16[256,512]{1,0:T(8,128)(2,1)S(1)}, bf16[256,512]{1,0:T(8,128)(2,1)S(1)}, u32[]{:S(2)}, u32[]{:S(2)}) collective-permute-start(bf16[256,512]{1,0:T(8,128)(2,1)S(1)} %constant_dynamic-update-slice_fusion), channel_id=1, source_target_pairs={{0,8},{8,0},{16,24},{24,16},{1,9},{9,1},{17,25},{25,17},{2,10},{10... | collective-permute-start | bytes 786440 | tf_op jit(solution)/shard_map/ppermute | solution.py:233
  98.6 9.6 %collective-permute-start.37 = (bf16[192,512]{1,0:T(8,128)(2,1)S(1)}, bf16[192,512]{1,0:T(8,128)(2,1)S(1)}, u32[]{:S(2)}, u32[]{:S(2)}) collective-permute-start(bf16[192,512]{1,0:T(8,128)(2,1)S(1)} %pad_maximum_fusion), channel_id=1, source_target_pairs={{0,24},{8,16},{16,8},{24,0},{1,25},{9,17},{17,9},{25,1},{2,26},{10... | collective-permute-start | bytes 589832 | tf_op jit(solution)/shard_map/ppermute | solution.py:233
  101.2 9.6 %collective-permute-start.41 = (bf16[64,512]{1,0:T(8,128)(2,1)S(1)}, bf16[64,512]{1,0:T(8,128)(2,1)S(1)}, u32[]{:S(2)}, u32[]{:S(2)}) collective-permute-start(bf16[64,512]{1,0:T(8,128)(2,1)S(1)} %get-tuple-element.159), channel_id=1, source_target_pairs={{0,4},{1,5},{2,6},{3,7},{4,0},{5,1},{6,2},{7,3},{8,12},{9,13},{10,... | collective-permute-start | bytes 196616 | tf_op jit(solution)/shard_map/ppermute | solution.py:233
  102.7 8.0 %collective-permute-start.42 = (bf16[64,512]{1,0:T(8,128)(2,1)S(1)}, bf16[64,512]{1,0:T(8,128)(2,1)S(1)}, u32[]{:S(2)}, u32[]{:S(2)}) collective-permute-start(bf16[64,512]{1,0:T(8,128)(2,1)S(1)} %get-tuple-element.158), channel_id=1, source_target_pairs={{0,6},{1,7},{2,4},{3,5},{4,2},{5,3},{6,0},{7,1},{8,14},{9,15},{10,... | collective-permute-start | bytes 196616 | tf_op jit(solution)/shard_map/ppermute | solution.py:233
  108.2 6.2 %collective-permute-start.38 = (bf16[64,1280]{1,0:T(8,128)(2,1)S(1)}, bf16[64,1280]{1,0:T(8,128)(2,1)S(1)}, u32[]{:S(2)}, u32[]{:S(2)}) collective-permute-start(bf16[64,1280]{1,0:T(8,128)(2,1)S(1)} %get-tuple-element.133), channel_id=1, source_target_pairs={{0,24},{8,16},{16,8},{24,0},{1,25},{9,17},{17,9},{25,1},{2,26},{10... | collective-permute-start | bytes 491528 | tf_op jit(solution)/shard_map/ppermute | solution.py:233
  (42 other events, 264.8 us)

commit v15 on v14

--- a/solution.py
+++ b/solution.py
@@ -10,7 +10,7 @@
 F32, BF16 = jnp.float32, jnp.bfloat16
 LOG2E = 1.4426950408889634
 SMALL = pltpu.CompilerParams(vmem_limit_bytes=16 * 2**20)
-LARGE = pltpu.CompilerParams(vmem_limit_bytes=40 * 2**20)
+LARGE = pltpu.CompilerParams(vmem_limit_bytes=56 * 2**20)
 
 
 def norm_keys(key_pre, key_gain):

time: 117 us -> 116 us (level)
  local copies, waits for them, and re-layouts: 13.6 us -> 9.63 us
    unnamed x61 -> x83, local copies, waits for them, and re-layouts: 7.36 us -> 4.22 us
  transfers between devices with their start and end apart: 44 -> 44, of which waited for: 12 -> 12; matrix products, arithmetic and copies ran while one was open for 9% -> 10% of each run, Pallas kernels for 20% -> 21%
where the time goes in v15:
time: 116 us; the launch traced here: 115 us
  starting transfers between devices  46.4 us (40%)
  Pallas kernels  24.4 us (21%)
  waiting for transfers between devices  18.7 us (16%)
  local copies, waits for them, and re-layouts  9.63 us (8%)
  other arithmetic  8.64 us (7%)
  matrix products  5.31 us (5%)
  between operations  2.04 us (2%)
    ppermute x44, starting transfers between devices, swap(): return lax.ppermute(array, axis, [(i, i ^ distance) for i in range(size)])  46.4 us
    pallas_call x1, Pallas kernels, attend(): pl.pallas_call(partial(attend_kernel, len(key_pieces)), grid=(kv_heads,),...  21.7 us
    ppermute x44, waiting for transfers between devices, swap(): return lax.ppermute(array, axis, [(i, i ^ distance) for i in range(size)])  18.7 us
    dot_general x14, matrix products, dot(): return lax.dot_general(left, right, dims, preferred_element_type=F32)  5.31 us
    unnamed x83, local copies, waits for them, and re-layouts  4.22 us
    pallas_call x4, Pallas kernels, in_vmem(): pl.pallas_call(kernel, in_specs=[whole] * len(arrays), out_specs=[whole]...  2.72 us
  transfers between devices with their start and end apart: 44, of which 12 were waited for; matrix products, arithmetic and copies ran while one was open for 10% of the time, Pallas kernels for 21%

profile of v15, /device:TPU:0, one launch (start us, length us, event | category | flops | bytes accessed | tf_op | source)
XLA Modules:
  0.0 115.1 jit_solution(11174893825103350045)
XLA Ops:
  1.9 4.0 %collective-permute-start.2 = (bf16[64,1280]{1,0:T(8,128)(2,1)S(1)}, bf16[64,1280]{1,0:T(8,128)(2,1)S(1)}, u32[]{:S(2)}, u32[]{:S(2)}) collective-permute-start(bf16[64,1280]{1,0:T(8,128)(2,1)S(1)} %get-tuple-element.84), channel_id=1, source_target_pairs={{0,24},{8,16},{16,8},{24,0},{1,25},{9,17},{17,9},{25,1},{2,26},{10... | collective-permute-start | bytes 491528 | tf_op jit(solution)/shard_map/ppermute | solution.py:233
  6.5 1.6 %fusion.15 = f32[64,512]{1,0:T(8,128)S(1)} fusion(bf16[64,1280]{1,0:T(8,128)(2,1)S(1)} %get-tuple-element.81.refs_0_, bf16[1280,512]{1,0:T(8,128)(2,1)} %own_ref.1), kind=kOutput, calls=%fused_computation.37 | convolution fusion | flops 83886080 | bytes 1605632 | tf_op jit(solution)/shard_map/dot_general | solution.py:24
  8.2 2.7 %collective-permute-done.2.refs_3_ = bf16[64,1280]{1,0:T(8,128)(2,1)S(1)} collective-permute-done((bf16[64,1280]{1,0:T(8,128)(2,1)S(1)}, bf16[64,1280]{1,0:T(8,128)(2,1)S(1)}, u32[]{:S(2)}, u32[]{:S(2)}) %collective-permute-start.2) | collective-permute-done | bytes 163872 | tf_op jit(solution)/shard_map/ppermute | solution.py:233
  11.2 3.0 %collective-permute-start.5 = (f32[64,512]{1,0:T(8,128)S(1)}, f32[64,512]{1,0:T(8,128)S(1)}, u32[]{:S(2)}, u32[]{:S(2)}) collective-permute-start(f32[64,512]{1,0:T(8,128)S(1)} %fusion.18), channel_id=1, source_target_pairs={{0,24},{8,16},{16,8},{24,0},{1,25},{9,17},{17,9},{25,1},{2,26},{10... | collective-permute-start | bytes 393224 | tf_op jit(solution)/shard_map/ppermute | solution.py:233
  14.6 1.6 %collective-permute-start.4 = (f32[64,512]{1,0:T(8,128)S(1)}, f32[64,512]{1,0:T(8,128)S(1)}, u32[]{:S(2)}, u32[]{:S(2)}) collective-permute-start(f32[64,512]{1,0:T(8,128)S(1)} %fusion.17), channel_id=1, source_target_pairs={{0,16},{8,24},{16,0},{24,8},{1,17},{9,25},{17,1},{25,9},{2,18},{10... | collective-permute-start | bytes 393224 | tf_op jit(solution)/shard_map/ppermute | solution.py:233
  16.8 1.7 %collective-permute-start.13 = (bf16[64,512]{1,0:T(8,128)(2,1)S(1)}, bf16[64,512]{1,0:T(8,128)(2,1)S(1)}, u32[]{:S(2)}, u32[]{:S(2)}) collective-permute-start(bf16[64,512]{1,0:T(8,128)(2,1)S(1)} %bitcast.69), channel_id=1, source_target_pairs={{0,2},{1,3},{2,0},{3,1},{4,6},{5,7},{6,4},{7,5},{8,10},{9,11},{10,... | collective-permute-start | bytes 196616 | tf_op jit(solution)/shard_map/ppermute | solution.py:233
  18.5 2.6 %collective-permute-start.14 = (bf16[64,512]{1,0:T(8,128)(2,1)S(1)}, bf16[64,512]{1,0:T(8,128)(2,1)S(1)}, u32[]{:S(2)}, u32[]{:S(2)}) collective-permute-start(bf16[64,512]{1,0:T(8,128)(2,1)S(1)} %bitcast.70), channel_id=1, source_target_pairs={{0,4},{1,5},{2,6},{3,7},{4,0},{5,1},{6,2},{7,3},{8,12},{9,13},{10,... | collective-permute-start | bytes 196616 | tf_op jit(solution)/shard_map/ppermute | solution.py:233
  22.3 1.6 %collective-permute-start.6 = (bf16[64,512]{1,0:T(8,128)(2,1)S(1)}, bf16[64,512]{1,0:T(8,128)(2,1)S(1)}, u32[]{:S(2)}, u32[]{:S(2)}) collective-permute-start(bf16[64,512]{1,0:T(8,128)(2,1)S(1)} %fusion.9.refs_0_), channel_id=1, source_target_pairs={{0,2},{1,3},{2,0},{3,1},{4,6},{5,7},{6,4},{7,5},{8,10},{9,11},{10,... | collective-permute-start | bytes 196616 | tf_op jit(solution)/shard_map/ppermute | solution.py:233
  23.9 2.6 %collective-permute-start.7 = (bf16[64,512]{1,0:T(8,128)(2,1)S(1)}, bf16[64,512]{1,0:T(8,128)(2,1)S(1)}, u32[]{:S(2)}, u32[]{:S(2)}) collective-permute-start(bf16[64,512]{1,0:T(8,128)(2,1)S(1)} %fusion.9.refs_0_), channel_id=1, source_target_pairs={{0,4},{1,5},{2,6},{3,7},{4,0},{5,1},{6,2},{7,3},{8,12},{9,13},{10,... | collective-permute-start | bytes 196616 | tf_op jit(solution)/shard_map/ppermute | solution.py:233
  28.9 2.1 %collective-permute-done.7.refs_2_ = bf16[64,512]{1,0:T(8,128)(2,1)S(1)} collective-permute-done((bf16[64,512]{1,0:T(8,128)(2,1)S(1)}, bf16[64,512]{1,0:T(8,128)(2,1)S(1)}, u32[]{:S(2)}, u32[]{:S(2)}) %collective-permute-start.7) | collective-permute-done | bytes 65568 | tf_op jit(solution)/shard_map/ppermute | solution.py:233
  31.0 1.6 %collective-permute-done.8.refs_3_ = bf16[64,512]{1,0:T(8,128)(2,1)S(1)} collective-permute-done((bf16[64,512]{1,0:T(8,128)(2,1)S(1)}, bf16[64,512]{1,0:T(8,128)(2,1)S(1)}, u32[]{:S(2)}, u32[]{:S(2)}) %collective-permute-start.8) | collective-permute-done | bytes 65568 | tf_op jit(solution)/shard_map/ppermute | solution.py:233
  34.3 1.5 %collective-permute-start.23 = (bf16[1280,256]{1,0:T(8,128)(2,1)S(1)}, bf16[1280,256]{1,0:T(8,128)(2,1)S(1)}, u32[]{:S(2)}, u32[]{:S(2)}) collective-permute-start(bf16[1280,256]{1,0:T(8,128)(2,1)S(1)} %constant_dynamic-slice_fusion), channel_id=1, source_target_pairs={{0,8},{8,0},{16,24},{24,16},{1,9},{9,1},{17,25},{25,17},{2,10},{10... | collective-permute-start | bytes 1966088 | tf_op jit(solution)/shard_map/ppermute | solution.py:233
  36.6 2.2 %collective-permute-start.21 = (bf16[320,256]{1,0:T(8,128)(2,1)S(1)}, bf16[320,256]{1,0:T(8,128)(2,1)S(1)}, u32[]{:S(2)}, u32[]{:S(2)}) collective-permute-start(bf16[320,256]{1,0:T(8,128)(2,1)S(1)} %get-tuple-element.100), channel_id=1, source_target_pairs={{0,4},{1,5},{2,6},{3,7},{4,0},{5,1},{6,2},{7,3},{8,12},{9,13},{10,... | collective-permute-start | bytes 491528 | tf_op jit(solution)/shard_map/ppermute | solution.py:233
  38.8 2.1 %collective-permute-start.22 = (bf16[320,256]{1,0:T(8,128)(2,1)S(1)}, bf16[320,256]{1,0:T(8,128)(2,1)S(1)}, u32[]{:S(2)}, u32[]{:S(2)}) collective-permute-start(bf16[320,256]{1,0:T(8,128)(2,1)S(1)} %get-tuple-element.101), channel_id=1, source_target_pairs={{0,6},{1,7},{2,4},{3,5},{4,2},{5,3},{6,0},{7,1},{8,14},{9,15},{10,... | collective-permute-start | bytes 491528 | tf_op jit(solution)/shard_map/ppermute | solution.py:233
  41.0 21.7 %attend.1 = (bf16[256,4096]{1,0:T(8,128)(2,1)}, bf16[256,512]{1,0:T(8,128)(2,1)}, bf16[256,512]{1,0:T(8,128)(2,1)}, f32[256,512]{1,0:T(8,128)}, f32[256,512]{1,0...) custom-call(s32[1,1]{1,0:T(1,128)S(6)} %copy.30.length_ref, bf16[256,4096]{1,0:T(8,128)(2,1)} %bitcast.63, ...), custom_call_target="tpu_custom_call" | custom-call | flops 16106127360 | bytes 10000000 | tf_op jit(solution)/shard_map/attend/pallas_call | solution.py:92
  66.1 1.7 %collective-permute-start.28 = (bf16[64,512]{1,0:T(8,128)(2,1)S(1)}, bf16[64,512]{1,0:T(8,128)(2,1)S(1)}, u32[]{:S(2)}, u32[]{:S(2)}) collective-permute-start(bf16[64,512]{1,0:T(8,128)(2,1)S(1)} %get-tuple-element.161), channel_id=1, source_target_pairs={{0,6},{1,7},{2,4},{3,5},{4,2},{5,3},{6,0},{7,1},{8,14},{9,15},{10,... | collective-permute-start | bytes 196616 | tf_op jit(solution)/shard_map/ppermute | solution.py:233
  67.9 2.7 %collective-permute-start.26 = (bf16[64,512]{1,0:T(8,128)(2,1)S(1)}, bf16[64,512]{1,0:T(8,128)(2,1)S(1)}, u32[]{:S(2)}, u32[]{:S(2)}) collective-permute-start(bf16[64,512]{1,0:T(8,128)(2,1)S(1)} %get-tuple-element.160), channel_id=1, source_target_pairs={{0,2},{1,3},{2,0},{3,1},{4,6},{5,7},{6,4},{7,5},{8,10},{9,11},{10,... | collective-permute-start | bytes 196616 | tf_op jit(solution)/shard_map/ppermute | solution.py:233
  73.0 2.0 %collective-permute-done.27 = bf16[64,512]{1,0:T(8,128)(2,1)S(1)} collective-permute-done((bf16[64,512]{1,0:T(8,128)(2,1)S(1)}, bf16[64,512]{1,0:T(8,128)(2,1)S(1)}, u32[]{:S(2)}, u32[]{:S(2)}) %collective-permute-start.27) | collective-permute-done | bytes 65568 | tf_op jit(solution)/shard_map/ppermute | solution.py:233
  76.5 1.6 %reshape.46 = f32[64,4,128]{2,1,0:T(4,128)} reshape(f32[64,512]{1,0:T(8,128)} %slice_add_fusion) | data formatting | bytes 262144 | tf_op jit(solution)/shard_map/transpose(jvp())/reshape | solution.py:19
  80.7 1.5 %slice.47 = bf16[64,512]{1,0:T(8,128)(2,1)} slice(f32[256,512]{1,0:T(8,128)} %add.91), slice={[64:128], [0:512]} | slice | bytes 131072 | tf_op jit(solution)/shard_map/slice | solution.py:254
  82.2 2.0 %collective-permute-start.33 = (bf16[64,512]{1,0:T(8,128)(2,1)S(1)}, bf16[64,512]{1,0:T(8,128)(2,1)}, u32[]{:S(2)}, u32[]{:S(2)}) collective-permute-start(bf16[64,512]{1,0:T(8,128)(2,1)S(1)} %fusion.7.refs_0_), channel_id=1, source_target_pairs={{0,2},{1,3},{2,0},{3,1},{4,6},{5,7},{6,4},{7,5},{8,10},{9,11},{10,... | collective-permute-start | bytes 196616 | tf_op jit(solution)/shard_map/ppermute | solution.py:233
  84.8 1.8 %collective-permute-start.35 = (bf16[64,512]{1,0:T(8,128)(2,1)S(1)}, bf16[64,512]{1,0:T(8,128)(2,1)}, u32[]{:S(2)}, u32[]{:S(2)}) collective-permute-start(bf16[64,512]{1,0:T(8,128)(2,1)S(1)} %fusion.7.refs_0_), channel_id=1, source_target_pairs={{0,6},{1,7},{2,4},{3,5},{4,2},{5,3},{6,0},{7,1},{8,14},{9,15},{10,... | collective-permute-start | bytes 196616 | tf_op jit(solution)/shard_map/ppermute | solution.py:233
  86.6 1.4 %collective-permute-start.36 = (bf16[64,512]{1,0:T(8,128)(2,1)S(1)}, bf16[64,512]{1,0:T(8,128)(2,1)S(1)}, u32[]{:S(2)}, u32[]{:S(2)}) collective-permute-start(bf16[64,512]{1,0:T(8,128)(2,1)S(1)} %fusion.7.refs_0_), channel_id=1, source_target_pairs={{0,24},{8,16},{16,8},{24,0},{1,25},{9,17},{17,9},{25,1},{2,26},{10... | collective-permute-start | bytes 196616 | tf_op jit(solution)/shard_map/ppermute | solution.py:233
  88.6 3.6 %collective-permute-done.34 = bf16[64,512]{1,0:T(8,128)(2,1)} collective-permute-done((bf16[64,512]{1,0:T(8,128)(2,1)S(1)}, bf16[64,512]{1,0:T(8,128)(2,1)}, u32[]{:S(2)}, u32[]{:S(2)}) %collective-permute-start.34) | collective-permute-done | bytes 65568 | tf_op jit(solution)/shard_map/ppermute | solution.py:233
  95.7 1.4 %collective-permute-start.40 = (bf16[256,512]{1,0:T(8,128)(2,1)S(1)}, bf16[256,512]{1,0:T(8,128)(2,1)S(1)}, u32[]{:S(2)}, u32[]{:S(2)}) collective-permute-start(bf16[256,512]{1,0:T(8,128)(2,1)S(1)} %constant_dynamic-update-slice_fusion), channel_id=1, source_target_pairs={{0,16},{8,24},{16,0},{24,8},{1,17},{9,25},{17,1},{25,9},{2,18},{10... | collective-permute-start | bytes 786440 | tf_op jit(solution)/shard_map/ppermute | solution.py:233
  97.6 1.5 %collective-permute-start.37 = (bf16[192,512]{1,0:T(8,128)(2,1)S(1)}, bf16[192,512]{1,0:T(8,128)(2,1)S(1)}, u32[]{:S(2)}, u32[]{:S(2)}) collective-permute-start(bf16[192,512]{1,0:T(8,128)(2,1)S(1)} %pad_maximum_fusion), channel_id=1, source_target_pairs={{0,24},{8,16},{16,8},{24,0},{1,25},{9,17},{17,9},{25,1},{2,26},{10... | collective-permute-start | bytes 589832 | tf_op jit(solution)/shard_map/ppermute | solution.py:233
  100.3 1.5 %collective-permute-start.41 = (bf16[64,512]{1,0:T(8,128)(2,1)S(1)}, bf16[64,512]{1,0:T(8,128)(2,1)S(1)}, u32[]{:S(2)}, u32[]{:S(2)}) collective-permute-start(bf16[64,512]{1,0:T(8,128)(2,1)S(1)} %get-tuple-element.159), channel_id=1, source_target_pairs={{0,4},{1,5},{2,6},{3,7},{4,0},{5,1},{6,2},{7,3},{8,12},{9,13},{10,... | collective-permute-start | bytes 196616 | tf_op jit(solution)/shard_map/ppermute | solution.py:233
  101.8 2.1 %collective-permute-start.42 = (bf16[64,512]{1,0:T(8,128)(2,1)S(1)}, bf16[64,512]{1,0:T(8,128)(2,1)S(1)}, u32[]{:S(2)}, u32[]{:S(2)}) collective-permute-start(bf16[64,512]{1,0:T(8,128)(2,1)S(1)} %get-tuple-element.158), channel_id=1, source_target_pairs={{0,6},{1,7},{2,4},{3,5},{4,2},{5,3},{6,0},{7,1},{8,14},{9,15},{10,... | collective-permute-start | bytes 196616 | tf_op jit(solution)/shard_map/ppermute | solution.py:233
  104.2 2.1 %hidden_grad.1 = (bf16[64,5120]{1,0:T(8,128)(2,1)}, bf16[64,1280]{1,0:T(8,128)(2,1)S(1)}) custom-call(bf16[1280,512]{1,0:T(8,128)(2,1)S(1)} %copy-done, bf16[64,512]{1,0:T(8,128)(2,1)S(1)} %fusion.7.refs_0_, bf16[64,512]{1,0:T(8,128)(2,1)S(1)} %collective-permute-done.36.refs_1_, bf16[1280,256]{1,0:T(8,128)(2,1)S(1)} %collective-permute-done.23.refs_2_, ...), custom_call_target="tpu_custom_call" | custom-call | flops 335544320 | bytes 3000000 | tf_op jit(solution)/shard_map/hidden_grad/pallas_call | solution.py:109
  107.3 1.4 %collective-permute-start.38 = (bf16[64,1280]{1,0:T(8,128)(2,1)S(1)}, bf16[64,1280]{1,0:T(8,128)(2,1)S(1)}, u32[]{:S(2)}, u32[]{:S(2)}) collective-permute-start(bf16[64,1280]{1,0:T(8,128)(2,1)S(1)} %get-tuple-element.133), channel_id=1, source_target_pairs={{0,24},{8,16},{16,8},{24,0},{1,25},{9,17},{17,9},{25,1},{2,26},{10... | collective-permute-start | bytes 491528 | tf_op jit(solution)/shard_map/ppermute | solution.py:233
  110.6 1.5 %fusion.10 = bf16[1,64,512]{2,1,0:T(8,128)(2,1)} fusion(f32[64,512]{1,0:T(8,128)S(1)} %slice-done, bf16[64,512]{1,0:T(8,128)(2,1)S(1)} %collective-permute-done.42, bf16[64,512]{1,0:T(8,128)(2,1)S(1)} %collective-permute-done.41, bf16[64,512]{1,0:T(8,128)(2,1)} %collective-permute-done.32), kind=kLoop, calls=%fused_computation.24 | loop fusion | flops 229376 | bytes 393216 | tf_op jit(solution)/shard_map/broadcast_in_dim | solution.py:347
  112.1 1.4 %collective-permute-done.38 = bf16[64,1280]{1,0:T(8,128)(2,1)S(1)} collective-permute-done((bf16[64,1280]{1,0:T(8,128)(2,1)S(1)}, bf16[64,1280]{1,0:T(8,128)(2,1)S(1)}, u32[]{:S(2)}, u32[]{:S(2)}) %collective-permute-start.38) | collective-permute-done | bytes 163872 | tf_op jit(solution)/shard_map/ppermute | solution.py:233
  (188 shorter events, 29.1 us)
Async XLA Ops:
  1.9 9.0 %collective-permute-start.2 = (bf16[64,1280]{1,0:T(8,128)(2,1)S(1)}, bf16[64,1280]{1,0:T(8,128)(2,1)S(1)}, u32[]{:S(2)}, u32[]{:S(2)}) collective-permute-start(bf16[64,1280]{1,0:T(8,128)(2,1)S(1)} %get-tuple-element.84), channel_id=1, source_target_pairs={{0,24},{8,16},{16,8},{24,0},{1,25},{9,17},{17,9},{25,1},{2,26},{10... | collective-permute-start | bytes 491528 | tf_op jit(solution)/shard_map/ppermute | solution.py:233
  5.8 8.4 %collective-permute-start.1 = (bf16[64,1280]{1,0:T(8,128)(2,1)S(1)}, bf16[64,1280]{1,0:T(8,128)(2,1)S(1)}, u32[]{:S(2)}, u32[]{:S(2)}) collective-permute-start(bf16[64,1280]{1,0:T(8,128)(2,1)S(1)} %get-tuple-element.83), channel_id=1, source_target_pairs={{0,16},{8,24},{16,0},{24,8},{1,17},{9,25},{17,1},{25,9},{2,18},{10... | collective-permute-start | bytes 491528 | tf_op jit(solution)/shard_map/ppermute | solution.py:233
  6.3 9.8 %collective-permute-start = (bf16[64,1280]{1,0:T(8,128)(2,1)S(1)}, bf16[64,1280]{1,0:T(8,128)(2,1)S(1)}, u32[]{:S(2)}, u32[]{:S(2)}) collective-permute-start(bf16[64,1280]{1,0:T(8,128)(2,1)S(1)} %get-tuple-element.82), channel_id=1, source_target_pairs={{0,8},{8,0},{16,24},{24,16},{1,9},{9,1},{17,25},{25,17},{2,10},{10... | collective-permute-start | bytes 491528 | tf_op jit(solution)/shard_map/ppermute | solution.py:233
  11.2 9.8 %collective-permute-start.5 = (f32[64,512]{1,0:T(8,128)S(1)}, f32[64,512]{1,0:T(8,128)S(1)}, u32[]{:S(2)}, u32[]{:S(2)}) collective-permute-start(f32[64,512]{1,0:T(8,128)S(1)} %fusion.18), channel_id=1, source_target_pairs={{0,24},{8,16},{16,8},{24,0},{1,25},{9,17},{17,9},{25,1},{2,26},{10... | collective-permute-start | bytes 393224 | tf_op jit(solution)/shard_map/ppermute | solution.py:233
  14.6 6.6 %collective-permute-start.4 = (f32[64,512]{1,0:T(8,128)S(1)}, f32[64,512]{1,0:T(8,128)S(1)}, u32[]{:S(2)}, u32[]{:S(2)}) collective-permute-start(f32[64,512]{1,0:T(8,128)S(1)} %fusion.17), channel_id=1, source_target_pairs={{0,16},{8,24},{16,0},{24,8},{1,17},{9,25},{17,1},{25,9},{2,18},{10... | collective-permute-start | bytes 393224 | tf_op jit(solution)/shard_map/ppermute | solution.py:233
  16.8 9.7 %collective-permute-start.13 = (bf16[64,512]{1,0:T(8,128)(2,1)S(1)}, bf16[64,512]{1,0:T(8,128)(2,1)S(1)}, u32[]{:S(2)}, u32[]{:S(2)}) collective-permute-start(bf16[64,512]{1,0:T(8,128)(2,1)S(1)} %bitcast.69), channel_id=1, source_target_pairs={{0,2},{1,3},{2,0},{3,1},{4,6},{5,7},{6,4},{7,5},{8,10},{9,11},{10,... | collective-permute-start | bytes 196616 | tf_op jit(solution)/shard_map/ppermute | solution.py:233
  18.5 8.3 %collective-permute-start.14 = (bf16[64,512]{1,0:T(8,128)(2,1)S(1)}, bf16[64,512]{1,0:T(8,128)(2,1)S(1)}, u32[]{:S(2)}, u32[]{:S(2)}) collective-permute-start(bf16[64,512]{1,0:T(8,128)(2,1)S(1)} %bitcast.70), channel_id=1, source_target_pairs={{0,4},{1,5},{2,6},{3,7},{4,0},{5,1},{6,2},{7,3},{8,12},{9,13},{10,... | collective-permute-start | bytes 196616 | tf_op jit(solution)/shard_map/ppermute | solution.py:233
  21.0 6.9 %collective-permute-start.15 = (bf16[64,512]{1,0:T(8,128)(2,1)S(1)}, bf16[64,512]{1,0:T(8,128)(2,1)}, u32[]{:S(2)}, u32[]{:S(2)}) collective-permute-start(bf16[64,512]{1,0:T(8,128)(2,1)S(1)} %bitcast.71), channel_id=1, source_target_pairs={{0,6},{1,7},{2,4},{3,5},{4,2},{5,3},{6,0},{7,1},{8,14},{9,15},{10,... | collective-permute-start | bytes 196616 | tf_op jit(solution)/shard_map/ppermute | solution.py:233
  22.3 5.7 %collective-permute-start.6 = (bf16[64,512]{1,0:T(8,128)(2,1)S(1)}, bf16[64,512]{1,0:T(8,128)(2,1)S(1)}, u32[]{:S(2)}, u32[]{:S(2)}) collective-permute-start(bf16[64,512]{1,0:T(8,128)(2,1)S(1)} %fusion.9.refs_0_), channel_id=1, source_target_pairs={{0,2},{1,3},{2,0},{3,1},{4,6},{5,7},{6,4},{7,5},{8,10},{9,11},{10,... | collective-permute-start | bytes 196616 | tf_op jit(solution)/shard_map/ppermute | solution.py:233
  23.9 7.1 %collective-permute-start.7 = (bf16[64,512]{1,0:T(8,128)(2,1)S(1)}, bf16[64,512]{1,0:T(8,128)(2,1)S(1)}, u32[]{:S(2)}, u32[]{:S(2)}) collective-permute-start(bf16[64,512]{1,0:T(8,128)(2,1)S(1)} %fusion.9.refs_0_), channel_id=1, source_target_pairs={{0,4},{1,5},{2,6},{3,7},{4,0},{5,1},{6,2},{7,3},{8,12},{9,13},{10,... | collective-permute-start | bytes 196616 | tf_op jit(solution)/shard_map/ppermute | solution.py:233
  26.5 6.1 %collective-permute-start.8 = (bf16[64,512]{1,0:T(8,128)(2,1)S(1)}, bf16[64,512]{1,0:T(8,128)(2,1)S(1)}, u32[]{:S(2)}, u32[]{:S(2)}) collective-permute-start(bf16[64,512]{1,0:T(8,128)(2,1)S(1)} %fusion.9.refs_0_), channel_id=1, source_target_pairs={{0,6},{1,7},{2,4},{3,5},{4,2},{5,3},{6,0},{7,1},{8,14},{9,15},{10,... | collective-permute-start | bytes 196616 | tf_op jit(solution)/shard_map/ppermute | solution.py:233
  26.7 5.8 %collective-permute-start.16 = (bf16[64,512]{1,0:T(8,128)(2,1)S(1)}, bf16[64,512]{1,0:T(8,128)(2,1)S(1)}, u32[]{:S(2)}, u32[]{:S(2)}) collective-permute-start(bf16[64,512]{1,0:T(8,128)(2,1)S(1)} %bitcast.72), channel_id=1, source_target_pairs={{0,1},{1,0},{2,3},{3,2},{4,5},{5,4},{6,7},{7,6},{8,9},{9,8},{10,11... | collective-permute-start | bytes 196616 | tf_op jit(solution)/shard_map/ppermute | solution.py:233
  34.3 28.5 %collective-permute-start.23 = (bf16[1280,256]{1,0:T(8,128)(2,1)S(1)}, bf16[1280,256]{1,0:T(8,128)(2,1)S(1)}, u32[]{:S(2)}, u32[]{:S(2)}) collective-permute-start(bf16[1280,256]{1,0:T(8,128)(2,1)S(1)} %constant_dynamic-slice_fusion), channel_id=1, source_target_pairs={{0,8},{8,0},{16,24},{24,16},{1,9},{9,1},{17,25},{25,17},{2,10},{10... | collective-permute-start | bytes 1966088 | tf_op jit(solution)/shard_map/ppermute | solution.py:233
  35.8 27.0 %collective-permute-start.24 = (bf16[1280,256]{1,0:T(8,128)(2,1)S(1)}, bf16[1280,256]{1,0:T(8,128)(2,1)S(1)}, u32[]{:S(2)}, u32[]{:S(2)}) collective-permute-start(bf16[1280,256]{1,0:T(8,128)(2,1)S(1)} %constant_dynamic-slice_fusion), channel_id=1, source_target_pairs={{0,16},{8,24},{16,0},{24,8},{1,17},{9,25},{17,1},{25,9},{2,18},{10... | collective-permute-start | bytes 1966088 | tf_op jit(solution)/shard_map/ppermute | solution.py:233
  36.5 26.2 %collective-permute-start.20 = (bf16[320,256]{1,0:T(8,128)(2,1)S(1)}, bf16[320,256]{1,0:T(8,128)(2,1)S(1)}, u32[]{:S(2)}, u32[]{:S(2)}) collective-permute-start(bf16[320,256]{1,0:T(8,128)(2,1)S(1)} %get-tuple-element.99), channel_id=1, source_target_pairs={{0,2},{1,3},{2,0},{3,1},{4,6},{5,7},{6,4},{7,5},{8,10},{9,11},{10,... | collective-permute-start | bytes 491528 | tf_op jit(solution)/shard_map/ppermute | solution.py:233
  36.6 26.2 %collective-permute-start.21 = (bf16[320,256]{1,0:T(8,128)(2,1)S(1)}, bf16[320,256]{1,0:T(8,128)(2,1)S(1)}, u32[]{:S(2)}, u32[]{:S(2)}) collective-permute-start(bf16[320,256]{1,0:T(8,128)(2,1)S(1)} %get-tuple-element.100), channel_id=1, source_target_pairs={{0,4},{1,5},{2,6},{3,7},{4,0},{5,1},{6,2},{7,3},{8,12},{9,13},{10,... | collective-permute-start | bytes 491528 | tf_op jit(solution)/shard_map/ppermute | solution.py:233
  38.8 24.0 %collective-permute-start.22 = (bf16[320,256]{1,0:T(8,128)(2,1)S(1)}, bf16[320,256]{1,0:T(8,128)(2,1)S(1)}, u32[]{:S(2)}, u32[]{:S(2)}) collective-permute-start(bf16[320,256]{1,0:T(8,128)(2,1)S(1)} %get-tuple-element.101), channel_id=1, source_target_pairs={{0,6},{1,7},{2,4},{3,5},{4,2},{5,3},{6,0},{7,1},{8,14},{9,15},{10,... | collective-permute-start | bytes 491528 | tf_op jit(solution)/shard_map/ppermute | solution.py:233
  63.4 12.3 %collective-permute-start.30 = (bf16[1280,256]{1,0:T(8,128)(2,1)S(1)}, bf16[1280,256]{1,0:T(8,128)(2,1)S(1)}, u32[]{:S(2)}, u32[]{:S(2)}) collective-permute-start(bf16[1280,256]{1,0:T(8,128)(2,1)S(1)} %collective-permute-done.23.refs_2_), channel_id=1, source_target_pairs={{0,1},{1,0},{2,3},{3,2},{4,5},{5,4},{6,7},{7,6},{8,9},{9,8},{10,11... | collective-permute-start | bytes 1966088 | tf_op jit(solution)/shard_map/ppermute | solution.py:233
  63.5 12.2 %collective-permute-start.31 = (bf16[1280,256]{1,0:T(8,128)(2,1)S(1)}, bf16[1280,256]{1,0:T(8,128)(2,1)S(1)}, u32[]{:S(2)}, u32[]{:S(2)}) collective-permute-start(bf16[1280,256]{1,0:T(8,128)(2,1)S(1)} %collective-permute-done.24.refs_3_), channel_id=1, source_target_pairs={{0,1},{1,0},{2,3},{3,2},{4,5},{5,4},{6,7},{7,6},{8,9},{9,8},{10,11... | collective-permute-start | bytes 1966088 | tf_op jit(solution)/shard_map/ppermute | solution.py:233
  66.1 6.8 %collective-permute-start.28 = (bf16[64,512]{1,0:T(8,128)(2,1)S(1)}, bf16[64,512]{1,0:T(8,128)(2,1)S(1)}, u32[]{:S(2)}, u32[]{:S(2)}) collective-permute-start(bf16[64,512]{1,0:T(8,128)(2,1)S(1)} %get-tuple-element.161), channel_id=1, source_target_pairs={{0,6},{1,7},{2,4},{3,5},{4,2},{5,3},{6,0},{7,1},{8,14},{9,15},{10,... | collective-permute-start | bytes 196616 | tf_op jit(solution)/shard_map/ppermute | solution.py:233
  67.9 7.1 %collective-permute-start.27 = (bf16[64,512]{1,0:T(8,128)(2,1)S(1)}, bf16[64,512]{1,0:T(8,128)(2,1)S(1)}, u32[]{:S(2)}, u32[]{:S(2)}) collective-permute-start(bf16[64,512]{1,0:T(8,128)(2,1)S(1)} %get-tuple-element.162), channel_id=1, source_target_pairs={{0,4},{1,5},{2,6},{3,7},{4,0},{5,1},{6,2},{7,3},{8,12},{9,13},{10,... | collective-permute-start | bytes 196616 | tf_op jit(solution)/shard_map/ppermute | solution.py:233
  67.9 7.1 %collective-permute-start.26 = (bf16[64,512]{1,0:T(8,128)(2,1)S(1)}, bf16[64,512]{1,0:T(8,128)(2,1)S(1)}, u32[]{:S(2)}, u32[]{:S(2)}) collective-permute-start(bf16[64,512]{1,0:T(8,128)(2,1)S(1)} %get-tuple-element.160), channel_id=1, source_target_pairs={{0,2},{1,3},{2,0},{3,1},{4,6},{5,7},{6,4},{7,5},{8,10},{9,11},{10,... | collective-permute-start | bytes 196616 | tf_op jit(solution)/shard_map/ppermute | solution.py:233
  82.2 5.8 %collective-permute-start.32 = (bf16[64,512]{1,0:T(8,128)(2,1)}, bf16[64,512]{1,0:T(8,128)(2,1)}, u32[]{:S(2)}, u32[]{:S(2)}) collective-permute-start(bf16[64,512]{1,0:T(8,128)(2,1)} %slice.47), channel_id=1, source_target_pairs={{0,2},{1,3},{2,0},{3,1},{4,6},{5,7},{6,4},{7,5},{8,10},{9,11},{10,... | collective-permute-start | bytes 196616 | tf_op jit(solution)/shard_map/ppermute | solution.py:233
  82.2 6.4 %collective-permute-start.33 = (bf16[64,512]{1,0:T(8,128)(2,1)S(1)}, bf16[64,512]{1,0:T(8,128)(2,1)}, u32[]{:S(2)}, u32[]{:S(2)}) collective-permute-start(bf16[64,512]{1,0:T(8,128)(2,1)S(1)} %fusion.7.refs_0_), channel_id=1, source_target_pairs={{0,2},{1,3},{2,0},{3,1},{4,6},{5,7},{6,4},{7,5},{8,10},{9,11},{10,... | collective-permute-start | bytes 196616 | tf_op jit(solution)/shard_map/ppermute | solution.py:233
  84.2 8.0 %collective-permute-start.34 = (bf16[64,512]{1,0:T(8,128)(2,1)S(1)}, bf16[64,512]{1,0:T(8,128)(2,1)}, u32[]{:S(2)}, u32[]{:S(2)}) collective-permute-start(bf16[64,512]{1,0:T(8,128)(2,1)S(1)} %fusion.7.refs_0_), channel_id=1, source_target_pairs={{0,4},{1,5},{2,6},{3,7},{4,0},{5,1},{6,2},{7,3},{8,12},{9,13},{10,... | collective-permute-start | bytes 196616 | tf_op jit(solution)/shard_map/ppermute | solution.py:233
  84.8 7.4 %collective-permute-start.35 = (bf16[64,512]{1,0:T(8,128)(2,1)S(1)}, bf16[64,512]{1,0:T(8,128)(2,1)}, u32[]{:S(2)}, u32[]{:S(2)}) collective-permute-start(bf16[64,512]{1,0:T(8,128)(2,1)S(1)} %fusion.7.refs_0_), channel_id=1, source_target_pairs={{0,6},{1,7},{2,4},{3,5},{4,2},{5,3},{6,0},{7,1},{8,14},{9,15},{10,... | collective-permute-start | bytes 196616 | tf_op jit(solution)/shard_map/ppermute | solution.py:233
  95.7 13.4 %collective-permute-start.40 = (bf16[256,512]{1,0:T(8,128)(2,1)S(1)}, bf16[256,512]{1,0:T(8,128)(2,1)S(1)}, u32[]{:S(2)}, u32[]{:S(2)}) collective-permute-start(bf16[256,512]{1,0:T(8,128)(2,1)S(1)} %constant_dynamic-update-slice_fusion), channel_id=1, source_target_pairs={{0,16},{8,24},{16,0},{24,8},{1,17},{9,25},{17,1},{25,9},{2,18},{10... | collective-permute-start | bytes 786440 | tf_op jit(solution)/shard_map/ppermute | solution.py:233
  97.0 12.3 %collective-permute-start.39 = (bf16[256,512]{1,0:T(8,128)(2,1)S(1)}, bf16[256,512]{1,0:T(8,128)(2,1)S(1)}, u32[]{:S(2)}, u32[]{:S(2)}) collective-permute-start(bf16[256,512]{1,0:T(8,128)(2,1)S(1)} %constant_dynamic-update-slice_fusion), channel_id=1, source_target_pairs={{0,8},{8,0},{16,24},{24,16},{1,9},{9,1},{17,25},{25,17},{2,10},{10... | collective-permute-start | bytes 786440 | tf_op jit(solution)/shard_map/ppermute | solution.py:233
  97.6 9.7 %collective-permute-start.37 = (bf16[192,512]{1,0:T(8,128)(2,1)S(1)}, bf16[192,512]{1,0:T(8,128)(2,1)S(1)}, u32[]{:S(2)}, u32[]{:S(2)}) collective-permute-start(bf16[192,512]{1,0:T(8,128)(2,1)S(1)} %pad_maximum_fusion), channel_id=1, source_target_pairs={{0,24},{8,16},{16,8},{24,0},{1,25},{9,17},{17,9},{25,1},{2,26},{10... | collective-permute-start | bytes 589832 | tf_op jit(solution)/shard_map/ppermute | solution.py:233
  100.3 9.5 %collective-permute-start.41 = (bf16[64,512]{1,0:T(8,128)(2,1)S(1)}, bf16[64,512]{1,0:T(8,128)(2,1)S(1)}, u32[]{:S(2)}, u32[]{:S(2)}) collective-permute-start(bf16[64,512]{1,0:T(8,128)(2,1)S(1)} %get-tuple-element.159), channel_id=1, source_target_pairs={{0,4},{1,5},{2,6},{3,7},{4,0},{5,1},{6,2},{7,3},{8,12},{9,13},{10,... | collective-permute-start | bytes 196616 | tf_op jit(solution)/shard_map/ppermute | solution.py:233
  101.8 8.0 %collective-permute-start.42 = (bf16[64,512]{1,0:T(8,128)(2,1)S(1)}, bf16[64,512]{1,0:T(8,128)(2,1)S(1)}, u32[]{:S(2)}, u32[]{:S(2)}) collective-permute-start(bf16[64,512]{1,0:T(8,128)(2,1)S(1)} %get-tuple-element.158), channel_id=1, source_target_pairs={{0,6},{1,7},{2,4},{3,5},{4,2},{5,3},{6,0},{7,1},{8,14},{9,15},{10,... | collective-permute-start | bytes 196616 | tf_op jit(solution)/shard_map/ppermute | solution.py:233
  107.3 6.2 %collective-permute-start.38 = (bf16[64,1280]{1,0:T(8,128)(2,1)S(1)}, bf16[64,1280]{1,0:T(8,128)(2,1)S(1)}, u32[]{:S(2)}, u32[]{:S(2)}) collective-permute-start(bf16[64,1280]{1,0:T(8,128)(2,1)S(1)} %get-tuple-element.133), channel_id=1, source_target_pairs={{0,24},{8,16},{16,8},{24,0},{1,25},{9,17},{17,9},{25,1},{2,26},{10... | collective-permute-start | bytes 491528 | tf_op jit(solution)/shard_map/ppermute | solution.py:233
  (53 other events, 340.3 us)
